TPU v7x, 256 devices: a whole 4x4x8 slice. The times are simulated.
256 devices in a mesh: ctx: 16 (over y_lo, z), tp: 16 (over x, y_hi, core).
Axes of the slice: x: 4, y: 4 (y_hi: 2, y_lo: 2; y = y_hi * 2 + y_lo), z: 8, core: 2. Of those that a mesh axis runs over, the one named last changes fastest.
Arguments:
- tokens: bfloat16 [8192, 4096], P('ctx', 'tp'), may hold values from -6 to 6
- seg_ids: int32 [8192], P('ctx'), may hold values from 0 to 5, never falling along the last dimension, each value on 1 to 4096 neighbouring positions
- w_x: bfloat16 [4096, 8192], P(None, 'tp'), may hold values from -0.09375 to 0.09375
- w_z: bfloat16 [4096, 8192], P(None, 'tp'), may hold values from -0.09375 to 0.09375
- w_bc: bfloat16 [4096, 2048], P('tp'), may hold values from -0.09375 to 0.09375
- w_dt: bfloat16 [4096, 128], P('tp'), may hold values from -0.09375 to 0.09375
- conv_x: float32 [4, 8192], P(None, 'tp'), may hold values from -3 to 3
- conv_x_bias: float32 [8192], P('tp'), may hold values from -3 to 3
- conv_bc: float32 [4, 2048], replicated, may hold values from -3 to 3
- conv_bc_bias: float32 [2048], replicated, may hold values from -3 to 3
- dt_bias: float32 [128], P('tp'), may hold values from -2 to 1
- decay_rate: float32 [128], P('tp'), may hold values from 1.2207031e-06 to 0.03
- skip_gain: float32 [128], P('tp'), may hold values from 0.5 to 1.5
- norm_weight: float32 [8192], P('tp'), may hold values from 0.5 to 1.5
- w_out: bfloat16 [8192, 4096], P('tp', 'ctx'), may hold values from -0.09375 to 0.09375
Outputs:
- mixed: bfloat16 [8192, 4096], P('ctx', 'tp')
Inputs may be any that keep to these rules, and one draw needn't show every extreme that they name: `seg_ids`: document ids never fall along the sequence, start at 0 and rise by one where a document starts; one document covers 8192 / 2 tokens.
All inputs are finite; a program needn't handle non-finite values.
Results may differ from a plain program's by a relative error of at most 0.015.
Values may be sent and summed in bfloat16 or wider, within the bound.
No kernel may reach another device: no remote copies, remote signals or barrier semaphores. Data moves between devices by JAX's collectives and lax.ppermute only.
A program may use at most 128 MiB of HBM per device.

v0:
```python
import jax
import jax.numpy as jnp
import numpy as np
from jax import lax
from jax.sharding import PartitionSpec as P

H = 128
P_SIZE = 64
N = 128
G = 8
L = 256
CONV = 4


NORM_EPS = 1e-05
HIGHEST_PRECISION = lax.Precision.HIGHEST


def passed_along(value, axis, steps):
    count = lax.axis_size(axis)
    first, last = (max(0, -steps), min(count, count - steps))
    return lax.ppermute(value, axis, [(source, source + steps) for source in range(first, last)])


def prefix(value, axis, join, neutral):
    count, mine = (lax.axis_size(axis), lax.axis_index(axis))
    pieces = jax.tree.map(lambda part: lax.all_gather(part, axis), value)
    total = jax.tree.map(
        lambda part, zero: jnp.full_like(part, 0) + jnp.asarray(zero, part.dtype), value, neutral
    )

    def step(position, total):
        longer = join(total, jax.tree.map(lambda part: part[position], pieces))
        return jax.tree.map(lambda new, old: jnp.where(position < mine, new, old), longer, total)

    return lax.fori_loop(0, count - 1, step, total)


def causal_conv(values, seg_now, prior_vals, prior_seg, taps, offsets):
    padded = jnp.concatenate([prior_vals, values], axis=0).astype(jnp.float32)
    padded_seg = jnp.concatenate([prior_seg, seg_now], axis=0)
    num_rows = values.shape[0]
    summed = jnp.zeros(values.shape, jnp.float32) + offsets[None, :]
    for tap in range(taps.shape[0]):
        shifted = padded[tap : tap + num_rows]
        same_doc = (padded_seg[tap : tap + num_rows] == seg_now).astype(jnp.float32)[:, None]
        summed = summed + taps[tap][None, :] * shifted * same_doc
    return jax.nn.silu(summed).astype(jnp.bfloat16)


def stretch_pass(state_now, prior_id, x_vals, b_vals, c_vals, dt_vals, log_vals, seg_now):
    length = seg_now.shape[0]
    cum_decay = jnp.cumsum(log_vals, axis=0)
    positions = jnp.arange(length)
    causal = (positions[:, None] >= positions[None, :]) & (seg_now[:, None] == seg_now[None, :])
    causal_full = causal[:, :, None, None]
    gaps = cum_decay[:, None] - cum_decay[None, :]
    decays = jnp.where(causal_full, jnp.exp(jnp.where(causal_full, gaps, 0.0)), 0.0)
    scores = jnp.einsum("tgn,sgn->tsg", c_vals, b_vals, preferred_element_type=jnp.float32)
    weights = (scores[:, :, :, None] * decays * dt_vals[None]).astype(jnp.bfloat16)
    intra_out = jnp.einsum("tsgh,sghp->tghp", weights, x_vals, preferred_element_type=jnp.float32)
    c_float = c_vals.astype(jnp.float32)
    carried = jnp.exp(cum_decay) * (seg_now == prior_id).astype(jnp.float32)[:, None, None]
    inter_out = (
        jnp.einsum("tgn,ghpn->tghp", c_float, state_now, precision=HIGHEST_PRECISION)
        * carried[..., None]
    )
    last_id = seg_now[length - 1]
    tail_decay = (
        jnp.exp(cum_decay[length - 1][None] - cum_decay)
        * (seg_now == last_id).astype(jnp.float32)[:, None, None]
        * dt_vals
    )
    scaled_x = x_vals.astype(jnp.float32) * tail_decay[..., None]
    fresh_state = jnp.einsum(
        "sghp,sgn->ghpn", scaled_x, b_vals.astype(jnp.float32), precision=HIGHEST_PRECISION
    )
    new_state = carried[length - 1][..., None, None] * state_now + fresh_state
    return (new_state, intra_out + inter_out)


def run_stretches(state_now, prior_id, x_vals, b_vals, c_vals, dt_vals, log_vals, seg_now):
    num_stretches = seg_now.shape[0] // L

    def stretch_step(carry_pair, pieces):
        new_state, outputs = stretch_pass(carry_pair[0], carry_pair[1], *pieces)
        return ((new_state, pieces[5][L - 1]), outputs)

    shaped = tuple(
        (
            member.reshape((num_stretches, L) + member.shape[1:])
            for member in (x_vals, b_vals, c_vals, dt_vals, log_vals, seg_now)
        )
    )
    carry_end, outputs = lax.scan(stretch_step, (state_now, prior_id), shaped)
    return (carry_end[0], outputs.reshape((num_stretches * L,) + outputs.shape[2:]))


def column_table(tp_size):
    heads_dev = H // tp_size
    group_heads = H // G
    groups_dev = max(1, heads_dev // group_heads)
    members = np.arange(tp_size)
    firsts = members * heads_dev // group_heads
    bc_cols = firsts[:, None] * 2 * N + np.arange(groups_dev * 2 * N)[None, :]
    dt_cols = 2 * G * N + members[:, None] * heads_dev + np.arange(heads_dev)[None, :]
    return np.concatenate([bc_cols, dt_cols], axis=1).reshape(-1).astype(np.int32)


def combine_states(earlier, later):
    return (earlier[0] * later[0], later[0][..., None, None] * earlier[1] + later[1])


def local(
    tokens,
    seg_ids,
    w_x,
    w_z,
    w_bc,
    w_dt,
    conv_x,
    conv_x_bias,
    conv_bc,
    conv_bc_bias,
    dt_bias,
    decay_rate,
    skip_gain,
    norm_weight,
    w_out,
):
    tp_size = lax.axis_size("tp")
    tp_rank = lax.axis_index("tp")
    heads_dev = H // tp_size
    group_heads = H // G
    head_block = min(heads_dev, group_heads)
    groups_dev = heads_dev // head_block
    bc_width = groups_dev * 2 * N
    tok_rows = tokens.shape[0]
    inner_dev = w_x.shape[1]
    first_group = tp_rank * heads_dev // group_heads
    w_joined = jnp.concatenate([w_bc, w_dt], axis=1)
    w_spread = jnp.take(w_joined, jnp.asarray(column_table(tp_size)), axis=1)
    part_in = lax.all_gather(tokens, "tp", axis=1, tiled=True)
    x_acc = jnp.dot(part_in, w_x, preferred_element_type=jnp.float32)
    z_acc = jnp.dot(part_in, w_z, preferred_element_type=jnp.float32)
    col_block = lax.slice_in_dim(w_spread, 0, lax.axis_size("tp") * (bc_width + heads_dev), axis=1)
    bc_dt = lax.psum_scatter(
        lax.dot_general(
            col_block, tokens, (((0,), (1,)), ((), ())), preferred_element_type=jnp.float32
        ),
        "tp",
        scatter_dimension=0,
        tiled=True,
    ).T
    x_raw = x_acc.astype(jnp.bfloat16)
    z_raw = z_acc.astype(jnp.bfloat16)
    bc_raw = bc_dt[:, :bc_width].astype(jnp.bfloat16)
    dt_raw = bc_dt[:, bc_width:]
    rim_rows = CONV - 1
    x_prior, bc_prior = passed_along(
        (x_raw[tok_rows - rim_rows :], bc_raw[tok_rows - rim_rows :]), "ctx", 1
    )
    ids_sent = passed_along(seg_ids[tok_rows - rim_rows :] + 1, "ctx", 1)
    ids_prior = ids_sent - 1
    bc_taps = lax.dynamic_slice_in_dim(conv_bc, first_group * 2 * N, bc_width, 1)
    bc_offsets = lax.dynamic_slice_in_dim(conv_bc_bias, first_group * 2 * N, bc_width, 0)
    x_conv = causal_conv(x_raw, seg_ids, x_prior, ids_prior, conv_x, conv_x_bias)
    bc_conv = causal_conv(bc_raw, seg_ids, bc_prior, ids_prior, bc_taps, bc_offsets)
    dt_vals = jax.nn.softplus(dt_raw + dt_bias[None, :])
    log_vals = -decay_rate[None, :] * dt_vals
    shape_heads = (tok_rows, groups_dev, head_block)
    x_vals = x_conv.reshape(shape_heads + (P_SIZE,))
    bc_four = bc_conv.reshape(tok_rows, groups_dev, 2, N)
    b_vals = bc_four[:, :, 0]
    c_vals = bc_four[:, :, 1]
    dt_heads = dt_vals.reshape(shape_heads)
    log_heads = log_vals.reshape(shape_heads)
    prior_id = ids_prior[rim_rows - 1]
    zero_state = jnp.zeros((groups_dev, head_block, P_SIZE, N), jnp.float32)
    local_final, y_zero = run_stretches(
        zero_state, prior_id, x_vals, b_vals, c_vals, dt_heads, log_heads, seg_ids
    )
    slab_factor = jnp.exp(jnp.sum(log_heads, axis=0)) * (seg_ids[tok_rows - 1] == prior_id).astype(
        jnp.float32
    )
    identity = (jnp.ones_like(slab_factor), jnp.zeros_like(local_final))
    factor_in, state_in = prefix((slab_factor, local_final), "ctx", combine_states, identity)
    final_again, y_ssd = run_stretches(
        state_in, prior_id, x_vals, b_vals, c_vals, dt_heads, log_heads, seg_ids
    )
    y_all = y_ssd + skip_gain.reshape(groups_dev, head_block)[None, :, :, None] * x_vals.astype(
        jnp.float32
    )
    gated = y_all * jax.nn.silu(z_raw.astype(jnp.float32)).reshape(shape_heads + (P_SIZE,))
    head_sq = jnp.sum(gated * gated, axis=3).reshape(tok_rows, heads_dev)
    head_group = (tp_rank * heads_dev + jnp.arange(heads_dev)) // group_heads
    member_of = (head_group[:, None] == jnp.arange(G)[None, :]).astype(jnp.float32)
    group_sq = jnp.dot(head_sq, member_of, precision=HIGHEST_PRECISION)
    group_sq = lax.psum(group_sq, "tp")
    mean_sq = jnp.dot(group_sq, member_of.T, precision=HIGHEST_PRECISION) / (group_heads * P_SIZE)
    scale_rows = lax.rsqrt(mean_sq + NORM_EPS).reshape(shape_heads)
    normed = (gated * scale_rows[..., None]).reshape(tok_rows, inner_dev) * norm_weight[None, :]
    normed = normed.astype(jnp.bfloat16)
    partial_out = jnp.dot(
        normed, lax.all_gather(w_out, "ctx", axis=1, tiled=True), preferred_element_type=jnp.float32
    )
    mixed = lax.psum_scatter(partial_out, "tp", scatter_dimension=1, tiled=True)
    return mixed.astype(jnp.bfloat16)


def solution(mesh):
    return jax.shard_map(
        local,
        mesh=mesh,
        in_specs=(
            P("ctx", "tp"),
            P("ctx"),
            P(None, "tp"),
            P(None, "tp"),
            P("tp", None),
            P("tp", None),
            P(None, "tp"),
            P("tp"),
            P(),
            P(),
            P("tp"),
            P("tp"),
            P("tp"),
            P("tp"),
            P("tp", "ctx"),
        ),
        out_specs=P("ctx", "tp"),
        check_vma=False,
    )
```

profile of v0, /device:TPU:1, one launch (start us, length us, event | category | flops | bytes accessed | tf_op | source)
XLA Modules:
  0.0 512.0 jit_solution(2688863102592803506)
XLA Ops:
  7.3 1.5 copy.78
  9.0 12.8 %gather_fusion = bf16[4224,256]{1,0:T(8,128)(2,1)S(1)} fusion(bf16[256,2176]{0,1:T(8,128)(2,1)S(1)} %pad_maximum_fusion, s32[5120]{0:T(1024)S(1)} %pad_clamp_fusion), kind=kCustom, calls=%fused_computation | custom fusion | bytes 4342272 | tf_op jit(solution)/shard_map/jit(_take)/gather | solution.py:142
  21.8 5.6 %fusion.81 = f32[4224,512]{1,0:T(8,128)} fusion(bf16[4224,256]{1,0:T(8,128)(2,1)S(1)} %gather_fusion, bf16[512,256]{1,0:T(8,128)(2,1)} %param.22), kind=kOutput, calls=%fused_computation.151 | convolution fusion | flops 1107296256 | bytes 11075584 | tf_op jit(solution)/shard_map/dot_general | solution.py:148
  28.2 4.4 collective-permute-start
  33.4 0.9 constant_dynamic-slice_fusion.2
  34.4 44.0 %all-gather.6.cloned.1.call-done = bf16[512,4096]{1,0:T(8,128)(2,1)} async-done(((bf16[512,256]{1,0:T(8,128)(2,1)}), bf16[512,4096]{1,0:T(8,128)(2,1)}) %all-gather.6.cloned.1.call-update) | async-done | bytes 4194320 | tf_op jit(solution)/shard_map/all_gather | solution.py:143
  78.3 5.8 %convolution_convert_fusion.1 = bf16[512,512]{1,0:T(8,128)(2,1)S(1)} fusion(bf16[512,4096]{1,0:T(8,128)(2,1)} %all-gather.6.cloned.1.call-done, bf16[4096,512]{1,0:T(8,128)(2,1)} %param.24), kind=kOutput, calls=%fused_computation.84 | convolution fusion | flops 2147745792 | bytes 8912896 | tf_op jit(solution)/shard_map/dot_general | solution.py:144
  84.2 3.2 collective-permute-start.1
  90.7 100.8 %reduce-scatter.3.cloned.1.call-done = f32[264,512]{1,0:T(8,128)} async-done(((f32[4224,512]{1,0:T(8,128)}), f32[264,512]{1,0:T(8,128)}) %reduce-scatter.3.cloned.1.call-update) | async-done | bytes 540688 | tf_op jit(solution)/shard_map/reduce_scatter | solution.py:147
  191.5 1.1 bitcast_convert_fusion
  192.7 3.2 collective-permute-start.2
  195.9 0.9 fusion.78
  198.2 9.7 %while.42 = (s32[]{:T(128)}, f32[1,8,64,128]{3,2,1,0:T(8,128)S(1)}, s32[]{:T(128)}, f32[2,256,1,8]{1,3,2,0:T(8,128)S(1)}, s32[2,256]{1,0:T(2,128)S(1)}, /*index=...) while((s32[]{:T(128)}, f32[1,8,64,128]{3,2,1,0:T(8,128)S(1)}, ...), condition=%wide.region_5.6_spmd.clone, body=%wide.region_2.5_spmd.clone.sunk | while | flops 202054688 | bytes 940327 | solution.py:95
  201.0 0.9 multiply_reduce_fusion.3
  205.8 0.9 multiply_reduce_fusion.3
  212.6 5.9 %convert_multiply_fusion = f32[512,512]{1,0:T(8,128)S(1)} fusion(bf16[512,4096]{1,0:T(8,128)(2,1)} %all-gather.6.cloned.1.call-done, bf16[4096,512]{1,0:T(8,128)(2,1)} %param.25), kind=kOutput, calls=%fused_computation.81 | convolution fusion | flops 2149056512 | bytes 9437184 | tf_op jit(solution)/shard_map/dot_general | solution.py:145
  218.6 1.3 copy.96
  219.9 1.2 copy.95
  221.2 29.0 %all-reduce = f32[128]{0:T(128)S(1)} all-reduce(f32[128]{0:T(128)S(1)} %multiply_dynamic-update-slice_fusion), channel_id=2, replica_groups=mesh['ctx'=16,'tp'=16] {'ctx'}, use_global_device_ids=true, to_apply=%add | all-reduce | flops 128 | bytes 1024
  250.4 28.8 %all-gather.10.cloned.1.call-done = f32[16,8,64,128]{3,2,1,0:T(8,128)} async-done(((f32[1,8,64,128]{3,2,1,0:T(8,128)}), f32[16,8,64,128]{3,2,1,0:T(8,128)}) %all-gather.10.cloned.1.call-update) | async-done | bytes 4194320 | tf_op jit(solution)/shard_map/all_gather | solution.py:27
  279.2 16.3 %while.43 = (s32[]{:T(128)}, f32[1,8,64,128]{3,2,1,0:T(8,128)S(1)}, s32[]{:T(128)}, f32[16,1,8]{2,1,0:T(1,128)S(1)}, f32[16,1,8,64,128]{4,3,2,1,0:T(8,128)}, /*index=5*/s32[]{:T(128)}, s32[]{:T(128)}) while((s32[]{:T(128)}, f32[1,8,64,128]{3,2,1,0:T(8,128)S(1)}, s32[]{:T(128)}, f32[16,1,8]{2,1,0:T(1,128)S(1)}, ...), condition=%wide.region_7.8_spmd.clone, body=%wide.region_6.7_spmd.clone.sunk | while | flops 262148 | bytes 786633 | solution.py:36
  279.2 1.0 fusion.128
  280.3 1.1 fusion.128
  281.4 1.1 fusion.128
  282.5 1.1 fusion.128
  283.5 1.1 fusion.128
  284.6 1.1 fusion.128
  285.7 1.1 fusion.128
  286.8 1.1 fusion.128
  287.9 1.1 fusion.128
  289.0 1.1 fusion.128
  290.1 1.1 fusion.128
  291.2 1.1 fusion.128
  292.3 1.1 fusion.128
  293.4 1.1 fusion.128
  294.5 1.1 fusion.128
  295.5 11.9 %while.41 = (s32[]{:T(128)}, f32[1,8,64,128]{3,2,1,0:T(8,128)S(1)}, s32[]{:T(128)}, f32[2,256,1,8,64]{1,4,3,2,0:T(8,128)}, f32[2,256,1,8]{1,3,2,0:T(8,128)S(1)},...) while((s32[]{:T(128)}, f32[1,8,64,128]{3,2,1,0:T(8,128)S(1)}, ...), condition=%wide.region_11.12_spmd, body=%wide.region_8.11_spmd.sunk | while | flops 490810400 | bytes 4493705 | solution.py:95
  299.1 1.6 fusion.122
  305.0 1.6 fusion.122
  307.5 2.0 copy.99
  309.5 1.5 copy.103
  312.1 69.5 %psum.7 = f32[512,8]{0,1:T(8,128)S(1)} all-reduce(f32[512,8]{0,1:T(8,128)S(1)} %fusion.71), channel_id=1, replica_groups=mesh['ctx'=16,'tp'=16] {'tp'}, use_global_device_ids=true, to_apply=%region_13.14 | all-reduce | flops 4096 | bytes 32768 | tf_op jit(solution)/shard_map/psum | solution.py:199
  381.8 1.1 mul.451
  382.9 2.5 copy.97
  385.5 1.5 reshape.412
  387.0 8.7 %fusion.60 = f32[512,4096]{1,0:T(8,128)} fusion(bf16[512,4096]{1,0:T(8,128)(2,1)} %all-gather.8.cloned.1.call-done, f32[512,512]{1,0:T(8,128)} %copy.97, f32[512,512]{1,0:T(8,128)} %copy-done.1, f32[512,512]{1,0:T(8,128)} %reshape.412, f32[512]{0:T(512)S(1)} %copy-done.5, f32[512]{0:T(512)S(1)} %mul.442, bf16[512,512]{1,0:T(8,128)(2,1)S(1)} %multiply_convert_fusion.3), kind=kOutput, calls=%fused_computation.107 | convolution fusion | flops 2149318656 | bytes 16257024 | tf_op jit(solution)/shard_map/dot_general | solution.py:204
  395.7 108.0 %reduce-scatter.5.cloned.1.call-done = f32[512,256]{1,0:T(8,128)} async-done(((f32[512,4096]{1,0:T(8,128)}), f32[512,256]{1,0:T(8,128)}) %reduce-scatter.5.cloned.1.call-update) | async-done | bytes 524304 | tf_op jit(solution)/shard_map/reduce_scatter | solution.py:207
  503.7 1.8 convert_element_type.134
  (153 shorter events, 25.2 us)
Async XLA Ops:
  6.5 2.4 copy-start.6
  6.5 2.3 copy-start.4
  6.5 71.8 %all-gather.6.cloned.1.call-start = ((), (), s32[]{:S(2)}) async-start(), calls=%async_computation.3 | async-start | bytes 4456448 | tf_op jit(solution)/shard_map/all_gather | solution.py:143
  7.3 184.2 %reduce-scatter.3.cloned.1.call-start = ((), (), s32[]{:S(2)}) async-start(), calls=%async_computation.2 | async-start | bytes 9191424 | tf_op jit(solution)/shard_map/reduce_scatter | solution.py:147
  27.4 0.7 copy-start.7
  27.4 5.2 %copy-start.12 = (f32[8]{0:T(128)S(1)}, f32[8]{0:T(128)}, u32[]{:S(2)}) copy-start(f32[8]{0:T(128)} %param.33) | copy-start | bytes 100
  27.4 6.9 %copy-start.8 = (f32[4,512]{1,0:T(4,128)S(1)}, f32[4,512]{1,0:T(4,128)}, u32[]{:S(2)}) copy-start(f32[4,512]{1,0:T(4,128)} %param.28) | copy-start | bytes 24580
  27.4 251.8 %all-gather.10.cloned.1.call-start = ((), (), s32[]{:S(2)}) async-start(), calls=%async_computation.6 | async-start | bytes 4456448 | tf_op jit(solution)/shard_map/all_gather | solution.py:27
  28.2 6.1 %collective-permute-start = (s32[3]{0:T(128)S(1)}, s32[3]{0:T(128)S(1)}, u32[]{:S(2)}, u32[]{:S(2)}) collective-permute-start(s32[3]{0:T(128)S(1)} %slice_add_fusion.1), channel_id=1, source_target_pairs={{0,16},{16,32},{32,48},{48,64},{64,80},{80,96},{96,112},{112,128},... | collective-permute-start | bytes 44 | tf_op jit(solution)/shard_map/ppermute | solution.py:22
  34.4 54.4 %copy-start.9 = (f32[512]{0:T(512)S(1)}, f32[512]{0:T(512)}, u32[]{:S(2)}) copy-start(f32[512]{0:T(512)} %param.29) | copy-start | bytes 6148
  84.2 4.4 collective-permute-start.1
  89.6 106.3 %copy-start.11 = (f32[8]{0:T(128)S(1)}, f32[8]{0:T(128)}, u32[]{:S(2)}) copy-start(f32[8]{0:T(128)} %param.32) | copy-start | bytes 100
  192.7 4.5 collective-permute-start.2
  198.2 11.7 %copy-start.10 = (f32[8]{0:T(128)S(1)}, f32[8]{0:T(128)}, u32[]{:S(2)}) copy-start(f32[8]{0:T(128)} %param.34) | copy-start | bytes 100
  198.2 11.9 %copy-start.13 = (u32[256]{0:T(256)S(1)}, u32[256]{0:T(256)}, u32[]{:S(2)}) copy-start(u32[256]{0:T(256)} %constant.148) | copy-start | bytes 3076
  207.9 0.7 copy-start
  208.6 178.3 %all-gather.8.cloned.1.call-start = ((), (), s32[]{:S(2)}) async-start(), calls=%async_computation.4 | async-start | bytes 4456448 | tf_op jit(solution)/shard_map/all_gather | solution.py:205
  209.2 294.5 %reduce-scatter.5.cloned.1.call-start = ((), (), s32[]{:S(2)}) async-start(), calls=%async_computation.5 | async-start | bytes 8912896 | tf_op jit(solution)/shard_map/reduce_scatter | solution.py:207
  218.5 31.7 %copy-start.1 = (f32[512,512]{1,0:T(8,128)}, f32[512,512]{1,0:T(8,128)S(1)}, u32[]{:S(2)}) copy-start(f32[512,512]{1,0:T(8,128)S(1)} %convert_multiply_fusion) | copy-start | bytes 3145732
  309.5 1.5 copy-start.2
  309.5 1.8 copy-start.3
  382.9 4.0 copy-start.5
Sparse Core Ops, SparseCore 0:
  9.9 68.3 all-gather.5
  83.0 108.4 reduce-scatter.2
  208.7 70.3 all-gather.9
  280.7 86.5 all-gather.7
  395.9 107.8 reduce-scatter.4
where the time goes:
time: 513 us; the launch traced here: 512 us
  waiting for transfers between devices  283 us (55%)
  blocking collectives  98.5 us (19%)
  local copies, waits for them, and re-layouts  37.8 us (7%)
  matrix products  32.8 us (6%)
  other arithmetic  29.8 us (6%)
  between operations  16 us (3%)
  starting transfers between devices  10.9 us (2%)
    reduce_scatter x1, waiting for transfers between devices, local(): mixed = lax.psum_scatter(partial_out, 'tp', scatter_dimension=1, tiled=True)  108 us
    reduce_scatter x1, waiting for transfers between devices, local(): lax.psum_scatter(lax.dot_general(col_block, tokens, (((0,), (1,)), ((), (...  101 us
    psum x1, blocking collectives, local(): group_sq = lax.psum(group_sq, 'tp')  69.5 us
    all_gather x1, waiting for transfers between devices, local(): part_in = lax.all_gather(tokens, 'tp', axis=1, tiled=True)  44 us
    unnamed x1, blocking collectives  29 us
    all_gather x1, waiting for transfers between devices, prefix(): pieces = jax.tree.map(lambda part: lax.all_gather(part, axis), value)  28.8 us
    select_n x15, other arithmetic, step(): jnp.where(position < mine, new, old)  15.8 us
    gather x1, local copies, waits for them, and re-layouts, local(): w_spread = jnp.take(w_joined, jnp.asarray(column_table(tp_size)), axis=1)  12.8 us
  transfers between devices with their start and end apart: 8, of which 5 were waited for; matrix products, arithmetic and copies ran while one was open for 15% of the time, Pallas kernels for 0%

commit v1 on v0

v1 whole, which is shorter than its diff:
```python
import functools

import jax
import jax.numpy as jnp
from jax import lax
from jax.experimental import pallas as pl
from jax.experimental.pallas import tpu as pltpu
from jax.sharding import PartitionSpec as P

H = 128
P_SIZE = 64
N = 128
G = 8
L = 256
CONV = 4
HALO = 16
NORM_EPS = 1e-05
HIGHEST = lax.Precision.HIGHEST

CHIPS = 8
CORES = 2
HEADS = 8
CH = HEADS * P_SIZE
ROWS = 512
FEAT = 256
X_RING = 4
VMEM = pl.BlockSpec(memory_space=pltpu.VMEM)
BF16 = jnp.bfloat16
F32 = jnp.float32


def params(mib, grid=False):
    more = {"dimension_semantics": ("arbitrary",)} if grid else {}
    return pltpu.CompilerParams(vmem_limit_bytes=mib * 2**20, **more)


def dot(a, b):
    return jnp.dot(a, b, preferred_element_type=F32)


def dot_nt(a, b):
    return lax.dot_general(a, b, (((1,), (1,)), ((), ())), preferred_element_type=F32)


def dot_tn(a, b):
    return lax.dot_general(a, b, (((0,), (0,)), ((), ())), preferred_element_type=F32)


def silu(v):
    return v / (1.0 + jnp.exp(-v))


def spread(cols, first=0, count=HEADS):
    shape = (HEADS, count * P_SIZE)
    head = lax.broadcasted_iota(jnp.int32, shape, 0)
    lane = lax.broadcasted_iota(jnp.int32, shape, 1)
    pick = (head == lane // P_SIZE + first).astype(F32)
    return jnp.dot(cols, pick, precision=HIGHEST, preferred_element_type=F32)


def my_core():
    return lax.rem(lax.axis_index("tp"), CORES)


def add_to(acc, step, value):
    @pl.when(step == 0)
    def _():
        acc[...] = value

    @pl.when(step > 0)
    def _():
        acc[...] += value


def weight_rows(ref, pair, core):
    start = pl.multiple_of(pair * 2 * FEAT + core * FEAT, FEAT)
    return ref[pl.ds(start, FEAT), :]


def conv_chunk(raw, at, rows, masks, taps, offsets):
    total = offsets + taps[CONV - 1 : CONV, :] * raw[at + HALO : at + HALO + rows, :]
    for tap in range(CONV - 1):
        first = at + HALO - (CONV - 1) + tap
        shifted = raw[first : first + rows, :]
        total = total + taps[tap : tap + 1, :] * (shifted * masks[:, tap : tap + 1])
    return silu(total).astype(BF16)


def scan_input_kernel(
    own,
    sib,
    w_x,
    w_own,
    w_sib,
    cols,
    taps_x,
    bias_x,
    taps_bc,
    bias_bc,
    dt_bias,
    decay,
    xc,
    bcc,
    hcol,
    hrow,
    s0,
    pay,
    acc_x,
    acc_bc,
):
    step = pl.program_id(0)
    core = my_core()
    part_x, part_bc = 0.0, 0.0
    for pair in range(own.shape[0]):
        part_x += dot(own[pair], weight_rows(w_x, pair, core))
        part_x += dot(sib[pair], weight_rows(w_x, pair, 1 - core))
        part_bc += dot_nt(own[pair], w_own[pair])
        part_bc += dot_nt(sib[pair], w_sib[pair])
    add_to(acc_x, step, part_x)
    add_to(acc_bc, step, part_bc)

    @pl.when(step == pl.num_programs(0) - 1)
    def _():
        raw_dt = acc_bc[HALO:, 2 * N : 2 * N + 2 * HEADS]
        raw_dt = jnp.where(core == 0, raw_dt[:, :HEADS], raw_dt[:, HEADS:])
        pre = raw_dt + dt_bias[...]
        dt = jnp.maximum(pre, 0.0) + jnp.log1p(jnp.exp(-jnp.abs(pre)))
        loga = -decay[...] * dt
        acc_x[...] = acc_x[...].astype(BF16).astype(F32)
        acc_bc[...] = acc_bc[...].astype(BF16).astype(F32)
        for at in range(0, ROWS, 64):
            masks = cols[at : at + 64, :]
            xc[at : at + 64, :] = conv_chunk(acc_x, at, 64, masks, taps_x, bias_x[...])
            bcc[at : at + 64, :] = conv_chunk(
                acc_bc.at[:, : 2 * N], at, 64, masks, taps_bc, bias_bc[...]
            )
        lower = (
            lax.broadcasted_iota(jnp.int32, (L, L), 0) >= lax.broadcasted_iota(jnp.int32, (L, L), 1)
        ).astype(F32)
        cum0 = jnp.dot(lower, loga[:L], precision=HIGHEST, preferred_element_type=F32)
        cum1 = jnp.dot(lower, loga[L:], precision=HIGHEST, preferred_element_type=F32)
        end0, end1 = cum0[L - 1 :], cum1[L - 1 :]
        slab = jnp.exp(jnp.concatenate([cum0, cum1 + end0], axis=0)) * cols[:, 3:4]
        inner = jnp.exp(cum1) * cols[L:, 5:6]
        tail0 = jnp.exp(end0 - cum0) * cols[:L, 6:7] * dt[:L]
        tail1 = jnp.exp(end1 - cum1) * cols[L:, 4:5] * dt[L:]
        cum = jnp.concatenate([cum0, cum1], axis=0)
        blank = jnp.zeros((ROWS, 128 - 4 * HEADS), F32)
        wide = jnp.concatenate(
            [cum, dt, slab, jnp.concatenate([inner, inner], axis=0), blank], axis=1
        )
        hcol[...] = wide
        hrow[...] = wide.T[: 2 * HEADS]
        scaled0 = (xc[:L, :].astype(F32) * spread(tail0)).astype(BF16)
        scaled1 = (xc[L:, :].astype(F32) * spread(tail1)).astype(BF16)
        state0 = dot_tn(bcc[:L, :N], scaled0)
        state1 = dot_tn(bcc[L:, :N], scaled1)
        s0[...] = state0.astype(BF16)
        ends = jnp.concatenate(
            [inner[L - 1 :], slab[ROWS - 1 :], jnp.zeros((6, HEADS), F32)], axis=0
        )
        ends = spread(ends)
        final = ends[0:1] * state0 + state1
        high = ends[1:2].astype(BF16).astype(F32)
        low = ends[1:2] - high
        row = lax.broadcasted_iota(jnp.int32, (8, CH), 0)
        factor = jnp.where(row == 0, high, jnp.where(row == 1, low, 0.0))
        for piece in range(16):
            pay[piece] = jnp.concatenate(
                [final[8 * piece : 8 * piece + 8], factor], axis=0
            ).astype(BF16)


def scan_input(own, sib, w_x, w_own, w_sib, cols, small):
    steps = 4
    each = CHIPS // steps
    rows = ROWS + HALO
    whole = lambda a: pl.BlockSpec(a.shape, lambda i: (0,) * a.ndim)
    blocks = lambda a: pl.BlockSpec((each,) + a.shape[1:], lambda i: (i, 0, 0))
    shapes = [
        jax.ShapeDtypeStruct((ROWS, CH), BF16),
        jax.ShapeDtypeStruct((ROWS, 2 * N), BF16),
        jax.ShapeDtypeStruct((ROWS, 128), F32),
        jax.ShapeDtypeStruct((2 * HEADS, ROWS), F32),
        jax.ShapeDtypeStruct((N, CH), BF16),
        jax.ShapeDtypeStruct((16, 16, CH), BF16),
    ]
    return pl.pallas_call(
        scan_input_kernel,
        grid=(steps,),
        in_specs=[
            blocks(own),
            blocks(sib),
            pl.BlockSpec((each * 2 * FEAT, CH), lambda i: (i, 0)),
            blocks(w_own),
            blocks(w_sib),
            whole(cols),
        ]
        + [whole(a) for a in small],
        out_specs=[whole(a) for a in shapes],
        out_shape=shapes,
        scratch_shapes=[
            pltpu.VMEM((rows, CH), F32),
            pltpu.VMEM((rows, 2 * N + 2 * HEADS), F32),
        ],
        compiler_params=params(40, True),
        cost_estimate=pl.CostEstimate(
            flops=2 * rows * 4096 * (CH + 272), bytes_accessed=12 * 2**20, transcendentals=10**6
        ),
        name="scan_input",
    )(own, sib, w_x, w_own, w_sib, cols, *small)


def intra_kernel(xc, bcc, hcol, hrow, s0, cols, seg_row, skip, y):
    for block in range(2):
        at = block * L
        b_vals, c_vals = bcc[at : at + L, :N], bcc[at : at + L, N:]
        after = lax.broadcasted_iota(jnp.int32, (L, L), 0) >= lax.broadcasted_iota(
            jnp.int32, (L, L), 1
        )
        same = cols[at : at + L, 7:8] == seg_row[0:1, at : at + L]
        scores = jnp.where(after & same, dot_nt(c_vals, b_vals), 0.0)
        for half in range(2):
            lanes = slice(half * 256, half * 256 + 256)
            weights, values = [], []
            x_half = xc[at : at + L, lanes]
            head_of = lax.broadcasted_iota(jnp.int32, (1, 256), 1) // P_SIZE
            for part in range(4):
                head = half * 4 + part
                gap = hcol[at : at + L, head : head + 1] - hrow[head : head + 1, at : at + L]
                decay = jnp.exp(jnp.minimum(gap, 0.0))
                dt_row = hrow[HEADS + head : HEADS + head + 1, at : at + L]
                weights.append((scores * decay * dt_row).astype(BF16))
                values.append(x_half * (head_of == part).astype(BF16))
            out = dot(jnp.concatenate(weights, axis=1), jnp.concatenate(values, axis=0))
            out = out + skip[:, lanes] * x_half.astype(F32)
            if block == 1:
                carried = spread(hcol[at : at + L, 3 * HEADS : 4 * HEADS], half * 4, 4)
                out = out + carried * dot(c_vals, s0[:, lanes])
            y[at : at + L, lanes] = out


def intra(*args):
    return pl.pallas_call(
        intra_kernel,
        in_specs=[VMEM] * len(args),
        out_specs=VMEM,
        out_shape=jax.ShapeDtypeStruct((ROWS, CH), F32),
        compiler_params=params(24),
        cost_estimate=pl.CostEstimate(
            flops=2 * ROWS * L * CH * 4, bytes_accessed=4 * 2**20, transcendentals=2 * 10**6
        ),
        name="intra",
    )(*args)


def gate_kernel(own, sib, w_z, out, acc):
    step = pl.program_id(0)
    core = my_core()
    part = 0.0
    for pair in range(own.shape[0]):
        part += dot(own[pair, HALO:, :], weight_rows(w_z, pair, core))
        part += dot(sib[pair, HALO:, :], weight_rows(w_z, pair, 1 - core))
    add_to(acc, step, part)

    @pl.when(step == pl.num_programs(0) - 1)
    def _():
        for at in range(0, ROWS, 64):
            out[at : at + 64, :] = silu(acc[at : at + 64, :].astype(BF16).astype(F32))


def gate(own, sib, w_z):
    steps = 4
    each = CHIPS // steps
    blocks = pl.BlockSpec((each,) + own.shape[1:], lambda i: (i, 0, 0))
    return pl.pallas_call(
        gate_kernel,
        grid=(steps,),
        in_specs=[blocks, blocks, pl.BlockSpec((each * 2 * FEAT, CH), lambda i: (i, 0))],
        out_specs=pl.BlockSpec((ROWS, CH), lambda i: (0, 0)),
        out_shape=jax.ShapeDtypeStruct((ROWS, CH), F32),
        scratch_shapes=[pltpu.VMEM((ROWS, CH), F32)],
        compiler_params=params(24, True),
        cost_estimate=pl.CostEstimate(
            flops=2 * ROWS * 4096 * CH, bytes_accessed=9 * 2**20, transcendentals=3 * 10**5
        ),
        name="gate",
    )(own, sib, w_z)


def prefix_kernel(pieces, out):
    total = jnp.zeros((8, CH), F32)
    for pair in range(8):
        held = []
        for place in (2 * pair, 2 * pair + 1):
            held.append(total)
            piece = pieces[place].astype(F32)
            total = total * (piece[8:9] + piece[9:10]) + piece[:8]
        out[16 * pair : 16 * pair + 16, :] = jnp.concatenate(held, axis=0).astype(BF16)


def prefix(pieces):
    return pl.pallas_call(
        prefix_kernel,
        in_specs=[VMEM],
        out_specs=VMEM,
        out_shape=jax.ShapeDtypeStruct((N, CH), BF16),
        compiler_params=params(8),
        name="prefix",
    )(pieces)


def join_kernel(y, gates, bcc, hcol, state, gain, out):
    for at in range(0, ROWS, 128):
        c_vals = bcc[at : at + 128, N:]
        carried = spread(hcol[at : at + 128, 2 * HEADS : 3 * HEADS])
        total = y[at : at + 128, :] + carried * dot(c_vals, state[...])
        gated = total * gates[at : at + 128, :]
        square = jnp.sum(gated * gated, axis=1, keepdims=True)
        high = square.astype(BF16).astype(F32)
        lane = lax.broadcasted_iota(jnp.int32, (128, 128), 1)
        out[at : at + 128, :CH] = (gated * gain[...]).astype(BF16)
        out[at : at + 128, CH:] = jnp.where(lane < 64, high, square - high).astype(BF16)


def join(*args):
    return pl.pallas_call(
        join_kernel,
        in_specs=[VMEM] * len(args),
        out_specs=VMEM,
        out_shape=jax.ShapeDtypeStruct((ROWS, CH + 128), BF16),
        compiler_params=params(24),
        cost_estimate=pl.CostEstimate(
            flops=2 * ROWS * N * CH, bytes_accessed=4 * 2**20, transcendentals=0
        ),
        name="join",
    )(*args)


def project_kernel(place, own, sib, w, out):
    del place
    square = own[:, CH:].astype(F32) + sib[:, CH:].astype(F32)
    mean = (square[:, 0:1] + square[:, 64:65]) / (2.0 * CH)
    part = dot(own[:, :CH], w[:CH, :]) + dot(sib[:, :CH], w[CH:, :])
    out[...] = (part * lax.rsqrt(mean + NORM_EPS)).astype(out.dtype)


def project(own, sib, w_all, place, dtype):
    width = 256
    count = w_all.shape[1] // X_RING // width
    whole = pl.BlockSpec(own.shape, lambda i, place: (0, 0))
    return pl.pallas_call(
        project_kernel,
        grid_spec=pltpu.PrefetchScalarGridSpec(
            num_scalar_prefetch=1,
            grid=(count,),
            in_specs=[
                whole,
                whole,
                pl.BlockSpec(
                    (2 * CH, width), lambda i, place: (0, place[0] * count + i)
                ),
            ],
            out_specs=pl.BlockSpec((ROWS, width), lambda i, place: (0, i)),
        ),
        out_shape=jax.ShapeDtypeStruct((ROWS, count * width), dtype),
        compiler_params=params(24, True),
        cost_estimate=pl.CostEstimate(
            flops=2 * ROWS * 2 * CH * count * width, bytes_accessed=3 * 2**20, transcendentals=0
        ),
        name="project",
    )(place, own, sib, w_all)


def swapped(value, bit):
    return lax.ppermute(value, "tp", [(i, i ^ bit) for i in range(16)])


def along_x(value, steps):
    return lax.ppermute(value, "tp", [(i, (i + 4 * steps) % 16) for i in range(16)])


def next_ctx(value):
    return lax.ppermute(value, "ctx", [(i, i + 1) for i in range(15)])


def between_chips(value):
    same_core = [[2 * chip + core for chip in range(CHIPS)] for core in range(CORES)]
    return lax.all_to_all(value, "tp", 0, 0, axis_index_groups=same_core)


def pick(core, first, second):
    return jnp.where(core == 0, first, second)


def local(
    tokens,
    seg_ids,
    w_x,
    w_z,
    w_bc,
    w_dt,
    conv_x,
    conv_x_bias,
    conv_bc,
    conv_bc_bias,
    dt_bias,
    decay_rate,
    skip_gain,
    norm_weight,
    w_out,
):
    rank = lax.axis_index("tp")
    core = rank % CORES
    chip = rank // CORES
    x_place = rank // 4
    y_place = chip % 2

    ids_row = jnp.zeros((1, FEAT), BF16).at[0, :3].set((seg_ids[-3:] + 1).astype(BF16))
    halo = next_ctx(jnp.concatenate([ids_row, tokens[1 - HALO :]], axis=0))
    ids_prior = halo[0, :3].astype(jnp.int32) - 1
    padded = jnp.concatenate([halo, tokens], axis=0)
    own = between_chips(jnp.broadcast_to(padded[None], (CHIPS,) + padded.shape))
    sib = swapped(own, 1)

    w_cols = jnp.concatenate(
        [w_bc.T.reshape(CHIPS, 2 * N, FEAT), w_dt.T.reshape(CHIPS, 2 * HEADS, FEAT)], axis=1
    )
    w_own = between_chips(w_cols)
    w_sib = swapped(w_own, 1)

    halves = (w_out[:, :128], w_out[:, 128:])
    w_pair = jnp.concatenate(
        [pick(core, *halves), swapped(pick(core, halves[1], halves[0]), 1)], axis=0
    )
    w_all = lax.all_gather(w_pair, "ctx", axis=1, tiled=True)

    ids_all = jnp.concatenate([ids_prior, seg_ids])
    prior = ids_prior[2]
    same = lambda a: (seg_ids == a).astype(F32)
    columns = [same(ids_all[tap : tap + ROWS]) for tap in range(CONV - 1)]
    columns += [same(prior), same(seg_ids[-1]), same(seg_ids[L - 1]), same(seg_ids[L - 1])]
    columns += [seg_ids.astype(F32)]
    cols = jnp.pad(jnp.stack(columns, axis=1), ((0, 0), (0, 128 - len(columns))))
    seg_row = jnp.broadcast_to(seg_ids.astype(F32)[None], (8, ROWS))

    taps_bc = lax.dynamic_slice_in_dim(conv_bc, chip * 2 * N, 2 * N, 1)
    bias_bc = lax.dynamic_slice_in_dim(conv_bc_bias, chip * 2 * N, 2 * N, 0)
    small = [conv_x, conv_x_bias[None], taps_bc, bias_bc[None], dt_bias[None], decay_rate[None]]
    xc, bcc, hcol, hrow, s0, pay = scan_input(own, sib, w_x, w_own, w_sib, cols, small)

    pieces = lax.all_to_all(pay, "ctx", 0, 0)
    skip = jnp.repeat(skip_gain, P_SIZE)[None]
    y = intra(xc, bcc, hcol, hrow, s0, cols, seg_row, skip)
    states = prefix(pieces)
    state = lax.all_to_all(states.reshape(16, 8, CH), "ctx", 0, 0).reshape(N, CH)
    own_late, sib_late, _ = lax.optimization_barrier((own, sib, hcol))
    gates = gate(own_late, sib_late, w_z)
    mine = join(y, gates, bcc, hcol, state, norm_weight[None])
    other = swapped(mine, 1)

    def outputs(ahead, dtype=BF16):
        place = ((x_place + ahead) % X_RING).astype(jnp.int32)[None]
        return project(mine, other, w_all, place, dtype)

    far = outputs(2)
    from_left = along_x(far[: ROWS // 2], 1)
    from_right = along_x(far[ROWS // 2 :], -1)
    right, left = outputs(1), outputs(3)
    right = jnp.concatenate([right[: ROWS // 2] + from_left, right[ROWS // 2 :]], axis=0)
    left = jnp.concatenate([left[: ROWS // 2], left[ROWS // 2 :] + from_right], axis=0)
    from_left, from_right = along_x(right, 1), along_x(left, -1)
    total = outputs(0, F32) + from_left.astype(F32) + from_right.astype(F32)
    parts = (total[:, :256], total[:, 256:])
    across = swapped(pick(y_place, parts[1], parts[0]).astype(BF16), 2)
    total = (pick(y_place, *parts) + across.astype(F32)).astype(BF16)
    parts = (total[:, :128], total[:, 128:])
    kept = pick(core, *parts)
    given = swapped(pick(core, parts[1], parts[0]), 1)
    return jnp.concatenate([pick(core, kept, given), pick(core, given, kept)], axis=1)


def solution(mesh):
    return jax.shard_map(
        local,
        mesh=mesh,
        in_specs=(
            P("ctx", "tp"),
            P("ctx"),
            P(None, "tp"),
            P(None, "tp"),
            P("tp", None),
            P("tp", None),
            P(None, "tp"),
            P("tp"),
            P(),
            P(),
            P("tp"),
            P("tp"),
            P("tp"),
            P("tp"),
            P("tp", "ctx"),
        ),
        out_specs=P("ctx", "tp"),
        check_vma=False,
    )
```

time: 513 us -> 227 us (0.44)
  waiting for transfers between devices: 283 us -> 82.2 us
  blocking collectives: 98.5 us -> 29.7 us
  matrix products: 32.8 us -> 0 us
  starting transfers between devices: 10.9 us -> 37.1 us
  Pallas kernels: 0 us -> 23.5 us
  other arithmetic: 29.8 us -> 7.45 us
  local copies, waits for them, and re-layouts: 37.8 us -> 31.6 us
    reduce_scatter x2 -> x0, waiting for transfers between devices: 209 us -> none  [the longest x1 108 us: local(): mixed = lax.psum_scatter(partial_out, 'tp', scatter_dimension=1, tiled=True)]
    all_gather x3 -> x1, waiting for transfers between devices: 72.7 us -> 0.01 us  [local(): w_all = lax.all_gather(w_pair, 'ctx', axis=1, tiled=True)]
    psum x1 -> x0, blocking collectives: 69.5 us -> none  [local(): group_sq = lax.psum(group_sq, 'tp')]
    all_to_all x0 -> x3, waiting for transfers between devices: none -> 61.3 us  [the longest x1 52.2 us: between_chips(): return lax.all_to_all(value, 'tp', 0, 0, axis_index_groups=same_core)]
    dot_general x16 -> x0, matrix products: 32.8 us -> none  [the longest x1 8.75 us: local(): jnp.dot(normed, lax.all_gather(w_out, 'ctx', axis=1, tiled=True), preferr...]
    all_to_all x0 -> x1, blocking collectives: none -> 29.7 us  [between_chips(): return lax.all_to_all(value, 'tp', 0, 0, axis_index_groups=same_core)]
    unnamed x1 -> x0, blocking collectives: 29 us -> none
    pallas_call x0 -> x9, Pallas kernels: none -> 23.5 us  [the longest x1 10.4 us: scan_input(): pl.pallas_call(scan_input_kernel, grid=(steps,), in_specs=[blocks(own), b...]
  transfers between devices with their start and end apart: 8 -> 15, of which waited for: 5 -> 9; matrix products, arithmetic and copies ran while one was open for 15% -> 6% of each run, Pallas kernels for 0% -> 10%
where the time goes in v1:
time: 227 us; the launch traced here: 225 us
  waiting for transfers between devices  82.2 us (36%)
  starting transfers between devices  37.1 us (16%)
  local copies, waits for them, and re-layouts  31.6 us (14%)
  blocking collectives  29.7 us (13%)
  Pallas kernels  23.5 us (10%)
  between operations  13.8 us (6%)
  other arithmetic  7.45 us (3%)
    all_to_all x1, waiting for transfers between devices, between_chips(): return lax.all_to_all(value, 'tp', 0, 0, axis_index_groups=same_core)  52.2 us
    all_to_all x1, blocking collectives, between_chips(): return lax.all_to_all(value, 'tp', 0, 0, axis_index_groups=same_core)  29.7 us
    unnamed x58, local copies, waits for them, and re-layouts  23.7 us
    ppermute x6, starting transfers between devices, swapped(): return lax.ppermute(value, 'tp', [(i, i ^ bit) for i in range(16)])  10.4 us
    ppermute x6, waiting for transfers between devices, swapped(): return lax.ppermute(value, 'tp', [(i, i ^ bit) for i in range(16)])  10.4 us
    pallas_call x1, Pallas kernels, scan_input(): pl.pallas_call(scan_input_kernel, grid=(steps,), in_specs=[blocks(own), b...  10.4 us
    ppermute x4, waiting for transfers between devices, along_x(): lax.ppermute(value, 'tp', [(i, (i + 4 * steps) % 16) for i in range(16)])  9.76 us
    all_to_all x1, waiting for transfers between devices, local(): pieces = lax.all_to_all(pay, 'ctx', 0, 0)  9.06 us
  transfers between devices with their start and end apart: 15, of which 9 were waited for; matrix products, arithmetic and copies ran while one was open for 6% of the time, Pallas kernels for 10%

profile of v1, /device:TPU:1, one launch (start us, length us, event | category | flops | bytes accessed | tf_op | source)
XLA Modules:
  0.0 225.4 jit_solution(1933372511526662514)
XLA Ops:
  6.5 1.0 broadcast_select_fusion.5
  7.5 3.3 %collective-permute-start.4 = (bf16[512,128]{1,0:T(8,128)(2,1)S(1)}, bf16[512,128]{1,0:T(8,128)(2,1)S(1)}, u32[]{:S(2)}, u32[]{:S(2)}) collective-permute-start(bf16[512,128]{1,0:T(8,128)(2,1)S(1)} %get-tuple-element.42), channel_id=1, source_target_pairs={{0,1},{1,0},{2,3},{3,2},{4,5},{5,4},{6,7},{7,6},{8,9},{9,8},{10,11... | collective-permute-start | bytes 393224 | tf_op jit(solution)/shard_map/ppermute | solution.py:376
  10.9 1.0 collective-permute-done.4
  13.9 1.4 fusion.5
  15.4 1.8 collective-permute-start
  17.9 1.0 pad_maximum_fusion.3
  18.9 1.5 broadcast_in_dim.44
  20.4 6.8 %all-to-all-start = ((bf16[8,528,256]{2,1,0:T(8,128)(2,1)}), bf16[8,528,256]{2,1,0:T(8,128)(2,1)S(1)}, u32[]{:S(2)}, u32[]{:S(2)}) async-start(bf16[8,528,256]{2,1,0:T(8,128)(2,1)} %broadcast_in_dim.44), calls=%async_computation | async-start | bytes 4325376 | tf_op jit(solution)/shard_map/all_to_all | solution.py:389
  27.3 1.5 copy.28
  28.8 52.2 %all-to-all-done.own = bf16[8,528,256]{2,1,0:T(8,128)(2,1)S(1)} async-done(((bf16[8,528,256]{2,1,0:T(8,128)(2,1)}), bf16[8,528,256]{2,1,0:T(8,128)(2,1)S(1)}, u32[]{:S(2)}, u32[]{:S(2)}) %all-to-all-start) | async-done | bytes 2162720 | tf_op jit(solution)/shard_map/all_to_all | solution.py:389
  81.6 29.7 %all_to_all.20.w_own = bf16[8,272,256]{2,1,0:T(8,128)(2,1)S(1)} all-to-all(bf16[8,272,256]{2,1,0:T(8,128)(2,1)S(1)} %pad_maximum_fusion), channel_id=1, replica_groups={{0,2,4,6,8,10,12,14},{1,3,5,7,9,11,13,15},{16,18,20,22,24,26,28,30},{17..., dimensions={0} | all-to-all | bytes 2228224 | tf_op jit(solution)/shard_map/all_to_all | solution.py:389
  111.4 1.9 collective-permute-start.2
  115.3 1.9 compare_convert_fusion
  118.1 1.0 pad.9.cols
  119.2 2.2 copy-done.18
  121.4 10.4 %scan_input.1 = (bf16[512,512]{1,0:T(8,128)(2,1)S(1)}, bf16[512,256]{1,0:T(8,128)(2,1)S(1)}, f32[512,128]{1,0:T(8,128)S(1)}, f32[16,512]{1,0:T(8,128)S(1)}, bf16...) custom-call(bf16[8,528,256]{2,1,0:T(8,128)(2,1)S(1)} %all-to-all-done.own, ...), custom_call_target="tpu_custom_call" | custom-call | flops 3391094784 | bytes 12582912 | tf_op jit(solution)/shard_map/scan_input/pallas_call | solution.py:188
  134.7 5.2 %all-to-all-start.2 = ((bf16[16,16,512]{2,1,0:T(8,128)(2,1)}), bf16[16,16,512]{2,1,0:T(8,128)(2,1)S(1)}, u32[]{:S(2)}, u32[]{:S(2)}) async-start(bf16[16,16,512]{2,1,0:T(8,128)(2,1)} %copy-done.16), calls=%async_computation.2 | async-start | bytes 524288 | tf_op jit(solution)/shard_map/all_to_all | solution.py:452
  140.1 9.1 %all-to-all-done.2.pieces = bf16[16,16,512]{2,1,0:T(8,128)(2,1)S(1)} async-done(((bf16[16,16,512]{2,1,0:T(8,128)(2,1)}), bf16[16,16,512]{2,1,0:T(8,128)(2,1)S(1)}, u32[]{:S(2)}, u32[]{:S(2)}) %all-to-all-start.2) | async-done | bytes 262176 | tf_op jit(solution)/shard_map/all_to_all | solution.py:452
  149.9 5.6 %all-to-all-start.3 = ((bf16[16,8,512]{2,1,0:T(8,128)(2,1)}), bf16[16,8,512]{2,1,0:T(8,128)(2,1)S(1)}, u32[]{:S(2)}, u32[]{:S(2)}) async-start(bf16[16,8,512]{2,1,0:T(8,128)(2,1)} %bitcast.21), calls=%async_computation.3 | async-start | bytes 262144 | tf_op jit(solution)/shard_map/all_to_all | solution.py:456
  155.5 0.9 copy-done.9
  156.5 0.9 copy-done.12
  157.4 0.9 copy-done.15
  158.4 1.0 copy-done.24
  159.4 1.8 intra.1.y
  161.2 1.0 copy-done.6
  162.2 2.2 copy-done.5
  164.4 4.8 %gate.1.gates = f32[512,512]{1,0:T(8,128)S(1)} custom-call(bf16[8,528,256]{2,1,0:T(8,128)(2,1)S(1)} %all-to-all-done.own, bf16[8,528,256]{2,1,0:T(8,128)(2,1)} %collective-permute-done.1.sib, bf16[4096,512]{1,0:T(8,128)(2,1)S(1)} %copy-done.5), custom_call_target="tpu_custom_call" | custom-call | flops 2147483648 | bytes 9437184 | tf_op jit(solution)/shard_map/gate/pallas_call | solution.py:276
  169.3 1.2 copy-done.7
  170.5 0.9 copy-done.10
  171.5 0.9 copy-done.13
  172.4 1.3 join.1.own
  173.7 1.0 collective-permute-start.3
  174.8 1.7 collective-permute-done.3.sib
  176.5 2.2 copy-done.1
  178.7 1.1 project.6
  179.8 3.9 %collective-permute-start.7 = (bf16[256,512]{1,0:T(8,128)(2,1)S(1)}, bf16[256,512]{1,0:T(8,128)(2,1)S(1)}, u32[]{:S(2)}, u32[]{:S(2)}) collective-permute-start(bf16[256,512]{1,0:T(8,128)(2,1)S(1)} %get-tuple-element.36), channel_id=1, source_target_pairs={{0,12},{1,13},{2,14},{3,15},{4,0},{5,1},{6,2},{7,3},{8,4},{9,5},{1... | collective-permute-start | bytes 786440 | tf_op jit(solution)/shard_map/ppermute | solution.py:380
  183.7 2.2 copy-done.2
  185.9 1.1 project.7
  187.0 1.1 copy-done.3
  188.1 1.1 project.5
  189.3 3.3 %collective-permute-start.8 = (bf16[512,512]{1,0:T(8,128)(2,1)S(1)}, bf16[512,512]{1,0:T(8,128)(2,1)S(1)}, u32[]{:S(2)}, u32[]{:S(2)}) collective-permute-start(bf16[512,512]{1,0:T(8,128)(2,1)S(1)} %pad_maximum_fusion.2), channel_id=1, source_target_pairs={{0,12},{1,13},{2,14},{3,15},{4,0},{5,1},{6,2},{7,3},{8,4},{9,5},{1... | collective-permute-start | bytes 1572872 | tf_op jit(solution)/shard_map/ppermute | solution.py:380
  192.9 2.2 copy-done.4
  195.0 1.1 project.4
  196.2 6.5 %collective-permute-done.8 = bf16[512,512]{1,0:T(8,128)(2,1)S(1)} collective-permute-done((bf16[512,512]{1,0:T(8,128)(2,1)S(1)}, bf16[512,512]{1,0:T(8,128)(2,1)S(1)}, u32[]{:S(2)}, u32[]{:S(2)}) %collective-permute-start.8) | collective-permute-done | bytes 524320 | tf_op jit(solution)/shard_map/ppermute | solution.py:380
  202.6 3.3 %collective-permute-done.6 = bf16[512,512]{1,0:T(8,128)(2,1)S(1)} collective-permute-done((bf16[512,512]{1,0:T(8,128)(2,1)S(1)}, bf16[512,512]{1,0:T(8,128)(2,1)S(1)}, u32[]{:S(2)}, u32[]{:S(2)}) %collective-permute-start.6) | collective-permute-done | bytes 524320 | tf_op jit(solution)/shard_map/ppermute | solution.py:380
  206.3 6.7 %collective-permute-done.9 = bf16[512,256]{1,0:T(8,128)(2,1)S(1)} collective-permute-done((bf16[512,256]{1,0:T(8,128)(2,1)S(1)}, bf16[512,256]{1,0:T(8,128)(2,1)S(1)}, u32[]{:S(2)}, u32[]{:S(2)}) %collective-permute-start.9) | collective-permute-done | bytes 262176 | tf_op jit(solution)/shard_map/ppermute | solution.py:376
  213.1 3.6 %collective-permute-start.10 = (bf16[512,128]{1,0:T(8,128)(2,1)S(1)}, bf16[512,128]{1,0:T(8,128)(2,1)S(1)}, u32[]{:S(2)}, u32[]{:S(2)}) collective-permute-start(bf16[512,128]{1,0:T(8,128)(2,1)S(1)} %broadcast_select_fusion.2), channel_id=1, source_target_pairs={{0,1},{1,0},{2,3},{3,2},{4,5},{5,4},{6,7},{7,6},{8,9},{9,8},{10,11... | collective-permute-start | bytes 393224 | tf_op jit(solution)/shard_map/ppermute | solution.py:376
  216.8 1.0 collective-permute-done.10
  (87 shorter events, 11.9 us)
Async XLA Ops:
  6.5 107.5 %copy-start = (f32[4,2048]{1,0:T(4,128)S(1)}, f32[4,2048]{1,0:T(4,128)}, u32[]{:S(2)}) copy-start(f32[4,2048]{1,0:T(4,128)} %param.25) | copy-start | bytes 98308
  6.5 170.0 %all-gather.2.cloned.1.call-start = ((), (), s32[]{:S(2)}) async-start(), calls=%async_computation.4 | async-start | bytes 4456448 | tf_op jit(solution)/shard_map/all_gather | solution.py:436
  7.5 4.3 %collective-permute-start.4 = (bf16[512,128]{1,0:T(8,128)(2,1)S(1)}, bf16[512,128]{1,0:T(8,128)(2,1)S(1)}, u32[]{:S(2)}, u32[]{:S(2)}) collective-permute-start(bf16[512,128]{1,0:T(8,128)(2,1)S(1)} %get-tuple-element.42), channel_id=1, source_target_pairs={{0,1},{1,0},{2,3},{3,2},{4,5},{5,4},{6,7},{7,6},{8,9},{9,8},{10,11... | collective-permute-start | bytes 393224 | tf_op jit(solution)/shard_map/ppermute | solution.py:376
  15.4 2.6 %collective-permute-start = (bf16[16,256]{1,0:T(8,128)(2,1)S(1)}, bf16[16,256]{1,0:T(8,128)(2,1)S(1)}, u32[]{:S(2)}, u32[]{:S(2)}) collective-permute-start(bf16[16,256]{1,0:T(8,128)(2,1)S(1)} %fusion.1), channel_id=1, source_target_pairs={{0,16},{16,32},{32,48},{48,64},{64,80},{80,96},{96,112},{112,128},... | collective-permute-start | bytes 24584 | tf_op jit(solution)/shard_map/ppermute | solution.py:384
  20.4 6.8 %copy-start.25 = (bf16[256,128]{1,0:T(8,128)(2,1)S(1)}, bf16[256,128]{1,0:T(8,128)(2,1)}, u32[]{:S(2)}) copy-start(bf16[256,128]{1,0:T(8,128)(2,1)} %param.22) | copy-start | bytes 196612
  20.4 60.6 %all-to-all-start = ((bf16[8,528,256]{2,1,0:T(8,128)(2,1)}), bf16[8,528,256]{2,1,0:T(8,128)(2,1)S(1)}, u32[]{:S(2)}, u32[]{:S(2)}) async-start(bf16[8,528,256]{2,1,0:T(8,128)(2,1)} %broadcast_in_dim.44), calls=%async_computation | async-start | bytes 4325376 | tf_op jit(solution)/shard_map/all_to_all | solution.py:389
  81.0 38.1 %collective-permute-start.1 = (bf16[8,528,256]{2,1,0:T(8,128)(2,1)S(1)}, bf16[8,528,256]{2,1,0:T(8,128)(2,1)}, u32[]{:S(2)}, u32[]{:S(2)}) collective-permute-start(bf16[8,528,256]{2,1,0:T(8,128)(2,1)S(1)} %all-to-all-done.own), channel_id=1, source_target_pairs={{0,1},{1,0},{2,3},{3,2},{4,5},{5,4},{6,7},{7,6},{8,9},{9,8},{10,11... | collective-permute-start | bytes 6488072 | tf_op jit(solution)/shard_map/ppermute | solution.py:376
  81.5 31.7 %copy-start.26 = (s32[512]{0:T(512)S(1)}, s32[512]{0:T(512)}, u32[]{:S(2)}) copy-start(s32[512]{0:T(512)} %param.18) | copy-start | bytes 6148
  81.5 37.6 %copy-start.19 = (f32[4,512]{1,0:T(4,128)S(1)}, f32[4,512]{1,0:T(4,128)}, u32[]{:S(2)}) copy-start(f32[4,512]{1,0:T(4,128)} %taps_x.1) | copy-start | bytes 24580
  81.5 37.6 %copy-start.20 = (f32[512]{0:T(512)S(1)}, f32[512]{0:T(512)}, u32[]{:S(2)}) copy-start(f32[512]{0:T(512)} %param.24) | copy-start | bytes 6148
  81.5 37.6 %copy-start.21 = (f32[8]{0:T(128)S(1)}, f32[8]{0:T(128)}, u32[]{:S(2)}) copy-start(f32[8]{0:T(128)} %param.27) | copy-start | bytes 100
  81.5 37.6 %copy-start.22 = (f32[8]{0:T(128)S(1)}, f32[8]{0:T(128)}, u32[]{:S(2)}) copy-start(f32[8]{0:T(128)} %param.28) | copy-start | bytes 100
  111.4 7.7 %collective-permute-start.2 = (bf16[8,272,256]{2,1,0:T(8,128)(2,1)S(1)}, bf16[8,272,256]{2,1,0:T(8,128)(2,1)}, u32[]{:S(2)}, u32[]{:S(2)}) collective-permute-start(bf16[8,272,256]{2,1,0:T(8,128)(2,1)S(1)} %all_to_all.20.w_own), channel_id=1, source_target_pairs={{0,1},{1,0},{2,3},{3,2},{4,5},{5,4},{6,7},{7,6},{8,9},{9,8},{10,11... | collective-permute-start | bytes 3342344 | tf_op jit(solution)/shard_map/ppermute | solution.py:376
  119.1 12.7 %copy-start.14 = (f32[512,128]{1,0:T(8,128)}, f32[512,128]{1,0:T(8,128)S(1)}, u32[]{:S(2)}) copy-start(f32[512,128]{1,0:T(8,128)S(1)} %pad.9.cols) | copy-start | bytes 786436
  119.2 2.2 copy-start.18
  121.4 18.6 %copy-start.27 = (f32[8]{0:T(128)S(1)}, f32[8]{0:T(128)}, u32[]{:S(2)}) copy-start(f32[8]{0:T(128)} %param.29) | copy-start | bytes 100
  131.8 0.7 copy-start.8
  132.5 0.7 copy-start.11
  133.2 0.7 copy-start.16
  133.9 0.8 copy-start.23
  134.7 14.5 %all-to-all-start.2 = ((bf16[16,16,512]{2,1,0:T(8,128)(2,1)}), bf16[16,16,512]{2,1,0:T(8,128)(2,1)S(1)}, u32[]{:S(2)}, u32[]{:S(2)}) async-start(bf16[16,16,512]{2,1,0:T(8,128)(2,1)} %copy-done.16), calls=%async_computation.2 | async-start | bytes 524288 | tf_op jit(solution)/shard_map/all_to_all | solution.py:452
  149.9 19.3 %all-to-all-start.3 = ((bf16[16,8,512]{2,1,0:T(8,128)(2,1)}), bf16[16,8,512]{2,1,0:T(8,128)(2,1)S(1)}, u32[]{:S(2)}, u32[]{:S(2)}) async-start(bf16[16,8,512]{2,1,0:T(8,128)(2,1)} %bitcast.21), calls=%async_computation.3 | async-start | bytes 262144 | tf_op jit(solution)/shard_map/all_to_all | solution.py:456
  155.5 1.0 copy-start.9
  156.5 0.9 copy-start.12
  157.4 0.9 copy-start.15
  158.4 1.0 copy-start.24
  161.2 1.0 copy-start.6
  162.2 2.2 copy-start.5
  164.4 4.9 %copy-start.17 = (f32[512]{0:T(512)S(1)}, f32[512]{0:T(512)}, u32[]{:S(2)}) copy-start(f32[512]{0:T(512)} %param.30) | copy-start | bytes 6148
  169.3 1.2 copy-start.7
  170.5 0.9 copy-start.10
  171.5 0.9 copy-start.13
  173.7 2.8 %collective-permute-start.3 = (bf16[512,640]{1,0:T(8,128)(2,1)S(1)}, bf16[512,640]{1,0:T(8,128)(2,1)S(1)}, u32[]{:S(2)}, u32[]{:S(2)}) collective-permute-start(bf16[512,640]{1,0:T(8,128)(2,1)S(1)} %join.1.own), channel_id=1, source_target_pairs={{0,1},{1,0},{2,3},{3,2},{4,5},{5,4},{6,7},{7,6},{8,9},{9,8},{10,11... | collective-permute-start | bytes 1966088 | tf_op jit(solution)/shard_map/ppermute | solution.py:376
  176.5 2.2 copy-start.1
  179.8 9.4 %collective-permute-start.7 = (bf16[256,512]{1,0:T(8,128)(2,1)S(1)}, bf16[256,512]{1,0:T(8,128)(2,1)S(1)}, u32[]{:S(2)}, u32[]{:S(2)}) collective-permute-start(bf16[256,512]{1,0:T(8,128)(2,1)S(1)} %get-tuple-element.36), channel_id=1, source_target_pairs={{0,12},{1,13},{2,14},{3,15},{4,0},{5,1},{6,2},{7,3},{8,4},{9,5},{1... | collective-permute-start | bytes 786440 | tf_op jit(solution)/shard_map/ppermute | solution.py:380
  183.7 8.9 %collective-permute-start.5 = (bf16[256,512]{1,0:T(8,128)(2,1)S(1)}, bf16[256,512]{1,0:T(8,128)(2,1)S(1)}, u32[]{:S(2)}, u32[]{:S(2)}) collective-permute-start(bf16[256,512]{1,0:T(8,128)(2,1)S(1)} %get-tuple-element.35), channel_id=1, source_target_pairs={{0,4},{1,5},{2,6},{3,7},{4,8},{5,9},{6,10},{7,11},{8,12},{9,13},{1... | collective-permute-start | bytes 786440 | tf_op jit(solution)/shard_map/ppermute | solution.py:380
  183.7 2.2 copy-start.2
  185.9 2.2 copy-start.3
  189.3 13.3 %collective-permute-start.8 = (bf16[512,512]{1,0:T(8,128)(2,1)S(1)}, bf16[512,512]{1,0:T(8,128)(2,1)S(1)}, u32[]{:S(2)}, u32[]{:S(2)}) collective-permute-start(bf16[512,512]{1,0:T(8,128)(2,1)S(1)} %pad_maximum_fusion.2), channel_id=1, source_target_pairs={{0,12},{1,13},{2,14},{3,15},{4,0},{5,1},{6,2},{7,3},{8,4},{9,5},{1... | collective-permute-start | bytes 1572872 | tf_op jit(solution)/shard_map/ppermute | solution.py:380
  192.7 13.2 %collective-permute-start.6 = (bf16[512,512]{1,0:T(8,128)(2,1)S(1)}, bf16[512,512]{1,0:T(8,128)(2,1)S(1)}, u32[]{:S(2)}, u32[]{:S(2)}) collective-permute-start(bf16[512,512]{1,0:T(8,128)(2,1)S(1)} %pad_maximum_fusion.1), channel_id=1, source_target_pairs={{0,4},{1,5},{2,6},{3,7},{4,8},{5,9},{6,10},{7,11},{8,12},{9,13},{1... | collective-permute-start | bytes 1572872 | tf_op jit(solution)/shard_map/ppermute | solution.py:380
  192.8 2.2 copy-start.4
  206.2 6.8 %collective-permute-start.9 = (bf16[512,256]{1,0:T(8,128)(2,1)S(1)}, bf16[512,256]{1,0:T(8,128)(2,1)S(1)}, u32[]{:S(2)}, u32[]{:S(2)}) collective-permute-start(bf16[512,256]{1,0:T(8,128)(2,1)S(1)} %select_convert_fusion), channel_id=1, source_target_pairs={{0,2},{1,3},{2,0},{3,1},{4,6},{5,7},{6,4},{7,5},{8,10},{9,11},{10,... | collective-permute-start | bytes 786440 | tf_op jit(solution)/shard_map/ppermute | solution.py:376
  213.1 4.6 %collective-permute-start.10 = (bf16[512,128]{1,0:T(8,128)(2,1)S(1)}, bf16[512,128]{1,0:T(8,128)(2,1)S(1)}, u32[]{:S(2)}, u32[]{:S(2)}) collective-permute-start(bf16[512,128]{1,0:T(8,128)(2,1)S(1)} %broadcast_select_fusion.2), channel_id=1, source_target_pairs={{0,1},{1,0},{2,3},{3,2},{4,5},{5,4},{6,7},{7,6},{8,9},{9,8},{10,11... | collective-permute-start | bytes 393224 | tf_op jit(solution)/shard_map/ppermute | solution.py:376
  217.9 0.7 copy-start.28
Sparse Core Ops, SparseCore 0:
  12.7 90.2 all-gather.1

commit v2 on v1

v2 whole, which is shorter than its diff:
```python
import functools

import jax
import jax.numpy as jnp
from jax import lax
from jax.experimental import pallas as pl
from jax.experimental.pallas import tpu as pltpu
from jax.sharding import PartitionSpec as P

H = 128
P_SIZE = 64
N = 128
G = 8
L = 256
CONV = 4
HALO = 16
NORM_EPS = 1e-05
HIGHEST = lax.Precision.HIGHEST

CHIPS = 8
CORES = 2
HEADS = 8
CH = HEADS * P_SIZE
ROWS = 512
FEAT = 256
X_RING = 4
Z_RING = 8
A_ROWS = 272
B_ROWS = 256
ALL_ROWS = A_ROWS + B_ROWS
VMEM = pl.BlockSpec(memory_space=pltpu.VMEM)
BF16 = jnp.bfloat16
F32 = jnp.float32


def params(mib, grid=False):
    more = {"dimension_semantics": ("arbitrary",)} if grid else {}
    return pltpu.CompilerParams(vmem_limit_bytes=mib * 2**20, **more)


def dot(a, b):
    return jnp.dot(a, b, preferred_element_type=F32)


def dot_nt(a, b):
    return lax.dot_general(a, b, (((1,), (1,)), ((), ())), preferred_element_type=F32)


def dot_tn(a, b):
    return lax.dot_general(a, b, (((0,), (0,)), ((), ())), preferred_element_type=F32)


def silu(v):
    return v / (1.0 + jnp.exp(-v))


def spread(cols, first=0, count=HEADS):
    shape = (HEADS, count * P_SIZE)
    head = lax.broadcasted_iota(jnp.int32, shape, 0)
    lane = lax.broadcasted_iota(jnp.int32, shape, 1)
    pick = (head == lane // P_SIZE + first).astype(F32)
    return jnp.dot(cols, pick, precision=HIGHEST, preferred_element_type=F32)


def my_core():
    return lax.rem(lax.axis_index("tp"), CORES)


def add_to(acc, step, value):
    @pl.when(step == 0)
    def _():
        acc[...] = value

    @pl.when(step > 0)
    def _():
        acc[...] += value


def conv_chunk(raw, at, rows, masks, taps, offsets):
    total = offsets + taps[CONV - 1 : CONV, :] * raw[at + HALO : at + HALO + rows, :]
    for tap in range(CONV - 1):
        first = at + HALO - (CONV - 1) + tap
        shifted = raw[first : first + rows, :]
        total = total + taps[tap : tap + 1, :] * (shifted * masks[:, tap : tap + 1])
    return silu(total).astype(BF16)


def rounded(ref):
    ref[...] = ref[...].astype(BF16).astype(F32)


def step_tokens(places, first, last):
    joined = []
    for own, sib in (first, last):
        parts = [ref[slot] for slot in range(2) for ref in (own, sib)]
        joined.append(jnp.concatenate(parts, axis=1))
    return joined


def step_sources(places):
    for slot in range(2):
        chip = lax.rem(places[X_RING] + slot, 2)
        for same_core in (True, False):
            yield chip, same_core


def step_rows(places, w_ref):
    core = my_core()
    parts = []
    for chip, same_core in step_sources(places):
        from_core = core if same_core else 1 - core
        at = pl.multiple_of((chip * CORES + from_core) * FEAT, FEAT)
        parts.append(w_ref[pl.ds(at, FEAT), :])
    return jnp.concatenate(parts, axis=0)


def slot_blocks(a):
    return pl.BlockSpec((2,) + a.shape[1:], lambda i, places: (i, 0, 0))


def chip_blocks(a):
    return pl.BlockSpec((2,) + a.shape[1:], lambda i, places: (places[i], 0, 0))


def whole(a):
    return pl.BlockSpec(a.shape, lambda i, places: (0,) * len(a.shape))


def over_features(kernel, places, blocked, fixed, shapes, scratch, mib, flops, name):
    return pl.pallas_call(
        kernel,
        grid_spec=pltpu.PrefetchScalarGridSpec(
            num_scalar_prefetch=1,
            grid=(X_RING,),
            in_specs=[spec for _, spec in blocked] + [whole(a) for a in fixed],
            out_specs=[whole(a) for a in shapes],
            scratch_shapes=scratch,
        ),
        out_shape=shapes,
        compiler_params=params(mib, True),
        cost_estimate=pl.CostEstimate(
            flops=flops, bytes_accessed=8 * 2**20, transcendentals=10**6
        ),
        name=name,
    )(places, *[a for a, _ in blocked], *fixed)


def x_in_kernel(places, own_a, own_b, sib_a, sib_b, w_x, x_raw, acc):
    step = pl.program_id(0)
    toks_a, toks_b = step_tokens(places, (own_a, sib_a), (own_b, sib_b))
    rows = step_rows(places, w_x)
    add_to(acc.at[:A_ROWS], step, dot(toks_a, rows))
    add_to(acc.at[A_ROWS:], step, dot(toks_b, rows))

    @pl.when(step == pl.num_programs(0) - 1)
    def _():
        x_raw[...] = acc[...].astype(BF16)


def x_in(places, toks, w_x):
    shapes = [jax.ShapeDtypeStruct((ALL_ROWS, CH), BF16)]
    blocked = [(a, slot_blocks(a)) for a in toks]
    blocked += [(w_x, pl.BlockSpec((4 * FEAT, CH), lambda i, places: (places[i], 0)))]
    scratch = [pltpu.VMEM((ALL_ROWS, CH), F32)]
    flops = 2 * ALL_ROWS * 4096 * CH
    return over_features(x_in_kernel, places, blocked, [], shapes, scratch, 16, flops, "x_in")[0]


def scan_input_kernel(
    places,
    own_a,
    own_b,
    sib_a,
    sib_b,
    w_own,
    w_sib,
    x_raw,
    cols,
    taps_x,
    bias_x,
    taps_bc,
    bias_bc,
    dt_bias,
    decay,
    xc,
    bcc,
    hcol,
    hrow,
    s0,
    pay,
    acc_x,
    acc_bc,
    raw_bc,
):
    step = pl.program_id(0)
    core = my_core()
    toks_a, toks_b = step_tokens(places, (own_a, sib_a), (own_b, sib_b))
    w_cols = jnp.concatenate(
        [(w_own if same else w_sib)[chip] for chip, same in step_sources(places)], axis=1
    )
    add_to(acc_bc.at[:A_ROWS], step, dot_nt(toks_a, w_cols))
    add_to(acc_bc.at[A_ROWS:], step, dot_nt(toks_b, w_cols))

    @pl.when(step == 0)
    def _():
        acc_x[...] = x_raw[...].astype(F32)

    quarter = ROWS // X_RING
    for mine in range(X_RING):

        @pl.when(step == mine)
        def _():
            for at in range(mine * quarter, mine * quarter + quarter, 64):
                masks = cols[at : at + 64, :]
                xc[at : at + 64, :] = conv_chunk(acc_x, at, 64, masks, taps_x, bias_x[...])

    @pl.when(step == pl.num_programs(0) - 1)
    def _():
        raw_dt = acc_bc[HALO:, 2 * N : 2 * N + 2 * HEADS]
        raw_dt = jnp.where(core == 0, raw_dt[:, :HEADS], raw_dt[:, HEADS:])
        pre = raw_dt + dt_bias[...]
        dt = jnp.maximum(pre, 0.0) + jnp.log1p(jnp.exp(-jnp.abs(pre)))
        loga = -decay[...] * dt
        raw_bc[...] = acc_bc[:, : 2 * N].astype(BF16).astype(F32)
        for at in range(0, ROWS, 64):
            masks = cols[at : at + 64, :]
            bcc[at : at + 64, :] = conv_chunk(raw_bc, at, 64, masks, taps_bc, bias_bc[...])
        lower = (
            lax.broadcasted_iota(jnp.int32, (L, L), 0) >= lax.broadcasted_iota(jnp.int32, (L, L), 1)
        ).astype(F32)
        cum0 = jnp.dot(lower, loga[:L], precision=HIGHEST, preferred_element_type=F32)
        cum1 = jnp.dot(lower, loga[L:], precision=HIGHEST, preferred_element_type=F32)
        end0, end1 = cum0[L - 1 :], cum1[L - 1 :]
        slab = jnp.exp(jnp.concatenate([cum0, cum1 + end0], axis=0)) * cols[:, 3:4]
        inner = jnp.exp(cum1) * cols[L:, 5:6]
        tail0 = jnp.exp(end0 - cum0) * cols[:L, 6:7] * dt[:L]
        tail1 = jnp.exp(end1 - cum1) * cols[L:, 4:5] * dt[L:]
        cum = jnp.concatenate([cum0, cum1], axis=0)
        blank = jnp.zeros((ROWS, 128 - 4 * HEADS), F32)
        wide = jnp.concatenate(
            [cum, dt, slab, jnp.concatenate([inner, inner], axis=0), blank], axis=1
        )
        hcol[...] = wide
        hrow[...] = wide.T[: 2 * HEADS]
        scaled0 = (xc[:L, :].astype(F32) * spread(tail0)).astype(BF16)
        scaled1 = (xc[L:, :].astype(F32) * spread(tail1)).astype(BF16)
        state0 = dot_tn(bcc[:L, :N], scaled0)
        state1 = dot_tn(bcc[L:, :N], scaled1)
        s0[...] = state0.astype(BF16)
        ends = jnp.concatenate(
            [inner[L - 1 :], slab[ROWS - 1 :], jnp.zeros((6, HEADS), F32)], axis=0
        )
        ends = spread(ends)
        pay[:N, :] = (ends[0:1] * state0 + state1).astype(BF16)
        pay[N:, :] = factor_rows(ends[1:2])


def factor_rows(factor):
    high = factor.astype(BF16).astype(F32)
    row = lax.broadcasted_iota(jnp.int32, (16, CH), 0)
    return jnp.where(row == 0, high, jnp.where(row == 1, factor - high, 0.0)).astype(BF16)


def joined_states(refs):
    state, factor = None, None
    for ref in refs:
        tail = ref[N:, :].astype(F32)
        decay = tail[0:1] + tail[1:2]
        piece = ref[:N, :].astype(F32)
        state = piece if state is None else state + factor * piece
        factor = decay if factor is None else factor * decay
    return state, factor


def three_kernel(mine, one, two, out):
    state, factor = joined_states((mine, one, two))
    out[:N, :] = state.astype(BF16)
    out[N:, :] = factor_rows(factor)


def three(*args):
    return pl.pallas_call(
        three_kernel,
        in_specs=[VMEM] * 3,
        out_specs=VMEM,
        out_shape=jax.ShapeDtypeStruct((N + 16, CH), BF16),
        compiler_params=params(4),
        cost_estimate=pl.CostEstimate(flops=10**6, bytes_accessed=10**6, transcendentals=0),
        name="three",
    )(*args)


def scan_input(places, toks, w_own, w_sib, fixed):
    shapes = [
        jax.ShapeDtypeStruct((ROWS, CH), BF16),
        jax.ShapeDtypeStruct((ROWS, 2 * N), BF16),
        jax.ShapeDtypeStruct((ROWS, 128), F32),
        jax.ShapeDtypeStruct((2 * HEADS, ROWS), F32),
        jax.ShapeDtypeStruct((N, CH), BF16),
        jax.ShapeDtypeStruct((N + 16, CH), BF16),
    ]
    blocked = [(a, slot_blocks(a)) for a in toks]
    blocked += [(a, chip_blocks(a)) for a in (w_own, w_sib)]
    scratch = [
        pltpu.VMEM((ALL_ROWS, CH), F32),
        pltpu.VMEM((ALL_ROWS, 2 * N + 2 * HEADS), F32),
        pltpu.VMEM((ALL_ROWS, 2 * N), F32),
    ]
    flops = 2 * ALL_ROWS * 4096 * 272
    return over_features(
        scan_input_kernel, places, blocked, fixed, shapes, scratch, 20, flops, "scan_input"
    )


def gate_kernel(places, own_a, own_b, sib_a, sib_b, w_z, gates, acc):
    step = pl.program_id(0)
    toks_a, toks_b = step_tokens(places, (own_a, sib_a), (own_b, sib_b))
    rows = step_rows(places, w_z)
    add_to(acc.at[:A_ROWS], step, dot(toks_a, rows))
    add_to(acc.at[A_ROWS:], step, dot(toks_b, rows))

    @pl.when(step == pl.num_programs(0) - 1)
    def _():
        for at in range(0, ROWS, 64):
            z_raw = acc[HALO + at : HALO + at + 64, :].astype(BF16).astype(F32)
            gates[at : at + 64, :] = silu(z_raw)


def gate(places, toks, w_z):
    shapes = [jax.ShapeDtypeStruct((ROWS, CH), F32)]
    blocked = [(a, slot_blocks(a)) for a in toks]
    blocked += [(w_z, pl.BlockSpec((4 * FEAT, CH), lambda i, places: (places[i], 0)))]
    scratch = [pltpu.VMEM((ALL_ROWS, CH), F32)]
    flops = 2 * ALL_ROWS * 4096 * CH
    return over_features(gate_kernel, places, blocked, [], shapes, scratch, 16, flops, "gate")[0]


def intra_kernel(xc, bcc, hcol, hrow, s0, cols, seg_row, skip, y):
    for block in range(2):
        intra_block(block * L, xc, bcc, hcol, hrow, s0, cols, seg_row, skip, y)


def intra_block(at, xc, bcc, hcol, hrow, s0, cols, seg_row, skip, y):
    b_vals, c_vals = bcc[at : at + L, :N], bcc[at : at + L, N:]
    after = lax.broadcasted_iota(jnp.int32, (L, L), 0) >= lax.broadcasted_iota(
        jnp.int32, (L, L), 1
    )
    same = cols[at : at + L, 7:8] == seg_row[0:1, at : at + L]
    scores = jnp.where(after & same, dot_nt(c_vals, b_vals), 0.0)
    for half in range(2):
        lanes = slice(half * 256, half * 256 + 256)
        weights, values = [], []
        x_half = xc[at : at + L, lanes]
        head_of = lax.broadcasted_iota(jnp.int32, (1, 256), 1) // P_SIZE
        for part in range(4):
            head = half * 4 + part
            gap = hcol[at : at + L, head : head + 1] - hrow[head : head + 1, at : at + L]
            decay = jnp.exp(jnp.minimum(gap, 0.0))
            dt_row = hrow[HEADS + head : HEADS + head + 1, at : at + L]
            weights.append((scores * decay * dt_row).astype(BF16))
            values.append(x_half * (head_of == part).astype(BF16))
        out = dot(jnp.concatenate(weights, axis=1), jnp.concatenate(values, axis=0))
        out = out + skip[:, lanes] * x_half.astype(F32)
        if at:
            carried = spread(hcol[at : at + L, 3 * HEADS : 4 * HEADS], half * 4, 4)
            out = out + carried * dot(c_vals, s0[:, lanes])
        y[at : at + L, lanes] = out


def intra(*args):
    return pl.pallas_call(
        intra_kernel,
        in_specs=[VMEM] * len(args),
        out_specs=VMEM,
        out_shape=jax.ShapeDtypeStruct((ROWS, CH), F32),
        compiler_params=params(12),
        cost_estimate=pl.CostEstimate(
            flops=2 * ROWS * L * CH * 4, bytes_accessed=4 * 2**20, transcendentals=2 * 10**6
        ),
        name="intra",
    )(*args)


def join_kernel(y, gates, bcc, hcol, gain, one, four, seven, out, state):
    @pl.when(pl.program_id(0) == 0)
    def _():
        state[...] = joined_states((one, four, seven))[0].astype(BF16)

    rows = y.shape[0]
    carried = spread(hcol[:, 2 * HEADS : 3 * HEADS])
    total = y[...] + carried * dot(bcc[:, N:], state[...])
    gated = total * gates[...]
    square = jnp.sum(gated * gated, axis=1, keepdims=True)
    high = square.astype(BF16).astype(F32)
    lane = lax.broadcasted_iota(jnp.int32, (rows, 128), 1)
    out[:, :CH] = (gated * gain[...]).astype(BF16)
    out[:, CH:] = jnp.where(lane < 64, high, square - high).astype(BF16)


def join(y, gates, bcc, hcol, gain, pieces):
    rows = 128
    part = lambda a: pl.BlockSpec((rows, a.shape[1]), lambda i: (i, 0))
    all_of = lambda a: pl.BlockSpec(a.shape, lambda i: (0, 0))
    out = jax.ShapeDtypeStruct((ROWS, CH + 128), BF16)
    return pl.pallas_call(
        join_kernel,
        grid=(ROWS // rows,),
        in_specs=[part(a) for a in (y, gates, bcc, hcol)] + [all_of(a) for a in (gain, *pieces)],
        out_specs=part(out),
        out_shape=out,
        scratch_shapes=[pltpu.VMEM((N, CH), BF16)],
        compiler_params=params(10, True),
        cost_estimate=pl.CostEstimate(
            flops=2 * ROWS * N * CH, bytes_accessed=4 * 2**20, transcendentals=0
        ),
        name="join",
    )(y, gates, bcc, hcol, gain, *pieces)


def weight_copies(own_w, far_w, held, sems, blocks):
    y_low = lax.div(lax.axis_index("ctx"), Z_RING)

    def copy(ref, slot):
        x_place, y_place = blocks[slot]
        at = lax.rem(x_place, 2) * 4 + y_place * 2
        return pltpu.make_async_copy(ref.at[pl.ds(at, 2)], held.at[slot], sems.at[slot])

    for slot, (x_place, _) in enumerate(blocks):
        mine = lax.div(x_place, 2) == y_low

        @pl.when(mine)
        def _():
            copy(own_w, slot).start()

        @pl.when(jnp.logical_not(mine))
        def _():
            copy(far_w, slot).start()

    def ready(slot):
        copy(own_w, slot).wait()
        return column_block(held, slot)

    return ready


def column_block(held, slot):
    return jnp.concatenate([held[slot, 0], held[slot, 1]], axis=1)


def normed_rows(own, sib, rows):
    square = own[rows, CH:].astype(F32) + sib[rows, CH:].astype(F32)
    scale = lax.rsqrt((square[:, 0:1] + square[:, 64:65]) / (2.0 * CH) + NORM_EPS)
    return jnp.concatenate([own[rows, :CH], sib[rows, :CH]], axis=1), scale


def x_places():
    x_place = lax.div(lax.axis_index("tp"), 4)
    return [lax.rem(x_place + ahead, X_RING) for ahead in (0, 1, 3, 2)]


def my_y():
    return lax.rem(lax.div(lax.axis_index("tp"), CORES), 2)


def project_far_kernel(own, sib, own_w, far_w, b_sent, held, sems):
    blocks = [(x_place, 1 - my_y()) for x_place in x_places()]
    ready = weight_copies(own_w, far_w, held, sems, blocks)
    values, scale = normed_rows(own, sib, slice(ROWS // 2, ROWS))
    for n in range(X_RING):
        b_sent[:, 256 * n : 256 * n + 256] = (dot(values, ready(n)) * scale).astype(BF16)


def project_near_kernel(own, sib, own_w, far_w, *rest):
    outs, (held, sems) = rest[:5], rest[5:]
    blocks = []
    for x_place in x_places()[1:] + x_places()[:1]:
        blocks += [(x_place, my_y()), (x_place, 1 - my_y())]
    ready = weight_copies(own_w, far_w, held, sems, blocks)
    values, scale = normed_rows(own, sib, slice(0, ROWS // 2))
    low = my_y() == 0
    for n, out in enumerate(outs[:4]):
        near = dot(values, ready(2 * n)) * scale
        far = dot(values, ready(2 * n + 1)) * scale
        out[:, :256] = jnp.where(low, near, far).astype(out.dtype)
        out[:, 256:] = jnp.where(low, far, near).astype(out.dtype)
    values, scale = normed_rows(own, sib, slice(ROWS // 2, ROWS))
    for n, slot in enumerate((6, 0, 2, 4)):
        outs[4][:, 256 * n : 256 * n + 256] = dot(values, column_block(held, slot)) * scale


def project(kernel, own, sib, w_pieces, shapes, blocks, slots, name):
    return pl.pallas_call(
        kernel,
        in_specs=[VMEM] * 2 + [pl.BlockSpec(memory_space=pl.ANY)] * 2,
        out_specs=[VMEM] * len(shapes),
        out_shape=shapes,
        scratch_shapes=[
            pltpu.VMEM((slots, 2, 2 * CH, 128), BF16),
            pltpu.SemaphoreType.DMA((slots,)),
        ],
        compiler_params=params(16),
        cost_estimate=pl.CostEstimate(
            flops=2 * blocks * 256 * 256 * 2 * CH, bytes_accessed=5 * 2**20, transcendentals=0
        ),
        name=name,
    )(own, sib, *w_pieces)


def swapped(value, bit):
    return lax.ppermute(value, "tp", [(i, i ^ bit) for i in range(16)])


def along_x(value, steps):
    return lax.ppermute(value, "tp", [(i, (i + 4 * steps) % 16) for i in range(16)])


def next_ctx(value):
    return lax.ppermute(value, "ctx", [(i, i + 1) for i in range(15)])


def between_chips(value):
    same_core = [[2 * chip + core for chip in range(CHIPS)] for core in range(CORES)]
    return lax.all_to_all(value, "tp", 0, 0, axis_index_groups=same_core)


def together(*values):
    return lax.optimization_barrier(values)


def later_ctx(value, steps):
    return lax.ppermute(value, "ctx", [(i, i + steps) for i in range(16 - steps)])


def pick(core, first, second):
    return jnp.where(core == 0, first, second)


def local(
    tokens,
    seg_ids,
    w_x,
    w_z,
    w_bc,
    w_dt,
    conv_x,
    conv_x_bias,
    conv_bc,
    conv_bc_bias,
    dt_bias,
    decay_rate,
    skip_gain,
    norm_weight,
    w_out,
):
    rank = lax.axis_index("tp")
    core = rank % CORES
    chip = rank // CORES
    x_place = rank // 4
    y_place = chip % 2

    ring = jnp.stack([x_place, x_place + 3, x_place + 1, x_place + 2]) % X_RING
    places = jnp.concatenate([ring, y_place[None]]).astype(jnp.int32)
    w_cols = jnp.concatenate(
        [w_bc.T.reshape(CHIPS, 2 * N, FEAT), w_dt.T.reshape(CHIPS, 2 * HEADS, FEAT)], axis=1
    )
    taps_bc = lax.dynamic_slice_in_dim(conv_bc, chip * 2 * N, 2 * N, 1)
    bias_bc = lax.dynamic_slice_in_dim(conv_bc_bias, chip * 2 * N, 2 * N, 0)[None]
    skip = jnp.repeat(skip_gain, P_SIZE)[None]
    small = [conv_x, conv_x_bias[None], taps_bc, bias_bc, dt_bias[None], decay_rate[None]]
    halves = (w_out[:, :128], w_out[:, 128:])
    w_given, w_kept = pick(core, halves[1], halves[0]), pick(core, *halves)

    ids_row = jnp.pad((seg_ids[-3:] + 1).astype(BF16), (0, FEAT - 3))[None]
    halo = next_ctx(jnp.concatenate([ids_row, tokens[1 - HALO :]], axis=0))
    b_rows = tokens[B_ROWS:]
    b_near = [b_rows] + [along_x(b_rows, ahead) for ahead in (1, -1, 2)]
    a_rows = jnp.concatenate([halo, tokens[:B_ROWS]], axis=0)
    ids_prior = halo[0, :3].astype(jnp.int32) - 1
    a_far = swapped(a_rows, 2)
    w_pair = jnp.concatenate([w_kept, swapped(w_given, 1)], axis=0)
    same_y = [list(range(Z_RING)), list(range(Z_RING, 2 * Z_RING))]
    w_near = lax.all_to_all(
        jnp.broadcast_to(w_pair[None], (Z_RING,) + w_pair.shape),
        "ctx",
        0,
        0,
        axis_index_groups=same_y,
    )
    b_near, a_near = together(b_near, [a_rows, a_far])

    a_near, b_near = jnp.stack(a_near), jnp.stack(b_near)
    a_left, a_right, b_far = along_x(a_near, 1), along_x(a_near, -1), swapped(b_near, 2)
    early = document_columns(seg_ids, ids_prior) + (places, skip, small, w_cols)
    (a_left, a_right, b_far), early = together((a_left, a_right, b_far), early)
    cols, seg_row, places, skip, small, w_cols = early

    a_last = (along_x(a_left[0], 1), along_x(a_right[1], -1))
    a_last, w_cols = together(a_last, w_cols)
    own_a = jnp.concatenate([a_near, a_left, a_right, jnp.stack(a_last)], axis=0)
    own_b = jnp.stack([b_near, b_far], axis=1).reshape(CHIPS, B_ROWS, FEAT)
    w_own = between_chips(w_cols)
    toks = (own_a, own_b, swapped(own_a, 1), swapped(own_b, 1))
    x_raw = x_in(places, toks, w_x)
    w_own, x_raw = together(w_own, x_raw)
    xc, bcc, hcol, hrow, s0, pay = scan_input(
        places, toks, w_own, swapped(w_own, 1), [x_raw, cols] + small
    )

    pay, toks, w_near = together(pay, toks, w_near)
    one, two = later_ctx(pay, 1), later_ctx(pay, 2)
    w_far = lax.ppermute(w_near, "ctx", [(i, i ^ Z_RING) for i in range(2 * Z_RING)])
    gates = gate(places, toks, w_z)
    one, two, gates = together(one, two, gates)
    held = three(pay, one, two)
    held, xc, bcc, hcol = together(held, xc, bcc, hcol)
    pieces = [later_ctx(held, steps) for steps in (1, 4, 7)]
    y = intra(xc, bcc, hcol, hrow, s0, cols, seg_row, skip)
    y, pieces = together(y, pieces)
    mine = join(y, gates, bcc, hcol, norm_weight[None], pieces)
    other = swapped(mine, 1)
    return summed_outputs(mine, other, (w_near, w_far), y_place, core)


def document_columns(seg_ids, ids_prior):
    ids_all = jnp.concatenate([ids_prior, seg_ids])
    prior = ids_prior[2]
    same = lambda a: (seg_ids == a).astype(F32)
    columns = [same(ids_all[tap : tap + ROWS]) for tap in range(CONV - 1)]
    columns += [same(prior), same(seg_ids[-1]), same(seg_ids[L - 1]), same(seg_ids[L - 1])]
    columns += [seg_ids.astype(F32)]
    cols = jnp.pad(jnp.stack(columns, axis=1), ((0, 0), (0, 128 - len(columns))))
    return cols, jnp.broadcast_to(seg_ids.astype(F32)[None], (8, ROWS))


def summed_outputs(mine, other, w_pieces, y_place, core):
    half = ROWS // 2
    shape = lambda lanes, dtype: jax.ShapeDtypeStruct((half, lanes), dtype)
    (b_sent,) = project(
        project_far_kernel, mine, other, w_pieces, [shape(1024, BF16)], 4, 4, "project_far"
    )
    b_sent, other = together(b_sent, other)
    b_far = swapped(b_sent, 2)
    shapes = [shape(512, BF16)] * 3 + [shape(512, F32), shape(1024, F32)]
    *a_sent, a_kept, b_kept = project(
        project_near_kernel, mine, other, w_pieces, shapes, 12, 8, "project_near"
    )
    steps = (1, -1, 2)
    a_got = [along_x(part, ahead) for part, ahead in zip(a_sent, steps)]
    b_sum = b_kept + b_far.astype(F32)
    b_parts = [b_sum[:, 256 * n : 256 * n + 256] for n in range(4)]
    b_got = [along_x(part.astype(BF16), ahead) for part, ahead in zip(b_parts[1:], steps)]
    a_sum = a_kept + sum(part.astype(F32) for part in a_got)
    halves = (a_sum[:, :256], a_sum[:, 256:])
    a_far = swapped(pick(y_place, halves[1], halves[0]).astype(BF16), 2)
    a_sum = pick(y_place, *halves) + a_far.astype(F32)
    b_sum = b_parts[0] + sum(part.astype(F32) for part in b_got)
    total = jnp.concatenate([a_sum, b_sum], axis=0).astype(BF16)
    parts = (total[:, :128], total[:, 128:])
    kept = pick(core, *parts)
    given = swapped(pick(core, parts[1], parts[0]), 1)
    return jnp.concatenate([pick(core, kept, given), pick(core, given, kept)], axis=1)


def solution(mesh):
    return jax.shard_map(
        local,
        mesh=mesh,
        in_specs=(
            P("ctx", "tp"),
            P("ctx"),
            P(None, "tp"),
            P(None, "tp"),
            P("tp", None),
            P("tp", None),
            P(None, "tp"),
            P("tp"),
            P(),
            P(),
            P("tp"),
            P("tp"),
            P("tp"),
            P("tp"),
            P("tp", "ctx"),
        ),
        out_specs=P("ctx", "tp"),
        check_vma=False,
    )
```

time: 227 us -> 215 us (0.947)
  starting transfers between devices: 37.1 us -> 94 us
  blocking collectives: 29.7 us -> 0 us
  waiting for transfers between devices: 82.2 us -> 61.4 us
  local copies, waits for them, and re-layouts: 31.6 us -> 18.3 us
  between operations: 13.8 us -> 0.63 us
  Pallas kernels: 23.5 us -> 30 us
    all_to_all x1, waiting for transfers between devices: 52.2 us -> 4.68 us  [between_chips(): return lax.all_to_all(value, 'tp', 0, 0, axis_index_groups=same_core)]
    ppermute x6 -> x10, starting transfers between devices: 10.4 us -> 41.5 us  [swapped(): return lax.ppermute(value, 'tp', [(i, i ^ bit) for i in range(16)])]
    all_to_all x1 -> x0, blocking collectives: 29.7 us -> none  [between_chips(): return lax.all_to_all(value, 'tp', 0, 0, axis_index_groups=same_core)]
    ppermute x0 -> x6, starting transfers between devices: none -> 21.1 us  [the longest x5 20.6 us: later_ctx(): lax.ppermute(value, 'ctx', [(i, i + steps) for i in range(16 - steps)])]
    ppermute x0 -> x6, waiting for transfers between devices: none -> 18.3 us  [the longest x1 15.7 us: local(): lax.ppermute(w_near, 'ctx', [(i, i ^ Z_RING) for i in range(2 * Z_RING)])]
    unnamed x58 -> x67, local copies, waits for them, and re-layouts: 23.7 us -> 7.92 us
    ppermute x4 -> x13, starting transfers between devices: 7.27 us -> 16.4 us  [along_x(): lax.ppermute(value, 'tp', [(i, (i + 4 * steps) % 16) for i in range(16)])]
    pallas_call x8 -> x7, Pallas kernels: 21.7 us -> 28.3 us  [the longest x3 18 us: over_features(): pl.pallas_call(kernel, grid_spec=pltpu.PrefetchScalarGridSpec(num_scalar_...]
  transfers between devices with their start and end apart: 15 -> 32, of which waited for: 9 -> 20; matrix products, arithmetic and copies ran while one was open for 6% -> 7% of each run, Pallas kernels for 10% -> 10%
where the time goes in v2:
time: 215 us; the launch traced here: 213 us
  starting transfers between devices  94 us (44%)
  waiting for transfers between devices  61.4 us (29%)
  Pallas kernels  30 us (14%)
  local copies, waits for them, and re-layouts  18.3 us (9%)
  other arithmetic  8.25 us (4%)
    ppermute x10, starting transfers between devices, swapped(): return lax.ppermute(value, 'tp', [(i, i ^ bit) for i in range(16)])  41.5 us
    ppermute x5, starting transfers between devices, later_ctx(): lax.ppermute(value, 'ctx', [(i, i + steps) for i in range(16 - steps)])  20.6 us
    pallas_call x3, Pallas kernels, over_features(): pl.pallas_call(kernel, grid_spec=pltpu.PrefetchScalarGridSpec(num_scalar_...  18 us
    ppermute x13, starting transfers between devices, along_x(): lax.ppermute(value, 'tp', [(i, (i + 4 * steps) % 16) for i in range(16)])  16.4 us
    ppermute x1, waiting for transfers between devices, local(): lax.ppermute(w_near, 'ctx', [(i, i ^ Z_RING) for i in range(2 * Z_RING)])  15.7 us
    all_to_all x1, waiting for transfers between devices, local(): lax.all_to_all(jnp.broadcast_to(w_pair[None], (Z_RING,) + w_pair.shape),...  14 us
    ppermute x13, waiting for transfers between devices, along_x(): lax.ppermute(value, 'tp', [(i, (i + 4 * steps) % 16) for i in range(16)])  13.5 us
    ppermute x10, waiting for transfers between devices, swapped(): return lax.ppermute(value, 'tp', [(i, i ^ bit) for i in range(16)])  11 us
  transfers between devices with their start and end apart: 32, of which 20 were waited for; matrix products, arithmetic and copies ran while one was open for 7% of the time, Pallas kernels for 10%

profile of v2, /device:TPU:1, one launch (start us, length us, event | category | flops | bytes accessed | tf_op | source)
XLA Modules:
  0.0 212.7 jit_solution(5777293920720448811)
XLA Ops:
  1.0 3.7 %collective-permute-start.2 = (bf16[256,256]{1,0:T(8,128)(2,1)S(1)}, bf16[256,256]{1,0:T(8,128)(2,1)S(1)}, u32[]{:S(2)}, u32[]{:S(2)}) collective-permute-start(bf16[256,256]{1,0:T(8,128)(2,1)S(1)} %get-tuple-element.62), channel_id=1, source_target_pairs={{0,8},{1,9},{2,10},{3,11},{4,12},{5,13},{6,14},{7,15},{8,0},{9,1},... | collective-permute-start | bytes 393224 | tf_op jit(solution)/shard_map/ppermute | solution.py:514
  7.6 3.5 %collective-permute-start.3 = (bf16[16,256]{1,0:T(8,128)(2,1)S(1)}, bf16[16,256]{1,0:T(8,128)(2,1)S(1)}, u32[]{:S(2)}, u32[]{:S(2)}) collective-permute-start(bf16[16,256]{1,0:T(8,128)(2,1)S(1)} %pad_maximum_fusion.8), channel_id=1, source_target_pairs={{0,16},{16,32},{32,48},{48,64},{64,80},{80,96},{96,112},{112,128},... | collective-permute-start | bytes 24584 | tf_op jit(solution)/shard_map/ppermute | solution.py:518
  11.2 1.4 fusion.12
  15.9 1.5 copy.31
  17.4 3.0 %collective-permute-start.4 = (bf16[272,256]{1,0:T(8,128)(2,1)S(1)}, bf16[272,256]{1,0:T(8,128)(2,1)S(1)}, u32[]{:S(2)}, u32[]{:S(2)}) collective-permute-start(bf16[272,256]{1,0:T(8,128)(2,1)S(1)} %pad_maximum_fusion.6), channel_id=1, source_target_pairs={{0,2},{1,3},{2,0},{3,1},{4,6},{5,7},{6,4},{7,5},{8,10},{9,11},{10,... | collective-permute-start | bytes 417800 | tf_op jit(solution)/shard_map/ppermute | solution.py:510
  21.6 1.4 collective-permute-done.4
  23.8 2.9 %collective-permute-start.7 = (bf16[4,256,256]{2,1,0:T(8,128)(2,1)S(1)}, bf16[4,256,256]{2,1,0:T(8,128)(2,1)S(1)}, u32[]{:S(2)}, u32[]{:S(2)}) collective-permute-start(bf16[4,256,256]{2,1,0:T(8,128)(2,1)S(1)} %get-tuple-element.121), channel_id=1, source_target_pairs={{0,2},{1,3},{2,0},{3,1},{4,6},{5,7},{6,4},{7,5},{8,10},{9,11},{10,... | collective-permute-start | bytes 1572872 | tf_op jit(solution)/shard_map/ppermute | solution.py:510
  26.8 2.1 %collective-permute-start.6 = (bf16[2,272,256]{2,1,0:T(8,128)(2,1)S(1)}, bf16[2,272,256]{2,1,0:T(8,128)(2,1)S(1)}, u32[]{:S(2)}, u32[]{:S(2)}) collective-permute-start(bf16[2,272,256]{2,1,0:T(8,128)(2,1)S(1)} %pad_maximum_fusion.3), channel_id=1, source_target_pairs={{0,12},{1,13},{2,14},{3,15},{4,0},{5,1},{6,2},{7,3},{8,4},{9,5},{1... | collective-permute-start | bytes 835592 | tf_op jit(solution)/shard_map/ppermute | solution.py:514
  29.6 2.0 compare_convert_fusion
  32.6 3.3 %collective-permute-done.5 = bf16[2,272,256]{2,1,0:T(8,128)(2,1)S(1)} collective-permute-done((bf16[2,272,256]{2,1,0:T(8,128)(2,1)S(1)}, bf16[2,272,256]{2,1,0:T(8,128)(2,1)S(1)}, u32[]{:S(2)}, u32[]{:S(2)}) %collective-permute-start.5) | collective-permute-done | bytes 278560 | tf_op jit(solution)/shard_map/ppermute | solution.py:514
  35.9 2.1 collective-permute-start.9
  38.0 2.0 collective-permute-done.9
  40.0 3.1 %collective-permute-done.8 = bf16[272,256]{1,0:T(8,128)(2,1)S(1)} collective-permute-done((bf16[272,256]{1,0:T(8,128)(2,1)S(1)}, bf16[272,256]{1,0:T(8,128)(2,1)S(1)}, u32[]{:S(2)}, u32[]{:S(2)}) %collective-permute-start.8) | collective-permute-done | bytes 139296 | tf_op jit(solution)/shard_map/ppermute | solution.py:514
  43.8 4.2 %all-to-all-start = ((bf16[8,272,256]{2,1,0:T(8,128)(2,1)}), bf16[8,272,256]{2,1,0:T(8,128)(2,1)S(1)}, u32[]{:S(2)}, u32[]{:S(2)}) async-start(bf16[8,272,256]{2,1,0:T(8,128)(2,1)} %pad_maximum_fusion), calls=%async_computation | async-start | bytes 2228224 | tf_op jit(solution)/shard_map/all_to_all | solution.py:523
  48.0 5.7 %collective-permute-start.13 = (bf16[512,128]{1,0:T(8,128)(2,1)S(1)}, bf16[512,128]{1,0:T(8,128)(2,1)S(1)}, u32[]{:S(2)}, u32[]{:S(2)}) collective-permute-start(bf16[512,128]{1,0:T(8,128)(2,1)S(1)} %get-tuple-element.125), channel_id=1, source_target_pairs={{0,1},{1,0},{2,3},{3,2},{4,5},{5,4},{6,7},{7,6},{8,9},{9,8},{10,11... | collective-permute-start | bytes 393224 | tf_op jit(solution)/shard_map/ppermute | solution.py:510
  54.7 4.7 %all-to-all-done.w_own = bf16[8,272,256]{2,1,0:T(8,128)(2,1)S(1)} async-done(((bf16[8,272,256]{2,1,0:T(8,128)(2,1)}), bf16[8,272,256]{2,1,0:T(8,128)(2,1)S(1)}, u32[]{:S(2)}, u32[]{:S(2)}) %all-to-all-start) | async-done | bytes 1114144 | tf_op jit(solution)/shard_map/all_to_all | solution.py:523
  59.4 1.7 broadcast_in_dim.44
  61.1 7.3 %all-to-all-start.1 = ((bf16[8,1024,128]{2,1,0:T(8,128)(2,1)}), bf16[8,1024,128]{2,1,0:T(8,128)(2,1)}, u32[]{:S(2)}, u32[]{:S(2)}) async-start(bf16[8,1024,128]{2,1,0:T(8,128)(2,1)} %broadcast_in_dim.44), calls=%async_computation.1 | async-start | bytes 4194304 | tf_op jit(solution)/shard_map/all_to_all | solution.py:582
  69.3 7.3 %collective-permute-start.10 = (bf16[8,272,256]{2,1,0:T(8,128)(2,1)S(1)}, bf16[8,272,256]{2,1,0:T(8,128)(2,1)S(1)}, u32[]{:S(2)}, u32[]{:S(2)}) collective-permute-start(bf16[8,272,256]{2,1,0:T(8,128)(2,1)S(1)} %bitcast_dynamic-update-slice_fusion.own_a), channel_id=1, source_target_pairs={{0,1},{1,0},{2,3},{3,2},{4,5},{5,4},{6,7},{7,6},{8,9},{9,8},{10,11... | collective-permute-start | bytes 3342344 | tf_op jit(solution)/shard_map/ppermute | solution.py:510
  77.2 3.3 %collective-permute-done.11.sib_b = bf16[8,256,256]{2,1,0:T(8,128)(2,1)S(1)} collective-permute-done((bf16[8,256,256]{2,1,0:T(8,128)(2,1)S(1)}, bf16[8,256,256]{2,1,0:T(8,128)(2,1)S(1)}, u32[]{:S(2)}, u32[]{:S(2)}) %collective-permute-start.11) | collective-permute-done | bytes 1048608 | tf_op jit(solution)/shard_map/ppermute | solution.py:510
  80.5 4.7 %x_in.1.x_raw = bf16[528,512]{1,0:T(8,128)(2,1)S(1)} custom-call(s32[5]{0:T(128)S(1)} %pad_add_fusion.1.places, bf16[8,272,256]{2,1,0:T(8,128)(2,1)S(1)} %bitcast_dynamic-update-slice_fusion.own_a, bf16[8,256,256]{2,1,0:T(8,128)(2,1)S(1)} %bitcast.47, bf16[8,272,256]{2,1,0:T(8,128)(2,1)S(1)} %collective-permute-done.10.sib_a, ...), custom_call_target="tpu_custom_call" | custom-call | flops 2214592512 | bytes 8388608 | tf_op jit(solution)/shard_map/x_in/pallas_call | solution.py:130
  85.9 2.4 %collective-permute-done.12.w_sib = bf16[8,272,256]{2,1,0:T(8,128)(2,1)S(1)} collective-permute-done((bf16[8,272,256]{2,1,0:T(8,128)(2,1)S(1)}, bf16[8,272,256]{2,1,0:T(8,128)(2,1)S(1)}, u32[]{:S(2)}, u32[]{:S(2)}) %collective-permute-start.12) | collective-permute-done | bytes 1114144 | tf_op jit(solution)/shard_map/ppermute | solution.py:510
  88.3 8.4 %scan_input.1 = (bf16[512,512]{1,0:T(8,128)(2,1)S(1)}, bf16[512,256]{1,0:T(8,128)(2,1)S(1)}, f32[512,128]{1,0:T(8,128)S(1)}, f32[16,512]{1,0:T(8,128)S(1)}, bf16...) custom-call(s32[5]{0:T(128)S(1)} %pad_add_fusion.1.places, ...), custom_call_target="tpu_custom_call" | custom-call | flops 1176502272 | bytes 8388608 | tf_op jit(solution)/shard_map/scan_input/pallas_call | solution.py:130
  99.5 14.0 %all-to-all-done.1.own_w = bf16[8,1024,128]{2,1,0:T(8,128)(2,1)} async-done(((bf16[8,1024,128]{2,1,0:T(8,128)(2,1)}), bf16[8,1024,128]{2,1,0:T(8,128)(2,1)}, u32[]{:S(2)}, u32[]{:S(2)}) %all-to-all-start.1) | async-done | bytes 2097184 | tf_op jit(solution)/shard_map/all_to_all | solution.py:582
  114.1 3.5 %collective-permute-start.15 = (bf16[144,512]{1,0:T(8,128)(2,1)S(1)}, bf16[144,512]{1,0:T(8,128)(2,1)S(1)}, u32[]{:S(2)}, u32[]{:S(2)}) collective-permute-start(bf16[144,512]{1,0:T(8,128)(2,1)S(1)} %get-tuple-element.84.mine), channel_id=1, source_target_pairs={{0,32},{16,48},{32,64},{48,80},{64,96},{80,112},{96,128},{112,144}... | collective-permute-start | bytes 442376 | tf_op jit(solution)/shard_map/ppermute | solution.py:531
  117.5 1.3 collective-permute-start.14
  118.9 1.2 copy-done.2
  120.1 2.2 %copy-done.5 = bf16[4096,512]{1,0:T(8,128)(2,1)S(1)} copy-done((bf16[4096,512]{1,0:T(8,128)(2,1)S(1)}, bf16[4096,512]{1,0:T(8,128)(2,1)}, u32[]{:S(2)}) %copy-start.5) | copy-done | bytes 4194328
  122.3 4.9 %gate.1.gates = f32[512,512]{1,0:T(8,128)S(1)} custom-call(s32[5]{0:T(128)S(1)} %pad_add_fusion.1.places, bf16[8,272,256]{2,1,0:T(8,128)(2,1)S(1)} %bitcast_dynamic-update-slice_fusion.own_a, bf16[8,256,256]{2,1,0:T(8,128)(2,1)S(1)} %bitcast.49, bf16[8,272,256]{2,1,0:T(8,128)(2,1)S(1)} %collective-permute-done.10.sib_a, bf16[8,256,256]{2,1,0:T(8,128)(2,1)S(1)} %copy-done.2, ...), custom_call_target="tpu_custom_call" | custom-call | flops 2214592512 | bytes 8388608 | tf_op jit(solution)/shard_map/gate/pallas_call | solution.py:130
  127.3 6.4 %collective-permute-start.18 = (bf16[144,512]{1,0:T(8,128)(2,1)S(1)}, bf16[144,512]{1,0:T(8,128)(2,1)S(1)}, u32[]{:S(2)}, u32[]{:S(2)}) collective-permute-start(bf16[144,512]{1,0:T(8,128)(2,1)S(1)} %three.1), channel_id=1, source_target_pairs={{0,112},{16,128},{32,144},{48,160},{64,176},{80,192},{96,208},{112... | collective-permute-start | bytes 442376 | tf_op jit(solution)/shard_map/ppermute | solution.py:531
  133.7 8.2 %collective-permute-start.17 = (bf16[144,512]{1,0:T(8,128)(2,1)S(1)}, bf16[144,512]{1,0:T(8,128)(2,1)S(1)}, u32[]{:S(2)}, u32[]{:S(2)}) collective-permute-start(bf16[144,512]{1,0:T(8,128)(2,1)S(1)} %three.1), channel_id=1, source_target_pairs={{0,64},{16,80},{32,96},{48,112},{64,128},{80,144},{96,160},{112,17... | collective-permute-start | bytes 442376 | tf_op jit(solution)/shard_map/ppermute | solution.py:531
  141.9 1.3 collective-permute-start.16
  143.3 1.8 intra.1.y
  145.1 2.6 %collective-permute-done.16.one = bf16[144,512]{1,0:T(8,128)(2,1)S(1)} collective-permute-done((bf16[144,512]{1,0:T(8,128)(2,1)S(1)}, bf16[144,512]{1,0:T(8,128)(2,1)S(1)}, u32[]{:S(2)}, u32[]{:S(2)}) %collective-permute-start.16) | collective-permute-done | bytes 147488 | tf_op jit(solution)/shard_map/ppermute | solution.py:531
  147.7 2.3 %join.1.own = bf16[512,640]{1,0:T(8,128)(2,1)S(1)} custom-call(f32[512,512]{1,0:T(8,128)S(1)} %intra.1.y, f32[512,512]{1,0:T(8,128)S(1)} %gate.1.gates, bf16[512,256]{1,0:T(8,128)(2,1)S(1)} %copy-done.10, f32[512,128]{1,0:T(8,128)S(1)} %copy-done.12, f32[1,512]{1,0:T(1,128)S(1)} %bitcast.51, bf16[144,512]{1,0:T(8,128)(2,1)S(1)} %collective-permute-done.16.one, ...), custom_call_target="tpu_custom_call" | custom-call | flops 67108864 | bytes 4194304 | tf_op jit(solution)/shard_map/join/pallas_call | solution.py:405
  150.0 3.1 %collective-permute-start.19 = (bf16[512,640]{1,0:T(8,128)(2,1)S(1)}, bf16[512,640]{1,0:T(8,128)(2,1)S(1)}, u32[]{:S(2)}, u32[]{:S(2)}) collective-permute-start(bf16[512,640]{1,0:T(8,128)(2,1)S(1)} %join.1.own), channel_id=1, source_target_pairs={{0,1},{1,0},{2,3},{3,2},{4,5},{5,4},{6,7},{7,6},{8,9},{9,8},{10,11... | collective-permute-start | bytes 1966088 | tf_op jit(solution)/shard_map/ppermute | solution.py:510
  153.1 1.7 collective-permute-done.19.sib
  154.9 15.7 %collective-permute-done.20.far_w = bf16[8,1024,128]{2,1,0:T(8,128)(2,1)S(1)} collective-permute-done((bf16[8,1024,128]{2,1,0:T(8,128)(2,1)}, bf16[8,1024,128]{2,1,0:T(8,128)(2,1)S(1)}, u32[]{:S(2)}, u32[]{:S(2)}) %collective-permute-start.20) | collective-permute-done | bytes 2097184 | tf_op jit(solution)/shard_map/ppermute | solution.py:611
  170.6 2.8 %project_far.1 = bf16[256,1024]{1,0:T(8,128)(2,1)S(1)} custom-call(bf16[512,640]{1,0:T(8,128)(2,1)S(1)} %join.1.own, bf16[512,640]{1,0:T(8,128)(2,1)S(1)} %collective-permute-done.19.sib, bf16[8,1024,128]{2,1,0:T(8,128)(2,1)} %all-to-all-done.1.own_w, bf16[8,1024,128]{2,1,0:T(8,128)(2,1)S(1)} %collective-permute-done.20.far_w), custom_call_target="tpu_custom_call" | custom-call | flops 536870912 | bytes 5242880 | tf_op jit(solution)/shard_map/project_far/pallas_call | solution.py:492
  173.3 5.1 %project_near.1 = (bf16[256,512]{1,0:T(8,128)(2,1)S(1)}, bf16[256,512]{1,0:T(8,128)(2,1)S(1)}, bf16[256,512]{1,0:T(8,128)(2,1)S(1)}, f32[256,512]{1,0:T(8,128)S(1)}, f32[256,1024]{1,0:T(8,128)S(1)}) custom-call(bf16[512,640]{1,0:T(8,128)(2,1)S(1)} %join.1.own, bf16[512,640]{1,0:T(8,128)(2,1)S(1)} %collective-permute-done.19.sib, ...), custom_call_target="tpu_custom_call" | custom-call | flops 1610612736 | bytes 5242880 | tf_op jit(solution)/shard_map/project_near/pallas_call | solution.py:492
  178.7 2.7 %collective-permute-start.22 = (bf16[256,512]{1,0:T(8,128)(2,1)S(1)}, bf16[256,512]{1,0:T(8,128)(2,1)}, u32[]{:S(2)}, u32[]{:S(2)}) collective-permute-start(bf16[256,512]{1,0:T(8,128)(2,1)S(1)} %get-tuple-element.111), channel_id=1, source_target_pairs={{0,12},{1,13},{2,14},{3,15},{4,0},{5,1},{6,2},{7,3},{8,4},{9,5},{1... | collective-permute-start | bytes 786440 | tf_op jit(solution)/shard_map/ppermute | solution.py:514
  181.4 5.2 %collective-permute-start.25 = (bf16[256,1024]{1,0:T(8,128)(2,1)S(1)}, bf16[256,1024]{1,0:T(8,128)(2,1)S(1)}, u32[]{:S(2)}, u32[]{:S(2)}) collective-permute-start(bf16[256,1024]{1,0:T(8,128)(2,1)S(1)} %project_far.1), channel_id=1, source_target_pairs={{0,2},{1,3},{2,0},{3,1},{4,6},{5,7},{6,4},{7,5},{8,10},{9,11},{10,... | collective-permute-start | bytes 1572872 | tf_op jit(solution)/shard_map/ppermute | solution.py:510
  188.3 1.2 add_add_fusion
  189.6 3.7 %collective-permute-start.24 = (bf16[256,256]{1,0:T(8,128)(2,1)S(1)}, bf16[256,256]{1,0:T(8,128)(2,1)S(1)}, u32[]{:S(2)}, u32[]{:S(2)}) collective-permute-start(bf16[256,256]{1,0:T(8,128)(2,1)S(1)} %select_convert_fusion), channel_id=1, source_target_pairs={{0,2},{1,3},{2,0},{3,1},{4,6},{5,7},{6,4},{7,5},{8,10},{9,11},{10,... | collective-permute-start | bytes 393224 | tf_op jit(solution)/shard_map/ppermute | solution.py:510
  194.9 1.8 collective-permute-start.28
  197.9 1.3 collective-permute-done.26
  199.2 1.6 collective-permute-done.28
  201.2 9.6 %collective-permute-start.29 = (bf16[512,128]{1,0:T(8,128)(2,1)S(1)}, bf16[512,128]{1,0:T(8,128)(2,1)S(1)}, u32[]{:S(2)}, u32[]{:S(2)}) collective-permute-start(bf16[512,128]{1,0:T(8,128)(2,1)S(1)} %broadcast_select_fusion.2), channel_id=1, source_target_pairs={{0,1},{1,0},{2,3},{3,2},{4,5},{5,4},{6,7},{7,6},{8,9},{9,8},{10,11... | collective-permute-start | bytes 393224 | tf_op jit(solution)/shard_map/ppermute | solution.py:510
  (136 shorter events, 25.4 us)
Async XLA Ops:
  0.0 12.6 %copy-start = (f32[4,2048]{1,0:T(4,128)S(1)}, f32[4,2048]{1,0:T(4,128)}, u32[]{:S(2)}) copy-start(f32[4,2048]{1,0:T(4,128)} %param.23) | copy-start | bytes 98308
  1.0 20.5 %collective-permute-start.2 = (bf16[256,256]{1,0:T(8,128)(2,1)S(1)}, bf16[256,256]{1,0:T(8,128)(2,1)S(1)}, u32[]{:S(2)}, u32[]{:S(2)}) collective-permute-start(bf16[256,256]{1,0:T(8,128)(2,1)S(1)} %get-tuple-element.62), channel_id=1, source_target_pairs={{0,8},{1,9},{2,10},{3,11},{4,12},{5,13},{6,14},{7,15},{8,0},{9,1},... | collective-permute-start | bytes 393224 | tf_op jit(solution)/shard_map/ppermute | solution.py:514
  4.7 16.9 %collective-permute-start.1 = (bf16[256,256]{1,0:T(8,128)(2,1)S(1)}, bf16[256,256]{1,0:T(8,128)(2,1)S(1)}, u32[]{:S(2)}, u32[]{:S(2)}) collective-permute-start(bf16[256,256]{1,0:T(8,128)(2,1)S(1)} %get-tuple-element.62), channel_id=1, source_target_pairs={{0,12},{1,13},{2,14},{3,15},{4,0},{5,1},{6,2},{7,3},{8,4},{9,5},{1... | collective-permute-start | bytes 393224 | tf_op jit(solution)/shard_map/ppermute | solution.py:514
  5.5 16.0 %collective-permute-start = (bf16[256,256]{1,0:T(8,128)(2,1)S(1)}, bf16[256,256]{1,0:T(8,128)(2,1)S(1)}, u32[]{:S(2)}, u32[]{:S(2)}) collective-permute-start(bf16[256,256]{1,0:T(8,128)(2,1)S(1)} %get-tuple-element.62), channel_id=1, source_target_pairs={{0,4},{1,5},{2,6},{3,7},{4,8},{5,9},{6,10},{7,11},{8,12},{9,13},{1... | collective-permute-start | bytes 393224 | tf_op jit(solution)/shard_map/ppermute | solution.py:514
  7.6 9.8 %collective-permute-start.3 = (bf16[16,256]{1,0:T(8,128)(2,1)S(1)}, bf16[16,256]{1,0:T(8,128)(2,1)S(1)}, u32[]{:S(2)}, u32[]{:S(2)}) collective-permute-start(bf16[16,256]{1,0:T(8,128)(2,1)S(1)} %pad_maximum_fusion.8), channel_id=1, source_target_pairs={{0,16},{16,32},{32,48},{48,64},{64,80},{80,96},{96,112},{112,128},... | collective-permute-start | bytes 24584 | tf_op jit(solution)/shard_map/ppermute | solution.py:518
  17.4 5.5 %collective-permute-start.4 = (bf16[272,256]{1,0:T(8,128)(2,1)S(1)}, bf16[272,256]{1,0:T(8,128)(2,1)S(1)}, u32[]{:S(2)}, u32[]{:S(2)}) collective-permute-start(bf16[272,256]{1,0:T(8,128)(2,1)S(1)} %pad_maximum_fusion.6), channel_id=1, source_target_pairs={{0,2},{1,3},{2,0},{3,1},{4,6},{5,7},{6,4},{7,5},{8,10},{9,11},{10,... | collective-permute-start | bytes 417800 | tf_op jit(solution)/shard_map/ppermute | solution.py:510
  23.8 12.0 %collective-permute-start.7 = (bf16[4,256,256]{2,1,0:T(8,128)(2,1)S(1)}, bf16[4,256,256]{2,1,0:T(8,128)(2,1)S(1)}, u32[]{:S(2)}, u32[]{:S(2)}) collective-permute-start(bf16[4,256,256]{2,1,0:T(8,128)(2,1)S(1)} %get-tuple-element.121), channel_id=1, source_target_pairs={{0,2},{1,3},{2,0},{3,1},{4,6},{5,7},{6,4},{7,5},{8,10},{9,11},{10,... | collective-permute-start | bytes 1572872 | tf_op jit(solution)/shard_map/ppermute | solution.py:510
  26.8 5.8 %collective-permute-start.6 = (bf16[2,272,256]{2,1,0:T(8,128)(2,1)S(1)}, bf16[2,272,256]{2,1,0:T(8,128)(2,1)S(1)}, u32[]{:S(2)}, u32[]{:S(2)}) collective-permute-start(bf16[2,272,256]{2,1,0:T(8,128)(2,1)S(1)} %pad_maximum_fusion.3), channel_id=1, source_target_pairs={{0,12},{1,13},{2,14},{3,15},{4,0},{5,1},{6,2},{7,3},{8,4},{9,5},{1... | collective-permute-start | bytes 835592 | tf_op jit(solution)/shard_map/ppermute | solution.py:514
  28.9 6.9 %collective-permute-start.5 = (bf16[2,272,256]{2,1,0:T(8,128)(2,1)S(1)}, bf16[2,272,256]{2,1,0:T(8,128)(2,1)S(1)}, u32[]{:S(2)}, u32[]{:S(2)}) collective-permute-start(bf16[2,272,256]{2,1,0:T(8,128)(2,1)S(1)} %pad_maximum_fusion.3), channel_id=1, source_target_pairs={{0,4},{1,5},{2,6},{3,7},{4,8},{5,9},{6,10},{7,11},{8,12},{9,13},{1... | collective-permute-start | bytes 835592 | tf_op jit(solution)/shard_map/ppermute | solution.py:514
  35.9 12.1 %copy-start.25 = (bf16[512,256]{1,0:T(8,128)(2,1)S(1)}, bf16[512,256]{1,0:T(8,128)(2,1)}, u32[]{:S(2)}) copy-start(bf16[512,256]{1,0:T(8,128)(2,1)} %param.29) | copy-start | bytes 786436
  35.9 4.1 %collective-permute-start.9 = (bf16[272,256]{1,0:T(8,128)(2,1)S(1)}, bf16[272,256]{1,0:T(8,128)(2,1)S(1)}, u32[]{:S(2)}, u32[]{:S(2)}) collective-permute-start(bf16[272,256]{1,0:T(8,128)(2,1)S(1)} %slice_bitcast_fusion), channel_id=1, source_target_pairs={{0,12},{1,13},{2,14},{3,15},{4,0},{5,1},{6,2},{7,3},{8,4},{9,5},{1... | collective-permute-start | bytes 417800 | tf_op jit(solution)/shard_map/ppermute | solution.py:514
  38.0 5.1 %collective-permute-start.8 = (bf16[272,256]{1,0:T(8,128)(2,1)S(1)}, bf16[272,256]{1,0:T(8,128)(2,1)S(1)}, u32[]{:S(2)}, u32[]{:S(2)}) collective-permute-start(bf16[272,256]{1,0:T(8,128)(2,1)S(1)} %slice_bitcast_fusion.1), channel_id=1, source_target_pairs={{0,4},{1,5},{2,6},{3,7},{4,8},{5,9},{6,10},{7,11},{8,12},{9,13},{1... | collective-permute-start | bytes 417800 | tf_op jit(solution)/shard_map/ppermute | solution.py:514
  40.0 7.9 %copy-start.26 = (bf16[272,256]{1,0:T(8,128)(2,1)}, bf16[272,256]{1,0:T(8,128)(2,1)S(1)}, u32[]{:S(2)}) copy-start(bf16[272,256]{1,0:T(8,128)(2,1)S(1)} %collective-permute-done.9) | copy-start | bytes 417796
  43.8 15.6 %all-to-all-start = ((bf16[8,272,256]{2,1,0:T(8,128)(2,1)}), bf16[8,272,256]{2,1,0:T(8,128)(2,1)S(1)}, u32[]{:S(2)}, u32[]{:S(2)}) async-start(bf16[8,272,256]{2,1,0:T(8,128)(2,1)} %pad_maximum_fusion), calls=%async_computation | async-start | bytes 2228224 | tf_op jit(solution)/shard_map/all_to_all | solution.py:523
  48.0 6.7 %collective-permute-start.13 = (bf16[512,128]{1,0:T(8,128)(2,1)S(1)}, bf16[512,128]{1,0:T(8,128)(2,1)S(1)}, u32[]{:S(2)}, u32[]{:S(2)}) collective-permute-start(bf16[512,128]{1,0:T(8,128)(2,1)S(1)} %get-tuple-element.125), channel_id=1, source_target_pairs={{0,1},{1,0},{2,3},{3,2},{4,5},{5,4},{6,7},{7,6},{8,9},{9,8},{10,11... | collective-permute-start | bytes 393224 | tf_op jit(solution)/shard_map/ppermute | solution.py:510
  61.1 52.5 %all-to-all-start.1 = ((bf16[8,1024,128]{2,1,0:T(8,128)(2,1)}), bf16[8,1024,128]{2,1,0:T(8,128)(2,1)}, u32[]{:S(2)}, u32[]{:S(2)}) async-start(bf16[8,1024,128]{2,1,0:T(8,128)(2,1)} %broadcast_in_dim.44), calls=%async_computation.1 | async-start | bytes 4194304 | tf_op jit(solution)/shard_map/all_to_all | solution.py:582
  68.4 8.2 %copy-start.22 = (bf16[4,1,256,256]{3,2,0,1:T(8,128)(2,1)S(1)}, bf16[4,1,256,256]{3,2,0,1:T(8,128)(2,1)}, u32[]{:S(2)}) copy-start(bf16[4,1,256,256]{3,2,0,1:T(8,128)(2,1)} %get-tuple-element.120) | copy-start | bytes 1572868
  68.4 8.2 %copy-start.24 = (bf16[4,256,256]{2,1,0:T(8,128)(2,1)S(1)}, bf16[4,256,256]{2,1,0:T(8,128)(2,1)}, u32[]{:S(2)}) copy-start(bf16[4,256,256]{2,1,0:T(8,128)(2,1)} %copy-done.23) | copy-start | bytes 1572868
  69.3 11.1 %collective-permute-start.10 = (bf16[8,272,256]{2,1,0:T(8,128)(2,1)S(1)}, bf16[8,272,256]{2,1,0:T(8,128)(2,1)S(1)}, u32[]{:S(2)}, u32[]{:S(2)}) collective-permute-start(bf16[8,272,256]{2,1,0:T(8,128)(2,1)S(1)} %bitcast_dynamic-update-slice_fusion.own_a), channel_id=1, source_target_pairs={{0,1},{1,0},{2,3},{3,2},{4,5},{5,4},{6,7},{7,6},{8,9},{9,8},{10,11... | collective-permute-start | bytes 3342344 | tf_op jit(solution)/shard_map/ppermute | solution.py:510
  76.8 8.4 %copy-start.4 = (bf16[8,272,256]{2,1,0:T(8,128)(2,1)S(1)}, bf16[8,272,256]{2,1,0:T(8,128)(2,1)}, u32[]{:S(2)}) copy-start(bf16[8,272,256]{2,1,0:T(8,128)(2,1)} %copy-done.3) | copy-start | bytes 3342340
  76.8 11.4 %copy-start.7 = (f32[512,128]{1,0:T(8,128)S(1)}, f32[512,128]{1,0:T(8,128)}, u32[]{:S(2)}) copy-start(f32[512,128]{1,0:T(8,128)} %pad.9.cols) | copy-start | bytes 786436
  76.8 11.4 %copy-start.13 = (f32[4,512]{1,0:T(4,128)S(1)}, f32[4,512]{1,0:T(4,128)}, u32[]{:S(2)}) copy-start(f32[4,512]{1,0:T(4,128)} %taps_x) | copy-start | bytes 24580
  76.8 11.4 %copy-start.15 = (f32[512]{0:T(512)S(1)}, f32[512]{0:T(512)}, u32[]{:S(2)}) copy-start(f32[512]{0:T(512)} %param.22) | copy-start | bytes 6148
  76.8 11.4 %copy-start.16 = (f32[8]{0:T(128)S(1)}, f32[8]{0:T(128)}, u32[]{:S(2)}) copy-start(f32[8]{0:T(128)} %param.25) | copy-start | bytes 100
  76.8 11.4 %copy-start.17 = (f32[8]{0:T(128)S(1)}, f32[8]{0:T(128)}, u32[]{:S(2)}) copy-start(f32[8]{0:T(128)} %param.26) | copy-start | bytes 100
  76.8 3.6 %collective-permute-start.11 = (bf16[8,256,256]{2,1,0:T(8,128)(2,1)S(1)}, bf16[8,256,256]{2,1,0:T(8,128)(2,1)S(1)}, u32[]{:S(2)}, u32[]{:S(2)}) collective-permute-start(bf16[8,256,256]{2,1,0:T(8,128)(2,1)S(1)} %bitcast.46), channel_id=1, source_target_pairs={{0,1},{1,0},{2,3},{3,2},{4,5},{5,4},{6,7},{7,6},{8,9},{9,8},{10,11... | collective-permute-start | bytes 3145736 | tf_op jit(solution)/shard_map/ppermute | solution.py:510
  85.2 3.0 %collective-permute-start.12 = (bf16[8,272,256]{2,1,0:T(8,128)(2,1)S(1)}, bf16[8,272,256]{2,1,0:T(8,128)(2,1)S(1)}, u32[]{:S(2)}, u32[]{:S(2)}) collective-permute-start(bf16[8,272,256]{2,1,0:T(8,128)(2,1)S(1)} %copy-done.4), channel_id=1, source_target_pairs={{0,1},{1,0},{2,3},{3,2},{4,5},{5,4},{6,7},{7,6},{8,9},{9,8},{10,11... | collective-permute-start | bytes 3342344 | tf_op jit(solution)/shard_map/ppermute | solution.py:510
  113.5 57.0 %collective-permute-start.20 = (bf16[8,1024,128]{2,1,0:T(8,128)(2,1)}, bf16[8,1024,128]{2,1,0:T(8,128)(2,1)S(1)}, u32[]{:S(2)}, u32[]{:S(2)}) collective-permute-start(bf16[8,1024,128]{2,1,0:T(8,128)(2,1)} %all-to-all-done.1.own_w), channel_id=1, source_target_pairs={{0,128},{16,144},{32,160},{48,176},{64,192},{80,208},{96,224},{112... | collective-permute-start | bytes 6291464 | tf_op jit(solution)/shard_map/ppermute | solution.py:611
  114.1 13.2 %collective-permute-start.15 = (bf16[144,512]{1,0:T(8,128)(2,1)S(1)}, bf16[144,512]{1,0:T(8,128)(2,1)S(1)}, u32[]{:S(2)}, u32[]{:S(2)}) collective-permute-start(bf16[144,512]{1,0:T(8,128)(2,1)S(1)} %get-tuple-element.84.mine), channel_id=1, source_target_pairs={{0,32},{16,48},{32,64},{48,80},{64,96},{80,112},{96,128},{112,144}... | collective-permute-start | bytes 442376 | tf_op jit(solution)/shard_map/ppermute | solution.py:531
  117.5 9.7 %collective-permute-start.14 = (bf16[144,512]{1,0:T(8,128)(2,1)S(1)}, bf16[144,512]{1,0:T(8,128)(2,1)S(1)}, u32[]{:S(2)}, u32[]{:S(2)}) collective-permute-start(bf16[144,512]{1,0:T(8,128)(2,1)S(1)} %get-tuple-element.84.mine), channel_id=1, source_target_pairs={{0,16},{16,32},{32,48},{48,64},{64,80},{80,96},{96,112},{112,128},... | collective-permute-start | bytes 442376 | tf_op jit(solution)/shard_map/ppermute | solution.py:531
  122.3 20.9 %copy-start.8 = (f32[512,128]{1,0:T(8,128)S(1)}, f32[512,128]{1,0:T(8,128)}, u32[]{:S(2)}) copy-start(f32[512,128]{1,0:T(8,128)} %pad.9.cols) | copy-start | bytes 786436
  122.3 21.0 %copy-start.10 = (bf16[512,256]{1,0:T(8,128)(2,1)S(1)}, bf16[512,256]{1,0:T(8,128)(2,1)}, u32[]{:S(2)}) copy-start(bf16[512,256]{1,0:T(8,128)(2,1)} %copy-done.9) | copy-start | bytes 786436
  122.3 21.0 %copy-start.12 = (f32[512,128]{1,0:T(8,128)S(1)}, f32[512,128]{1,0:T(8,128)}, u32[]{:S(2)}) copy-start(f32[512,128]{1,0:T(8,128)} %copy-done.11) | copy-start | bytes 786436
  122.3 21.0 %copy-start.19 = (bf16[512,512]{1,0:T(8,128)(2,1)S(1)}, bf16[512,512]{1,0:T(8,128)(2,1)}, u32[]{:S(2)}) copy-start(bf16[512,512]{1,0:T(8,128)(2,1)} %copy-done.18) | copy-start | bytes 1572868
  122.3 21.0 %copy-start.21 = (bf16[128,512]{1,0:T(8,128)(2,1)S(1)}, bf16[128,512]{1,0:T(8,128)(2,1)}, u32[]{:S(2)}) copy-start(bf16[128,512]{1,0:T(8,128)(2,1)} %copy-done.20) | copy-start | bytes 393220
  127.3 17.7 %collective-permute-start.18 = (bf16[144,512]{1,0:T(8,128)(2,1)S(1)}, bf16[144,512]{1,0:T(8,128)(2,1)S(1)}, u32[]{:S(2)}, u32[]{:S(2)}) collective-permute-start(bf16[144,512]{1,0:T(8,128)(2,1)S(1)} %three.1), channel_id=1, source_target_pairs={{0,112},{16,128},{32,144},{48,160},{64,176},{80,192},{96,208},{112... | collective-permute-start | bytes 442376 | tf_op jit(solution)/shard_map/ppermute | solution.py:531
  133.7 11.3 %collective-permute-start.17 = (bf16[144,512]{1,0:T(8,128)(2,1)S(1)}, bf16[144,512]{1,0:T(8,128)(2,1)S(1)}, u32[]{:S(2)}, u32[]{:S(2)}) collective-permute-start(bf16[144,512]{1,0:T(8,128)(2,1)S(1)} %three.1), channel_id=1, source_target_pairs={{0,64},{16,80},{32,96},{48,112},{64,128},{80,144},{96,160},{112,17... | collective-permute-start | bytes 442376 | tf_op jit(solution)/shard_map/ppermute | solution.py:531
  141.9 5.8 %collective-permute-start.16 = (bf16[144,512]{1,0:T(8,128)(2,1)S(1)}, bf16[144,512]{1,0:T(8,128)(2,1)S(1)}, u32[]{:S(2)}, u32[]{:S(2)}) collective-permute-start(bf16[144,512]{1,0:T(8,128)(2,1)S(1)} %three.1), channel_id=1, source_target_pairs={{0,16},{16,32},{32,48},{48,64},{64,80},{80,96},{96,112},{112,128},... | collective-permute-start | bytes 442376 | tf_op jit(solution)/shard_map/ppermute | solution.py:531
  150.0 4.9 %collective-permute-start.19 = (bf16[512,640]{1,0:T(8,128)(2,1)S(1)}, bf16[512,640]{1,0:T(8,128)(2,1)S(1)}, u32[]{:S(2)}, u32[]{:S(2)}) collective-permute-start(bf16[512,640]{1,0:T(8,128)(2,1)S(1)} %join.1.own), channel_id=1, source_target_pairs={{0,1},{1,0},{2,3},{3,2},{4,5},{5,4},{6,7},{7,6},{8,9},{9,8},{10,11... | collective-permute-start | bytes 1966088 | tf_op jit(solution)/shard_map/ppermute | solution.py:510
  178.4 8.2 %collective-permute-start.21 = (bf16[256,512]{1,0:T(8,128)(2,1)S(1)}, bf16[256,512]{1,0:T(8,128)(2,1)}, u32[]{:S(2)}, u32[]{:S(2)}) collective-permute-start(bf16[256,512]{1,0:T(8,128)(2,1)S(1)} %get-tuple-element.110), channel_id=1, source_target_pairs={{0,4},{1,5},{2,6},{3,7},{4,8},{5,9},{6,10},{7,11},{8,12},{9,13},{1... | collective-permute-start | bytes 786440 | tf_op jit(solution)/shard_map/ppermute | solution.py:514
  178.7 8.8 %collective-permute-start.22 = (bf16[256,512]{1,0:T(8,128)(2,1)S(1)}, bf16[256,512]{1,0:T(8,128)(2,1)}, u32[]{:S(2)}, u32[]{:S(2)}) collective-permute-start(bf16[256,512]{1,0:T(8,128)(2,1)S(1)} %get-tuple-element.111), channel_id=1, source_target_pairs={{0,12},{1,13},{2,14},{3,15},{4,0},{5,1},{6,2},{7,3},{8,4},{9,5},{1... | collective-permute-start | bytes 786440 | tf_op jit(solution)/shard_map/ppermute | solution.py:514
  181.4 7.0 %collective-permute-start.23 = (bf16[256,512]{1,0:T(8,128)(2,1)S(1)}, bf16[256,512]{1,0:T(8,128)(2,1)}, u32[]{:S(2)}, u32[]{:S(2)}) collective-permute-start(bf16[256,512]{1,0:T(8,128)(2,1)S(1)} %get-tuple-element.112), channel_id=1, source_target_pairs={{0,8},{1,9},{2,10},{3,11},{4,12},{5,13},{6,14},{7,15},{8,0},{9,1},... | collective-permute-start | bytes 786440 | tf_op jit(solution)/shard_map/ppermute | solution.py:514
  181.4 12.2 %collective-permute-start.25 = (bf16[256,1024]{1,0:T(8,128)(2,1)S(1)}, bf16[256,1024]{1,0:T(8,128)(2,1)S(1)}, u32[]{:S(2)}, u32[]{:S(2)}) collective-permute-start(bf16[256,1024]{1,0:T(8,128)(2,1)S(1)} %project_far.1), channel_id=1, source_target_pairs={{0,2},{1,3},{2,0},{3,1},{4,6},{5,7},{6,4},{7,5},{8,10},{9,11},{10,... | collective-permute-start | bytes 1572872 | tf_op jit(solution)/shard_map/ppermute | solution.py:510
  189.6 8.2 %collective-permute-start.24 = (bf16[256,256]{1,0:T(8,128)(2,1)S(1)}, bf16[256,256]{1,0:T(8,128)(2,1)S(1)}, u32[]{:S(2)}, u32[]{:S(2)}) collective-permute-start(bf16[256,256]{1,0:T(8,128)(2,1)S(1)} %select_convert_fusion), channel_id=1, source_target_pairs={{0,2},{1,3},{2,0},{3,1},{4,6},{5,7},{6,4},{7,5},{8,10},{9,11},{10,... | collective-permute-start | bytes 393224 | tf_op jit(solution)/shard_map/ppermute | solution.py:510
  193.8 5.4 %collective-permute-start.26 = (bf16[256,256]{1,0:T(8,128)(2,1)S(1)}, bf16[256,256]{1,0:T(8,128)(2,1)S(1)}, u32[]{:S(2)}, u32[]{:S(2)}) collective-permute-start(bf16[256,256]{1,0:T(8,128)(2,1)S(1)} %get-tuple-element.117), channel_id=1, source_target_pairs={{0,4},{1,5},{2,6},{3,7},{4,8},{5,9},{6,10},{7,11},{8,12},{9,13},{1... | collective-permute-start | bytes 393224 | tf_op jit(solution)/shard_map/ppermute | solution.py:514
  194.9 5.9 %collective-permute-start.28 = (bf16[256,256]{1,0:T(8,128)(2,1)S(1)}, bf16[256,256]{1,0:T(8,128)(2,1)S(1)}, u32[]{:S(2)}, u32[]{:S(2)}) collective-permute-start(bf16[256,256]{1,0:T(8,128)(2,1)S(1)} %get-tuple-element.118), channel_id=1, source_target_pairs={{0,8},{1,9},{2,10},{3,11},{4,12},{5,13},{6,14},{7,15},{8,0},{9,1},... | collective-permute-start | bytes 393224 | tf_op jit(solution)/shard_map/ppermute | solution.py:514
  196.8 4.4 %collective-permute-start.27 = (bf16[256,256]{1,0:T(8,128)(2,1)S(1)}, bf16[256,256]{1,0:T(8,128)(2,1)S(1)}, u32[]{:S(2)}, u32[]{:S(2)}) collective-permute-start(bf16[256,256]{1,0:T(8,128)(2,1)S(1)} %get-tuple-element.119), channel_id=1, source_target_pairs={{0,12},{1,13},{2,14},{3,15},{4,0},{5,1},{6,2},{7,3},{8,4},{9,5},{1... | collective-permute-start | bytes 393224 | tf_op jit(solution)/shard_map/ppermute | solution.py:514
  201.2 10.6 %collective-permute-start.29 = (bf16[512,128]{1,0:T(8,128)(2,1)S(1)}, bf16[512,128]{1,0:T(8,128)(2,1)S(1)}, u32[]{:S(2)}, u32[]{:S(2)}) collective-permute-start(bf16[512,128]{1,0:T(8,128)(2,1)S(1)} %broadcast_select_fusion.2), channel_id=1, source_target_pairs={{0,1},{1,0},{2,3},{3,2},{4,5},{5,4},{6,7},{7,6},{8,9},{9,8},{10,11... | collective-permute-start | bytes 393224 | tf_op jit(solution)/shard_map/ppermute | solution.py:510
  (15 other events, 41.3 us)

commit v3 on v2

--- a/solution.py
+++ b/solution.py
@@ -116,10 +116,6 @@
 
 def slot_blocks(a):
     return pl.BlockSpec((2,) + a.shape[1:], lambda i, places: (i, 0, 0))
-
-
-def chip_blocks(a):
-    return pl.BlockSpec((2,) + a.shape[1:], lambda i, places: (places[i], 0, 0))
 
 
 def whole(a):
@@ -195,9 +191,7 @@
     step = pl.program_id(0)
     core = my_core()
     toks_a, toks_b = step_tokens(places, (own_a, sib_a), (own_b, sib_b))
-    w_cols = jnp.concatenate(
-        [(w_own if same else w_sib)[chip] for chip, same in step_sources(places)], axis=1
-    )
+    w_cols = jnp.concatenate([ref[slot] for slot in range(2) for ref in (w_own, w_sib)], axis=1)
     add_to(acc_bc.at[:A_ROWS], step, dot_nt(toks_a, w_cols))
     add_to(acc_bc.at[A_ROWS:], step, dot_nt(toks_b, w_cols))
 
@@ -300,7 +294,7 @@
         jax.ShapeDtypeStruct((N + 16, CH), BF16),
     ]
     blocked = [(a, slot_blocks(a)) for a in toks]
-    blocked += [(a, chip_blocks(a)) for a in (w_own, w_sib)]
+    blocked += [(a, slot_blocks(a)) for a in (w_own, w_sib)]
     scratch = [
         pltpu.VMEM((ALL_ROWS, CH), F32),
         pltpu.VMEM((ALL_ROWS, 2 * N + 2 * HEADS), F32),
@@ -417,27 +411,21 @@
     )(y, gates, bcc, hcol, gain, *pieces)
 
 
-def weight_copies(own_w, far_w, held, sems, blocks):
+def weight_copies(w_all, held, sems, blocks):
     y_low = lax.div(lax.axis_index("ctx"), Z_RING)
 
-    def copy(ref, slot):
+    def copy(slot):
         x_place, y_place = blocks[slot]
         at = lax.rem(x_place, 2) * 4 + y_place * 2
-        return pltpu.make_async_copy(ref.at[pl.ds(at, 2)], held.at[slot], sems.at[slot])
-
-    for slot, (x_place, _) in enumerate(blocks):
-        mine = lax.div(x_place, 2) == y_low
-
-        @pl.when(mine)
-        def _():
-            copy(own_w, slot).start()
-
-        @pl.when(jnp.logical_not(mine))
-        def _():
-            copy(far_w, slot).start()
+        row = pl.multiple_of(lax.rem(lax.div(x_place, 2) + y_low, 2) * 2 * CH, 2 * CH)
+        part = w_all.at[pl.ds(at, 2), pl.ds(row, 2 * CH), :]
+        return pltpu.make_async_copy(part, held.at[slot], sems.at[slot])
+
+    for slot in range(len(blocks)):
+        copy(slot).start()
 
     def ready(slot):
-        copy(own_w, slot).wait()
+        copy(slot).wait()
         return column_block(held, slot)
 
     return ready
@@ -462,48 +450,54 @@
     return lax.rem(lax.div(lax.axis_index("tp"), CORES), 2)
 
 
-def project_far_kernel(own, sib, own_w, far_w, b_sent, held, sems):
+def project_far_kernel(own, sib, w_all, b_sent, held, sems):
     blocks = [(x_place, 1 - my_y()) for x_place in x_places()]
-    ready = weight_copies(own_w, far_w, held, sems, blocks)
+    ready = weight_copies(w_all, held, sems, blocks)
     values, scale = normed_rows(own, sib, slice(ROWS // 2, ROWS))
     for n in range(X_RING):
         b_sent[:, 256 * n : 256 * n + 256] = (dot(values, ready(n)) * scale).astype(BF16)
 
 
-def project_near_kernel(own, sib, own_w, far_w, *rest):
-    outs, (held, sems) = rest[:5], rest[5:]
+def project_a_kernel(own, sib, w_all, *rest):
+    outs, (held, sems) = rest[:4], rest[4:]
     blocks = []
     for x_place in x_places()[1:] + x_places()[:1]:
-        blocks += [(x_place, my_y()), (x_place, 1 - my_y())]
-    ready = weight_copies(own_w, far_w, held, sems, blocks)
+        blocks += [(x_place, 0), (x_place, 1)]
+    ready = weight_copies(w_all, held, sems, blocks)
     values, scale = normed_rows(own, sib, slice(0, ROWS // 2))
-    low = my_y() == 0
-    for n, out in enumerate(outs[:4]):
-        near = dot(values, ready(2 * n)) * scale
-        far = dot(values, ready(2 * n + 1)) * scale
-        out[:, :256] = jnp.where(low, near, far).astype(out.dtype)
-        out[:, 256:] = jnp.where(low, far, near).astype(out.dtype)
+    for n, out in enumerate(outs):
+        for side in range(2):
+            part = dot(values, ready(2 * n + side)) * scale
+            out[:, 256 * side : 256 * side + 256] = part.astype(out.dtype)
+
+
+def project_b_kernel(own, sib, w_all, b_far, *rest):
+    outs, (held, sems) = rest[:4], rest[4:]
+    blocks = [(x_place, my_y()) for x_place in x_places()]
+    ready = weight_copies(w_all, held, sems, blocks)
     values, scale = normed_rows(own, sib, slice(ROWS // 2, ROWS))
-    for n, slot in enumerate((6, 0, 2, 4)):
-        outs[4][:, 256 * n : 256 * n + 256] = dot(values, column_block(held, slot)) * scale
-
-
-def project(kernel, own, sib, w_pieces, shapes, blocks, slots, name):
+    for n in (1, 2, 3, 0):
+        part = dot(values, ready(n)) * scale
+        part = part + b_far[:, 256 * n : 256 * n + 256].astype(F32)
+        outs[n][...] = part.astype(outs[n].dtype)
+
+
+def project(kernel, own, sib, w_all, more, shapes, blocks, slots, name):
     return pl.pallas_call(
         kernel,
-        in_specs=[VMEM] * 2 + [pl.BlockSpec(memory_space=pl.ANY)] * 2,
+        in_specs=[VMEM] * 2 + [pl.BlockSpec(memory_space=pl.ANY)] + [VMEM] * len(more),
         out_specs=[VMEM] * len(shapes),
         out_shape=shapes,
         scratch_shapes=[
             pltpu.VMEM((slots, 2, 2 * CH, 128), BF16),
             pltpu.SemaphoreType.DMA((slots,)),
         ],
-        compiler_params=params(16),
+        compiler_params=params(58),
         cost_estimate=pl.CostEstimate(
             flops=2 * blocks * 256 * 256 * 2 * CH, bytes_accessed=5 * 2**20, transcendentals=0
         ),
         name=name,
-    )(own, sib, *w_pieces)
+    )(own, sib, w_all, *more)
 
 
 def swapped(value, bit):
@@ -516,11 +510,6 @@
 
 def next_ctx(value):
     return lax.ppermute(value, "ctx", [(i, i + 1) for i in range(15)])
-
-
-def between_chips(value):
-    same_core = [[2 * chip + core for chip in range(CHIPS)] for core in range(CORES)]
-    return lax.all_to_all(value, "tp", 0, 0, axis_index_groups=same_core)
 
 
 def together(*values):
@@ -563,6 +552,11 @@
     w_cols = jnp.concatenate(
         [w_bc.T.reshape(CHIPS, 2 * N, FEAT), w_dt.T.reshape(CHIPS, 2 * HEADS, FEAT)], axis=1
     )
+    x_ahead = [(x_place + ahead) % X_RING for ahead in (0, 1, 3, 2)]
+    cols_for = lambda side: [
+        lax.dynamic_index_in_dim(w_cols, 2 * place + side, 0, False) for place in x_ahead
+    ]
+    w_given_cols, w_kept_cols = jnp.stack(cols_for(1 - y_place)), jnp.stack(cols_for(y_place))
     taps_bc = lax.dynamic_slice_in_dim(conv_bc, chip * 2 * N, 2 * N, 1)
     bias_bc = lax.dynamic_slice_in_dim(conv_bc_bias, chip * 2 * N, 2 * N, 0)[None]
     skip = jnp.repeat(skip_gain, P_SIZE)[None]
@@ -578,39 +572,36 @@
     ids_prior = halo[0, :3].astype(jnp.int32) - 1
     a_far = swapped(a_rows, 2)
     w_pair = jnp.concatenate([w_kept, swapped(w_given, 1)], axis=0)
-    same_y = [list(range(Z_RING)), list(range(Z_RING, 2 * Z_RING))]
-    w_near = lax.all_to_all(
-        jnp.broadcast_to(w_pair[None], (Z_RING,) + w_pair.shape),
-        "ctx",
-        0,
-        0,
-        axis_index_groups=same_y,
-    )
-    b_near, a_near = together(b_near, [a_rows, a_far])
+    w_far_cols = swapped(w_given_cols, 2)
+    b_near, a_near, w_far_cols = together(b_near, [a_rows, a_far], w_far_cols)
 
     a_near, b_near = jnp.stack(a_near), jnp.stack(b_near)
     a_left, a_right, b_far = along_x(a_near, 1), along_x(a_near, -1), swapped(b_near, 2)
-    early = document_columns(seg_ids, ids_prior) + (places, skip, small, w_cols)
+    early = document_columns(seg_ids, ids_prior) + (places, skip, small, w_kept_cols, w_pair)
     (a_left, a_right, b_far), early = together((a_left, a_right, b_far), early)
-    cols, seg_row, places, skip, small, w_cols = early
+    cols, seg_row, places, skip, small, w_kept_cols, w_pair = early
 
     a_last = (along_x(a_left[0], 1), along_x(a_right[1], -1))
-    a_last, w_cols = together(a_last, w_cols)
+    w_far = lax.ppermute(w_pair, "ctx", [(i, i ^ Z_RING) for i in range(2 * Z_RING)])
+    a_last, w_both = together(a_last, [w_pair, w_far])
+    same_y = [list(range(Z_RING)), list(range(Z_RING, 2 * Z_RING))]
+    w_all = lax.all_gather(
+        jnp.concatenate(w_both, axis=0), "ctx", axis=0, axis_index_groups=same_y
+    )
     own_a = jnp.concatenate([a_near, a_left, a_right, jnp.stack(a_last)], axis=0)
     own_b = jnp.stack([b_near, b_far], axis=1).reshape(CHIPS, B_ROWS, FEAT)
-    w_own = between_chips(w_cols)
     toks = (own_a, own_b, swapped(own_a, 1), swapped(own_b, 1))
+    toks, w_kept_cols, w_far_cols = together(toks, w_kept_cols, w_far_cols)
+    w_pairs = [jnp.stack(pair) for pair in zip(w_kept_cols, w_far_cols)]
+    w_moved = [along_x(pair, ahead) for pair, ahead in zip(w_pairs[1:], (1, -1, 2))]
     x_raw = x_in(places, toks, w_x)
-    w_own, x_raw = together(w_own, x_raw)
+    gates = gate(places, toks, w_z)
+    w_moved, x_raw, gates = together(w_moved, x_raw, gates)
+    w_own = jnp.concatenate([w_pairs[0]] + list(w_moved), axis=0)
     xc, bcc, hcol, hrow, s0, pay = scan_input(
         places, toks, w_own, swapped(w_own, 1), [x_raw, cols] + small
     )
-
-    pay, toks, w_near = together(pay, toks, w_near)
     one, two = later_ctx(pay, 1), later_ctx(pay, 2)
-    w_far = lax.ppermute(w_near, "ctx", [(i, i ^ Z_RING) for i in range(2 * Z_RING)])
-    gates = gate(places, toks, w_z)
-    one, two, gates = together(one, two, gates)
     held = three(pay, one, two)
     held, xc, bcc, hcol = together(held, xc, bcc, hcol)
     pieces = [later_ctx(held, steps) for steps in (1, 4, 7)]
@@ -618,7 +609,7 @@
     y, pieces = together(y, pieces)
     mine = join(y, gates, bcc, hcol, norm_weight[None], pieces)
     other = swapped(mine, 1)
-    return summed_outputs(mine, other, (w_near, w_far), y_place, core)
+    return summed_outputs(mine, other, w_all, y_place, core)
 
 
 def document_columns(seg_ids, ids_prior):
@@ -632,28 +623,30 @@
     return cols, jnp.broadcast_to(seg_ids.astype(F32)[None], (8, ROWS))
 
 
-def summed_outputs(mine, other, w_pieces, y_place, core):
-    half = ROWS // 2
-    shape = lambda lanes, dtype: jax.ShapeDtypeStruct((half, lanes), dtype)
+def summed_outputs(mine, other, w_all, y_place, core):
+    shape = lambda lanes, dtype: jax.ShapeDtypeStruct((ROWS // 2, lanes), dtype)
+    steps = (1, -1, 2)
     (b_sent,) = project(
-        project_far_kernel, mine, other, w_pieces, [shape(1024, BF16)], 4, 4, "project_far"
-    )
-    b_sent, other = together(b_sent, other)
+        project_far_kernel, mine, other, w_all, [], [shape(1024, BF16)], 4, 4, "project_far"
+    )
+    b_sent, mine, other = together(b_sent, mine, other)
     b_far = swapped(b_sent, 2)
-    shapes = [shape(512, BF16)] * 3 + [shape(512, F32), shape(1024, F32)]
-    *a_sent, a_kept, b_kept = project(
-        project_near_kernel, mine, other, w_pieces, shapes, 12, 8, "project_near"
-    )
-    steps = (1, -1, 2)
+    shapes = [shape(512, BF16)] * 3 + [shape(512, F32)]
+    *a_sent, a_kept = project(
+        project_a_kernel, mine, other, w_all, [], shapes, 8, 8, "project_a"
+    )
     a_got = [along_x(part, ahead) for part, ahead in zip(a_sent, steps)]
-    b_sum = b_kept + b_far.astype(F32)
-    b_parts = [b_sum[:, 256 * n : 256 * n + 256] for n in range(4)]
-    b_got = [along_x(part.astype(BF16), ahead) for part, ahead in zip(b_parts[1:], steps)]
+    b_far, a_kept = together(b_far, a_kept)
+    shapes = [shape(256, F32)] + [shape(256, BF16)] * 3
+    b_kept, *b_sent = project(
+        project_b_kernel, mine, other, w_all, [b_far], shapes, 4, 4, "project_b"
+    )
+    b_got = [along_x(part, ahead) for part, ahead in zip(b_sent, steps)]
     a_sum = a_kept + sum(part.astype(F32) for part in a_got)
     halves = (a_sum[:, :256], a_sum[:, 256:])
     a_far = swapped(pick(y_place, halves[1], halves[0]).astype(BF16), 2)
     a_sum = pick(y_place, *halves) + a_far.astype(F32)
-    b_sum = b_parts[0] + sum(part.astype(F32) for part in b_got)
+    b_sum = b_kept + sum(part.astype(F32) for part in b_got)
     total = jnp.concatenate([a_sum, b_sum], axis=0).astype(BF16)
     parts = (total[:, :128], total[:, 128:])
     kept = pick(core, *parts)

time: 215 us -> 204 us (0.949)
  starting transfers between devices: 94 us -> 76.3 us
  between operations: 0.63 us -> 14.1 us
  local copies, waits for them, and re-layouts: 18.3 us -> 6.92 us
  Pallas kernels: 30 us -> 38.7 us
  waiting for transfers between devices: 61.4 us -> 54 us
  other arithmetic: 8.25 us -> 11.8 us
    ppermute x10 -> x11, starting transfers between devices: 41.5 us -> 21.5 us  [swapped(): return lax.ppermute(value, 'tp', [(i, i ^ bit) for i in range(16)])]
    all_to_all x2 -> x0, waiting for transfers between devices: 18.7 us -> none  [the longest x1 14 us: local(): lax.all_to_all(jnp.broadcast_to(w_pair[None], (Z_RING,) + w_pair.shape),...]
    ppermute x1, waiting for transfers between devices: 15.7 us -> 0.01 us  [local(): lax.ppermute(w_pair, 'ctx', [(i, i ^ Z_RING) for i in range(2 * Z_RING)])]
    all_to_all x2 -> x0, starting transfers between devices: 11.5 us -> none  [the longest x1 7.29 us: local(): lax.all_to_all(jnp.broadcast_to(w_pair[None], (Z_RING,) + w_pair.shape),...]
    ppermute x10 -> x11, waiting for transfers between devices: 11 us -> 20.4 us  [swapped(): return lax.ppermute(value, 'tp', [(i, i ^ bit) for i in range(16)])]
    ppermute x5, waiting for transfers between devices: 2.61 us -> 11.8 us  [later_ctx(): lax.ppermute(value, 'ctx', [(i, i + steps) for i in range(16 - steps)])]
    pallas_call x2 -> x3, Pallas kernels: 7.82 us -> 16.6 us  [project(): pl.pallas_call(kernel, in_specs=[VMEM] * 2 + [pl.BlockSpec(memory_space=p...]
    ppermute x13 -> x16, waiting for transfers between devices: 13.5 us -> 21.9 us  [along_x(): lax.ppermute(value, 'tp', [(i, (i + 4 * steps) % 16) for i in range(16)])]
  transfers between devices with their start and end apart: 32 -> 35, of which waited for: 20 -> 21; matrix products, arithmetic and copies ran while one was open for 7% -> 6% of each run, Pallas kernels for 10% -> 17%
where the time goes in v3:
time: 204 us; the launch traced here: 202 us
  starting transfers between devices  76.3 us (37%)
  waiting for transfers between devices  54 us (26%)
  Pallas kernels  38.7 us (19%)
  between operations  14.1 us (7%)
  other arithmetic  11.8 us (6%)
  local copies, waits for them, and re-layouts  6.92 us (3%)
    ppermute x5, starting transfers between devices, later_ctx(): lax.ppermute(value, 'ctx', [(i, i + steps) for i in range(16 - steps)])  28.1 us
    ppermute x16, starting transfers between devices, along_x(): lax.ppermute(value, 'tp', [(i, (i + 4 * steps) % 16) for i in range(16)])  22.2 us
    ppermute x16, waiting for transfers between devices, along_x(): lax.ppermute(value, 'tp', [(i, (i + 4 * steps) % 16) for i in range(16)])  21.9 us
    ppermute x11, starting transfers between devices, swapped(): return lax.ppermute(value, 'tp', [(i, i ^ bit) for i in range(16)])  21.5 us
    ppermute x11, waiting for transfers between devices, swapped(): return lax.ppermute(value, 'tp', [(i, i ^ bit) for i in range(16)])  20.4 us
    pallas_call x3, Pallas kernels, over_features(): pl.pallas_call(kernel, grid_spec=pltpu.PrefetchScalarGridSpec(num_scalar_...  18 us
    pallas_call x3, Pallas kernels, project(): pl.pallas_call(kernel, in_specs=[VMEM] * 2 + [pl.BlockSpec(memory_space=p...  16.6 us
    ppermute x5, waiting for transfers between devices, later_ctx(): lax.ppermute(value, 'ctx', [(i, i + steps) for i in range(16 - steps)])  11.8 us
  transfers between devices with their start and end apart: 35, of which 21 were waited for; matrix products, arithmetic and copies ran while one was open for 6% of the time, Pallas kernels for 17%

profile of v3, /device:TPU:1, one launch (start us, length us, event | category | flops | bytes accessed | tf_op | source)
XLA Modules:
  0.0 201.8 jit_solution(3501875080583961731)
XLA Ops:
  7.5 2.1 %collective-permute-start = (bf16[256,256]{1,0:T(8,128)(2,1)S(1)}, bf16[256,256]{1,0:T(8,128)(2,1)S(1)}, u32[]{:S(2)}, u32[]{:S(2)}) collective-permute-start(bf16[256,256]{1,0:T(8,128)(2,1)S(1)} %get-tuple-element.71), channel_id=1, source_target_pairs={{0,4},{1,5},{2,6},{3,7},{4,8},{5,9},{6,10},{7,11},{8,12},{9,13},{1... | collective-permute-start | bytes 393224 | tf_op jit(solution)/shard_map/ppermute | solution.py:508
  9.7 1.4 collective-permute-start.1
  11.0 1.6 collective-permute-start.2
  14.1 3.5 %collective-permute-start.3 = (bf16[16,256]{1,0:T(8,128)(2,1)S(1)}, bf16[16,256]{1,0:T(8,128)(2,1)S(1)}, u32[]{:S(2)}, u32[]{:S(2)}) collective-permute-start(bf16[16,256]{1,0:T(8,128)(2,1)S(1)} %pad_maximum_fusion.13), channel_id=1, source_target_pairs={{0,16},{16,32},{32,48},{48,64},{64,80},{80,96},{96,112},{112,128},... | collective-permute-start | bytes 24584 | tf_op jit(solution)/shard_map/ppermute | solution.py:512
  17.8 1.5 copy.30
  19.7 3.0 %collective-permute-start.5 = (bf16[4,272,256]{2,1,0:T(8,128)(2,1)S(1)}, bf16[4,272,256]{2,1,0:T(8,128)(2,1)S(1)}, u32[]{:S(2)}, u32[]{:S(2)}) collective-permute-start(bf16[4,272,256]{2,1,0:T(8,128)(2,1)S(1)} %pad_maximum_fusion.1), channel_id=1, source_target_pairs={{0,2},{1,3},{2,0},{3,1},{4,6},{5,7},{6,4},{7,5},{8,10},{9,11},{10,... | collective-permute-start | bytes 1671176 | tf_op jit(solution)/shard_map/ppermute | solution.py:504
  26.4 2.1 %collective-permute-start.9 = (bf16[512,128]{1,0:T(8,128)(2,1)}, bf16[512,128]{1,0:T(8,128)(2,1)}, u32[]{:S(2)}, u32[]{:S(2)}) collective-permute-start(bf16[512,128]{1,0:T(8,128)(2,1)} %get-tuple-element.154), channel_id=1, source_target_pairs={{0,1},{1,0},{2,3},{3,2},{4,5},{5,4},{6,7},{7,6},{8,9},{9,8},{10,11... | collective-permute-start | bytes 393224 | tf_op jit(solution)/shard_map/ppermute | solution.py:504
  28.4 8.4 %collective-permute-done.4 = bf16[272,256]{1,0:T(8,128)(2,1)S(1)} collective-permute-done((bf16[272,256]{1,0:T(8,128)(2,1)S(1)}, bf16[272,256]{1,0:T(8,128)(2,1)S(1)}, u32[]{:S(2)}, u32[]{:S(2)}) %collective-permute-start.4) | collective-permute-done | bytes 139296 | tf_op jit(solution)/shard_map/ppermute | solution.py:504
  36.8 1.9 fusion.15
  38.7 2.8 %collective-permute-start.8 = (bf16[4,256,256]{2,1,0:T(8,128)(2,1)}, bf16[4,256,256]{2,1,0:T(8,128)(2,1)}, u32[]{:S(2)}, u32[]{:S(2)}) collective-permute-start(bf16[4,256,256]{2,1,0:T(8,128)(2,1)} %get-tuple-element.150), channel_id=1, source_target_pairs={{0,2},{1,3},{2,0},{3,1},{4,6},{5,7},{6,4},{7,5},{8,10},{9,11},{10,... | collective-permute-start | bytes 1572872 | tf_op jit(solution)/shard_map/ppermute | solution.py:504
  42.0 2.4 %collective-permute-start.7 = (bf16[2,272,256]{2,1,0:T(8,128)(2,1)S(1)}, bf16[2,272,256]{2,1,0:T(8,128)(2,1)S(1)}, u32[]{:S(2)}, u32[]{:S(2)}) collective-permute-start(bf16[2,272,256]{2,1,0:T(8,128)(2,1)S(1)} %pad_maximum_fusion.5), channel_id=1, source_target_pairs={{0,12},{1,13},{2,14},{3,15},{4,0},{5,1},{6,2},{7,3},{8,4},{9,5},{1... | collective-permute-start | bytes 835592 | tf_op jit(solution)/shard_map/ppermute | solution.py:508
  44.4 1.9 compare_convert_fusion
  47.4 1.3 collective-permute-done.6
  48.7 2.6 %collective-permute-done.8 = bf16[4,256,256]{2,1,0:T(8,128)(2,1)} collective-permute-done((bf16[4,256,256]{2,1,0:T(8,128)(2,1)}, bf16[4,256,256]{2,1,0:T(8,128)(2,1)}, u32[]{:S(2)}, u32[]{:S(2)}) %collective-permute-start.8) | collective-permute-done | bytes 524320 | tf_op jit(solution)/shard_map/ppermute | solution.py:504
  52.7 2.4 %collective-permute-start.11 = (bf16[272,256]{1,0:T(8,128)(2,1)S(1)}, bf16[272,256]{1,0:T(8,128)(2,1)S(1)}, u32[]{:S(2)}, u32[]{:S(2)}) collective-permute-start(bf16[272,256]{1,0:T(8,128)(2,1)S(1)} %slice_bitcast_fusion), channel_id=1, source_target_pairs={{0,12},{1,13},{2,14},{3,15},{4,0},{5,1},{6,2},{7,3},{8,4},{9,5},{1... | collective-permute-start | bytes 417800 | tf_op jit(solution)/shard_map/ppermute | solution.py:508
  55.1 1.4 collective-permute-done.10
  58.1 5.1 %collective-permute-start.13 = (bf16[8,272,256]{2,1,0:T(8,128)(2,1)S(1)}, bf16[8,272,256]{2,1,0:T(8,128)(2,1)S(1)}, u32[]{:S(2)}, u32[]{:S(2)}) collective-permute-start(bf16[8,272,256]{2,1,0:T(8,128)(2,1)S(1)} %bitcast_dynamic-update-slice_fusion.own_a), channel_id=1, source_target_pairs={{0,1},{1,0},{2,3},{3,2},{4,5},{5,4},{6,7},{7,6},{8,9},{9,8},{10,11... | collective-permute-start | bytes 3342344 | tf_op jit(solution)/shard_map/ppermute | solution.py:504
  64.6 2.6 %collective-permute-done.14.sib_b = bf16[8,256,256]{2,1,0:T(8,128)(2,1)S(1)} collective-permute-done((bf16[8,256,256]{2,1,0:T(8,128)(2,1)S(1)}, bf16[8,256,256]{2,1,0:T(8,128)(2,1)S(1)}, u32[]{:S(2)}, u32[]{:S(2)}) %collective-permute-start.14) | collective-permute-done | bytes 1048608 | tf_op jit(solution)/shard_map/ppermute | solution.py:504
  68.1 3.0 %collective-permute-start.16 = (bf16[2,272,256]{2,1,0:T(8,128)(2,1)S(1)}, bf16[2,272,256]{2,1,0:T(8,128)(2,1)S(1)}, u32[]{:S(2)}, u32[]{:S(2)}) collective-permute-start(bf16[2,272,256]{2,1,0:T(8,128)(2,1)S(1)} %pad_maximum_fusion.7), channel_id=1, source_target_pairs={{0,12},{1,13},{2,14},{3,15},{4,0},{5,1},{6,2},{7,3},{8,4},{9,5},{1... | collective-permute-start | bytes 835592 | tf_op jit(solution)/shard_map/ppermute | solution.py:508
  71.2 1.3 collective-permute-start.17
  72.5 4.7 %x_in.1.x_raw = bf16[528,512]{1,0:T(8,128)(2,1)S(1)} custom-call(s32[5]{0:T(128)S(1)} %pad_add_fusion.1.places, bf16[8,272,256]{2,1,0:T(8,128)(2,1)S(1)} %bitcast_dynamic-update-slice_fusion.own_a, bf16[8,256,256]{2,1,0:T(8,128)(2,1)S(1)} %bitcast.48, bf16[8,272,256]{2,1,0:T(8,128)(2,1)S(1)} %collective-permute-done.13.sib_a, ...), custom_call_target="tpu_custom_call" | custom-call | flops 2214592512 | bytes 8388608 | tf_op jit(solution)/shard_map/x_in/pallas_call | solution.py:126
  77.2 4.9 %gate.1.gates = f32[512,512]{1,0:T(8,128)S(1)} custom-call(s32[5]{0:T(128)S(1)} %pad_add_fusion.1.places, bf16[8,272,256]{2,1,0:T(8,128)(2,1)S(1)} %bitcast_dynamic-update-slice_fusion.own_a, bf16[8,256,256]{2,1,0:T(8,128)(2,1)S(1)} %bitcast.49, bf16[8,272,256]{2,1,0:T(8,128)(2,1)S(1)} %collective-permute-done.13.sib_a, ...), custom_call_target="tpu_custom_call" | custom-call | flops 2214592512 | bytes 8388608 | tf_op jit(solution)/shard_map/gate/pallas_call | solution.py:126
  82.8 1.8 collective-permute-done.17
  85.8 2.4 %collective-permute-done.18.w_sib = bf16[8,272,256]{2,1,0:T(8,128)(2,1)S(1)} collective-permute-done((bf16[8,272,256]{2,1,0:T(8,128)(2,1)S(1)}, bf16[8,272,256]{2,1,0:T(8,128)(2,1)S(1)}, u32[]{:S(2)}, u32[]{:S(2)}) %collective-permute-start.18) | collective-permute-done | bytes 1114144 | tf_op jit(solution)/shard_map/ppermute | solution.py:504
  88.2 8.3 %scan_input.1 = (bf16[512,512]{1,0:T(8,128)(2,1)S(1)}, bf16[512,256]{1,0:T(8,128)(2,1)S(1)}, f32[512,128]{1,0:T(8,128)S(1)}, f32[16,512]{1,0:T(8,128)S(1)}, bf16...) custom-call(s32[5]{0:T(128)S(1)} %pad_add_fusion.1.places, ...), custom_call_target="tpu_custom_call" | custom-call | flops 1176502272 | bytes 8388608 | tf_op jit(solution)/shard_map/scan_input/pallas_call | solution.py:126
  96.5 3.6 %collective-permute-start.19 = (bf16[144,512]{1,0:T(8,128)(2,1)S(1)}, bf16[144,512]{1,0:T(8,128)(2,1)S(1)}, u32[]{:S(2)}, u32[]{:S(2)}) collective-permute-start(bf16[144,512]{1,0:T(8,128)(2,1)S(1)} %get-tuple-element.101.mine), channel_id=1, source_target_pairs={{0,16},{16,32},{32,48},{48,64},{64,80},{80,96},{96,112},{112,128},... | collective-permute-start | bytes 442376 | tf_op jit(solution)/shard_map/ppermute | solution.py:520
  100.0 6.1 %collective-permute-start.20 = (bf16[144,512]{1,0:T(8,128)(2,1)S(1)}, bf16[144,512]{1,0:T(8,128)(2,1)S(1)}, u32[]{:S(2)}, u32[]{:S(2)}) collective-permute-start(bf16[144,512]{1,0:T(8,128)(2,1)S(1)} %get-tuple-element.101.mine), channel_id=1, source_target_pairs={{0,32},{16,48},{32,64},{48,80},{64,96},{80,112},{96,128},{112,144}... | collective-permute-start | bytes 442376 | tf_op jit(solution)/shard_map/ppermute | solution.py:520
  106.4 7.7 %collective-permute-done.20.two = bf16[144,512]{1,0:T(8,128)(2,1)S(1)} collective-permute-done((bf16[144,512]{1,0:T(8,128)(2,1)S(1)}, bf16[144,512]{1,0:T(8,128)(2,1)S(1)}, u32[]{:S(2)}, u32[]{:S(2)}) %collective-permute-start.20) | collective-permute-done | bytes 147488 | tf_op jit(solution)/shard_map/ppermute | solution.py:520
  114.2 4.8 %collective-permute-start.21 = (bf16[144,512]{1,0:T(8,128)(2,1)S(1)}, bf16[144,512]{1,0:T(8,128)(2,1)S(1)}, u32[]{:S(2)}, u32[]{:S(2)}) collective-permute-start(bf16[144,512]{1,0:T(8,128)(2,1)S(1)} %three.1), channel_id=1, source_target_pairs={{0,16},{16,32},{32,48},{48,64},{64,80},{80,96},{96,112},{112,128},... | collective-permute-start | bytes 442376 | tf_op jit(solution)/shard_map/ppermute | solution.py:520
  119.0 9.2 %collective-permute-start.22 = (bf16[144,512]{1,0:T(8,128)(2,1)S(1)}, bf16[144,512]{1,0:T(8,128)(2,1)S(1)}, u32[]{:S(2)}, u32[]{:S(2)}) collective-permute-start(bf16[144,512]{1,0:T(8,128)(2,1)S(1)} %three.1), channel_id=1, source_target_pairs={{0,64},{16,80},{32,96},{48,112},{64,128},{80,144},{96,160},{112,17... | collective-permute-start | bytes 442376 | tf_op jit(solution)/shard_map/ppermute | solution.py:520
  128.2 4.5 %collective-permute-start.23 = (bf16[144,512]{1,0:T(8,128)(2,1)S(1)}, bf16[144,512]{1,0:T(8,128)(2,1)S(1)}, u32[]{:S(2)}, u32[]{:S(2)}) collective-permute-start(bf16[144,512]{1,0:T(8,128)(2,1)S(1)} %three.1), channel_id=1, source_target_pairs={{0,112},{16,128},{32,144},{48,160},{64,176},{80,192},{96,208},{112... | collective-permute-start | bytes 442376 | tf_op jit(solution)/shard_map/ppermute | solution.py:520
  132.6 1.7 intra.1.y
  134.4 3.8 %collective-permute-done.23.seven = bf16[144,512]{1,0:T(8,128)(2,1)S(1)} collective-permute-done((bf16[144,512]{1,0:T(8,128)(2,1)S(1)}, bf16[144,512]{1,0:T(8,128)(2,1)S(1)}, u32[]{:S(2)}, u32[]{:S(2)}) %collective-permute-start.23) | collective-permute-done | bytes 147488 | tf_op jit(solution)/shard_map/ppermute | solution.py:520
  138.2 2.3 %join.1.own = bf16[512,640]{1,0:T(8,128)(2,1)S(1)} custom-call(f32[512,512]{1,0:T(8,128)S(1)} %intra.1.y, f32[512,512]{1,0:T(8,128)S(1)} %gate.1.gates, bf16[512,256]{1,0:T(8,128)(2,1)S(1)} %get-tuple-element.106.bcc, f32[512,128]{1,0:T(8,128)S(1)} %get-tuple-element.107.hcol, f32[1,512]{1,0:T(1,128)S(1)} %bitcast.52, ...), custom_call_target="tpu_custom_call" | custom-call | flops 67108864 | bytes 4194304 | tf_op jit(solution)/shard_map/join/pallas_call | solution.py:399
  141.6 1.7 collective-permute-done.24.sib
  144.2 4.9 %project_far.1 = bf16[256,1024]{1,0:T(8,128)(2,1)} custom-call(bf16[512,640]{1,0:T(8,128)(2,1)} %copy-done.1, bf16[512,640]{1,0:T(8,128)(2,1)} %copy-done.9, bf16[8,2048,128]{2,1,0:T(8,128)(2,1)} %bitcast.56), custom_call_target="tpu_custom_call" | custom-call | flops 536870912 | bytes 5242880 | tf_op jit(solution)/shard_map/project_far/pallas_call | solution.py:486
  149.1 3.2 %collective-permute-start.25 = (bf16[256,1024]{1,0:T(8,128)(2,1)}, bf16[256,1024]{1,0:T(8,128)(2,1)S(1)}, u32[]{:S(2)}, u32[]{:S(2)}) collective-permute-start(bf16[256,1024]{1,0:T(8,128)(2,1)} %project_far.1), channel_id=1, source_target_pairs={{0,2},{1,3},{2,0},{3,1},{4,6},{5,7},{6,4},{7,5},{8,10},{9,11},{10,... | collective-permute-start | bytes 1572872 | tf_op jit(solution)/shard_map/ppermute | solution.py:504
  152.3 6.6 %project_a.1 = (bf16[256,512]{1,0:T(8,128)(2,1)}, bf16[256,512]{1,0:T(8,128)(2,1)}, bf16[256,512]{1,0:T(8,128)(2,1)}, f32[256,512]{1,0:T(8,128)}) custom-call(bf16[512,640]{1,0:T(8,128)(2,1)} %copy-done.1, bf16[512,640]{1,0:T(8,128)(2,1)} %copy-done.9, bf16[8,2048,128]{2,1,0:T(8,128)(2,1)} %bitcast.57), custom_call_target="tpu_custom_call" | custom-call | flops 1073741824 | bytes 5242880 | tf_op jit(solution)/shard_map/project_a/pallas_call | solution.py:486
  159.2 3.3 %collective-permute-start.27 = (bf16[256,512]{1,0:T(8,128)(2,1)}, bf16[256,512]{1,0:T(8,128)(2,1)S(1)}, u32[]{:S(2)}, u32[]{:S(2)}) collective-permute-start(bf16[256,512]{1,0:T(8,128)(2,1)} %get-tuple-element.126), channel_id=1, source_target_pairs={{0,12},{1,13},{2,14},{3,15},{4,0},{5,1},{6,2},{7,3},{8,4},{9,5},{1... | collective-permute-start | bytes 786440 | tf_op jit(solution)/shard_map/ppermute | solution.py:508
  162.6 1.7 collective-permute-done.25.b_far
  164.3 3.7 %collective-permute-done.28 = bf16[256,512]{1,0:T(8,128)(2,1)S(1)} collective-permute-done((bf16[256,512]{1,0:T(8,128)(2,1)}, bf16[256,512]{1,0:T(8,128)(2,1)S(1)}, u32[]{:S(2)}, u32[]{:S(2)}) %collective-permute-start.28) | collective-permute-done | bytes 262176 | tf_op jit(solution)/shard_map/ppermute | solution.py:508
  167.9 4.9 %collective-permute-done.27 = bf16[256,512]{1,0:T(8,128)(2,1)S(1)} collective-permute-done((bf16[256,512]{1,0:T(8,128)(2,1)}, bf16[256,512]{1,0:T(8,128)(2,1)S(1)}, u32[]{:S(2)}, u32[]{:S(2)}) %collective-permute-start.27) | collective-permute-done | bytes 262176 | tf_op jit(solution)/shard_map/ppermute | solution.py:508
  172.9 1.6 collective-permute-done.26
  175.8 5.1 %project_b.1 = (f32[256,256]{1,0:T(8,128)}, bf16[256,256]{1,0:T(8,128)(2,1)}, bf16[256,256]{1,0:T(8,128)(2,1)}, bf16[256,256]{1,0:T(8,128)(2,1)}) custom-call(bf16[512,640]{1,0:T(8,128)(2,1)} %copy-done.1, bf16[512,640]{1,0:T(8,128)(2,1)} %copy-done.9, bf16[8,2048,128]{2,1,0:T(8,128)(2,1)} %bitcast.58, bf16[256,1024]{1,0:T(8,128)(2,1)} %copy-done.10), custom_call_target="tpu_custom_call" | custom-call | flops 536870912 | bytes 5242880 | tf_op jit(solution)/shard_map/project_b/pallas_call | solution.py:486
  182.0 1.9 collective-permute-start.31
  183.9 2.7 %collective-permute-done.32 = bf16[256,256]{1,0:T(8,128)(2,1)S(1)} collective-permute-done((bf16[256,256]{1,0:T(8,128)(2,1)}, bf16[256,256]{1,0:T(8,128)(2,1)S(1)}, u32[]{:S(2)}, u32[]{:S(2)}) %collective-permute-start.32) | collective-permute-done | bytes 131104 | tf_op jit(solution)/shard_map/ppermute | solution.py:508
  186.6 2.6 %collective-permute-done.31 = bf16[256,256]{1,0:T(8,128)(2,1)S(1)} collective-permute-done((bf16[256,256]{1,0:T(8,128)(2,1)}, bf16[256,256]{1,0:T(8,128)(2,1)S(1)}, u32[]{:S(2)}, u32[]{:S(2)}) %collective-permute-start.31) | collective-permute-done | bytes 131104 | tf_op jit(solution)/shard_map/ppermute | solution.py:508
  191.0 2.2 %collective-permute-start.33 = (bf16[512,128]{1,0:T(8,128)(2,1)S(1)}, bf16[512,128]{1,0:T(8,128)(2,1)S(1)}, u32[]{:S(2)}, u32[]{:S(2)}) collective-permute-start(bf16[512,128]{1,0:T(8,128)(2,1)S(1)} %broadcast_select_fusion.2), channel_id=1, source_target_pairs={{0,1},{1,0},{2,3},{3,2},{4,5},{5,4},{6,7},{7,6},{8,9},{9,8},{10,11... | collective-permute-start | bytes 393224 | tf_op jit(solution)/shard_map/ppermute | solution.py:504
  (121 shorter events, 23.5 us)
Async XLA Ops:
  6.5 16.8 %copy-start = (f32[4,2048]{1,0:T(4,128)S(1)}, f32[4,2048]{1,0:T(4,128)}, u32[]{:S(2)}) copy-start(f32[4,2048]{1,0:T(4,128)} %param.23) | copy-start | bytes 98308
  6.5 136.8 %all-gather.3.cloned.1.call-start = ((), (), s32[]{:S(2)}) async-start(), calls=%async_computation | async-start | bytes 4718592 | tf_op jit(solution)/shard_map/all_gather | solution.py:588
  7.5 18.8 %collective-permute-start = (bf16[256,256]{1,0:T(8,128)(2,1)S(1)}, bf16[256,256]{1,0:T(8,128)(2,1)S(1)}, u32[]{:S(2)}, u32[]{:S(2)}) collective-permute-start(bf16[256,256]{1,0:T(8,128)(2,1)S(1)} %get-tuple-element.71), channel_id=1, source_target_pairs={{0,4},{1,5},{2,6},{3,7},{4,8},{5,9},{6,10},{7,11},{8,12},{9,13},{1... | collective-permute-start | bytes 393224 | tf_op jit(solution)/shard_map/ppermute | solution.py:508
  9.7 18.8 %collective-permute-start.1 = (bf16[256,256]{1,0:T(8,128)(2,1)S(1)}, bf16[256,256]{1,0:T(8,128)(2,1)}, u32[]{:S(2)}, u32[]{:S(2)}) collective-permute-start(bf16[256,256]{1,0:T(8,128)(2,1)S(1)} %get-tuple-element.71), channel_id=1, source_target_pairs={{0,12},{1,13},{2,14},{3,15},{4,0},{5,1},{6,2},{7,3},{8,4},{9,5},{1... | collective-permute-start | bytes 393224 | tf_op jit(solution)/shard_map/ppermute | solution.py:508
  11.0 17.4 %collective-permute-start.2 = (bf16[256,256]{1,0:T(8,128)(2,1)S(1)}, bf16[256,256]{1,0:T(8,128)(2,1)}, u32[]{:S(2)}, u32[]{:S(2)}) collective-permute-start(bf16[256,256]{1,0:T(8,128)(2,1)S(1)} %get-tuple-element.71), channel_id=1, source_target_pairs={{0,8},{1,9},{2,10},{3,11},{4,12},{5,13},{6,14},{7,15},{8,0},{9,1},... | collective-permute-start | bytes 393224 | tf_op jit(solution)/shard_map/ppermute | solution.py:508
  14.1 11.0 %collective-permute-start.3 = (bf16[16,256]{1,0:T(8,128)(2,1)S(1)}, bf16[16,256]{1,0:T(8,128)(2,1)S(1)}, u32[]{:S(2)}, u32[]{:S(2)}) collective-permute-start(bf16[16,256]{1,0:T(8,128)(2,1)S(1)} %pad_maximum_fusion.13), channel_id=1, source_target_pairs={{0,16},{16,32},{32,48},{48,64},{64,80},{80,96},{96,112},{112,128},... | collective-permute-start | bytes 24584 | tf_op jit(solution)/shard_map/ppermute | solution.py:512
  17.7 1.6 copy-start.12
  19.5 3.2 %copy-start.13 = (s32[512]{0:T(512)S(1)}, s32[512]{0:T(512)}, u32[]{:S(2)}) copy-start(s32[512]{0:T(512)} %param.16) | copy-start | bytes 6148
  19.6 3.8 %copy-start.11 = (bf16[512,256]{1,0:T(8,128)(2,1)S(1)}, bf16[512,256]{1,0:T(8,128)(2,1)}, u32[]{:S(2)}) copy-start(bf16[512,256]{1,0:T(8,128)(2,1)} %param.29) | copy-start | bytes 786436
  19.7 17.2 %collective-permute-start.5 = (bf16[4,272,256]{2,1,0:T(8,128)(2,1)S(1)}, bf16[4,272,256]{2,1,0:T(8,128)(2,1)S(1)}, u32[]{:S(2)}, u32[]{:S(2)}) collective-permute-start(bf16[4,272,256]{2,1,0:T(8,128)(2,1)S(1)} %pad_maximum_fusion.1), channel_id=1, source_target_pairs={{0,2},{1,3},{2,0},{3,1},{4,6},{5,7},{6,4},{7,5},{8,10},{9,11},{10,... | collective-permute-start | bytes 1671176 | tf_op jit(solution)/shard_map/ppermute | solution.py:504
  25.2 11.6 %collective-permute-start.4 = (bf16[272,256]{1,0:T(8,128)(2,1)S(1)}, bf16[272,256]{1,0:T(8,128)(2,1)S(1)}, u32[]{:S(2)}, u32[]{:S(2)}) collective-permute-start(bf16[272,256]{1,0:T(8,128)(2,1)S(1)} %pad_maximum_fusion.11), channel_id=1, source_target_pairs={{0,2},{1,3},{2,0},{3,1},{4,6},{5,7},{6,4},{7,5},{8,10},{9,11},{10,... | collective-permute-start | bytes 417800 | tf_op jit(solution)/shard_map/ppermute | solution.py:504
  26.4 20.1 %collective-permute-start.9 = (bf16[512,128]{1,0:T(8,128)(2,1)}, bf16[512,128]{1,0:T(8,128)(2,1)}, u32[]{:S(2)}, u32[]{:S(2)}) collective-permute-start(bf16[512,128]{1,0:T(8,128)(2,1)} %get-tuple-element.154), channel_id=1, source_target_pairs={{0,1},{1,0},{2,3},{3,2},{4,5},{5,4},{6,7},{7,6},{8,9},{9,8},{10,11... | collective-permute-start | bytes 393224 | tf_op jit(solution)/shard_map/ppermute | solution.py:504
  38.7 12.6 %collective-permute-start.8 = (bf16[4,256,256]{2,1,0:T(8,128)(2,1)}, bf16[4,256,256]{2,1,0:T(8,128)(2,1)}, u32[]{:S(2)}, u32[]{:S(2)}) collective-permute-start(bf16[4,256,256]{2,1,0:T(8,128)(2,1)} %get-tuple-element.150), channel_id=1, source_target_pairs={{0,2},{1,3},{2,0},{3,1},{4,6},{5,7},{6,4},{7,5},{8,10},{9,11},{10,... | collective-permute-start | bytes 1572872 | tf_op jit(solution)/shard_map/ppermute | solution.py:504
  41.6 7.1 %collective-permute-start.6 = (bf16[2,272,256]{2,1,0:T(8,128)(2,1)S(1)}, bf16[2,272,256]{2,1,0:T(8,128)(2,1)S(1)}, u32[]{:S(2)}, u32[]{:S(2)}) collective-permute-start(bf16[2,272,256]{2,1,0:T(8,128)(2,1)S(1)} %pad_maximum_fusion.5), channel_id=1, source_target_pairs={{0,4},{1,5},{2,6},{3,7},{4,8},{5,9},{6,10},{7,11},{8,12},{9,13},{1... | collective-permute-start | bytes 835592 | tf_op jit(solution)/shard_map/ppermute | solution.py:508
  42.0 6.7 %collective-permute-start.7 = (bf16[2,272,256]{2,1,0:T(8,128)(2,1)S(1)}, bf16[2,272,256]{2,1,0:T(8,128)(2,1)S(1)}, u32[]{:S(2)}, u32[]{:S(2)}) collective-permute-start(bf16[2,272,256]{2,1,0:T(8,128)(2,1)S(1)} %pad_maximum_fusion.5), channel_id=1, source_target_pairs={{0,12},{1,13},{2,14},{3,15},{4,0},{5,1},{6,2},{7,3},{8,4},{9,5},{1... | collective-permute-start | bytes 835592 | tf_op jit(solution)/shard_map/ppermute | solution.py:508
  51.3 5.2 %collective-permute-start.10 = (bf16[272,256]{1,0:T(8,128)(2,1)S(1)}, bf16[272,256]{1,0:T(8,128)(2,1)S(1)}, u32[]{:S(2)}, u32[]{:S(2)}) collective-permute-start(bf16[272,256]{1,0:T(8,128)(2,1)S(1)} %slice_bitcast_fusion.1), channel_id=1, source_target_pairs={{0,4},{1,5},{2,6},{3,7},{4,8},{5,9},{6,10},{7,11},{8,12},{9,13},{1... | collective-permute-start | bytes 417800 | tf_op jit(solution)/shard_map/ppermute | solution.py:508
  51.7 5.4 %collective-permute-start.12 = (bf16[1024,128]{1,0:T(8,128)(2,1)S(1)}, bf16[1024,128]{1,0:T(8,128)(2,1)S(1)}, u32[]{:S(2)}, u32[]{:S(2)}) collective-permute-start(bf16[1024,128]{1,0:T(8,128)(2,1)S(1)} %pad_maximum_fusion.9), channel_id=1, source_target_pairs={{0,128},{16,144},{32,160},{48,176},{64,192},{80,208},{96,224},{112... | collective-permute-start | bytes 786440 | tf_op jit(solution)/shard_map/ppermute | solution.py:585
  52.7 4.5 %collective-permute-start.11 = (bf16[272,256]{1,0:T(8,128)(2,1)S(1)}, bf16[272,256]{1,0:T(8,128)(2,1)S(1)}, u32[]{:S(2)}, u32[]{:S(2)}) collective-permute-start(bf16[272,256]{1,0:T(8,128)(2,1)S(1)} %slice_bitcast_fusion), channel_id=1, source_target_pairs={{0,12},{1,13},{2,14},{3,15},{4,0},{5,1},{6,2},{7,3},{8,4},{9,5},{1... | collective-permute-start | bytes 417800 | tf_op jit(solution)/shard_map/ppermute | solution.py:508
  58.1 9.1 %collective-permute-start.13 = (bf16[8,272,256]{2,1,0:T(8,128)(2,1)S(1)}, bf16[8,272,256]{2,1,0:T(8,128)(2,1)S(1)}, u32[]{:S(2)}, u32[]{:S(2)}) collective-permute-start(bf16[8,272,256]{2,1,0:T(8,128)(2,1)S(1)} %bitcast_dynamic-update-slice_fusion.own_a), channel_id=1, source_target_pairs={{0,1},{1,0},{2,3},{3,2},{4,5},{5,4},{6,7},{7,6},{8,9},{9,8},{10,11... | collective-permute-start | bytes 3342344 | tf_op jit(solution)/shard_map/ppermute | solution.py:504
  64.4 8.0 %copy-start.3 = (bf16[4096,512]{1,0:T(8,128)(2,1)S(1)}, bf16[4096,512]{1,0:T(8,128)(2,1)}, u32[]{:S(2)}) copy-start(bf16[4096,512]{1,0:T(8,128)(2,1)} %w_x.1) | copy-start | bytes 12582916
  64.5 2.7 %collective-permute-start.14 = (bf16[8,256,256]{2,1,0:T(8,128)(2,1)S(1)}, bf16[8,256,256]{2,1,0:T(8,128)(2,1)S(1)}, u32[]{:S(2)}, u32[]{:S(2)}) collective-permute-start(bf16[8,256,256]{2,1,0:T(8,128)(2,1)S(1)} %bitcast.47), channel_id=1, source_target_pairs={{0,1},{1,0},{2,3},{3,2},{4,5},{5,4},{6,7},{7,6},{8,9},{9,8},{10,11... | collective-permute-start | bytes 3145736 | tf_op jit(solution)/shard_map/ppermute | solution.py:504
  67.4 14.8 %collective-permute-start.15 = (bf16[2,272,256]{2,1,0:T(8,128)(2,1)S(1)}, bf16[2,272,256]{2,1,0:T(8,128)(2,1)S(1)}, u32[]{:S(2)}, u32[]{:S(2)}) collective-permute-start(bf16[2,272,256]{2,1,0:T(8,128)(2,1)S(1)} %pad_maximum_fusion.6), channel_id=1, source_target_pairs={{0,4},{1,5},{2,6},{3,7},{4,8},{5,9},{6,10},{7,11},{8,12},{9,13},{1... | collective-permute-start | bytes 835592 | tf_op jit(solution)/shard_map/ppermute | solution.py:508
  68.1 14.7 %collective-permute-start.16 = (bf16[2,272,256]{2,1,0:T(8,128)(2,1)S(1)}, bf16[2,272,256]{2,1,0:T(8,128)(2,1)S(1)}, u32[]{:S(2)}, u32[]{:S(2)}) collective-permute-start(bf16[2,272,256]{2,1,0:T(8,128)(2,1)S(1)} %pad_maximum_fusion.7), channel_id=1, source_target_pairs={{0,12},{1,13},{2,14},{3,15},{4,0},{5,1},{6,2},{7,3},{8,4},{9,5},{1... | collective-permute-start | bytes 835592 | tf_op jit(solution)/shard_map/ppermute | solution.py:508
  71.2 13.3 %collective-permute-start.17 = (bf16[2,272,256]{2,1,0:T(8,128)(2,1)S(1)}, bf16[2,272,256]{2,1,0:T(8,128)(2,1)S(1)}, u32[]{:S(2)}, u32[]{:S(2)}) collective-permute-start(bf16[2,272,256]{2,1,0:T(8,128)(2,1)S(1)} %pad_maximum_fusion.8), channel_id=1, source_target_pairs={{0,8},{1,9},{2,10},{3,11},{4,12},{5,13},{6,14},{7,15},{8,0},{9,1},... | collective-permute-start | bytes 835592 | tf_op jit(solution)/shard_map/ppermute | solution.py:508
  72.5 4.7 %copy-start.2 = (bf16[4096,512]{1,0:T(8,128)(2,1)S(1)}, bf16[4096,512]{1,0:T(8,128)(2,1)}, u32[]{:S(2)}) copy-start(bf16[4096,512]{1,0:T(8,128)(2,1)} %w_z.1) | copy-start | bytes 12582916
  82.1 6.0 %copy-start.4 = (f32[4,512]{1,0:T(4,128)S(1)}, f32[4,512]{1,0:T(4,128)}, u32[]{:S(2)}) copy-start(f32[4,512]{1,0:T(4,128)} %taps_x) | copy-start | bytes 24580
  82.1 6.0 %copy-start.6 = (f32[512]{0:T(512)S(1)}, f32[512]{0:T(512)}, u32[]{:S(2)}) copy-start(f32[512]{0:T(512)} %param.22) | copy-start | bytes 6148
  82.2 6.0 %copy-start.7 = (f32[8]{0:T(128)S(1)}, f32[8]{0:T(128)}, u32[]{:S(2)}) copy-start(f32[8]{0:T(128)} %param.25) | copy-start | bytes 100
  82.2 6.0 %copy-start.8 = (f32[8]{0:T(128)S(1)}, f32[8]{0:T(128)}, u32[]{:S(2)}) copy-start(f32[8]{0:T(128)} %param.26) | copy-start | bytes 100
  84.6 3.6 %collective-permute-start.18 = (bf16[8,272,256]{2,1,0:T(8,128)(2,1)S(1)}, bf16[8,272,256]{2,1,0:T(8,128)(2,1)S(1)}, u32[]{:S(2)}, u32[]{:S(2)}) collective-permute-start(bf16[8,272,256]{2,1,0:T(8,128)(2,1)S(1)} %constant_dynamic-update-slice_fusion.4.w_own), channel_id=1, source_target_pairs={{0,1},{1,0},{2,3},{3,2},{4,5},{5,4},{6,7},{7,6},{8,9},{9,8},{10,11... | collective-permute-start | bytes 3342344 | tf_op jit(solution)/shard_map/ppermute | solution.py:504
  96.5 9.9 %collective-permute-start.19 = (bf16[144,512]{1,0:T(8,128)(2,1)S(1)}, bf16[144,512]{1,0:T(8,128)(2,1)S(1)}, u32[]{:S(2)}, u32[]{:S(2)}) collective-permute-start(bf16[144,512]{1,0:T(8,128)(2,1)S(1)} %get-tuple-element.101.mine), channel_id=1, source_target_pairs={{0,16},{16,32},{32,48},{48,64},{64,80},{80,96},{96,112},{112,128},... | collective-permute-start | bytes 442376 | tf_op jit(solution)/shard_map/ppermute | solution.py:520
  100.0 14.1 %collective-permute-start.20 = (bf16[144,512]{1,0:T(8,128)(2,1)S(1)}, bf16[144,512]{1,0:T(8,128)(2,1)S(1)}, u32[]{:S(2)}, u32[]{:S(2)}) collective-permute-start(bf16[144,512]{1,0:T(8,128)(2,1)S(1)} %get-tuple-element.101.mine), channel_id=1, source_target_pairs={{0,32},{16,48},{32,64},{48,80},{64,96},{80,112},{96,128},{112,144}... | collective-permute-start | bytes 442376 | tf_op jit(solution)/shard_map/ppermute | solution.py:520
  114.2 20.2 %collective-permute-start.21 = (bf16[144,512]{1,0:T(8,128)(2,1)S(1)}, bf16[144,512]{1,0:T(8,128)(2,1)S(1)}, u32[]{:S(2)}, u32[]{:S(2)}) collective-permute-start(bf16[144,512]{1,0:T(8,128)(2,1)S(1)} %three.1), channel_id=1, source_target_pairs={{0,16},{16,32},{32,48},{48,64},{64,80},{80,96},{96,112},{112,128},... | collective-permute-start | bytes 442376 | tf_op jit(solution)/shard_map/ppermute | solution.py:520
  119.0 15.4 %collective-permute-start.22 = (bf16[144,512]{1,0:T(8,128)(2,1)S(1)}, bf16[144,512]{1,0:T(8,128)(2,1)S(1)}, u32[]{:S(2)}, u32[]{:S(2)}) collective-permute-start(bf16[144,512]{1,0:T(8,128)(2,1)S(1)} %three.1), channel_id=1, source_target_pairs={{0,64},{16,80},{32,96},{48,112},{64,128},{80,144},{96,160},{112,17... | collective-permute-start | bytes 442376 | tf_op jit(solution)/shard_map/ppermute | solution.py:520
  128.2 10.0 %collective-permute-start.23 = (bf16[144,512]{1,0:T(8,128)(2,1)S(1)}, bf16[144,512]{1,0:T(8,128)(2,1)S(1)}, u32[]{:S(2)}, u32[]{:S(2)}) collective-permute-start(bf16[144,512]{1,0:T(8,128)(2,1)S(1)} %three.1), channel_id=1, source_target_pairs={{0,112},{16,128},{32,144},{48,160},{64,176},{80,192},{96,208},{112... | collective-permute-start | bytes 442376 | tf_op jit(solution)/shard_map/ppermute | solution.py:520
  132.6 5.6 %copy-start.5 = (f32[512]{0:T(512)S(1)}, f32[512]{0:T(512)}, u32[]{:S(2)}) copy-start(f32[512]{0:T(512)} %param.28) | copy-start | bytes 6148
  140.5 2.8 %copy-start.1 = (bf16[512,640]{1,0:T(8,128)(2,1)}, bf16[512,640]{1,0:T(8,128)(2,1)S(1)}, u32[]{:S(2)}) copy-start(bf16[512,640]{1,0:T(8,128)(2,1)S(1)} %join.1.own) | copy-start | bytes 1966084
  140.5 2.8 %collective-permute-start.24 = (bf16[512,640]{1,0:T(8,128)(2,1)S(1)}, bf16[512,640]{1,0:T(8,128)(2,1)S(1)}, u32[]{:S(2)}, u32[]{:S(2)}) collective-permute-start(bf16[512,640]{1,0:T(8,128)(2,1)S(1)} %join.1.own), channel_id=1, source_target_pairs={{0,1},{1,0},{2,3},{3,2},{4,5},{5,4},{6,7},{7,6},{8,9},{9,8},{10,11... | collective-permute-start | bytes 1966088 | tf_op jit(solution)/shard_map/ppermute | solution.py:504
  149.1 15.2 %collective-permute-start.25 = (bf16[256,1024]{1,0:T(8,128)(2,1)}, bf16[256,1024]{1,0:T(8,128)(2,1)S(1)}, u32[]{:S(2)}, u32[]{:S(2)}) collective-permute-start(bf16[256,1024]{1,0:T(8,128)(2,1)} %project_far.1), channel_id=1, source_target_pairs={{0,2},{1,3},{2,0},{3,1},{4,6},{5,7},{6,4},{7,5},{8,10},{9,11},{10,... | collective-permute-start | bytes 1572872 | tf_op jit(solution)/shard_map/ppermute | solution.py:504
  158.9 9.0 %collective-permute-start.28 = (bf16[256,512]{1,0:T(8,128)(2,1)}, bf16[256,512]{1,0:T(8,128)(2,1)S(1)}, u32[]{:S(2)}, u32[]{:S(2)}) collective-permute-start(bf16[256,512]{1,0:T(8,128)(2,1)} %get-tuple-element.127), channel_id=1, source_target_pairs={{0,8},{1,9},{2,10},{3,11},{4,12},{5,13},{6,14},{7,15},{8,0},{9,1},... | collective-permute-start | bytes 786440 | tf_op jit(solution)/shard_map/ppermute | solution.py:508
  159.2 13.6 %collective-permute-start.27 = (bf16[256,512]{1,0:T(8,128)(2,1)}, bf16[256,512]{1,0:T(8,128)(2,1)S(1)}, u32[]{:S(2)}, u32[]{:S(2)}) collective-permute-start(bf16[256,512]{1,0:T(8,128)(2,1)} %get-tuple-element.126), channel_id=1, source_target_pairs={{0,12},{1,13},{2,14},{3,15},{4,0},{5,1},{6,2},{7,3},{8,4},{9,5},{1... | collective-permute-start | bytes 786440 | tf_op jit(solution)/shard_map/ppermute | solution.py:508
  162.6 11.9 %collective-permute-start.26 = (bf16[256,512]{1,0:T(8,128)(2,1)}, bf16[256,512]{1,0:T(8,128)(2,1)S(1)}, u32[]{:S(2)}, u32[]{:S(2)}) collective-permute-start(bf16[256,512]{1,0:T(8,128)(2,1)} %get-tuple-element.125), channel_id=1, source_target_pairs={{0,4},{1,5},{2,6},{3,7},{4,8},{5,9},{6,10},{7,11},{8,12},{9,13},{1... | collective-permute-start | bytes 786440 | tf_op jit(solution)/shard_map/ppermute | solution.py:508
  164.3 11.4 %copy-start.10 = (bf16[256,1024]{1,0:T(8,128)(2,1)}, bf16[256,1024]{1,0:T(8,128)(2,1)S(1)}, u32[]{:S(2)}) copy-start(bf16[256,1024]{1,0:T(8,128)(2,1)S(1)} %collective-permute-done.25.b_far) | copy-start | bytes 1572868
  175.7 8.2 %collective-permute-start.29 = (bf16[256,256]{1,0:T(8,128)(2,1)S(1)}, bf16[256,256]{1,0:T(8,128)(2,1)S(1)}, u32[]{:S(2)}, u32[]{:S(2)}) collective-permute-start(bf16[256,256]{1,0:T(8,128)(2,1)S(1)} %select_convert_fusion), channel_id=1, source_target_pairs={{0,2},{1,3},{2,0},{3,1},{4,6},{5,7},{6,4},{7,5},{8,10},{9,11},{10,... | collective-permute-start | bytes 393224 | tf_op jit(solution)/shard_map/ppermute | solution.py:504
  180.9 5.6 %collective-permute-start.32 = (bf16[256,256]{1,0:T(8,128)(2,1)}, bf16[256,256]{1,0:T(8,128)(2,1)S(1)}, u32[]{:S(2)}, u32[]{:S(2)}) collective-permute-start(bf16[256,256]{1,0:T(8,128)(2,1)} %get-tuple-element.132), channel_id=1, source_target_pairs={{0,8},{1,9},{2,10},{3,11},{4,12},{5,13},{6,14},{7,15},{8,0},{9,1},... | collective-permute-start | bytes 393224 | tf_op jit(solution)/shard_map/ppermute | solution.py:508
  182.0 7.2 %collective-permute-start.31 = (bf16[256,256]{1,0:T(8,128)(2,1)}, bf16[256,256]{1,0:T(8,128)(2,1)S(1)}, u32[]{:S(2)}, u32[]{:S(2)}) collective-permute-start(bf16[256,256]{1,0:T(8,128)(2,1)} %get-tuple-element.131), channel_id=1, source_target_pairs={{0,12},{1,13},{2,14},{3,15},{4,0},{5,1},{6,2},{7,3},{8,4},{9,5},{1... | collective-permute-start | bytes 393224 | tf_op jit(solution)/shard_map/ppermute | solution.py:508
  183.8 6.1 %collective-permute-start.30 = (bf16[256,256]{1,0:T(8,128)(2,1)}, bf16[256,256]{1,0:T(8,128)(2,1)S(1)}, u32[]{:S(2)}, u32[]{:S(2)}) collective-permute-start(bf16[256,256]{1,0:T(8,128)(2,1)} %get-tuple-element.130), channel_id=1, source_target_pairs={{0,4},{1,5},{2,6},{3,7},{4,8},{5,9},{6,10},{7,11},{8,12},{9,13},{1... | collective-permute-start | bytes 393224 | tf_op jit(solution)/shard_map/ppermute | solution.py:508
  191.0 3.2 %collective-permute-start.33 = (bf16[512,128]{1,0:T(8,128)(2,1)S(1)}, bf16[512,128]{1,0:T(8,128)(2,1)S(1)}, u32[]{:S(2)}, u32[]{:S(2)}) collective-permute-start(bf16[512,128]{1,0:T(8,128)(2,1)S(1)} %broadcast_select_fusion.2), channel_id=1, source_target_pairs={{0,1},{1,0},{2,3},{3,2},{4,5},{5,4},{6,7},{7,6},{8,9},{9,8},{10,11... | collective-permute-start | bytes 393224 | tf_op jit(solution)/shard_map/ppermute | solution.py:504
  (2 other events, 1.8 us)
Sparse Core Ops, SparseCore 0:
  58.1 73.5 all-gather.2

commit v4 on v1

v4 whole, which is shorter than its diff:
```python
import functools

import jax
import jax.numpy as jnp
from jax import lax
from jax.experimental import pallas as pl
from jax.experimental.pallas import tpu as pltpu
from jax.sharding import PartitionSpec as P

H = 128
P_SIZE = 64
N = 128
G = 8
L = 256
CONV = 4
HALO = 16
NORM_EPS = 1e-05
HIGHEST = lax.Precision.HIGHEST

CHIPS = 8
CORES = 2
HEADS = 8
CH = HEADS * P_SIZE
ROWS = 512
FEAT = 256
Z_RING = 8
CTX = 16
ALL_ROWS = HALO + ROWS
COLS = 2 * N + 2 * HEADS
VMEM = pl.BlockSpec(memory_space=pltpu.VMEM)
BF16 = jnp.bfloat16
F32 = jnp.float32


def params(mib, grid=False):
    more = {"dimension_semantics": ("arbitrary",)} if grid else {}
    return pltpu.CompilerParams(vmem_limit_bytes=mib * 2**20, **more)


def dot(a, b):
    return jnp.dot(a, b, preferred_element_type=F32)


def dot_nt(a, b):
    return lax.dot_general(a, b, (((1,), (1,)), ((), ())), preferred_element_type=F32)


def dot_tn(a, b):
    return lax.dot_general(a, b, (((0,), (0,)), ((), ())), preferred_element_type=F32)


def silu(v):
    return v / (1.0 + jnp.exp(-v))


def spread(cols, first=0, count=HEADS):
    shape = (HEADS, count * P_SIZE)
    head = lax.broadcasted_iota(jnp.int32, shape, 0)
    lane = lax.broadcasted_iota(jnp.int32, shape, 1)
    pick = (head == lane // P_SIZE + first).astype(F32)
    return jnp.dot(cols, pick, precision=HIGHEST, preferred_element_type=F32)


def my_core():
    return lax.rem(lax.axis_index("tp"), CORES)


def add_to(acc, step, value):
    @pl.when(step == 0)
    def _():
        acc[...] = value

    @pl.when(step > 0)
    def _():
        acc[...] += value


def conv_chunk(raw, at, rows, masks, taps, offsets):
    total = offsets + taps[CONV - 1 : CONV, :] * raw[at + HALO : at + HALO + rows, :]
    for tap in range(CONV - 1):
        first = at + HALO - (CONV - 1) + tap
        shifted = raw[first : first + rows, :]
        total = total + taps[tap : tap + 1, :] * (shifted * masks[:, tap : tap + 1])
    return silu(total).astype(BF16)


def rounded(ref):
    ref[...] = ref[...].astype(BF16).astype(F32)


def step_sources():
    for slot in range(2):
        for same_core in (True, False):
            yield slot, same_core


def step_tokens(own, sib, halo_own=None, halo_sib=None):
    parts = []
    for slot, same_core in step_sources():
        part = (own if same_core else sib)[slot, :ROWS]
        if halo_own is not None:
            part = jnp.concatenate([(halo_own if same_core else halo_sib)[slot], part], axis=0)
        parts.append(part)
    return jnp.concatenate(parts, axis=1)


def step_cols(own, sib):
    parts = [(own if same_core else sib)[slot, ROWS:] for slot, same_core in step_sources()]
    return jnp.concatenate(parts, axis=1)


def step_rows(w_ref):
    core = my_core()
    parts = []
    for slot, same_core in step_sources():
        from_core = core if same_core else 1 - core
        at = pl.multiple_of((slot * CORES + from_core) * FEAT, FEAT)
        parts.append(w_ref[pl.ds(at, FEAT), :])
    return jnp.concatenate(parts, axis=0)


def scan_input_kernel(
    own,
    sib,
    halo_own,
    halo_sib,
    w_x,
    cols,
    taps_x,
    bias_x,
    taps_bc,
    bias_bc,
    dt_bias,
    decay,
    xc,
    bcc,
    hcol,
    hrow,
    s0,
    pay,
    acc_x,
    acc_bc,
    raw_bc,
):
    step = pl.program_id(0)
    core = my_core()
    toks = step_tokens(own, sib, halo_own, halo_sib)
    add_to(acc_x, step, dot(toks, step_rows(w_x)))
    add_to(acc_bc, step, dot_nt(toks, step_cols(own, sib)))

    @pl.when(step == pl.num_programs(0) - 1)
    def _():
        raw_dt = acc_bc[HALO:, 2 * N :]
        raw_dt = jnp.where(core == 0, raw_dt[:, :HEADS], raw_dt[:, HEADS:])
        pre = raw_dt + dt_bias[...]
        dt = jnp.maximum(pre, 0.0) + jnp.log1p(jnp.exp(-jnp.abs(pre)))
        loga = -decay[...] * dt
        acc_x[...] = acc_x[...].astype(BF16).astype(F32)
        raw_bc[...] = acc_bc[:, : 2 * N].astype(BF16).astype(F32)
        for at in range(0, ROWS, 64):
            masks = cols[at : at + 64, :]
            xc[at : at + 64, :] = conv_chunk(acc_x, at, 64, masks, taps_x, bias_x[...])
            bcc[at : at + 64, :] = conv_chunk(raw_bc, at, 64, masks, taps_bc, bias_bc[...])
        lower = (
            lax.broadcasted_iota(jnp.int32, (L, L), 0) >= lax.broadcasted_iota(jnp.int32, (L, L), 1)
        ).astype(F32)
        cum0 = jnp.dot(lower, loga[:L], precision=HIGHEST, preferred_element_type=F32)
        cum1 = jnp.dot(lower, loga[L:], precision=HIGHEST, preferred_element_type=F32)
        end0, end1 = cum0[L - 1 :], cum1[L - 1 :]
        slab = jnp.exp(jnp.concatenate([cum0, cum1 + end0], axis=0)) * cols[:, 3:4]
        inner = jnp.exp(cum1) * cols[L:, 5:6]
        tail0 = jnp.exp(end0 - cum0) * cols[:L, 6:7] * dt[:L]
        tail1 = jnp.exp(end1 - cum1) * cols[L:, 4:5] * dt[L:]
        cum = jnp.concatenate([cum0, cum1], axis=0)
        blank = jnp.zeros((ROWS, 128 - 4 * HEADS), F32)
        wide = jnp.concatenate(
            [cum, dt, slab, jnp.concatenate([inner, inner], axis=0), blank], axis=1
        )
        hcol[...] = wide
        hrow[...] = wide.T[: 2 * HEADS]
        scaled0 = (xc[:L, :].astype(F32) * spread(tail0)).astype(BF16)
        scaled1 = (xc[L:, :].astype(F32) * spread(tail1)).astype(BF16)
        state0 = dot_tn(bcc[:L, :N], scaled0)
        state1 = dot_tn(bcc[L:, :N], scaled1)
        s0[...] = state0.astype(BF16)
        ends = jnp.concatenate(
            [inner[L - 1 :], slab[ROWS - 1 :], jnp.zeros((6, HEADS), F32)], axis=0
        )
        ends = spread(ends)
        final = ends[0:1] * state0 + state1
        factor = factor_rows(ends[1:2])
        for piece in range(CTX):
            part = final[8 * piece : 8 * piece + 8]
            pay[piece] = jnp.concatenate([part, factor], axis=0).astype(BF16)


def factor_rows(factor):
    high = factor.astype(BF16).astype(F32)
    row = lax.broadcasted_iota(jnp.int32, (8, CH), 0)
    return jnp.where(row == 0, high, jnp.where(row == 1, factor - high, 0.0))


def over_chips(kernel, blocked, fixed, shapes, scratch, mib, flops, name):
    whole = lambda a: pl.BlockSpec(a.shape, lambda i: (0,) * len(a.shape))
    return pl.pallas_call(
        kernel,
        grid=(CHIPS // 2,),
        in_specs=[spec for _, spec in blocked] + [whole(a) for a in fixed],
        out_specs=[whole(a) for a in shapes],
        out_shape=shapes,
        scratch_shapes=scratch,
        compiler_params=params(mib, True),
        cost_estimate=pl.CostEstimate(
            flops=flops, bytes_accessed=8 * 2**20, transcendentals=10**6
        ),
        name=name,
    )(*[a for a, _ in blocked], *fixed)


def two_chips(a, rows):
    return a, pl.BlockSpec((2, rows, FEAT), lambda i: (i, 0, 0))


def their_rows(w):
    return w, pl.BlockSpec((4 * FEAT, CH), lambda i: (i, 0))


def scan_input(own, sib, halo_own, halo_sib, w_x, fixed):
    shapes = [
        jax.ShapeDtypeStruct((ROWS, CH), BF16),
        jax.ShapeDtypeStruct((ROWS, 2 * N), BF16),
        jax.ShapeDtypeStruct((ROWS, 128), F32),
        jax.ShapeDtypeStruct((2 * HEADS, ROWS), F32),
        jax.ShapeDtypeStruct((N, CH), BF16),
        jax.ShapeDtypeStruct((CTX, 16, CH), BF16),
    ]
    blocked = [two_chips(a, ROWS + COLS) for a in (own, sib)]
    blocked += [two_chips(a, HALO) for a in (halo_own, halo_sib)] + [their_rows(w_x)]
    scratch = [
        pltpu.VMEM((ALL_ROWS, CH), F32),
        pltpu.VMEM((ALL_ROWS, COLS), F32),
        pltpu.VMEM((ALL_ROWS, 2 * N), F32),
    ]
    flops = 2 * ALL_ROWS * 4096 * (CH + COLS)
    return over_chips(
        scan_input_kernel, blocked, fixed, shapes, scratch, 24, flops, "scan_input"
    )


def gate_kernel(own, sib, w_z, gates, acc):
    step = pl.program_id(0)
    add_to(acc, step, dot(step_tokens(own, sib), step_rows(w_z)))

    @pl.when(step == pl.num_programs(0) - 1)
    def _():
        for at in range(0, ROWS, 64):
            gates[at : at + 64, :] = silu(acc[at : at + 64, :].astype(BF16).astype(F32))


def gate(own, sib, w_z):
    shapes = [jax.ShapeDtypeStruct((ROWS, CH), F32)]
    blocked = [two_chips(a, ROWS) for a in (own, sib)] + [their_rows(w_z)]
    scratch = [pltpu.VMEM((ROWS, CH), F32)]
    flops = 2 * ROWS * 4096 * CH
    return over_chips(gate_kernel, blocked, [], shapes, scratch, 16, flops, "gate")[0]


def intra_kernel(xc, bcc, hcol, hrow, s0, cols, seg_row, skip, y):
    for block in range(2):
        intra_block(block * L, xc, bcc, hcol, hrow, s0, cols, seg_row, skip, y)


def intra_block(at, xc, bcc, hcol, hrow, s0, cols, seg_row, skip, y):
    b_vals, c_vals = bcc[at : at + L, :N], bcc[at : at + L, N:]
    after = lax.broadcasted_iota(jnp.int32, (L, L), 0) >= lax.broadcasted_iota(
        jnp.int32, (L, L), 1
    )
    same = cols[at : at + L, 7:8] == seg_row[0:1, at : at + L]
    scores = jnp.where(after & same, dot_nt(c_vals, b_vals), 0.0)
    for half in range(2):
        lanes = slice(half * 256, half * 256 + 256)
        weights, values = [], []
        x_half = xc[at : at + L, lanes]
        head_of = lax.broadcasted_iota(jnp.int32, (1, 256), 1) // P_SIZE
        for part in range(4):
            head = half * 4 + part
            gap = hcol[at : at + L, head : head + 1] - hrow[head : head + 1, at : at + L]
            decay = jnp.exp(jnp.minimum(gap, 0.0))
            dt_row = hrow[HEADS + head : HEADS + head + 1, at : at + L]
            weights.append((scores * decay * dt_row).astype(BF16))
            values.append(x_half * (head_of == part).astype(BF16))
        out = dot(jnp.concatenate(weights, axis=1), jnp.concatenate(values, axis=0))
        out = out + skip[:, lanes] * x_half.astype(F32)
        if at:
            carried = spread(hcol[at : at + L, 3 * HEADS : 4 * HEADS], half * 4, 4)
            out = out + carried * dot(c_vals, s0[:, lanes])
        y[at : at + L, lanes] = out


def intra(*args):
    return pl.pallas_call(
        intra_kernel,
        in_specs=[VMEM] * len(args),
        out_specs=VMEM,
        out_shape=jax.ShapeDtypeStruct((ROWS, CH), F32),
        compiler_params=params(12),
        cost_estimate=pl.CostEstimate(
            flops=2 * ROWS * L * CH * 4, bytes_accessed=4 * 2**20, transcendentals=2 * 10**6
        ),
        name="intra",
    )(*args)


def prefix_kernel(pieces, out):
    total = jnp.zeros((8, CH), F32)
    for pair in range(8):
        held = []
        for place in (2 * pair, 2 * pair + 1):
            held.append(total)
            piece = pieces[place].astype(F32)
            total = total * (piece[8:9] + piece[9:10]) + piece[:8]
        out[16 * pair : 16 * pair + 16, :] = jnp.concatenate(held, axis=0).astype(BF16)


def prefix(pieces):
    return pl.pallas_call(
        prefix_kernel,
        in_specs=[VMEM],
        out_specs=VMEM,
        out_shape=jax.ShapeDtypeStruct((N, CH), BF16),
        compiler_params=params(8),
        name="prefix",
    )(pieces)


def join_kernel(y, gates, bcc, hcol, state, gain, out):
    for at in range(0, ROWS, 128):
        c_vals = bcc[at : at + 128, N:]
        carried = spread(hcol[at : at + 128, 2 * HEADS : 3 * HEADS])
        total = y[at : at + 128, :] + carried * dot(c_vals, state[...])
        gated = total * gates[at : at + 128, :]
        square = jnp.sum(gated * gated, axis=1, keepdims=True)
        high = square.astype(BF16).astype(F32)
        lane = lax.broadcasted_iota(jnp.int32, (128, 128), 1)
        out[at : at + 128, :CH] = (gated * gain[...]).astype(BF16)
        out[at : at + 128, CH:] = jnp.where(lane < 64, high, square - high).astype(BF16)


def join(*args):
    return pl.pallas_call(
        join_kernel,
        in_specs=[VMEM] * len(args),
        out_specs=VMEM,
        out_shape=jax.ShapeDtypeStruct((ROWS, CH + 128), BF16),
        compiler_params=params(12),
        cost_estimate=pl.CostEstimate(
            flops=2 * ROWS * N * CH, bytes_accessed=4 * 2**20, transcendentals=0
        ),
        name="join",
    )(*args)


def project_kernel(place, own, sib, w, out):
    del place
    square = own[:, CH:].astype(F32) + sib[:, CH:].astype(F32)
    scale = lax.rsqrt((square[:, 0:1] + square[:, 64:65]) / (2.0 * CH) + NORM_EPS)
    values = jnp.concatenate([own[:, :CH], sib[:, :CH]], axis=1)
    rows = jnp.concatenate([w[0], w[1]], axis=1)
    out[0] = (dot(values, rows) * scale).astype(BF16)


def project(own, sib, w_all, y_low):
    def columns(chip, place):
        return lax.rem(chip, 4), lax.rem(lax.div(chip, 4) + place[0], 2), 0

    whole = pl.BlockSpec(own.shape, lambda i, place: (0, 0))
    return pl.pallas_call(
        project_kernel,
        grid_spec=pltpu.PrefetchScalarGridSpec(
            num_scalar_prefetch=1,
            grid=(CHIPS,),
            in_specs=[whole, whole, pl.BlockSpec((2, 2 * CH, 128), columns)],
            out_specs=pl.BlockSpec((1, ROWS, 256), lambda i, place: (i, 0, 0)),
        ),
        out_shape=jax.ShapeDtypeStruct((CHIPS, ROWS, 256), BF16),
        compiler_params=params(14, True),
        cost_estimate=pl.CostEstimate(
            flops=8 * ROWS * CH * 2048, bytes_accessed=8 * 2**20, transcendentals=0
        ),
        name="project",
    )(y_low[None], own, sib, w_all)


def swapped(value, bit):
    return lax.ppermute(value, "tp", [(i, i ^ bit) for i in range(16)])


def next_ctx(value):
    return lax.ppermute(value, "ctx", [(i, i + 1) for i in range(15)])


def between_chips(value):
    same_core = [[2 * chip + core for chip in range(CHIPS)] for core in range(CORES)]
    return lax.all_to_all(value, "tp", 0, 0, axis_index_groups=same_core)


def between_slabs(value):
    return lax.all_to_all(value, "ctx", 0, 0)


def together(*values):
    return lax.optimization_barrier(values)


def pick(core, first, second):
    return jnp.where(core == 0, first, second)


def document_columns(seg_ids, ids_prior):
    ids_all = jnp.concatenate([ids_prior, seg_ids])
    prior = ids_prior[2]
    same = lambda a: (seg_ids == a).astype(F32)
    columns = [same(ids_all[tap : tap + ROWS]) for tap in range(CONV - 1)]
    columns += [same(prior), same(seg_ids[-1]), same(seg_ids[L - 1]), same(seg_ids[L - 1])]
    columns += [seg_ids.astype(F32)]
    cols = jnp.pad(jnp.stack(columns, axis=1), ((0, 0), (0, 128 - len(columns))))
    return cols, jnp.broadcast_to(seg_ids.astype(F32)[None], (8, ROWS))


def local(
    tokens,
    seg_ids,
    w_x,
    w_z,
    w_bc,
    w_dt,
    conv_x,
    conv_x_bias,
    conv_bc,
    conv_bc_bias,
    dt_bias,
    decay_rate,
    skip_gain,
    norm_weight,
    w_out,
):
    rank = lax.axis_index("tp")
    core = rank % CORES
    chip = rank // CORES
    y_low = (lax.axis_index("ctx") // Z_RING).astype(jnp.int32)

    w_cols = jnp.concatenate(
        [w_bc.T.reshape(CHIPS, 2 * N, FEAT), w_dt.T.reshape(CHIPS, 2 * HEADS, FEAT)], axis=1
    )
    shared = jnp.broadcast_to(tokens[None], (CHIPS, ROWS, FEAT))
    own = between_chips(jnp.concatenate([shared, w_cols], axis=1))

    ids_row = jnp.pad((seg_ids[-3:] + 1).astype(BF16), (0, FEAT - 3))[None]
    halo = next_ctx(jnp.concatenate([ids_row, tokens[1 - HALO :]], axis=0))
    ids_prior = halo[0, :3].astype(jnp.int32) - 1
    halo_own = between_chips(jnp.broadcast_to(halo[None], (CHIPS, HALO, FEAT)))
    halo_sib = swapped(halo_own, 1)

    halves = (w_out[:, :128], w_out[:, 128:])
    w_pair = jnp.concatenate(
        [pick(core, *halves), swapped(pick(core, halves[1], halves[0]), 1)], axis=0
    )
    w_far = lax.ppermute(w_pair, "ctx", [(i, i ^ Z_RING) for i in range(2 * Z_RING)])
    same_y = [list(range(Z_RING)), list(range(Z_RING, 2 * Z_RING))]
    w_both = jnp.concatenate([w_pair, w_far], axis=0)
    w_all = lax.all_gather(w_both, "ctx", axis=0, axis_index_groups=same_y)

    cols, seg_row = document_columns(seg_ids, ids_prior)
    taps_bc = lax.dynamic_slice_in_dim(conv_bc, chip * 2 * N, 2 * N, 1)
    bias_bc = lax.dynamic_slice_in_dim(conv_bc_bias, chip * 2 * N, 2 * N, 0)[None]
    skip = jnp.repeat(skip_gain, P_SIZE)[None]
    fixed = [cols, conv_x, conv_x_bias[None], taps_bc, bias_bc, dt_bias[None], decay_rate[None]]
    own, fixed, seg_row, skip, halo_own, halo_sib = together(
        own, fixed, seg_row, skip, halo_own, halo_sib
    )
    sib = swapped(own, 1)
    xc, bcc, hcol, hrow, s0, pay = scan_input(own, sib, halo_own, halo_sib, w_x, fixed)
    own, sib, pay = together(own, sib, pay)
    pieces = between_slabs(pay)
    gates = gate(own, sib, w_z)
    pieces, gates, xc, bcc = together(pieces, gates, xc, bcc)
    state = between_slabs(prefix(pieces).reshape(CTX, 8, CH)).reshape(N, CH)
    y = intra(xc, bcc, hcol, hrow, s0, fixed[0], seg_row, skip)
    mine = join(y, gates, bcc, hcol, state, norm_weight[None])
    parts = between_chips(project(mine, swapped(mine, 1), w_all, y_low))
    total = jnp.sum(parts.astype(F32), axis=0).astype(BF16)
    parts = (total[:, :128], total[:, 128:])
    kept = pick(core, *parts)
    given = swapped(pick(core, parts[1], parts[0]), 1)
    return jnp.concatenate([pick(core, kept, given), pick(core, given, kept)], axis=1)


def solution(mesh):
    return jax.shard_map(
        local,
        mesh=mesh,
        in_specs=(
            P("ctx", "tp"),
            P("ctx"),
            P(None, "tp"),
            P(None, "tp"),
            P("tp", None),
            P("tp", None),
            P(None, "tp"),
            P("tp"),
            P(),
            P(),
            P("tp"),
            P("tp"),
            P("tp"),
            P("tp"),
            P("tp", "ctx"),
        ),
        out_specs=P("ctx", "tp"),
        check_vma=False,
    )
```

time: 227 us -> 192 us (0.85)
  waiting for transfers between devices: 82.2 us -> 43.5 us
  starting transfers between devices: 37.1 us -> 43 us
    all_to_all x1 -> x2, waiting for transfers between devices: 52.2 us -> 35.1 us  [between_chips(): return lax.all_to_all(value, 'tp', 0, 0, axis_index_groups=same_core)]
    ppermute x4 -> x1, waiting for transfers between devices: 9.76 us -> 0.01 us  [local(): lax.ppermute(w_pair, 'ctx', [(i, i ^ Z_RING) for i in range(2 * Z_RING)])]
    all_to_all x2, waiting for transfers between devices: 9.07 us -> 0.26 us  [between_slabs(): return lax.all_to_all(value, 'ctx', 0, 0)]
    all_to_all x1 -> x2, starting transfers between devices: 6.78 us -> 14 us  [between_chips(): return lax.all_to_all(value, 'tp', 0, 0, axis_index_groups=same_core)]
    ppermute x4 -> x1, starting transfers between devices: 7.27 us -> 3.1 us  [local(): lax.ppermute(w_pair, 'ctx', [(i, i ^ Z_RING) for i in range(2 * Z_RING)])]
    unnamed x58 -> x64, local copies, waits for them, and re-layouts: 23.7 us -> 20 us
    concatenate x5 -> x3, other arithmetic: 1.19 us -> 3.71 us  [the longest x1 1.84 us: local(): w_both = jnp.concatenate([w_pair, w_far], axis=0)]
    ppermute x6 -> x5, waiting for transfers between devices: 10.4 us -> 8.09 us  [swapped(): return lax.ppermute(value, 'tp', [(i, i ^ bit) for i in range(16)])]
  transfers between devices with their start and end apart: 15 -> 12, of which waited for: 9 -> 5; matrix products, arithmetic and copies ran while one was open for 6% -> 9% of each run, Pallas kernels for 10% -> 10%
where the time goes in v4:
time: 192 us; the launch traced here: 191 us
  waiting for transfers between devices  43.5 us (23%)
  starting transfers between devices  43 us (22%)
  blocking collectives  30 us (16%)
  local copies, waits for them, and re-layouts  29.5 us (15%)
  Pallas kernels  22.3 us (12%)
  between operations  13.7 us (7%)
  other arithmetic  8.69 us (5%)
    all_to_all x2, waiting for transfers between devices, between_chips(): return lax.all_to_all(value, 'tp', 0, 0, axis_index_groups=same_core)  35.1 us
    all_to_all x1, blocking collectives, between_chips(): return lax.all_to_all(value, 'tp', 0, 0, axis_index_groups=same_core)  30 us
    unnamed x64, local copies, waits for them, and re-layouts  20 us
    pallas_call x2, Pallas kernels, over_chips(): pl.pallas_call(kernel, grid=(CHIPS // 2,), in_specs=[spec for _, spec in...  14.5 us
    all_to_all x2, starting transfers between devices, between_chips(): return lax.all_to_all(value, 'tp', 0, 0, axis_index_groups=same_core)  14 us
    all_to_all x2, starting transfers between devices, between_slabs(): return lax.all_to_all(value, 'ctx', 0, 0)  12.5 us
    ppermute x5, starting transfers between devices, swapped(): return lax.ppermute(value, 'tp', [(i, i ^ bit) for i in range(16)])  11.5 us
    ppermute x5, waiting for transfers between devices, swapped(): return lax.ppermute(value, 'tp', [(i, i ^ bit) for i in range(16)])  8.09 us
  transfers between devices with their start and end apart: 12, of which 5 were waited for; matrix products, arithmetic and copies ran while one was open for 9% of the time, Pallas kernels for 10%

profile of v4, /device:TPU:1, one launch (start us, length us, event | category | flops | bytes accessed | tf_op | source)
XLA Modules:
  0.0 190.6 jit_solution(10089005112567679999)
XLA Ops:
  6.5 1.0 broadcast_select_fusion.5
  7.5 3.3 %collective-permute-start.4 = (bf16[512,128]{1,0:T(8,128)(2,1)S(1)}, bf16[512,128]{1,0:T(8,128)(2,1)S(1)}, u32[]{:S(2)}, u32[]{:S(2)}) collective-permute-start(bf16[512,128]{1,0:T(8,128)(2,1)S(1)} %get-tuple-element.58), channel_id=1, source_target_pairs={{0,1},{1,0},{2,3},{3,2},{4,5},{5,4},{6,7},{7,6},{8,9},{9,8},{10,11... | collective-permute-start | bytes 393224 | tf_op jit(solution)/shard_map/ppermute | solution.py:395
  10.9 0.8 add_convert_fusion
  11.6 0.7 slice.42
  12.3 1.8 collective-permute-start
  14.2 0.9 copy.29
  15.1 1.5 copy.28
  17.2 6.7 %all-to-all-start.1 = ((bf16[8,16,256]{2,1,0:T(8,128)(2,1)}), bf16[8,16,256]{2,1,0:T(8,128)(2,1)}, u32[]{:S(2)}, u32[]{:S(2)}) async-start(bf16[8,16,256]{2,1,0:T(8,128)(2,1)} %broadcast_in_dim.51), calls=%async_computation.1 | async-start | bytes 131072 | tf_op jit(solution)/shard_map/all_to_all | solution.py:404
  23.9 0.7 pad_maximum_fusion.2
  24.6 3.1 %collective-permute-start.5 = (bf16[1024,128]{1,0:T(8,128)(2,1)}, bf16[1024,128]{1,0:T(8,128)(2,1)}, u32[]{:S(2)}, u32[]{:S(2)}) collective-permute-start(bf16[1024,128]{1,0:T(8,128)(2,1)} %pad_maximum_fusion.2), channel_id=1, source_target_pairs={{0,128},{16,144},{32,160},{48,176},{64,192},{80,208},{96,224},{112... | collective-permute-start | bytes 786440 | tf_op jit(solution)/shard_map/ppermute | solution.py:468
  27.7 1.1 broadcast_in_dim.43
  28.8 1.8 pad_maximum_fusion
  30.7 7.4 %all-to-all-start = ((bf16[8,784,256]{2,1,0:T(8,128)(2,1)}), bf16[8,784,256]{2,1,0:T(8,128)(2,1)S(1)}, u32[]{:S(2)}, u32[]{:S(2)}) async-start(bf16[8,784,256]{2,1,0:T(8,128)(2,1)} %pad_maximum_fusion), calls=%async_computation | async-start | bytes 6422528 | tf_op jit(solution)/shard_map/all_to_all | solution.py:404
  38.1 1.8 pad_maximum_fusion.1
  40.2 0.8 dynamic_slice.7
  42.2 2.0 %collective-permute-start.1 = (bf16[8,16,256]{2,1,0:T(8,128)(2,1)}, bf16[8,16,256]{2,1,0:T(8,128)(2,1)}, u32[]{:S(2)}, u32[]{:S(2)}) collective-permute-start(bf16[8,16,256]{2,1,0:T(8,128)(2,1)} %all-to-all-done.1.halo_own), channel_id=1, source_target_pairs={{0,1},{1,0},{2,3},{3,2},{4,5},{5,4},{6,7},{7,6},{8,9},{9,8},{10,11... | collective-permute-start | bytes 196616 | tf_op jit(solution)/shard_map/ppermute | solution.py:395
  44.3 2.0 %compare_convert_fusion = (f32[512]{0:T(512)S(1)}, f32[512]{0:T(512)S(1)}, f32[512]{0:T(512)S(1)}, f32[512]{0:T(512)S(1)}, f32[512]{0:T(512)S(1)}, /*index=5*/f32[512]{0:T(512)S(1)}) fusion(s32[512]{0:T(512)S(1)} %copy-done.28, s32[]{:T(128)} %bitcast.13, s32[]{:T(128)} %bitcast.11, s32[]{:T(128)} %bitcast.9, s32[515]{0:T(1024)S(1)} %pad_add_fusion), kind=kLoop, calls=%fused_computation.18 | loop fusion | flops 6144 | bytes 20492 | tf_op jit(solution)/shard_map/stack | solution.py:426
  46.3 0.8 copy.30
  47.1 1.0 pad.9.cols
  48.1 35.1 %all-to-all-done.own = bf16[8,784,256]{2,1,0:T(8,128)(2,1)S(1)} async-done(((bf16[8,784,256]{2,1,0:T(8,128)(2,1)}), bf16[8,784,256]{2,1,0:T(8,128)(2,1)S(1)}, u32[]{:S(2)}, u32[]{:S(2)}) %all-to-all-start) | async-done | bytes 3211296 | tf_op jit(solution)/shard_map/all_to_all | solution.py:404
  83.8 2.1 %collective-permute-start.2 = (bf16[8,784,256]{2,1,0:T(8,128)(2,1)S(1)}, bf16[8,784,256]{2,1,0:T(8,128)(2,1)S(1)}, u32[]{:S(2)}, u32[]{:S(2)}) collective-permute-start(bf16[8,784,256]{2,1,0:T(8,128)(2,1)S(1)} %all-to-all-done.own), channel_id=1, source_target_pairs={{0,1},{1,0},{2,3},{3,2},{4,5},{5,4},{6,7},{7,6},{8,9},{9,8},{10,11... | collective-permute-start | bytes 9633800 | tf_op jit(solution)/shard_map/ppermute | solution.py:395
  86.0 5.4 %collective-permute-done.2.sib = bf16[8,784,256]{2,1,0:T(8,128)(2,1)S(1)} collective-permute-done((bf16[8,784,256]{2,1,0:T(8,128)(2,1)S(1)}, bf16[8,784,256]{2,1,0:T(8,128)(2,1)S(1)}, u32[]{:S(2)}, u32[]{:S(2)}) %collective-permute-start.2) | collective-permute-done | bytes 3211296 | tf_op jit(solution)/shard_map/ppermute | solution.py:395
  91.4 2.2 %copy-done.16 = bf16[4096,512]{1,0:T(8,128)(2,1)S(1)} copy-done((bf16[4096,512]{1,0:T(8,128)(2,1)S(1)}, bf16[4096,512]{1,0:T(8,128)(2,1)}, u32[]{:S(2)}) %copy-start.16) | copy-done | bytes 4194328
  93.6 10.7 %scan_input.1 = (bf16[512,512]{1,0:T(8,128)(2,1)S(1)}, bf16[512,256]{1,0:T(8,128)(2,1)S(1)}, f32[512,128]{1,0:T(8,128)S(1)}, f32[16,512]{1,0:T(8,128)S(1)}, bf16...) custom-call(bf16[8,784,256]{2,1,0:T(8,128)(2,1)S(1)} %all-to-all-done.own, ...), custom_call_target="tpu_custom_call" | custom-call | flops 3391094784 | bytes 8388608 | tf_op jit(solution)/shard_map/scan_input/pallas_call | solution.py:205
  105.7 0.7 copy-done.14
  106.4 0.9 copy-done.22
  108.5 4.9 %all-to-all-start.2 = ((bf16[16,16,512]{2,1,0:T(8,128)(2,1)}), bf16[16,16,512]{2,1,0:T(8,128)(2,1)S(1)}, u32[]{:S(2)}, u32[]{:S(2)}) async-start(bf16[16,16,512]{2,1,0:T(8,128)(2,1)} %copy-done.14), calls=%async_computation.2 | async-start | bytes 524288 | tf_op jit(solution)/shard_map/all_to_all | solution.py:408
  113.5 2.2 %copy-done.3 = bf16[4096,512]{1,0:T(8,128)(2,1)S(1)} copy-done((bf16[4096,512]{1,0:T(8,128)(2,1)S(1)}, bf16[4096,512]{1,0:T(8,128)(2,1)}, u32[]{:S(2)}) %copy-start.3) | copy-done | bytes 4194328
  115.6 1.9 %copy-done.5 = bf16[8,784,256]{2,1,0:T(8,128)(2,1)S(1)} copy-done((bf16[8,784,256]{2,1,0:T(8,128)(2,1)S(1)}, bf16[8,784,256]{2,1,0:T(8,128)(2,1)}, u32[]{:S(2)}) %copy-start.5) | copy-done | bytes 3211288
  117.5 3.8 %gate.1.gates = f32[512,512]{1,0:T(8,128)S(1)} custom-call(bf16[8,784,256]{2,1,0:T(8,128)(2,1)S(1)} %all-to-all-done.own, bf16[8,784,256]{2,1,0:T(8,128)(2,1)S(1)} %copy-done.5, bf16[4096,512]{1,0:T(8,128)(2,1)S(1)} %copy-done.3), custom_call_target="tpu_custom_call" | custom-call | flops 2147483648 | bytes 8388608 | tf_op jit(solution)/shard_map/gate/pallas_call | solution.py:205
  121.4 1.0 copy-done.1
  122.4 0.7 prefix.1
  123.1 7.6 %all-to-all-start.3 = ((bf16[16,8,512]{2,1,0:T(8,128)(2,1)}), bf16[16,8,512]{2,1,0:T(8,128)(2,1)S(1)}, u32[]{:S(2)}, u32[]{:S(2)}) async-start(bf16[16,8,512]{2,1,0:T(8,128)(2,1)} %bitcast.20), calls=%async_computation.3 | async-start | bytes 262144 | tf_op jit(solution)/shard_map/all_to_all | solution.py:408
  130.7 0.9 copy-done.7
  131.7 0.9 copy-done.10
  132.6 0.9 copy-done.13
  133.6 1.0 copy-done.23
  134.6 0.9 copy-done.25
  135.5 0.8 copy-done.27
  136.3 1.7 intra.1.y
  138.2 1.3 join.1.own
  139.5 2.4 %collective-permute-start.3 = (bf16[512,640]{1,0:T(8,128)(2,1)S(1)}, bf16[512,640]{1,0:T(8,128)(2,1)S(1)}, u32[]{:S(2)}, u32[]{:S(2)}) collective-permute-start(bf16[512,640]{1,0:T(8,128)(2,1)S(1)} %join.1.own), channel_id=1, source_target_pairs={{0,1},{1,0},{2,3},{3,2},{4,5},{5,4},{6,7},{7,6},{8,9},{9,8},{10,11... | collective-permute-start | bytes 1966088 | tf_op jit(solution)/shard_map/ppermute | solution.py:395
  141.9 1.7 collective-permute-done.3.sib
  143.7 2.2 %copy-done.17 = bf16[16384,128]{1,0:T(8,128)(2,1)S(1)} copy-done((bf16[16384,128]{1,0:T(8,128)(2,1)S(1)}, bf16[16384,128]{1,0:T(8,128)(2,1)}, u32[]{:S(2)}) %copy-start.17) | copy-done | bytes 4194328
  145.8 4.1 %project.1 = bf16[8,512,256]{2,1,0:T(8,128)(2,1)S(1)} custom-call(s32[1]{0:T(128)} %bitcast.place, bf16[512,640]{1,0:T(8,128)(2,1)S(1)} %join.1.own, bf16[512,640]{1,0:T(8,128)(2,1)S(1)} %collective-permute-done.3.sib, bf16[8,2048,128]{2,1,0:T(8,128)(2,1)S(1)} %bitcast.28), custom_call_target="tpu_custom_call" | custom-call | flops 4294967296 | bytes 8388608 | tf_op jit(solution)/shard_map/project/pallas_call | solution.py:377
  149.9 30.0 %all_to_all.25 = bf16[8,512,256]{2,1,0:T(8,128)(2,1)S(1)} all-to-all(bf16[8,512,256]{2,1,0:T(8,128)(2,1)S(1)} %project.1), channel_id=1, replica_groups={{0,2,4,6,8,10,12,14},{1,3,5,7,9,11,13,15},{16,18,20,22,24,26,28,30},{17..., dimensions={0} | all-to-all | bytes 4194304 | tf_op jit(solution)/shard_map/all_to_all | solution.py:404
  180.3 1.6 collective-permute-start.6
  181.9 1.0 collective-permute-done.6
  (79 shorter events, 7.1 us)
Async XLA Ops:
  6.5 34.4 %copy-start = (f32[4,2048]{1,0:T(4,128)S(1)}, f32[4,2048]{1,0:T(4,128)}, u32[]{:S(2)}) copy-start(f32[4,2048]{1,0:T(4,128)} %param.23) | copy-start | bytes 98308
  7.5 16.4 %collective-permute-start.4 = (bf16[512,128]{1,0:T(8,128)(2,1)S(1)}, bf16[512,128]{1,0:T(8,128)(2,1)S(1)}, u32[]{:S(2)}, u32[]{:S(2)}) collective-permute-start(bf16[512,128]{1,0:T(8,128)(2,1)S(1)} %get-tuple-element.58), channel_id=1, source_target_pairs={{0,1},{1,0},{2,3},{3,2},{4,5},{5,4},{6,7},{7,6},{8,9},{9,8},{10,11... | collective-permute-start | bytes 393224 | tf_op jit(solution)/shard_map/ppermute | solution.py:395
  12.3 4.3 %collective-permute-start = (bf16[16,256]{1,0:T(8,128)(2,1)S(1)}, bf16[16,256]{1,0:T(8,128)(2,1)S(1)}, u32[]{:S(2)}, u32[]{:S(2)}) collective-permute-start(bf16[16,256]{1,0:T(8,128)(2,1)S(1)} %pad_maximum_fusion.4), channel_id=1, source_target_pairs={{0,16},{16,32},{32,48},{48,64},{64,80},{80,96},{96,112},{112,128},... | collective-permute-start | bytes 24584 | tf_op jit(solution)/shard_map/ppermute | solution.py:399
  17.2 13.4 %all-to-all-start.1 = ((bf16[8,16,256]{2,1,0:T(8,128)(2,1)}), bf16[8,16,256]{2,1,0:T(8,128)(2,1)}, u32[]{:S(2)}, u32[]{:S(2)}) async-start(bf16[8,16,256]{2,1,0:T(8,128)(2,1)} %broadcast_in_dim.51), calls=%async_computation.1 | async-start | bytes 131072 | tf_op jit(solution)/shard_map/all_to_all | solution.py:404
  24.6 13.5 %collective-permute-start.5 = (bf16[1024,128]{1,0:T(8,128)(2,1)}, bf16[1024,128]{1,0:T(8,128)(2,1)}, u32[]{:S(2)}, u32[]{:S(2)}) collective-permute-start(bf16[1024,128]{1,0:T(8,128)(2,1)} %pad_maximum_fusion.2), channel_id=1, source_target_pairs={{0,128},{16,144},{32,160},{48,176},{64,192},{80,208},{96,224},{112... | collective-permute-start | bytes 786440 | tf_op jit(solution)/shard_map/ppermute | solution.py:468
  30.6 9.4 %copy-start.28 = (s32[512]{0:T(512)S(1)}, s32[512]{0:T(512)}, u32[]{:S(2)}) copy-start(s32[512]{0:T(512)} %param.16) | copy-start | bytes 6148
  30.6 9.4 %copy-start.30 = (f32[8]{0:T(128)S(1)}, f32[8]{0:T(128)}, u32[]{:S(2)}) copy-start(f32[8]{0:T(128)} %param.27) | copy-start | bytes 100
  30.6 60.7 %copy-start.18 = (f32[4,512]{1,0:T(4,128)S(1)}, f32[4,512]{1,0:T(4,128)}, u32[]{:S(2)}) copy-start(f32[4,512]{1,0:T(4,128)} %taps_x) | copy-start | bytes 24580
  30.6 60.7 %copy-start.19 = (f32[512]{0:T(512)S(1)}, f32[512]{0:T(512)}, u32[]{:S(2)}) copy-start(f32[512]{0:T(512)} %param.22) | copy-start | bytes 6148
  30.6 60.7 %copy-start.20 = (f32[8]{0:T(128)S(1)}, f32[8]{0:T(128)}, u32[]{:S(2)}) copy-start(f32[8]{0:T(128)} %param.25) | copy-start | bytes 100
  30.6 60.7 %copy-start.21 = (f32[8]{0:T(128)S(1)}, f32[8]{0:T(128)}, u32[]{:S(2)}) copy-start(f32[8]{0:T(128)} %param.26) | copy-start | bytes 100
  30.7 52.5 %all-to-all-start = ((bf16[8,784,256]{2,1,0:T(8,128)(2,1)}), bf16[8,784,256]{2,1,0:T(8,128)(2,1)S(1)}, u32[]{:S(2)}, u32[]{:S(2)}) async-start(bf16[8,784,256]{2,1,0:T(8,128)(2,1)} %pad_maximum_fusion), calls=%async_computation | async-start | bytes 6422528 | tf_op jit(solution)/shard_map/all_to_all | solution.py:404
  38.1 105.6 %all-gather.3.cloned.1.call-start = ((), (), s32[]{:S(2)}) async-start(), calls=%async_computation.5 | async-start | bytes 4718592 | tf_op jit(solution)/shard_map/all_gather | solution.py:471
  40.0 6.3 %copy-start.29 = (f32[512]{0:T(512)}, f32[512]{0:T(512)S(1)}, u32[]{:S(2)}) copy-start(f32[512]{0:T(512)S(1)} %convert_element_type.12) | copy-start | bytes 6148
  42.2 5.9 %collective-permute-start.1 = (bf16[8,16,256]{2,1,0:T(8,128)(2,1)}, bf16[8,16,256]{2,1,0:T(8,128)(2,1)}, u32[]{:S(2)}, u32[]{:S(2)}) collective-permute-start(bf16[8,16,256]{2,1,0:T(8,128)(2,1)} %all-to-all-done.1.halo_own), channel_id=1, source_target_pairs={{0,1},{1,0},{2,3},{3,2},{4,5},{5,4},{6,7},{7,6},{8,9},{9,8},{10,11... | collective-permute-start | bytes 196616 | tf_op jit(solution)/shard_map/ppermute | solution.py:395
  48.1 56.2 %copy-start.12 = (f32[512,128]{1,0:T(8,128)}, f32[512,128]{1,0:T(8,128)S(1)}, u32[]{:S(2)}) copy-start(f32[512,128]{1,0:T(8,128)S(1)} %pad.9.cols) | copy-start | bytes 786436
  83.8 7.5 %collective-permute-start.2 = (bf16[8,784,256]{2,1,0:T(8,128)(2,1)S(1)}, bf16[8,784,256]{2,1,0:T(8,128)(2,1)S(1)}, u32[]{:S(2)}, u32[]{:S(2)}) collective-permute-start(bf16[8,784,256]{2,1,0:T(8,128)(2,1)S(1)} %all-to-all-done.own), channel_id=1, source_target_pairs={{0,1},{1,0},{2,3},{3,2},{4,5},{5,4},{6,7},{7,6},{8,9},{9,8},{10,11... | collective-permute-start | bytes 9633800 | tf_op jit(solution)/shard_map/ppermute | solution.py:395
  91.4 2.2 %copy-start.16 = (bf16[4096,512]{1,0:T(8,128)(2,1)S(1)}, bf16[4096,512]{1,0:T(8,128)(2,1)}, u32[]{:S(2)}) copy-start(bf16[4096,512]{1,0:T(8,128)(2,1)} %w_x.1) | copy-start | bytes 12582916
  93.6 10.7 %copy-start.4 = (bf16[8,784,256]{2,1,0:T(8,128)(2,1)}, bf16[8,784,256]{2,1,0:T(8,128)(2,1)S(1)}, u32[]{:S(2)}) copy-start(bf16[8,784,256]{2,1,0:T(8,128)(2,1)S(1)} %collective-permute-done.2.sib) | copy-start | bytes 9633796
  104.3 0.7 copy-start.6
  105.0 0.7 copy-start.9
  105.7 0.7 copy-start.14
  106.4 0.9 copy-start.22
  107.3 0.7 copy-start.24
  107.9 0.6 copy-start.26
  108.5 13.9 %all-to-all-start.2 = ((bf16[16,16,512]{2,1,0:T(8,128)(2,1)}), bf16[16,16,512]{2,1,0:T(8,128)(2,1)S(1)}, u32[]{:S(2)}, u32[]{:S(2)}) async-start(bf16[16,16,512]{2,1,0:T(8,128)(2,1)} %copy-done.14), calls=%async_computation.2 | async-start | bytes 524288 | tf_op jit(solution)/shard_map/all_to_all | solution.py:408
  113.4 2.2 %copy-start.3 = (bf16[4096,512]{1,0:T(8,128)(2,1)S(1)}, bf16[4096,512]{1,0:T(8,128)(2,1)}, u32[]{:S(2)}) copy-start(bf16[4096,512]{1,0:T(8,128)(2,1)} %w_z.1) | copy-start | bytes 12582916
  115.6 1.9 %copy-start.5 = (bf16[8,784,256]{2,1,0:T(8,128)(2,1)S(1)}, bf16[8,784,256]{2,1,0:T(8,128)(2,1)}, u32[]{:S(2)}) copy-start(bf16[8,784,256]{2,1,0:T(8,128)(2,1)} %copy-done.4) | copy-start | bytes 9633796
  117.5 20.7 %copy-start.15 = (f32[512]{0:T(512)S(1)}, f32[512]{0:T(512)}, u32[]{:S(2)}) copy-start(f32[512]{0:T(512)} %param.28) | copy-start | bytes 6148
  121.4 1.0 copy-start.1
  122.4 15.8 %copy-start.2 = (f32[512,512]{1,0:T(8,128)S(1)}, f32[512,512]{1,0:T(8,128)}, u32[]{:S(2)}) copy-start(f32[512,512]{1,0:T(8,128)} %copy-done.1) | copy-start | bytes 3145732
  123.1 15.1 %all-to-all-start.3 = ((bf16[16,8,512]{2,1,0:T(8,128)(2,1)}), bf16[16,8,512]{2,1,0:T(8,128)(2,1)S(1)}, u32[]{:S(2)}, u32[]{:S(2)}) async-start(bf16[16,8,512]{2,1,0:T(8,128)(2,1)} %bitcast.20), calls=%async_computation.3 | async-start | bytes 262144 | tf_op jit(solution)/shard_map/all_to_all | solution.py:408
  130.7 1.0 copy-start.7
  131.7 0.9 copy-start.10
  132.6 0.9 copy-start.13
  133.6 1.0 copy-start.23
  134.6 0.9 copy-start.25
  135.5 0.8 copy-start.27
  136.3 2.0 %copy-start.8 = (bf16[512,256]{1,0:T(8,128)(2,1)S(1)}, bf16[512,256]{1,0:T(8,128)(2,1)}, u32[]{:S(2)}) copy-start(bf16[512,256]{1,0:T(8,128)(2,1)} %copy-done.6) | copy-start | bytes 786436
  136.3 2.0 %copy-start.11 = (f32[512,128]{1,0:T(8,128)S(1)}, f32[512,128]{1,0:T(8,128)}, u32[]{:S(2)}) copy-start(f32[512,128]{1,0:T(8,128)} %copy-done.9) | copy-start | bytes 786436
  139.5 4.1 %collective-permute-start.3 = (bf16[512,640]{1,0:T(8,128)(2,1)S(1)}, bf16[512,640]{1,0:T(8,128)(2,1)S(1)}, u32[]{:S(2)}, u32[]{:S(2)}) collective-permute-start(bf16[512,640]{1,0:T(8,128)(2,1)S(1)} %join.1.own), channel_id=1, source_target_pairs={{0,1},{1,0},{2,3},{3,2},{4,5},{5,4},{6,7},{7,6},{8,9},{9,8},{10,11... | collective-permute-start | bytes 1966088 | tf_op jit(solution)/shard_map/ppermute | solution.py:395
  143.7 2.2 %copy-start.17 = (bf16[16384,128]{1,0:T(8,128)(2,1)S(1)}, bf16[16384,128]{1,0:T(8,128)(2,1)}, u32[]{:S(2)}) copy-start(bf16[16384,128]{1,0:T(8,128)(2,1)} %all-gather.3.cloned.1.call-done) | copy-start | bytes 12582916
  180.3 2.6 %collective-permute-start.6 = (bf16[512,128]{1,0:T(8,128)(2,1)S(1)}, bf16[512,128]{1,0:T(8,128)(2,1)S(1)}, u32[]{:S(2)}, u32[]{:S(2)}) collective-permute-start(bf16[512,128]{1,0:T(8,128)(2,1)S(1)} %broadcast_select_fusion.2), channel_id=1, source_target_pairs={{0,1},{1,0},{2,3},{3,2},{4,5},{5,4},{6,7},{7,6},{8,9},{9,8},{10,11... | collective-permute-start | bytes 393224 | tf_op jit(solution)/shard_map/ppermute | solution.py:395
  183.0 0.7 copy-start.31
Sparse Core Ops, SparseCore 0:
  40.7 56.5 all-gather.2

commit v5 on v4

--- a/solution.py
+++ b/solution.py
@@ -105,8 +105,10 @@
 
 
 def step_cols(own, sib):
-    parts = [(own if same_core else sib)[slot, ROWS:] for slot, same_core in step_sources()]
-    return jnp.concatenate(parts, axis=1)
+    refs = [(own if same_core else sib, slot) for slot, same_core in step_sources()]
+    w_bc = [ref[slot, ROWS : ROWS + FEAT] for ref, slot in refs]
+    w_dt = [ref[slot, ROWS + FEAT :] for ref, slot in refs]
+    return jnp.concatenate(w_bc, axis=0), jnp.concatenate(w_dt, axis=1)
 
 
 def step_rows(w_ref):
@@ -140,27 +142,29 @@
     pay,
     acc_x,
     acc_bc,
-    raw_bc,
+    acc_dt,
 ):
     step = pl.program_id(0)
     core = my_core()
     toks = step_tokens(own, sib, halo_own, halo_sib)
     add_to(acc_x, step, dot(toks, step_rows(w_x)))
-    add_to(acc_bc, step, dot_nt(toks, step_cols(own, sib)))
+    w_bc, w_dt = step_cols(own, sib)
+    add_to(acc_bc, step, dot(toks, w_bc))
+    add_to(acc_dt, step, dot_nt(toks, w_dt))
 
     @pl.when(step == pl.num_programs(0) - 1)
     def _():
-        raw_dt = acc_bc[HALO:, 2 * N :]
+        raw_dt = acc_dt[HALO:, :]
         raw_dt = jnp.where(core == 0, raw_dt[:, :HEADS], raw_dt[:, HEADS:])
         pre = raw_dt + dt_bias[...]
         dt = jnp.maximum(pre, 0.0) + jnp.log1p(jnp.exp(-jnp.abs(pre)))
         loga = -decay[...] * dt
         acc_x[...] = acc_x[...].astype(BF16).astype(F32)
-        raw_bc[...] = acc_bc[:, : 2 * N].astype(BF16).astype(F32)
+        acc_bc[...] = acc_bc[...].astype(BF16).astype(F32)
         for at in range(0, ROWS, 64):
             masks = cols[at : at + 64, :]
             xc[at : at + 64, :] = conv_chunk(acc_x, at, 64, masks, taps_x, bias_x[...])
-            bcc[at : at + 64, :] = conv_chunk(raw_bc, at, 64, masks, taps_bc, bias_bc[...])
+            bcc[at : at + 64, :] = conv_chunk(acc_bc, at, 64, masks, taps_bc, bias_bc[...])
         lower = (
             lax.broadcasted_iota(jnp.int32, (L, L), 0) >= lax.broadcasted_iota(jnp.int32, (L, L), 1)
         ).astype(F32)
@@ -238,12 +242,12 @@
     blocked += [two_chips(a, HALO) for a in (halo_own, halo_sib)] + [their_rows(w_x)]
     scratch = [
         pltpu.VMEM((ALL_ROWS, CH), F32),
-        pltpu.VMEM((ALL_ROWS, COLS), F32),
         pltpu.VMEM((ALL_ROWS, 2 * N), F32),
+        pltpu.VMEM((ALL_ROWS, 2 * HEADS), F32),
     ]
     flops = 2 * ALL_ROWS * 4096 * (CH + COLS)
     return over_chips(
-        scan_input_kernel, blocked, fixed, shapes, scratch, 24, flops, "scan_input"
+        scan_input_kernel, blocked, fixed, shapes, scratch, 58, flops, "scan_input"
     )
 
 
@@ -383,7 +387,7 @@
             out_specs=pl.BlockSpec((1, ROWS, 256), lambda i, place: (i, 0, 0)),
         ),
         out_shape=jax.ShapeDtypeStruct((CHIPS, ROWS, 256), BF16),
-        compiler_params=params(14, True),
+        compiler_params=params(58, True),
         cost_estimate=pl.CostEstimate(
             flops=8 * ROWS * CH * 2048, bytes_accessed=8 * 2**20, transcendentals=0
         ),
@@ -449,11 +453,12 @@
     chip = rank // CORES
     y_low = (lax.axis_index("ctx") // Z_RING).astype(jnp.int32)
 
-    w_cols = jnp.concatenate(
-        [w_bc.T.reshape(CHIPS, 2 * N, FEAT), w_dt.T.reshape(CHIPS, 2 * HEADS, FEAT)], axis=1
-    )
+    w_groups = jnp.stack([w_bc[:, 2 * N * n : 2 * N * (n + 1)] for n in range(CHIPS)])
+    w_steps = w_dt.T.reshape(CHIPS, 2 * HEADS, FEAT)
     shared = jnp.broadcast_to(tokens[None], (CHIPS, ROWS, FEAT))
-    own = between_chips(jnp.concatenate([shared, w_cols], axis=1))
+    sent = jnp.concatenate([shared, w_groups, w_steps], axis=1)
+    sent, tokens, seg_ids, w_out = together(sent, tokens, seg_ids, w_out)
+    own = between_chips(sent)
 
     ids_row = jnp.pad((seg_ids[-3:] + 1).astype(BF16), (0, FEAT - 3))[None]
     halo = next_ctx(jnp.concatenate([ids_row, tokens[1 - HALO :]], axis=0))
@@ -486,6 +491,7 @@
     pieces, gates, xc, bcc = together(pieces, gates, xc, bcc)
     state = between_slabs(prefix(pieces).reshape(CTX, 8, CH)).reshape(N, CH)
     y = intra(xc, bcc, hcol, hrow, s0, fixed[0], seg_row, skip)
+    y, state, w_all = together(y, state, w_all)
     mine = join(y, gates, bcc, hcol, state, norm_weight[None])
     parts = between_chips(project(mine, swapped(mine, 1), w_all, y_low))
     total = jnp.sum(parts.astype(F32), axis=0).astype(BF16)

time: 192 us -> 210 us (1.094)
  blocking collectives: 30 us -> 44.3 us
  waiting for transfers between devices: 43.5 us -> 54.4 us
  Pallas kernels: 22.3 us -> 32.6 us
  starting transfers between devices: 43 us -> 36.1 us
  local copies, waits for them, and re-layouts: 29.5 us -> 22.7 us
  other arithmetic: 8.69 us -> 5.32 us
    all_to_all x1 -> x2, blocking collectives: 30 us -> 44.3 us  [between_chips(): return lax.all_to_all(value, 'tp', 0, 0, axis_index_groups=same_core)]
    all_to_all x2 -> x1, starting transfers between devices: 14 us -> 3.79 us  [between_chips(): return lax.all_to_all(value, 'tp', 0, 0, axis_index_groups=same_core)]
    ppermute x1, waiting for transfers between devices: 0.01 us -> 7.52 us  [local(): lax.ppermute(w_pair, 'ctx', [(i, i ^ Z_RING) for i in range(2 * Z_RING)])]
    unnamed x64 -> x45, local copies, waits for them, and re-layouts: 20 us -> 13.1 us
    pallas_call x2, Pallas kernels: 14.5 us -> 20.8 us  [over_chips(): pl.pallas_call(kernel, grid=(CHIPS // 2,), in_specs=[spec for _, spec in...]
    all_to_all x2, starting transfers between devices: 12.5 us -> 17.1 us  [between_slabs(): return lax.all_to_all(value, 'ctx', 0, 0)]
    all_to_all x2, waiting for transfers between devices: 0.26 us -> 4.73 us  [between_slabs(): return lax.all_to_all(value, 'ctx', 0, 0)]
    pallas_call x1, Pallas kernels: 4.06 us -> 8.13 us  [project(): pl.pallas_call(project_kernel, grid_spec=pltpu.PrefetchScalarGridSpec(num...]
  transfers between devices with their start and end apart: 12 -> 11, of which waited for: 5 -> 8; matrix products, arithmetic and copies ran while one was open for 9% -> 4% of each run, Pallas kernels for 10% -> 11%
where the time goes in v5:
time: 210 us; the launch traced here: 209 us
  waiting for transfers between devices  54.4 us (26%)
  blocking collectives  44.3 us (21%)
  starting transfers between devices  36.1 us (17%)
  Pallas kernels  32.6 us (16%)
  local copies, waits for them, and re-layouts  22.7 us (11%)
  between operations  13.7 us (7%)
  other arithmetic  5.32 us (3%)
    all_to_all x2, blocking collectives, between_chips(): return lax.all_to_all(value, 'tp', 0, 0, axis_index_groups=same_core)  44.3 us
    all_to_all x1, waiting for transfers between devices, between_chips(): return lax.all_to_all(value, 'tp', 0, 0, axis_index_groups=same_core)  32.2 us
    pallas_call x2, Pallas kernels, over_chips(): pl.pallas_call(kernel, grid=(CHIPS // 2,), in_specs=[spec for _, spec in...  20.8 us
    all_to_all x2, starting transfers between devices, between_slabs(): return lax.all_to_all(value, 'ctx', 0, 0)  17.1 us
    ppermute x5, starting transfers between devices, swapped(): return lax.ppermute(value, 'tp', [(i, i ^ bit) for i in range(16)])  13.3 us
    unnamed x45, local copies, waits for them, and re-layouts  13.1 us
    ppermute x5, waiting for transfers between devices, swapped(): return lax.ppermute(value, 'tp', [(i, i ^ bit) for i in range(16)])  9.21 us
    pallas_call x1, Pallas kernels, project(): pl.pallas_call(project_kernel, grid_spec=pltpu.PrefetchScalarGridSpec(num...  8.13 us
  transfers between devices with their start and end apart: 11, of which 8 were waited for; matrix products, arithmetic and copies ran while one was open for 4% of the time, Pallas kernels for 11%

profile of v5, /device:TPU:1, one launch (start us, length us, event | category | flops | bytes accessed | tf_op | source)
XLA Modules:
  0.0 209.1 jit_solution(12543339887574571536)
XLA Ops:
  6.5 0.9 copy.26
  7.5 0.9 bitcast_dynamic-update-slice_fusion.7
  8.4 0.9 bitcast_dynamic-update-slice_fusion.6
  9.3 0.9 bitcast_dynamic-update-slice_fusion.5
  10.3 0.9 bitcast_dynamic-update-slice_fusion.4
  11.2 0.9 bitcast_dynamic-update-slice_fusion.3
  12.1 0.9 bitcast_dynamic-update-slice_fusion.2
  13.0 0.9 bitcast_dynamic-update-slice_fusion.1
  13.9 0.9 bitcast_dynamic-update-slice_fusion
  14.9 1.1 broadcast_in_dim.43
  16.0 1.8 pad_maximum_fusion
  17.8 3.3 %collective-permute-start.3 = (bf16[512,128]{1,0:T(8,128)(2,1)S(1)}, bf16[512,128]{1,0:T(8,128)(2,1)S(1)}, u32[]{:S(2)}, u32[]{:S(2)}) collective-permute-start(bf16[512,128]{1,0:T(8,128)(2,1)S(1)} %get-tuple-element.72), channel_id=1, source_target_pairs={{0,1},{1,0},{2,3},{3,2},{4,5},{5,4},{6,7},{7,6},{8,9},{9,8},{10,11... | collective-permute-start | bytes 393224 | tf_op jit(solution)/shard_map/ppermute | solution.py:399
  21.1 1.0 collective-permute-done.3
  22.2 7.5 %collective-permute-done.4 = bf16[1024,128]{1,0:T(8,128)(2,1)S(1)} collective-permute-done((bf16[1024,128]{1,0:T(8,128)(2,1)S(1)}, bf16[1024,128]{1,0:T(8,128)(2,1)S(1)}, u32[]{:S(2)}, u32[]{:S(2)}) %collective-permute-start.4) | collective-permute-done | bytes 262176 | tf_op jit(solution)/shard_map/ppermute | solution.py:473
  29.8 0.8 pad_maximum_fusion.1
  30.7 0.7 slice.74
  31.4 1.8 collective-permute-start
  33.2 0.8 collective-permute-done
  34.0 13.0 %all_to_all.25.halo_own = bf16[8,16,256]{2,1,0:T(8,128)(2,1)S(1)} all-to-all(bf16[8,16,256]{2,1,0:T(8,128)(2,1)S(1)} %broadcast_in_dim.51), channel_id=1, replica_groups={{0,2,4,6,8,10,12,14},{1,3,5,7,9,11,13,15},{16,18,20,22,24,26,28,30},{17..., dimensions={0} | all-to-all | bytes 131072 | tf_op jit(solution)/shard_map/all_to_all | solution.py:408
  47.1 3.8 %all-to-all-start = ((bf16[8,784,256]{2,1,0:T(8,128)(2,1)}), bf16[8,784,256]{2,1,0:T(8,128)(2,1)S(1)}, u32[]{:S(2)}, u32[]{:S(2)}) async-start(bf16[8,784,256]{2,1,0:T(8,128)(2,1)} %pad_maximum_fusion), calls=%async_computation | async-start | bytes 6422528 | tf_op jit(solution)/shard_map/all_to_all | solution.py:408
  51.1 1.3 dynamic_slice.7
  53.6 0.6 slice.79
  54.3 3.5 %collective-permute-start.1 = (bf16[8,16,256]{2,1,0:T(8,128)(2,1)S(1)}, bf16[8,16,256]{2,1,0:T(8,128)(2,1)S(1)}, u32[]{:S(2)}, u32[]{:S(2)}) collective-permute-start(bf16[8,16,256]{2,1,0:T(8,128)(2,1)S(1)} %all_to_all.25.halo_own), channel_id=1, source_target_pairs={{0,1},{1,0},{2,3},{3,2},{4,5},{5,4},{6,7},{7,6},{8,9},{9,8},{10,11... | collective-permute-start | bytes 196616 | tf_op jit(solution)/shard_map/ppermute | solution.py:399
  57.8 2.0 compare_convert_fusion
  59.8 0.8 copy.27
  60.6 1.7 pad.9.cols
  62.3 32.2 %all-to-all-done.own = bf16[8,784,256]{2,1,0:T(8,128)(2,1)S(1)} async-done(((bf16[8,784,256]{2,1,0:T(8,128)(2,1)}), bf16[8,784,256]{2,1,0:T(8,128)(2,1)S(1)}, u32[]{:S(2)}, u32[]{:S(2)}) %all-to-all-start) | async-done | bytes 3211296 | tf_op jit(solution)/shard_map/all_to_all | solution.py:408
  94.5 2.7 %collective-permute-start.2 = (bf16[8,784,256]{2,1,0:T(8,128)(2,1)S(1)}, bf16[8,784,256]{2,1,0:T(8,128)(2,1)}, u32[]{:S(2)}, u32[]{:S(2)}) collective-permute-start(bf16[8,784,256]{2,1,0:T(8,128)(2,1)S(1)} %all-to-all-done.own), channel_id=1, source_target_pairs={{0,1},{1,0},{2,3},{3,2},{4,5},{5,4},{6,7},{7,6},{8,9},{9,8},{10,11... | collective-permute-start | bytes 9633800 | tf_op jit(solution)/shard_map/ppermute | solution.py:399
  97.2 5.5 %collective-permute-done.2.sib = bf16[8,784,256]{2,1,0:T(8,128)(2,1)} collective-permute-done((bf16[8,784,256]{2,1,0:T(8,128)(2,1)S(1)}, bf16[8,784,256]{2,1,0:T(8,128)(2,1)}, u32[]{:S(2)}, u32[]{:S(2)}) %collective-permute-start.2) | collective-permute-done | bytes 3211296 | tf_op jit(solution)/shard_map/ppermute | solution.py:399
  102.7 15.7 %scan_input.1 = (bf16[512,512]{1,0:T(8,128)(2,1)}, bf16[512,256]{1,0:T(8,128)(2,1)}, f32[512,128]{1,0:T(8,128)}, f32[16,512]{1,0:T(8,128)}, bf16[128,512]{1,0:T(8,128)(2,1)}, /*index=5*/bf16[16,16,512]{2,1,0:T(8,128)(2,1)}) custom-call(bf16[8,784,256]{2,1,0:T(8,128)(2,1)} %copy-done.1, bf16[8,784,256]{2,1,0:T(8,128)(2,1)} %collective-permute-done.2.sib, ...), custom_call_target="tpu_custom_call" | custom-call | flops 3391094784 | bytes 8388608 | tf_op jit(solution)/shard_map/scan_input/pallas_call | solution.py:209
  118.5 9.6 %all-to-all-start.2 = ((bf16[16,16,512]{2,1,0:T(8,128)(2,1)}), bf16[16,16,512]{2,1,0:T(8,128)(2,1)S(1)}, u32[]{:S(2)}, u32[]{:S(2)}) async-start(bf16[16,16,512]{2,1,0:T(8,128)(2,1)} %get-tuple-element.51), calls=%async_computation.2 | async-start | bytes 524288 | tf_op jit(solution)/shard_map/all_to_all | solution.py:412
  128.0 1.9 copy-done.2
  129.9 2.2 %copy-done.3 = bf16[4096,512]{1,0:T(8,128)(2,1)S(1)} copy-done((bf16[4096,512]{1,0:T(8,128)(2,1)S(1)}, bf16[4096,512]{1,0:T(8,128)(2,1)}, u32[]{:S(2)}) %copy-start.3) | copy-done | bytes 4194328
  132.1 5.0 %gate.1.gates = f32[512,512]{1,0:T(8,128)S(1)} custom-call(bf16[8,784,256]{2,1,0:T(8,128)(2,1)S(1)} %copy-done.2, bf16[8,784,256]{2,1,0:T(8,128)(2,1)} %collective-permute-done.2.sib, bf16[4096,512]{1,0:T(8,128)(2,1)S(1)} %copy-done.3), custom_call_target="tpu_custom_call" | custom-call | flops 2147483648 | bytes 8388608 | tf_op jit(solution)/shard_map/gate/pallas_call | solution.py:209
  137.2 0.7 prefix.1
  137.9 7.6 %all-to-all-start.3 = ((bf16[16,8,512]{2,1,0:T(8,128)(2,1)}), bf16[16,8,512]{2,1,0:T(8,128)(2,1)S(1)}, u32[]{:S(2)}, u32[]{:S(2)}) async-start(bf16[16,8,512]{2,1,0:T(8,128)(2,1)} %bitcast.26), calls=%async_computation.3 | async-start | bytes 262144 | tf_op jit(solution)/shard_map/all_to_all | solution.py:412
  145.5 1.0 copy-done.9
  146.6 1.7 intra.1.y
  148.3 4.7 %all-to-all-done.3 = bf16[16,8,512]{2,1,0:T(8,128)(2,1)S(1)} async-done(((bf16[16,8,512]{2,1,0:T(8,128)(2,1)}), bf16[16,8,512]{2,1,0:T(8,128)(2,1)S(1)}, u32[]{:S(2)}, u32[]{:S(2)}) %all-to-all-start.3) | async-done | bytes 131104 | tf_op jit(solution)/shard_map/all_to_all | solution.py:412
  153.0 1.3 join.1.own
  154.3 2.4 %collective-permute-start.5 = (bf16[512,640]{1,0:T(8,128)(2,1)S(1)}, bf16[512,640]{1,0:T(8,128)(2,1)S(1)}, u32[]{:S(2)}, u32[]{:S(2)}) collective-permute-start(bf16[512,640]{1,0:T(8,128)(2,1)S(1)} %join.1.own), channel_id=1, source_target_pairs={{0,1},{1,0},{2,3},{3,2},{4,5},{5,4},{6,7},{7,6},{8,9},{9,8},{10,11... | collective-permute-start | bytes 1966088 | tf_op jit(solution)/shard_map/ppermute | solution.py:399
  156.7 1.7 collective-permute-done.5.sib
  158.4 0.8 copy-done.16
  159.2 8.1 %project.1 = bf16[8,512,256]{2,1,0:T(8,128)(2,1)} custom-call(s32[1]{0:T(128)} %bitcast.place, bf16[512,640]{1,0:T(8,128)(2,1)} %copy-done.4, bf16[512,640]{1,0:T(8,128)(2,1)} %copy-done.16, bf16[8,2048,128]{2,1,0:T(8,128)(2,1)} %bitcast.52), custom_call_target="tpu_custom_call" | custom-call | flops 4294967296 | bytes 8388608 | tf_op jit(solution)/shard_map/project/pallas_call | solution.py:381
  167.4 31.2 %all_to_all.26 = bf16[8,512,256]{2,1,0:T(8,128)(2,1)S(1)} all-to-all(bf16[8,512,256]{2,1,0:T(8,128)(2,1)} %project.1), channel_id=1, replica_groups={{0,2,4,6,8,10,12,14},{1,3,5,7,9,11,13,15},{16,18,20,22,24,26,28,30},{17..., dimensions={0} | all-to-all | bytes 4194304 | tf_op jit(solution)/shard_map/all_to_all | solution.py:408
  199.0 1.4 collective-permute-start.6
  200.4 1.0 collective-permute-done.6
  201.5 0.7 copy-done.17
  (59 shorter events, 2.3 us)
Async XLA Ops:
  6.5 45.9 %copy-start = (f32[4,2048]{1,0:T(4,128)S(1)}, f32[4,2048]{1,0:T(4,128)}, u32[]{:S(2)}) copy-start(f32[4,2048]{1,0:T(4,128)} %param.23) | copy-start | bytes 98308
  6.5 146.5 %all-gather.3.cloned.1.call-start = ((), (), s32[]{:S(2)}) async-start(), calls=%async_computation.5 | async-start | bytes 4718592 | tf_op jit(solution)/shard_map/all_gather | solution.py:476
  15.9 1.8 copy-start.12
  16.0 14.7 %copy-start.14 = (s32[512]{0:T(512)S(1)}, s32[512]{0:T(512)}, u32[]{:S(2)}) copy-start(s32[512]{0:T(512)} %param.16) | copy-start | bytes 6148
  17.8 4.3 %collective-permute-start.3 = (bf16[512,128]{1,0:T(8,128)(2,1)S(1)}, bf16[512,128]{1,0:T(8,128)(2,1)S(1)}, u32[]{:S(2)}, u32[]{:S(2)}) collective-permute-start(bf16[512,128]{1,0:T(8,128)(2,1)S(1)} %get-tuple-element.72), channel_id=1, source_target_pairs={{0,1},{1,0},{2,3},{3,2},{4,5},{5,4},{6,7},{7,6},{8,9},{9,8},{10,11... | collective-permute-start | bytes 393224 | tf_op jit(solution)/shard_map/ppermute | solution.py:399
  22.1 7.6 %collective-permute-start.4 = (bf16[1024,128]{1,0:T(8,128)(2,1)S(1)}, bf16[1024,128]{1,0:T(8,128)(2,1)S(1)}, u32[]{:S(2)}, u32[]{:S(2)}) collective-permute-start(bf16[1024,128]{1,0:T(8,128)(2,1)S(1)} %pad_maximum_fusion.2), channel_id=1, source_target_pairs={{0,128},{16,144},{32,160},{48,176},{64,192},{80,208},{96,224},{112... | collective-permute-start | bytes 786440 | tf_op jit(solution)/shard_map/ppermute | solution.py:473
  31.4 2.6 %collective-permute-start = (bf16[16,256]{1,0:T(8,128)(2,1)S(1)}, bf16[16,256]{1,0:T(8,128)(2,1)S(1)}, u32[]{:S(2)}, u32[]{:S(2)}) collective-permute-start(bf16[16,256]{1,0:T(8,128)(2,1)S(1)} %pad_maximum_fusion.4), channel_id=1, source_target_pairs={{0,16},{16,32},{32,48},{48,64},{64,80},{80,96},{96,112},{112,128},... | collective-permute-start | bytes 24584 | tf_op jit(solution)/shard_map/ppermute | solution.py:403
  47.1 7.2 %copy-start.13 = (bf16[8,16,256]{2,1,0:T(8,128)(2,1)}, bf16[8,16,256]{2,1,0:T(8,128)(2,1)S(1)}, u32[]{:S(2)}) copy-start(bf16[8,16,256]{2,1,0:T(8,128)(2,1)S(1)} %all_to_all.25.halo_own) | copy-start | bytes 196612
  47.1 3.8 %copy-start.15 = (f32[8]{0:T(128)S(1)}, f32[8]{0:T(128)}, u32[]{:S(2)}) copy-start(f32[8]{0:T(128)} %param.27) | copy-start | bytes 100
  47.1 47.4 %all-to-all-start = ((bf16[8,784,256]{2,1,0:T(8,128)(2,1)}), bf16[8,784,256]{2,1,0:T(8,128)(2,1)S(1)}, u32[]{:S(2)}, u32[]{:S(2)}) async-start(bf16[8,784,256]{2,1,0:T(8,128)(2,1)} %pad_maximum_fusion), calls=%async_computation | async-start | bytes 6422528 | tf_op jit(solution)/shard_map/all_to_all | solution.py:408
  54.3 8.0 %collective-permute-start.1 = (bf16[8,16,256]{2,1,0:T(8,128)(2,1)S(1)}, bf16[8,16,256]{2,1,0:T(8,128)(2,1)S(1)}, u32[]{:S(2)}, u32[]{:S(2)}) collective-permute-start(bf16[8,16,256]{2,1,0:T(8,128)(2,1)S(1)} %all_to_all.25.halo_own), channel_id=1, source_target_pairs={{0,1},{1,0},{2,3},{3,2},{4,5},{5,4},{6,7},{7,6},{8,9},{9,8},{10,11... | collective-permute-start | bytes 196616 | tf_op jit(solution)/shard_map/ppermute | solution.py:399
  62.3 40.4 %copy-start.18 = (bf16[8,16,256]{2,1,0:T(8,128)(2,1)}, bf16[8,16,256]{2,1,0:T(8,128)(2,1)S(1)}, u32[]{:S(2)}) copy-start(bf16[8,16,256]{2,1,0:T(8,128)(2,1)S(1)} %collective-permute-done.1.halo_sib) | copy-start | bytes 196612
  94.5 8.2 %copy-start.1 = (bf16[8,784,256]{2,1,0:T(8,128)(2,1)}, bf16[8,784,256]{2,1,0:T(8,128)(2,1)S(1)}, u32[]{:S(2)}) copy-start(bf16[8,784,256]{2,1,0:T(8,128)(2,1)S(1)} %all-to-all-done.own) | copy-start | bytes 9633796
  94.5 8.2 %collective-permute-start.2 = (bf16[8,784,256]{2,1,0:T(8,128)(2,1)S(1)}, bf16[8,784,256]{2,1,0:T(8,128)(2,1)}, u32[]{:S(2)}, u32[]{:S(2)}) collective-permute-start(bf16[8,784,256]{2,1,0:T(8,128)(2,1)S(1)} %all-to-all-done.own), channel_id=1, source_target_pairs={{0,1},{1,0},{2,3},{3,2},{4,5},{5,4},{6,7},{7,6},{8,9},{9,8},{10,11... | collective-permute-start | bytes 9633800 | tf_op jit(solution)/shard_map/ppermute | solution.py:399
  118.5 18.7 %all-to-all-start.2 = ((bf16[16,16,512]{2,1,0:T(8,128)(2,1)}), bf16[16,16,512]{2,1,0:T(8,128)(2,1)S(1)}, u32[]{:S(2)}, u32[]{:S(2)}) async-start(bf16[16,16,512]{2,1,0:T(8,128)(2,1)} %get-tuple-element.51), calls=%async_computation.2 | async-start | bytes 524288 | tf_op jit(solution)/shard_map/all_to_all | solution.py:412
  128.0 1.9 copy-start.2
  129.9 2.2 %copy-start.3 = (bf16[4096,512]{1,0:T(8,128)(2,1)S(1)}, bf16[4096,512]{1,0:T(8,128)(2,1)}, u32[]{:S(2)}) copy-start(bf16[4096,512]{1,0:T(8,128)(2,1)} %w_z.1) | copy-start | bytes 12582916
  132.1 13.4 %copy-start.5 = (bf16[512,256]{1,0:T(8,128)(2,1)S(1)}, bf16[512,256]{1,0:T(8,128)(2,1)}, u32[]{:S(2)}) copy-start(bf16[512,256]{1,0:T(8,128)(2,1)} %get-tuple-element.57.bcc) | copy-start | bytes 786436
  132.1 13.4 %copy-start.6 = (f32[512,128]{1,0:T(8,128)S(1)}, f32[512,128]{1,0:T(8,128)}, u32[]{:S(2)}) copy-start(f32[512,128]{1,0:T(8,128)} %get-tuple-element.58.hcol) | copy-start | bytes 786436
  132.1 13.4 %copy-start.7 = (f32[512,128]{1,0:T(8,128)S(1)}, f32[512,128]{1,0:T(8,128)}, u32[]{:S(2)}) copy-start(f32[512,128]{1,0:T(8,128)} %pad.9.cols) | copy-start | bytes 786436
  132.1 13.4 %copy-start.10 = (bf16[128,512]{1,0:T(8,128)(2,1)S(1)}, bf16[128,512]{1,0:T(8,128)(2,1)}, u32[]{:S(2)}) copy-start(bf16[128,512]{1,0:T(8,128)(2,1)} %get-tuple-element.60.s0) | copy-start | bytes 393220
  132.1 13.4 %copy-start.11 = (f32[16,512]{1,0:T(8,128)S(1)}, f32[16,512]{1,0:T(8,128)}, u32[]{:S(2)}) copy-start(f32[16,512]{1,0:T(8,128)} %get-tuple-element.59.hrow) | copy-start | bytes 98308
  137.2 15.8 %copy-start.8 = (f32[512]{0:T(512)S(1)}, f32[512]{0:T(512)}, u32[]{:S(2)}) copy-start(f32[512]{0:T(512)} %param.28) | copy-start | bytes 6148
  137.9 15.1 %all-to-all-start.3 = ((bf16[16,8,512]{2,1,0:T(8,128)(2,1)}), bf16[16,8,512]{2,1,0:T(8,128)(2,1)S(1)}, u32[]{:S(2)}, u32[]{:S(2)}) async-start(bf16[16,8,512]{2,1,0:T(8,128)(2,1)} %bitcast.26), calls=%async_computation.3 | async-start | bytes 262144 | tf_op jit(solution)/shard_map/all_to_all | solution.py:412
  145.5 1.0 copy-start.9
  154.3 4.1 %copy-start.4 = (bf16[512,640]{1,0:T(8,128)(2,1)}, bf16[512,640]{1,0:T(8,128)(2,1)S(1)}, u32[]{:S(2)}) copy-start(bf16[512,640]{1,0:T(8,128)(2,1)S(1)} %join.1.own) | copy-start | bytes 1966084
  154.3 4.1 %collective-permute-start.5 = (bf16[512,640]{1,0:T(8,128)(2,1)S(1)}, bf16[512,640]{1,0:T(8,128)(2,1)S(1)}, u32[]{:S(2)}, u32[]{:S(2)}) collective-permute-start(bf16[512,640]{1,0:T(8,128)(2,1)S(1)} %join.1.own), channel_id=1, source_target_pairs={{0,1},{1,0},{2,3},{3,2},{4,5},{5,4},{6,7},{7,6},{8,9},{9,8},{10,11... | collective-permute-start | bytes 1966088 | tf_op jit(solution)/shard_map/ppermute | solution.py:399
  158.4 0.8 copy-start.16
  199.0 2.4 %collective-permute-start.6 = (bf16[512,128]{1,0:T(8,128)(2,1)S(1)}, bf16[512,128]{1,0:T(8,128)(2,1)S(1)}, u32[]{:S(2)}, u32[]{:S(2)}) collective-permute-start(bf16[512,128]{1,0:T(8,128)(2,1)S(1)} %broadcast_select_fusion.2), channel_id=1, source_target_pairs={{0,1},{1,0},{2,3},{3,2},{4,5},{5,4},{6,7},{7,6},{8,9},{9,8},{10,11... | collective-permute-start | bytes 393224 | tf_op jit(solution)/shard_map/ppermute | solution.py:399
  201.5 0.7 copy-start.17
Sparse Core Ops, SparseCore 0:
  30.7 56.5 all-gather.2

commit v6 on v4

--- a/solution.py
+++ b/solution.py
@@ -94,27 +94,22 @@
             yield slot, same_core
 
 
-def step_tokens(own, sib, halo_own=None, halo_sib=None):
-    parts = []
-    for slot, same_core in step_sources():
-        part = (own if same_core else sib)[slot, :ROWS]
-        if halo_own is not None:
-            part = jnp.concatenate([(halo_own if same_core else halo_sib)[slot], part], axis=0)
-        parts.append(part)
-    return jnp.concatenate(parts, axis=1)
+def step_tokens(own, sib, first=0):
+    refs = [(own if same_core else sib, slot) for slot, same_core in step_sources()]
+    return jnp.concatenate([ref[slot, first:ALL_ROWS] for ref, slot in refs], axis=1)
 
 
 def step_cols(own, sib):
-    parts = [(own if same_core else sib)[slot, ROWS:] for slot, same_core in step_sources()]
-    return jnp.concatenate(parts, axis=1)
-
-
-def step_rows(w_ref):
+    refs = [(own if same_core else sib, slot) for slot, same_core in step_sources()]
+    return jnp.concatenate([ref[slot, ALL_ROWS:] for ref, slot in refs], axis=1)
+
+
+def step_rows(w_ref, first):
     core = my_core()
     parts = []
     for slot, same_core in step_sources():
         from_core = core if same_core else 1 - core
-        at = pl.multiple_of((slot * CORES + from_core) * FEAT, FEAT)
+        at = pl.multiple_of(first + (slot * CORES + from_core) * FEAT, FEAT)
         parts.append(w_ref[pl.ds(at, FEAT), :])
     return jnp.concatenate(parts, axis=0)
 
@@ -122,8 +117,6 @@
 def scan_input_kernel(
     own,
     sib,
-    halo_own,
-    halo_sib,
     w_x,
     cols,
     taps_x,
@@ -141,11 +134,31 @@
     acc_x,
     acc_bc,
     raw_bc,
+    held,
+    sems,
 ):
     step = pl.program_id(0)
     core = my_core()
-    toks = step_tokens(own, sib, halo_own, halo_sib)
-    add_to(acc_x, step, dot(toks, step_rows(w_x)))
+    rows = 4 * FEAT
+
+    def copy(n):
+        at = pl.ds(n * rows, rows)
+        return pltpu.make_async_copy(w_x.at[at], held.at[at], sems.at[n])
+
+    for n in range(CHIPS // 2):
+
+        @pl.when(step == 0)
+        def _():
+            copy(n).start()
+
+    for n in range(CHIPS // 2):
+
+        @pl.when(step == n)
+        def _():
+            copy(n).wait()
+
+    toks = step_tokens(own, sib)
+    add_to(acc_x, step, dot(toks, step_rows(held, step * rows)))
     add_to(acc_bc, step, dot_nt(toks, step_cols(own, sib)))
 
     @pl.when(step == pl.num_programs(0) - 1)
@@ -207,7 +220,7 @@
         grid=(CHIPS // 2,),
         in_specs=[spec for _, spec in blocked] + [whole(a) for a in fixed],
         out_specs=[whole(a) for a in shapes],
-        out_shape=shapes,
+        out_shape=[pltpu.HBM(a.shape, a.dtype) for a in shapes],
         scratch_shapes=scratch,
         compiler_params=params(mib, True),
         cost_estimate=pl.CostEstimate(
@@ -225,7 +238,7 @@
     return w, pl.BlockSpec((4 * FEAT, CH), lambda i: (i, 0))
 
 
-def scan_input(own, sib, halo_own, halo_sib, w_x, fixed):
+def scan_input(own, sib, w_x, fixed):
     shapes = [
         jax.ShapeDtypeStruct((ROWS, CH), BF16),
         jax.ShapeDtypeStruct((ROWS, 2 * N), BF16),
@@ -234,22 +247,24 @@
         jax.ShapeDtypeStruct((N, CH), BF16),
         jax.ShapeDtypeStruct((CTX, 16, CH), BF16),
     ]
-    blocked = [two_chips(a, ROWS + COLS) for a in (own, sib)]
-    blocked += [two_chips(a, HALO) for a in (halo_own, halo_sib)] + [their_rows(w_x)]
+    blocked = [two_chips(a, ALL_ROWS + COLS) for a in (own, sib)]
+    blocked += [(w_x, pl.BlockSpec(memory_space=pltpu.HBM))]
     scratch = [
         pltpu.VMEM((ALL_ROWS, CH), F32),
         pltpu.VMEM((ALL_ROWS, COLS), F32),
         pltpu.VMEM((ALL_ROWS, 2 * N), F32),
+        pltpu.VMEM((CHIPS * 2 * FEAT, CH), BF16),
+        pltpu.SemaphoreType.DMA((CHIPS // 2,)),
     ]
     flops = 2 * ALL_ROWS * 4096 * (CH + COLS)
     return over_chips(
-        scan_input_kernel, blocked, fixed, shapes, scratch, 24, flops, "scan_input"
+        scan_input_kernel, blocked, fixed, shapes, scratch, 52, flops, "scan_input"
     )
 
 
 def gate_kernel(own, sib, w_z, gates, acc):
     step = pl.program_id(0)
-    add_to(acc, step, dot(step_tokens(own, sib), step_rows(w_z)))
+    add_to(acc, step, dot(step_tokens(own, sib, HALO), step_rows(w_z, 0)))
 
     @pl.when(step == pl.num_programs(0) - 1)
     def _():
@@ -259,7 +274,7 @@
 
 def gate(own, sib, w_z):
     shapes = [jax.ShapeDtypeStruct((ROWS, CH), F32)]
-    blocked = [two_chips(a, ROWS) for a in (own, sib)] + [their_rows(w_z)]
+    blocked = [two_chips(a, ALL_ROWS) for a in (own, sib)] + [their_rows(w_z)]
     scratch = [pltpu.VMEM((ROWS, CH), F32)]
     flops = 2 * ROWS * 4096 * CH
     return over_chips(gate_kernel, blocked, [], shapes, scratch, 16, flops, "gate")[0]
@@ -360,35 +375,52 @@
     )(*args)
 
 
-def project_kernel(place, own, sib, w, out):
-    del place
+def project_kernel(own, sib, w_all, out, held, sems):
+    step = pl.program_id(0)
+    y_low = lax.div(lax.axis_index("ctx"), Z_RING)
+
+    def copy(chip):
+        row = pl.multiple_of(lax.rem(y_low + chip // 4, 2) * 2 * CH, 2 * CH)
+        part = w_all.at[pl.ds(chip % 4 * 2, 2), pl.ds(row, 2 * CH), :]
+        return pltpu.make_async_copy(part, held.at[chip], sems.at[chip])
+
+    for chip in range(CHIPS):
+
+        @pl.when(step == 0)
+        def _():
+            copy(chip).start()
+
+    for chip in range(CHIPS):
+
+        @pl.when(step == chip)
+        def _():
+            copy(chip).wait()
+
     square = own[:, CH:].astype(F32) + sib[:, CH:].astype(F32)
     scale = lax.rsqrt((square[:, 0:1] + square[:, 64:65]) / (2.0 * CH) + NORM_EPS)
     values = jnp.concatenate([own[:, :CH], sib[:, :CH]], axis=1)
-    rows = jnp.concatenate([w[0], w[1]], axis=1)
+    rows = jnp.concatenate([held[step, 0], held[step, 1]], axis=1)
     out[0] = (dot(values, rows) * scale).astype(BF16)
 
 
-def project(own, sib, w_all, y_low):
-    def columns(chip, place):
-        return lax.rem(chip, 4), lax.rem(lax.div(chip, 4) + place[0], 2), 0
-
-    whole = pl.BlockSpec(own.shape, lambda i, place: (0, 0))
+def project(own, sib, w_all):
+    whole = pl.BlockSpec(own.shape, lambda i: (0, 0))
     return pl.pallas_call(
         project_kernel,
-        grid_spec=pltpu.PrefetchScalarGridSpec(
-            num_scalar_prefetch=1,
-            grid=(CHIPS,),
-            in_specs=[whole, whole, pl.BlockSpec((2, 2 * CH, 128), columns)],
-            out_specs=pl.BlockSpec((1, ROWS, 256), lambda i, place: (i, 0, 0)),
-        ),
+        grid=(CHIPS,),
+        in_specs=[whole, whole, pl.BlockSpec(memory_space=pltpu.HBM)],
+        out_specs=pl.BlockSpec((1, ROWS, 256), lambda i: (i, 0, 0)),
         out_shape=jax.ShapeDtypeStruct((CHIPS, ROWS, 256), BF16),
-        compiler_params=params(14, True),
+        scratch_shapes=[
+            pltpu.VMEM((CHIPS, 2, 2 * CH, 128), BF16),
+            pltpu.SemaphoreType.DMA((CHIPS,)),
+        ],
+        compiler_params=params(57, True),
         cost_estimate=pl.CostEstimate(
             flops=8 * ROWS * CH * 2048, bytes_accessed=8 * 2**20, transcendentals=0
         ),
         name="project",
-    )(y_low[None], own, sib, w_all)
+    )(own, sib, w_all)
 
 
 def swapped(value, bit):
@@ -447,19 +479,16 @@
     rank = lax.axis_index("tp")
     core = rank % CORES
     chip = rank // CORES
-    y_low = (lax.axis_index("ctx") // Z_RING).astype(jnp.int32)
 
     w_cols = jnp.concatenate(
         [w_bc.T.reshape(CHIPS, 2 * N, FEAT), w_dt.T.reshape(CHIPS, 2 * HEADS, FEAT)], axis=1
     )
-    shared = jnp.broadcast_to(tokens[None], (CHIPS, ROWS, FEAT))
-    own = between_chips(jnp.concatenate([shared, w_cols], axis=1))
-
     ids_row = jnp.pad((seg_ids[-3:] + 1).astype(BF16), (0, FEAT - 3))[None]
     halo = next_ctx(jnp.concatenate([ids_row, tokens[1 - HALO :]], axis=0))
     ids_prior = halo[0, :3].astype(jnp.int32) - 1
-    halo_own = between_chips(jnp.broadcast_to(halo[None], (CHIPS, HALO, FEAT)))
-    halo_sib = swapped(halo_own, 1)
+    shared = jnp.concatenate([halo, tokens], axis=0)
+    shared = jnp.broadcast_to(shared[None], (CHIPS, ALL_ROWS, FEAT))
+    own = between_chips(jnp.concatenate([shared, w_cols], axis=1))
 
     halves = (w_out[:, :128], w_out[:, 128:])
     w_pair = jnp.concatenate(
@@ -475,19 +504,18 @@
     bias_bc = lax.dynamic_slice_in_dim(conv_bc_bias, chip * 2 * N, 2 * N, 0)[None]
     skip = jnp.repeat(skip_gain, P_SIZE)[None]
     fixed = [cols, conv_x, conv_x_bias[None], taps_bc, bias_bc, dt_bias[None], decay_rate[None]]
-    own, fixed, seg_row, skip, halo_own, halo_sib = together(
-        own, fixed, seg_row, skip, halo_own, halo_sib
-    )
+    own, fixed, seg_row, skip = together(own, fixed, seg_row, skip)
     sib = swapped(own, 1)
-    xc, bcc, hcol, hrow, s0, pay = scan_input(own, sib, halo_own, halo_sib, w_x, fixed)
+    xc, bcc, hcol, hrow, s0, pay = scan_input(own, sib, w_x, fixed)
     own, sib, pay = together(own, sib, pay)
     pieces = between_slabs(pay)
     gates = gate(own, sib, w_z)
     pieces, gates, xc, bcc = together(pieces, gates, xc, bcc)
     state = between_slabs(prefix(pieces).reshape(CTX, 8, CH)).reshape(N, CH)
     y = intra(xc, bcc, hcol, hrow, s0, fixed[0], seg_row, skip)
+    y, state, w_all = together(y, state, w_all)
     mine = join(y, gates, bcc, hcol, state, norm_weight[None])
-    parts = between_chips(project(mine, swapped(mine, 1), w_all, y_low))
+    parts = between_chips(project(mine, swapped(mine, 1), w_all))
     total = jnp.sum(parts.astype(F32), axis=0).astype(BF16)
     parts = (total[:, :128], total[:, 128:])
     kept = pick(core, *parts)

time: 192 us -> 190 us (0.990)
  waiting for transfers between devices: 43.5 us -> 54.1 us
  local copies, waits for them, and re-layouts: 29.5 us -> 19.3 us
  starting transfers between devices: 43 us -> 33.6 us
  Pallas kernels: 22.3 us -> 30 us
    unnamed x64 -> x50, local copies, waits for them, and re-layouts: 20 us -> 11.4 us
    all_to_all x2 -> x1, starting transfers between devices: 14 us -> 6.06 us  [between_chips(): return lax.all_to_all(value, 'tp', 0, 0, axis_index_groups=same_core)]
    all_to_all x2 -> x1, waiting for transfers between devices: 35.1 us -> 39.8 us  [between_chips(): return lax.all_to_all(value, 'tp', 0, 0, axis_index_groups=same_core)]
    all_to_all x2, waiting for transfers between devices: 0.26 us -> 4.69 us  [between_slabs(): return lax.all_to_all(value, 'ctx', 0, 0)]
    pallas_call x2, Pallas kernels: 14.5 us -> 18.7 us  [over_chips(): pl.pallas_call(kernel, grid=(CHIPS // 2,), in_specs=[spec for _, spec in...]
    pallas_call x1, Pallas kernels: 4.06 us -> 7.49 us  [project(): pl.pallas_call(project_kernel, grid=(CHIPS,), in_specs=[whole, whole, pl....]
    ppermute x1, starting transfers between devices: 3.1 us -> 0.09 us  [local(): lax.ppermute(w_pair, 'ctx', [(i, i ^ Z_RING) for i in range(2 * Z_RING)])]
    all_to_all x2, starting transfers between devices: 12.5 us -> 15.5 us  [between_slabs(): return lax.all_to_all(value, 'ctx', 0, 0)]
  transfers between devices with their start and end apart: 12 -> 10, of which waited for: 5 -> 7; matrix products, arithmetic and copies ran while one was open for 9% -> 7% of each run, Pallas kernels for 10% -> 11%
where the time goes in v6:
time: 190 us; the launch traced here: 189 us
  waiting for transfers between devices  54.1 us (28%)
  starting transfers between devices  33.6 us (18%)
  blocking collectives  31.2 us (16%)
  Pallas kernels  30 us (16%)
  local copies, waits for them, and re-layouts  19.3 us (10%)
  between operations  13.7 us (7%)
  other arithmetic  6.95 us (4%)
    all_to_all x1, waiting for transfers between devices, between_chips(): return lax.all_to_all(value, 'tp', 0, 0, axis_index_groups=same_core)  39.8 us
    all_to_all x1, blocking collectives, between_chips(): return lax.all_to_all(value, 'tp', 0, 0, axis_index_groups=same_core)  31.2 us
    pallas_call x2, Pallas kernels, over_chips(): pl.pallas_call(kernel, grid=(CHIPS // 2,), in_specs=[spec for _, spec in...  18.7 us
    all_to_all x2, starting transfers between devices, between_slabs(): return lax.all_to_all(value, 'ctx', 0, 0)  15.5 us
    unnamed x50, local copies, waits for them, and re-layouts  11.4 us
    ppermute x4, waiting for transfers between devices, swapped(): return lax.ppermute(value, 'tp', [(i, i ^ bit) for i in range(16)])  9.17 us
    ppermute x4, starting transfers between devices, swapped(): return lax.ppermute(value, 'tp', [(i, i ^ bit) for i in range(16)])  8.87 us
    pallas_call x1, Pallas kernels, project(): pl.pallas_call(project_kernel, grid=(CHIPS,), in_specs=[whole, whole, pl....  7.49 us
  transfers between devices with their start and end apart: 10, of which 7 were waited for; matrix products, arithmetic and copies ran while one was open for 7% of the time, Pallas kernels for 11%

profile of v6, /device:TPU:1, one launch (start us, length us, event | category | flops | bytes accessed | tf_op | source)
XLA Modules:
  0.0 188.8 jit_solution(12552327992697491537)
XLA Ops:
  6.5 1.0 broadcast_select_fusion.5
  7.6 3.3 %collective-permute-start.2 = (bf16[512,128]{1,0:T(8,128)(2,1)S(1)}, bf16[512,128]{1,0:T(8,128)(2,1)S(1)}, u32[]{:S(2)}, u32[]{:S(2)}) collective-permute-start(bf16[512,128]{1,0:T(8,128)(2,1)S(1)} %get-tuple-element.60), channel_id=1, source_target_pairs={{0,1},{1,0},{2,3},{3,2},{4,5},{5,4},{6,7},{7,6},{8,9},{9,8},{10,11... | collective-permute-start | bytes 393224 | tf_op jit(solution)/shard_map/ppermute | solution.py:427
  10.9 1.0 collective-permute-done.2
  11.9 0.1 collective-permute-start.3
  12.0 0.8 add_convert_fusion
  12.8 0.7 slice.42
  13.5 3.1 %collective-permute-start = (bf16[16,256]{1,0:T(8,128)(2,1)S(1)}, bf16[16,256]{1,0:T(8,128)(2,1)S(1)}, u32[]{:S(2)}, u32[]{:S(2)}) collective-permute-start(bf16[16,256]{1,0:T(8,128)(2,1)S(1)} %pad_maximum_fusion.5), channel_id=1, source_target_pairs={{0,16},{16,32},{32,48},{48,64},{64,80},{80,96},{96,112},{112,128},... | collective-permute-start | bytes 24584 | tf_op jit(solution)/shard_map/ppermute | solution.py:431
  16.6 0.9 copy.29
  17.5 1.5 copy.28
  19.1 0.5 collective-permute-done.3
  19.5 0.8 pad_maximum_fusion.1
  20.4 0.1 broadcast_in_dim.34
  20.5 1.8 pad_maximum_fusion
  22.4 6.1 %all-to-all-start = ((bf16[8,800,256]{2,1,0:T(8,128)(2,1)}), bf16[8,800,256]{2,1,0:T(8,128)(2,1)S(1)}, u32[]{:S(2)}, u32[]{:S(2)}) async-start(bf16[8,800,256]{2,1,0:T(8,128)(2,1)} %pad_maximum_fusion), calls=%async_computation | async-start | bytes 6553600 | tf_op jit(solution)/shard_map/all_to_all | solution.py:436
  28.5 0.1 broadcast_in_dim_reshape.3.skip
  28.6 0.8 dynamic_slice.7
  29.4 0.6 fusion.5
  30.0 0.6 slice.47
  30.6 1.9 compare_convert_fusion
  32.5 0.8 copy.30
  33.4 1.7 pad.9.cols
  35.1 39.8 %all-to-all-done.own = bf16[8,800,256]{2,1,0:T(8,128)(2,1)S(1)} async-done(((bf16[8,800,256]{2,1,0:T(8,128)(2,1)}), bf16[8,800,256]{2,1,0:T(8,128)(2,1)S(1)}, u32[]{:S(2)}, u32[]{:S(2)}) %all-to-all-start) | async-done | bytes 3276832 | tf_op jit(solution)/shard_map/all_to_all | solution.py:436
  74.8 1.8 collective-permute-start.1
  76.6 5.5 %collective-permute-done.1.sib = bf16[8,800,256]{2,1,0:T(8,128)(2,1)S(1)} collective-permute-done((bf16[8,800,256]{2,1,0:T(8,128)(2,1)S(1)}, bf16[8,800,256]{2,1,0:T(8,128)(2,1)S(1)}, u32[]{:S(2)}, u32[]{:S(2)}) %collective-permute-start.1) | collective-permute-done | bytes 3276832 | tf_op jit(solution)/shard_map/ppermute | solution.py:427
  82.1 1.8 copy-done.5
  83.9 0.9 copy-done.10
  84.9 13.8 %scan_input.1 = (bf16[512,512]{1,0:T(8,128)(2,1)}, bf16[512,256]{1,0:T(8,128)(2,1)}, f32[512,128]{1,0:T(8,128)}, f32[16,512]{1,0:T(8,128)}, bf16[128,512]{1,0:T(8,128)(2,1)}, /*index=5*/bf16[16,16,512]{2,1,0:T(8,128)(2,1)}) custom-call(bf16[8,800,256]{2,1,0:T(8,128)(2,1)} %copy-done.1, bf16[8,800,256]{2,1,0:T(8,128)(2,1)} %copy-done.5, ...), custom_call_target="tpu_custom_call" | custom-call | flops 3391094784 | bytes 8388608 | tf_op jit(solution)/shard_map/scan_input/pallas_call | solution.py:218
  98.7 7.9 %all-to-all-start.1 = ((bf16[16,16,512]{2,1,0:T(8,128)(2,1)}), bf16[16,16,512]{2,1,0:T(8,128)(2,1)S(1)}, u32[]{:S(2)}, u32[]{:S(2)}) async-start(bf16[16,16,512]{2,1,0:T(8,128)(2,1)} %get-tuple-element.40), calls=%async_computation.1 | async-start | bytes 524288 | tf_op jit(solution)/shard_map/all_to_all | solution.py:440
  106.6 1.9 %copy-done.2 = bf16[8,800,256]{2,1,0:T(8,128)(2,1)S(1)} copy-done((bf16[8,800,256]{2,1,0:T(8,128)(2,1)S(1)}, bf16[8,800,256]{2,1,0:T(8,128)(2,1)}, u32[]{:S(2)}) %copy-start.2) | copy-done | bytes 3276824
  108.5 2.2 %copy-done.3 = bf16[4096,512]{1,0:T(8,128)(2,1)S(1)} copy-done((bf16[4096,512]{1,0:T(8,128)(2,1)S(1)}, bf16[4096,512]{1,0:T(8,128)(2,1)}, u32[]{:S(2)}) %copy-start.3) | copy-done | bytes 4194328
  110.7 1.9 %copy-done.6 = bf16[8,800,256]{2,1,0:T(8,128)(2,1)S(1)} copy-done((bf16[8,800,256]{2,1,0:T(8,128)(2,1)S(1)}, bf16[8,800,256]{2,1,0:T(8,128)(2,1)}, u32[]{:S(2)}) %copy-start.6) | copy-done | bytes 3276824
  112.7 4.9 %gate.1.gates = f32[512,512]{1,0:T(8,128)} custom-call(bf16[8,800,256]{2,1,0:T(8,128)(2,1)S(1)} %copy-done.2, bf16[8,800,256]{2,1,0:T(8,128)(2,1)S(1)} %copy-done.6, bf16[4096,512]{1,0:T(8,128)(2,1)S(1)} %copy-done.3), custom_call_target="tpu_custom_call" | custom-call | flops 2147483648 | bytes 8388608 | tf_op jit(solution)/shard_map/gate/pallas_call | solution.py:218
  117.5 0.7 prefix.1
  118.3 7.6 %all-to-all-start.2 = ((bf16[16,8,512]{2,1,0:T(8,128)(2,1)}), bf16[16,8,512]{2,1,0:T(8,128)(2,1)S(1)}, u32[]{:S(2)}, u32[]{:S(2)}) async-start(bf16[16,8,512]{2,1,0:T(8,128)(2,1)} %bitcast.19), calls=%async_computation.2 | async-start | bytes 262144 | tf_op jit(solution)/shard_map/all_to_all | solution.py:440
  125.9 1.0 copy-done.17
  126.9 1.7 intra.1.y
  128.7 4.7 %all-to-all-done.2 = bf16[16,8,512]{2,1,0:T(8,128)(2,1)S(1)} async-done(((bf16[16,8,512]{2,1,0:T(8,128)(2,1)}), bf16[16,8,512]{2,1,0:T(8,128)(2,1)S(1)}, u32[]{:S(2)}, u32[]{:S(2)}) %all-to-all-start.2) | async-done | bytes 131104 | tf_op jit(solution)/shard_map/all_to_all | solution.py:440
  133.4 1.3 join.1.own
  134.7 2.4 %collective-permute-start.4 = (bf16[512,640]{1,0:T(8,128)(2,1)S(1)}, bf16[512,640]{1,0:T(8,128)(2,1)S(1)}, u32[]{:S(2)}, u32[]{:S(2)}) collective-permute-start(bf16[512,640]{1,0:T(8,128)(2,1)S(1)} %join.1.own), channel_id=1, source_target_pairs={{0,1},{1,0},{2,3},{3,2},{4,5},{5,4},{6,7},{7,6},{8,9},{9,8},{10,11... | collective-permute-start | bytes 1966088 | tf_op jit(solution)/shard_map/ppermute | solution.py:427
  137.1 1.7 collective-permute-done.4.sib
  138.8 0.8 copy-done.23
  139.6 7.5 %project.1 = bf16[8,512,256]{2,1,0:T(8,128)(2,1)} custom-call(bf16[512,640]{1,0:T(8,128)(2,1)} %copy-done.7, bf16[512,640]{1,0:T(8,128)(2,1)} %copy-done.23, bf16[8,2048,128]{2,1,0:T(8,128)(2,1)} %bitcast.42), custom_call_target="tpu_custom_call" | custom-call | flops 4294967296 | bytes 8388608 | tf_op jit(solution)/shard_map/project/pallas_call | solution.py:408
  147.1 31.2 %all_to_all.20 = bf16[8,512,256]{2,1,0:T(8,128)(2,1)S(1)} all-to-all(bf16[8,512,256]{2,1,0:T(8,128)(2,1)} %project.1), channel_id=1, replica_groups={{0,2,4,6,8,10,12,14},{1,3,5,7,9,11,13,15},{16,18,20,22,24,26,28,30},{17..., dimensions={0} | all-to-all | bytes 4194304 | tf_op jit(solution)/shard_map/all_to_all | solution.py:436
  178.3 0.4 reduce_sum.12
  178.8 1.4 collective-permute-start.5
  180.2 1.0 collective-permute-done.5
  181.2 0.1 broadcast_select_fusion.1
  181.3 0.7 copy-done.24
  (61 shorter events, 0.4 us)
Async XLA Ops:
  6.5 22.8 %copy-start = (f32[4,2048]{1,0:T(4,128)S(1)}, f32[4,2048]{1,0:T(4,128)}, u32[]{:S(2)}) copy-start(f32[4,2048]{1,0:T(4,128)} %param.23) | copy-start | bytes 98308
  6.5 12.5 %copy-start.20 = (bf16[512,256]{1,0:T(8,128)(2,1)S(1)}, bf16[512,256]{1,0:T(8,128)(2,1)}, u32[]{:S(2)}) copy-start(bf16[512,256]{1,0:T(8,128)(2,1)} %param.15) | copy-start | bytes 786436
  6.5 126.8 %all-gather.3.cloned.1.call-start = ((), (), s32[]{:S(2)}) async-start(), calls=%async_computation.4 | async-start | bytes 4718592 | tf_op jit(solution)/shard_map/all_gather | solution.py:500
  7.6 4.3 %collective-permute-start.2 = (bf16[512,128]{1,0:T(8,128)(2,1)S(1)}, bf16[512,128]{1,0:T(8,128)(2,1)S(1)}, u32[]{:S(2)}, u32[]{:S(2)}) collective-permute-start(bf16[512,128]{1,0:T(8,128)(2,1)S(1)} %get-tuple-element.60), channel_id=1, source_target_pairs={{0,1},{1,0},{2,3},{3,2},{4,5},{5,4},{6,7},{7,6},{8,9},{9,8},{10,11... | collective-permute-start | bytes 393224 | tf_op jit(solution)/shard_map/ppermute | solution.py:427
  11.9 7.6 %collective-permute-start.3 = (bf16[1024,128]{1,0:T(8,128)(2,1)S(1)}, bf16[1024,128]{1,0:T(8,128)(2,1)S(1)}, u32[]{:S(2)}, u32[]{:S(2)}) collective-permute-start(bf16[1024,128]{1,0:T(8,128)(2,1)S(1)} %pad_maximum_fusion.3), channel_id=1, source_target_pairs={{0,128},{16,144},{32,160},{48,176},{64,192},{80,208},{96,224},{112... | collective-permute-start | bytes 786440 | tf_op jit(solution)/shard_map/ppermute | solution.py:497
  13.5 5.5 %collective-permute-start = (bf16[16,256]{1,0:T(8,128)(2,1)S(1)}, bf16[16,256]{1,0:T(8,128)(2,1)S(1)}, u32[]{:S(2)}, u32[]{:S(2)}) collective-permute-start(bf16[16,256]{1,0:T(8,128)(2,1)S(1)} %pad_maximum_fusion.5), channel_id=1, source_target_pairs={{0,16},{16,32},{32,48},{48,64},{64,80},{80,96},{96,112},{112,128},... | collective-permute-start | bytes 24584 | tf_op jit(solution)/shard_map/ppermute | solution.py:431
  22.3 6.1 %copy-start.21 = (s32[512]{0:T(512)S(1)}, s32[512]{0:T(512)}, u32[]{:S(2)}) copy-start(s32[512]{0:T(512)} %param.16) | copy-start | bytes 6148
  22.3 6.1 %copy-start.22 = (f32[8]{0:T(128)S(1)}, f32[8]{0:T(128)}, u32[]{:S(2)}) copy-start(f32[8]{0:T(128)} %param.27) | copy-start | bytes 100
  22.3 61.6 %copy-start.13 = (f32[4,512]{1,0:T(4,128)S(1)}, f32[4,512]{1,0:T(4,128)}, u32[]{:S(2)}) copy-start(f32[4,512]{1,0:T(4,128)} %taps_x) | copy-start | bytes 24580
  22.3 61.6 %copy-start.14 = (f32[512]{0:T(512)S(1)}, f32[512]{0:T(512)}, u32[]{:S(2)}) copy-start(f32[512]{0:T(512)} %param.22) | copy-start | bytes 6148
  22.3 61.6 %copy-start.15 = (f32[8]{0:T(128)S(1)}, f32[8]{0:T(128)}, u32[]{:S(2)}) copy-start(f32[8]{0:T(128)} %param.25) | copy-start | bytes 100
  22.4 61.5 %copy-start.16 = (f32[8]{0:T(128)S(1)}, f32[8]{0:T(128)}, u32[]{:S(2)}) copy-start(f32[8]{0:T(128)} %param.26) | copy-start | bytes 100
  22.4 52.5 %all-to-all-start = ((bf16[8,800,256]{2,1,0:T(8,128)(2,1)}), bf16[8,800,256]{2,1,0:T(8,128)(2,1)S(1)}, u32[]{:S(2)}, u32[]{:S(2)}) async-start(bf16[8,800,256]{2,1,0:T(8,128)(2,1)} %pad_maximum_fusion), calls=%async_computation | async-start | bytes 6553600 | tf_op jit(solution)/shard_map/all_to_all | solution.py:436
  74.8 7.2 %copy-start.1 = (bf16[8,800,256]{2,1,0:T(8,128)(2,1)}, bf16[8,800,256]{2,1,0:T(8,128)(2,1)S(1)}, u32[]{:S(2)}) copy-start(bf16[8,800,256]{2,1,0:T(8,128)(2,1)S(1)} %all-to-all-done.own) | copy-start | bytes 9830404
  74.8 7.2 %collective-permute-start.1 = (bf16[8,800,256]{2,1,0:T(8,128)(2,1)S(1)}, bf16[8,800,256]{2,1,0:T(8,128)(2,1)S(1)}, u32[]{:S(2)}, u32[]{:S(2)}) collective-permute-start(bf16[8,800,256]{2,1,0:T(8,128)(2,1)S(1)} %all-to-all-done.own), channel_id=1, source_target_pairs={{0,1},{1,0},{2,3},{3,2},{4,5},{5,4},{6,7},{7,6},{8,9},{9,8},{10,11... | collective-permute-start | bytes 9830408 | tf_op jit(solution)/shard_map/ppermute | solution.py:427
  82.1 1.8 copy-start.5
  83.9 1.0 copy-start.10
  98.7 18.8 %all-to-all-start.1 = ((bf16[16,16,512]{2,1,0:T(8,128)(2,1)}), bf16[16,16,512]{2,1,0:T(8,128)(2,1)S(1)}, u32[]{:S(2)}, u32[]{:S(2)}) async-start(bf16[16,16,512]{2,1,0:T(8,128)(2,1)} %get-tuple-element.40), calls=%async_computation.1 | async-start | bytes 524288 | tf_op jit(solution)/shard_map/all_to_all | solution.py:440
  106.6 1.9 %copy-start.2 = (bf16[8,800,256]{2,1,0:T(8,128)(2,1)S(1)}, bf16[8,800,256]{2,1,0:T(8,128)(2,1)}, u32[]{:S(2)}) copy-start(bf16[8,800,256]{2,1,0:T(8,128)(2,1)} %copy-done.1) | copy-start | bytes 9830404
  108.5 2.2 %copy-start.3 = (bf16[4096,512]{1,0:T(8,128)(2,1)S(1)}, bf16[4096,512]{1,0:T(8,128)(2,1)}, u32[]{:S(2)}) copy-start(bf16[4096,512]{1,0:T(8,128)(2,1)} %w_z.1) | copy-start | bytes 12582916
  110.7 1.9 %copy-start.6 = (bf16[8,800,256]{2,1,0:T(8,128)(2,1)S(1)}, bf16[8,800,256]{2,1,0:T(8,128)(2,1)}, u32[]{:S(2)}) copy-start(bf16[8,800,256]{2,1,0:T(8,128)(2,1)} %copy-done.5) | copy-start | bytes 9830404
  112.7 13.2 %copy-start.8 = (bf16[512,256]{1,0:T(8,128)(2,1)S(1)}, bf16[512,256]{1,0:T(8,128)(2,1)}, u32[]{:S(2)}) copy-start(bf16[512,256]{1,0:T(8,128)(2,1)} %get-tuple-element.46.bcc) | copy-start | bytes 786436
  112.7 13.2 %copy-start.9 = (f32[512,128]{1,0:T(8,128)S(1)}, f32[512,128]{1,0:T(8,128)}, u32[]{:S(2)}) copy-start(f32[512,128]{1,0:T(8,128)} %get-tuple-element.47.hcol) | copy-start | bytes 786436
  112.7 13.2 %copy-start.11 = (f32[512,128]{1,0:T(8,128)S(1)}, f32[512,128]{1,0:T(8,128)}, u32[]{:S(2)}) copy-start(f32[512,128]{1,0:T(8,128)} %pad.9.cols) | copy-start | bytes 786436
  112.7 13.2 %copy-start.18 = (bf16[128,512]{1,0:T(8,128)(2,1)S(1)}, bf16[128,512]{1,0:T(8,128)(2,1)}, u32[]{:S(2)}) copy-start(bf16[128,512]{1,0:T(8,128)(2,1)} %get-tuple-element.49.s0) | copy-start | bytes 393220
  112.7 13.2 %copy-start.19 = (f32[16,512]{1,0:T(8,128)S(1)}, f32[16,512]{1,0:T(8,128)}, u32[]{:S(2)}) copy-start(f32[16,512]{1,0:T(8,128)} %get-tuple-element.48.hrow) | copy-start | bytes 98308
  117.5 15.8 %copy-start.4 = (f32[512,512]{1,0:T(8,128)S(1)}, f32[512,512]{1,0:T(8,128)}, u32[]{:S(2)}) copy-start(f32[512,512]{1,0:T(8,128)} %gate.1.gates) | copy-start | bytes 3145732
  117.5 15.8 %copy-start.12 = (f32[512]{0:T(512)S(1)}, f32[512]{0:T(512)}, u32[]{:S(2)}) copy-start(f32[512]{0:T(512)} %param.28) | copy-start | bytes 6148
  118.3 15.1 %all-to-all-start.2 = ((bf16[16,8,512]{2,1,0:T(8,128)(2,1)}), bf16[16,8,512]{2,1,0:T(8,128)(2,1)S(1)}, u32[]{:S(2)}, u32[]{:S(2)}) async-start(bf16[16,8,512]{2,1,0:T(8,128)(2,1)} %bitcast.19), calls=%async_computation.2 | async-start | bytes 262144 | tf_op jit(solution)/shard_map/all_to_all | solution.py:440
  125.9 1.0 copy-start.17
  134.7 4.1 %copy-start.7 = (bf16[512,640]{1,0:T(8,128)(2,1)}, bf16[512,640]{1,0:T(8,128)(2,1)S(1)}, u32[]{:S(2)}) copy-start(bf16[512,640]{1,0:T(8,128)(2,1)S(1)} %join.1.own) | copy-start | bytes 1966084
  134.7 4.1 %collective-permute-start.4 = (bf16[512,640]{1,0:T(8,128)(2,1)S(1)}, bf16[512,640]{1,0:T(8,128)(2,1)S(1)}, u32[]{:S(2)}, u32[]{:S(2)}) collective-permute-start(bf16[512,640]{1,0:T(8,128)(2,1)S(1)} %join.1.own), channel_id=1, source_target_pairs={{0,1},{1,0},{2,3},{3,2},{4,5},{5,4},{6,7},{7,6},{8,9},{9,8},{10,11... | collective-permute-start | bytes 1966088 | tf_op jit(solution)/shard_map/ppermute | solution.py:427
  138.8 0.8 copy-start.23
  178.8 2.4 %collective-permute-start.5 = (bf16[512,128]{1,0:T(8,128)(2,1)S(1)}, bf16[512,128]{1,0:T(8,128)(2,1)S(1)}, u32[]{:S(2)}, u32[]{:S(2)}) collective-permute-start(bf16[512,128]{1,0:T(8,128)(2,1)S(1)} %broadcast_select_fusion.2), channel_id=1, source_target_pairs={{0,1},{1,0},{2,3},{3,2},{4,5},{5,4},{6,7},{7,6},{8,9},{9,8},{10,11... | collective-permute-start | bytes 393224 | tf_op jit(solution)/shard_map/ppermute | solution.py:427
  181.3 0.7 copy-start.24
Sparse Core Ops, SparseCore 0:
  20.5 57.7 all-gather.2

commit v7 on v4

--- a/solution.py
+++ b/solution.py
@@ -94,19 +94,14 @@
             yield slot, same_core
 
 
-def step_tokens(own, sib, halo_own=None, halo_sib=None):
-    parts = []
-    for slot, same_core in step_sources():
-        part = (own if same_core else sib)[slot, :ROWS]
-        if halo_own is not None:
-            part = jnp.concatenate([(halo_own if same_core else halo_sib)[slot], part], axis=0)
-        parts.append(part)
-    return jnp.concatenate(parts, axis=1)
+def step_tokens(own, sib, first=0):
+    refs = [(own if same_core else sib, slot) for slot, same_core in step_sources()]
+    return jnp.concatenate([ref[slot, first:ALL_ROWS] for ref, slot in refs], axis=1)
 
 
 def step_cols(own, sib):
-    parts = [(own if same_core else sib)[slot, ROWS:] for slot, same_core in step_sources()]
-    return jnp.concatenate(parts, axis=1)
+    refs = [(own if same_core else sib, slot) for slot, same_core in step_sources()]
+    return jnp.concatenate([ref[slot, ALL_ROWS:] for ref, slot in refs], axis=1)
 
 
 def step_rows(w_ref):
@@ -122,8 +117,6 @@
 def scan_input_kernel(
     own,
     sib,
-    halo_own,
-    halo_sib,
     w_x,
     cols,
     taps_x,
@@ -144,7 +137,7 @@
 ):
     step = pl.program_id(0)
     core = my_core()
-    toks = step_tokens(own, sib, halo_own, halo_sib)
+    toks = step_tokens(own, sib)
     add_to(acc_x, step, dot(toks, step_rows(w_x)))
     add_to(acc_bc, step, dot_nt(toks, step_cols(own, sib)))
 
@@ -207,7 +200,7 @@
         grid=(CHIPS // 2,),
         in_specs=[spec for _, spec in blocked] + [whole(a) for a in fixed],
         out_specs=[whole(a) for a in shapes],
-        out_shape=shapes,
+        out_shape=[pltpu.HBM(a.shape, a.dtype) for a in shapes],
         scratch_shapes=scratch,
         compiler_params=params(mib, True),
         cost_estimate=pl.CostEstimate(
@@ -225,7 +218,7 @@
     return w, pl.BlockSpec((4 * FEAT, CH), lambda i: (i, 0))
 
 
-def scan_input(own, sib, halo_own, halo_sib, w_x, fixed):
+def scan_input(own, sib, w_x, fixed):
     shapes = [
         jax.ShapeDtypeStruct((ROWS, CH), BF16),
         jax.ShapeDtypeStruct((ROWS, 2 * N), BF16),
@@ -234,8 +227,8 @@
         jax.ShapeDtypeStruct((N, CH), BF16),
         jax.ShapeDtypeStruct((CTX, 16, CH), BF16),
     ]
-    blocked = [two_chips(a, ROWS + COLS) for a in (own, sib)]
-    blocked += [two_chips(a, HALO) for a in (halo_own, halo_sib)] + [their_rows(w_x)]
+    blocked = [two_chips(a, ALL_ROWS + COLS) for a in (own, sib)]
+    blocked += [their_rows(w_x)]
     scratch = [
         pltpu.VMEM((ALL_ROWS, CH), F32),
         pltpu.VMEM((ALL_ROWS, COLS), F32),
@@ -243,13 +236,13 @@
     ]
     flops = 2 * ALL_ROWS * 4096 * (CH + COLS)
     return over_chips(
-        scan_input_kernel, blocked, fixed, shapes, scratch, 24, flops, "scan_input"
+        scan_input_kernel, blocked, fixed, shapes, scratch, 22, flops, "scan_input"
     )
 
 
 def gate_kernel(own, sib, w_z, gates, acc):
     step = pl.program_id(0)
-    add_to(acc, step, dot(step_tokens(own, sib), step_rows(w_z)))
+    add_to(acc, step, dot(step_tokens(own, sib, HALO), step_rows(w_z)))
 
     @pl.when(step == pl.num_programs(0) - 1)
     def _():
@@ -259,7 +252,7 @@
 
 def gate(own, sib, w_z):
     shapes = [jax.ShapeDtypeStruct((ROWS, CH), F32)]
-    blocked = [two_chips(a, ROWS) for a in (own, sib)] + [their_rows(w_z)]
+    blocked = [two_chips(a, ALL_ROWS) for a in (own, sib)] + [their_rows(w_z)]
     scratch = [pltpu.VMEM((ROWS, CH), F32)]
     flops = 2 * ROWS * 4096 * CH
     return over_chips(gate_kernel, blocked, [], shapes, scratch, 16, flops, "gate")[0]
@@ -404,6 +397,30 @@
     return lax.all_to_all(value, "tp", 0, 0, axis_index_groups=same_core)
 
 
+def along_z(value, steps):
+    pairs = [(i, i // Z_RING * Z_RING + (i + steps) % Z_RING) for i in range(CTX)]
+    return lax.ppermute(value, "ctx", pairs)
+
+
+def gathered_along_z(mine):
+    rows, lanes = mine.shape
+    z_place = lax.axis_index("ctx") % Z_RING
+    held = jnp.zeros((Z_RING, rows, lanes), mine.dtype)
+
+    def put(held, piece, distance, row=0):
+        at = ((z_place + distance) % Z_RING, row, 0)
+        return lax.dynamic_update_slice(held, piece[None], at)
+
+    held = put(held, mine, 0)
+    above, below = mine, mine
+    for distance in range(1, Z_RING // 2):
+        below, above = along_z(below, 1), along_z(above, -1)
+        held = put(put(held, below, -distance), above, distance)
+    half = rows // 2
+    below, above = along_z(below[:half], 1), along_z(above[half:], -1)
+    return put(put(held, below, Z_RING // 2), above, Z_RING // 2, half)
+
+
 def between_slabs(value):
     return lax.all_to_all(value, "ctx", 0, 0)
 
@@ -452,34 +469,30 @@
     w_cols = jnp.concatenate(
         [w_bc.T.reshape(CHIPS, 2 * N, FEAT), w_dt.T.reshape(CHIPS, 2 * HEADS, FEAT)], axis=1
     )
-    shared = jnp.broadcast_to(tokens[None], (CHIPS, ROWS, FEAT))
-    own = between_chips(jnp.concatenate([shared, w_cols], axis=1))
-
     ids_row = jnp.pad((seg_ids[-3:] + 1).astype(BF16), (0, FEAT - 3))[None]
     halo = next_ctx(jnp.concatenate([ids_row, tokens[1 - HALO :]], axis=0))
     ids_prior = halo[0, :3].astype(jnp.int32) - 1
-    halo_own = between_chips(jnp.broadcast_to(halo[None], (CHIPS, HALO, FEAT)))
-    halo_sib = swapped(halo_own, 1)
+    shared = jnp.concatenate([halo, tokens], axis=0)
+    shared = jnp.broadcast_to(shared[None], (CHIPS, ALL_ROWS, FEAT))
+    sent = jnp.concatenate([shared, w_cols], axis=1)
+    sent, w_out = together(sent, w_out)
+    own = between_chips(sent)
 
     halves = (w_out[:, :128], w_out[:, 128:])
     w_pair = jnp.concatenate(
         [pick(core, *halves), swapped(pick(core, halves[1], halves[0]), 1)], axis=0
     )
     w_far = lax.ppermute(w_pair, "ctx", [(i, i ^ Z_RING) for i in range(2 * Z_RING)])
-    same_y = [list(range(Z_RING)), list(range(Z_RING, 2 * Z_RING))]
-    w_both = jnp.concatenate([w_pair, w_far], axis=0)
-    w_all = lax.all_gather(w_both, "ctx", axis=0, axis_index_groups=same_y)
+    w_all = gathered_along_z(jnp.concatenate([w_pair, w_far], axis=0))
 
     cols, seg_row = document_columns(seg_ids, ids_prior)
     taps_bc = lax.dynamic_slice_in_dim(conv_bc, chip * 2 * N, 2 * N, 1)
     bias_bc = lax.dynamic_slice_in_dim(conv_bc_bias, chip * 2 * N, 2 * N, 0)[None]
     skip = jnp.repeat(skip_gain, P_SIZE)[None]
     fixed = [cols, conv_x, conv_x_bias[None], taps_bc, bias_bc, dt_bias[None], decay_rate[None]]
-    own, fixed, seg_row, skip, halo_own, halo_sib = together(
-        own, fixed, seg_row, skip, halo_own, halo_sib
-    )
+    own, w_all, fixed, seg_row, skip = together(own, w_all, fixed, seg_row, skip)
     sib = swapped(own, 1)
-    xc, bcc, hcol, hrow, s0, pay = scan_input(own, sib, halo_own, halo_sib, w_x, fixed)
+    xc, bcc, hcol, hrow, s0, pay = scan_input(own, sib, w_x, fixed)
     own, sib, pay = together(own, sib, pay)
     pieces = between_slabs(pay)
     gates = gate(own, sib, w_z)

time: 192 us -> 185 us (0.964)
  between operations: 13.7 us -> 0.37 us
  waiting for transfers between devices: 43.5 us -> 36.1 us
  starting transfers between devices: 43 us -> 50.3 us
  blocking collectives: 30 us -> 32.9 us
  Pallas kernels: 22.3 us -> 24.8 us
    all_to_all x2 -> x1, waiting for transfers between devices: 35.1 us -> 0.01 us  [between_chips(): return lax.all_to_all(value, 'tp', 0, 0, axis_index_groups=same_core)]
    ppermute x0 -> x8, waiting for transfers between devices: none -> 25.8 us  [along_z(): return lax.ppermute(value, 'ctx', pairs)]
    ppermute x0 -> x8, starting transfers between devices: none -> 10.8 us  [along_z(): return lax.ppermute(value, 'ctx', pairs)]
    all_to_all x2 -> x1, starting transfers between devices: 14 us -> 6.65 us  [between_chips(): return lax.all_to_all(value, 'tp', 0, 0, axis_index_groups=same_core)]
    all_to_all x1, blocking collectives: 30 us -> 32.9 us  [between_chips(): return lax.all_to_all(value, 'tp', 0, 0, axis_index_groups=same_core)]
    dynamic_update_slice x0 -> x8, local copies, waits for them, and re-layouts: none -> 2.59 us  [put(): return lax.dynamic_update_slice(held, piece[None], at)]
    ppermute x1, starting transfers between devices: 1.81 us -> 4.37 us  [next_ctx(): return lax.ppermute(value, 'ctx', [(i, i + 1) for i in range(15)])]
    unnamed x64 -> x56, local copies, waits for them, and re-layouts: 20 us -> 17.9 us
  transfers between devices with their start and end apart: 12 -> 17, of which waited for: 5 -> 9; matrix products, arithmetic and copies ran while one was open for 9% -> 8% of each run, Pallas kernels for 10% -> 4%
where the time goes in v7:
time: 185 us; the launch traced here: 183 us
  starting transfers between devices  50.3 us (27%)
  waiting for transfers between devices  36.1 us (20%)
  blocking collectives  32.9 us (18%)
  local copies, waits for them, and re-layouts  29.2 us (16%)
  Pallas kernels  24.8 us (13%)
  other arithmetic  9.7 us (5%)
    all_to_all x1, blocking collectives, between_chips(): return lax.all_to_all(value, 'tp', 0, 0, axis_index_groups=same_core)  32.9 us
    ppermute x8, waiting for transfers between devices, along_z(): return lax.ppermute(value, 'ctx', pairs)  25.8 us
    unnamed x56, local copies, waits for them, and re-layouts  17.9 us
    pallas_call x2, Pallas kernels, over_chips(): pl.pallas_call(kernel, grid=(CHIPS // 2,), in_specs=[spec for _, spec in...  15.9 us
    all_to_all x2, starting transfers between devices, between_slabs(): return lax.all_to_all(value, 'ctx', 0, 0)  13.6 us
    ppermute x8, starting transfers between devices, along_z(): return lax.ppermute(value, 'ctx', pairs)  10.8 us
    ppermute x4, starting transfers between devices, swapped(): return lax.ppermute(value, 'tp', [(i, i ^ bit) for i in range(16)])  10.5 us
    ppermute x4, waiting for transfers between devices, swapped(): return lax.ppermute(value, 'tp', [(i, i ^ bit) for i in range(16)])  8.51 us
  transfers between devices with their start and end apart: 17, of which 9 were waited for; matrix products, arithmetic and copies ran while one was open for 8% of the time, Pallas kernels for 4%

profile of v7, /device:TPU:1, one launch (start us, length us, event | category | flops | bytes accessed | tf_op | source)
XLA Modules:
  0.0 183.4 jit_solution(3904133427104270825)
XLA Ops:
  1.5 4.4 %collective-permute-start = (bf16[16,256]{1,0:T(8,128)(2,1)S(1)}, bf16[16,256]{1,0:T(8,128)(2,1)S(1)}, u32[]{:S(2)}, u32[]{:S(2)}) collective-permute-start(bf16[16,256]{1,0:T(8,128)(2,1)S(1)} %pad_maximum_fusion.5), channel_id=1, source_target_pairs={{0,16},{16,32},{32,48},{48,64},{64,80},{80,96},{96,112},{112,128},... | collective-permute-start | bytes 24584 | tf_op jit(solution)/shard_map/ppermute | solution.py:392
  6.8 1.5 copy.28
  8.3 1.0 pad_maximum_fusion.2
  9.5 1.8 pad_maximum_fusion
  11.4 1.0 collective-permute-start.1
  14.1 4.3 %collective-permute-start.2 = (bf16[1024,128]{1,0:T(8,128)(2,1)}, bf16[1024,128]{1,0:T(8,128)(2,1)}, u32[]{:S(2)}, u32[]{:S(2)}) collective-permute-start(bf16[1024,128]{1,0:T(8,128)(2,1)} %pad_maximum_fusion.3), channel_id=1, source_target_pairs={{0,128},{16,144},{32,160},{48,176},{64,192},{80,208},{96,224},{112... | collective-permute-start | bytes 786440 | tf_op jit(solution)/shard_map/ppermute | solution.py:485
  19.3 6.7 %all-to-all-start = ((bf16[8,800,256]{2,1,0:T(8,128)(2,1)}), bf16[8,800,256]{2,1,0:T(8,128)(2,1)S(1)}, u32[]{:S(2)}, u32[]{:S(2)}) async-start(bf16[8,800,256]{2,1,0:T(8,128)(2,1)} %pad_maximum_fusion), calls=%async_computation | async-start | bytes 6553600 | tf_op jit(solution)/shard_map/all_to_all | solution.py:397
  26.6 1.8 pad_maximum_fusion.1
  28.5 2.7 %collective-permute-start.4 = (bf16[2048,128]{1,0:T(8,128)(2,1)}, bf16[2048,128]{1,0:T(8,128)(2,1)}, u32[]{:S(2)}, u32[]{:S(2)}) collective-permute-start(bf16[2048,128]{1,0:T(8,128)(2,1)} %pad_maximum_fusion.1), channel_id=1, source_target_pairs={{0,112},{16,0},{32,16},{48,32},{64,48},{80,64},{96,80},{112,96},{1... | collective-permute-start | bytes 1572872 | tf_op jit(solution)/shard_map/ppermute | solution.py:402
  31.2 1.9 %compare_convert_fusion = (f32[512]{0:T(512)S(1)}, f32[512]{0:T(512)S(1)}, f32[512]{0:T(512)S(1)}, f32[512]{0:T(512)S(1)}, f32[512]{0:T(512)S(1)}, /*index=5*/f32[512]{0:T(512)S(1)}) fusion(s32[512]{0:T(512)S(1)} %copy-done.25, s32[]{:T(128)} %bitcast.22, s32[]{:T(128)} %bitcast.20, s32[]{:T(128)} %bitcast.18, s32[515]{0:T(1024)S(1)} %pad_add_fusion), kind=kLoop, calls=%fused_computation.29 | loop fusion | flops 6144 | bytes 20492 | tf_op jit(solution)/shard_map/stack | solution.py:443
  34.0 1.7 pad.9.cols
  36.3 1.0 bitcast_dynamic-update-slice_fusion.6
  37.4 5.1 %collective-permute-done.3 = bf16[2048,128]{1,0:T(8,128)(2,1)} collective-permute-done((bf16[2048,128]{1,0:T(8,128)(2,1)}, bf16[2048,128]{1,0:T(8,128)(2,1)}, u32[]{:S(2)}, u32[]{:S(2)}) %collective-permute-start.3) | collective-permute-done | bytes 524320 | tf_op jit(solution)/shard_map/ppermute | solution.py:402
  42.5 2.7 %collective-permute-start.6 = (bf16[2048,128]{1,0:T(8,128)(2,1)}, bf16[2048,128]{1,0:T(8,128)(2,1)S(1)}, u32[]{:S(2)}, u32[]{:S(2)}) collective-permute-start(bf16[2048,128]{1,0:T(8,128)(2,1)} %collective-permute-done.4), channel_id=1, source_target_pairs={{0,112},{16,0},{32,16},{48,32},{64,48},{80,64},{96,80},{112,96},{1... | collective-permute-start | bytes 1572872 | tf_op jit(solution)/shard_map/ppermute | solution.py:402
  45.2 1.1 bitcast_dynamic-update-slice_fusion.5
  46.3 1.1 bitcast_dynamic-update-slice_fusion.4
  47.4 8.1 %collective-permute-done.5 = bf16[2048,128]{1,0:T(8,128)(2,1)S(1)} collective-permute-done((bf16[2048,128]{1,0:T(8,128)(2,1)}, bf16[2048,128]{1,0:T(8,128)(2,1)S(1)}, u32[]{:S(2)}, u32[]{:S(2)}) %collective-permute-start.5) | collective-permute-done | bytes 524320 | tf_op jit(solution)/shard_map/ppermute | solution.py:402
  55.5 2.7 %collective-permute-start.8 = (bf16[2048,128]{1,0:T(8,128)(2,1)S(1)}, bf16[2048,128]{1,0:T(8,128)(2,1)S(1)}, u32[]{:S(2)}, u32[]{:S(2)}) collective-permute-start(bf16[2048,128]{1,0:T(8,128)(2,1)S(1)} %collective-permute-done.6), channel_id=1, source_target_pairs={{0,112},{16,0},{32,16},{48,32},{64,48},{80,64},{96,80},{112,96},{1... | collective-permute-start | bytes 1572872 | tf_op jit(solution)/shard_map/ppermute | solution.py:402
  58.3 9.0 %collective-permute-done.7 = bf16[2048,128]{1,0:T(8,128)(2,1)S(1)} collective-permute-done((bf16[2048,128]{1,0:T(8,128)(2,1)S(1)}, bf16[2048,128]{1,0:T(8,128)(2,1)S(1)}, u32[]{:S(2)}, u32[]{:S(2)}) %collective-permute-start.7) | collective-permute-done | bytes 524320 | tf_op jit(solution)/shard_map/ppermute | solution.py:402
  67.5 2.7 %collective-permute-start.10 = (bf16[1024,128]{1,0:T(8,128)(2,1)S(1)}, bf16[1024,128]{1,0:T(8,128)(2,1)S(1)}, u32[]{:S(2)}, u32[]{:S(2)}) collective-permute-start(bf16[1024,128]{1,0:T(8,128)(2,1)S(1)} %slice.63), channel_id=1, source_target_pairs={{0,112},{16,0},{32,16},{48,32},{64,48},{80,64},{96,80},{112,96},{1... | collective-permute-start | bytes 786440 | tf_op jit(solution)/shard_map/ppermute | solution.py:402
  70.4 3.5 %collective-permute-done.9 = bf16[1024,128]{1,0:T(8,128)(2,1)S(1)} collective-permute-done((bf16[1024,128]{1,0:T(8,128)(2,1)S(1)}, bf16[1024,128]{1,0:T(8,128)(2,1)S(1)}, u32[]{:S(2)}, u32[]{:S(2)}) %collective-permute-start.9) | collective-permute-done | bytes 262176 | tf_op jit(solution)/shard_map/ppermute | solution.py:402
  74.0 2.0 %copy-done.3 = bf16[8,2048,128]{2,1,0:T(8,128)(2,1)} copy-done((bf16[8,2048,128]{2,1,0:T(8,128)(2,1)}, bf16[8,2048,128]{2,1,0:T(8,128)(2,1)S(1)}, u32[]{:S(2)}) %copy-start.3) | copy-done | bytes 4194328
  76.0 4.8 %collective-permute-start.11 = (bf16[8,800,256]{2,1,0:T(8,128)(2,1)S(1)}, bf16[8,800,256]{2,1,0:T(8,128)(2,1)S(1)}, u32[]{:S(2)}, u32[]{:S(2)}) collective-permute-start(bf16[8,800,256]{2,1,0:T(8,128)(2,1)S(1)} %all-to-all-done.own), channel_id=1, source_target_pairs={{0,1},{1,0},{2,3},{3,2},{4,5},{5,4},{6,7},{7,6},{8,9},{9,8},{10,11... | collective-permute-start | bytes 9830408 | tf_op jit(solution)/shard_map/ppermute | solution.py:388
  80.8 5.5 %collective-permute-done.11.sib = bf16[8,800,256]{2,1,0:T(8,128)(2,1)S(1)} collective-permute-done((bf16[8,800,256]{2,1,0:T(8,128)(2,1)S(1)}, bf16[8,800,256]{2,1,0:T(8,128)(2,1)S(1)}, u32[]{:S(2)}, u32[]{:S(2)}) %collective-permute-start.11) | collective-permute-done | bytes 3276832 | tf_op jit(solution)/shard_map/ppermute | solution.py:388
  86.3 0.9 copy-done.11
  87.3 2.2 %copy-done.14 = bf16[4096,512]{1,0:T(8,128)(2,1)S(1)} copy-done((bf16[4096,512]{1,0:T(8,128)(2,1)S(1)}, bf16[4096,512]{1,0:T(8,128)(2,1)}, u32[]{:S(2)}) %copy-start.14) | copy-done | bytes 4194328
  89.4 11.0 %scan_input.1 = (bf16[512,512]{1,0:T(8,128)(2,1)}, bf16[512,256]{1,0:T(8,128)(2,1)}, f32[512,128]{1,0:T(8,128)}, f32[16,512]{1,0:T(8,128)}, bf16[128,512]{1,0:T(8,128)(2,1)}, /*index=5*/bf16[16,16,512]{2,1,0:T(8,128)(2,1)}) custom-call(bf16[8,800,256]{2,1,0:T(8,128)(2,1)S(1)} %all-to-all-done.own, bf16[8,800,256]{2,1,0:T(8,128)(2,1)S(1)} %collective-permute-done.11.sib, ...), custom_call_target="tpu_custom_call" | custom-call | flops 3391094784 | bytes 8388608 | tf_op jit(solution)/shard_map/scan_input/pallas_call | solution.py:198
  100.5 6.1 %all-to-all-start.1 = ((bf16[16,16,512]{2,1,0:T(8,128)(2,1)}), bf16[16,16,512]{2,1,0:T(8,128)(2,1)}, u32[]{:S(2)}, u32[]{:S(2)}) async-start(bf16[16,16,512]{2,1,0:T(8,128)(2,1)} %get-tuple-element.42), calls=%async_computation.1 | async-start | bytes 524288 | tf_op jit(solution)/shard_map/all_to_all | solution.py:425
  106.7 2.2 %copy-done.1 = bf16[4096,512]{1,0:T(8,128)(2,1)S(1)} copy-done((bf16[4096,512]{1,0:T(8,128)(2,1)S(1)}, bf16[4096,512]{1,0:T(8,128)(2,1)}, u32[]{:S(2)}) %copy-start.1) | copy-done | bytes 4194328
  108.8 1.9 %copy-done.6 = bf16[8,800,256]{2,1,0:T(8,128)(2,1)S(1)} copy-done((bf16[8,800,256]{2,1,0:T(8,128)(2,1)S(1)}, bf16[8,800,256]{2,1,0:T(8,128)(2,1)}, u32[]{:S(2)}) %copy-start.6) | copy-done | bytes 3276824
  110.8 4.9 %gate.1.gates = f32[512,512]{1,0:T(8,128)} custom-call(bf16[8,800,256]{2,1,0:T(8,128)(2,1)S(1)} %all-to-all-done.own, bf16[8,800,256]{2,1,0:T(8,128)(2,1)S(1)} %copy-done.6, bf16[4096,512]{1,0:T(8,128)(2,1)S(1)} %copy-done.1), custom_call_target="tpu_custom_call" | custom-call | flops 2147483648 | bytes 8388608 | tf_op jit(solution)/shard_map/gate/pallas_call | solution.py:198
  115.6 1.7 prefix.1
  117.4 7.5 %all-to-all-start.2 = ((bf16[16,8,512]{2,1,0:T(8,128)(2,1)}), bf16[16,8,512]{2,1,0:T(8,128)(2,1)S(1)}, u32[]{:S(2)}, u32[]{:S(2)}) async-start(bf16[16,8,512]{2,1,0:T(8,128)(2,1)} %bitcast.29), calls=%async_computation.2 | async-start | bytes 262144 | tf_op jit(solution)/shard_map/all_to_all | solution.py:425
  125.9 0.9 copy-done.9
  126.8 0.9 copy-done.12
  127.8 1.0 copy-done.19
  128.8 1.8 intra.1.y
  130.6 1.8 all-to-all-done.2
  132.4 0.9 copy-done.8
  133.4 0.9 copy-done.10
  134.3 1.3 join.1.own
  135.6 2.4 %collective-permute-start.12 = (bf16[512,640]{1,0:T(8,128)(2,1)S(1)}, bf16[512,640]{1,0:T(8,128)(2,1)S(1)}, u32[]{:S(2)}, u32[]{:S(2)}) collective-permute-start(bf16[512,640]{1,0:T(8,128)(2,1)S(1)} %join.1.own), channel_id=1, source_target_pairs={{0,1},{1,0},{2,3},{3,2},{4,5},{5,4},{6,7},{7,6},{8,9},{9,8},{10,11... | collective-permute-start | bytes 1966088 | tf_op jit(solution)/shard_map/ppermute | solution.py:388
  138.0 1.7 collective-permute-done.12.sib
  139.7 2.2 %copy-done.4 = bf16[8,2048,128]{2,1,0:T(8,128)(2,1)S(1)} copy-done((bf16[8,2048,128]{2,1,0:T(8,128)(2,1)S(1)}, bf16[8,2048,128]{2,1,0:T(8,128)(2,1)}, u32[]{:S(2)}) %copy-start.4) | copy-done | bytes 4194328
  141.9 4.1 %project.1 = bf16[8,512,256]{2,1,0:T(8,128)(2,1)S(1)} custom-call(s32[1]{0:T(128)} %bitcast.place, bf16[512,640]{1,0:T(8,128)(2,1)S(1)} %join.1.own, bf16[512,640]{1,0:T(8,128)(2,1)S(1)} %collective-permute-done.12.sib, bf16[8,2048,128]{2,1,0:T(8,128)(2,1)S(1)} %copy-done.4), custom_call_target="tpu_custom_call" | custom-call | flops 4294967296 | bytes 8388608 | tf_op jit(solution)/shard_map/project/pallas_call | solution.py:370
  146.0 32.9 %all_to_all.20 = bf16[8,512,256]{2,1,0:T(8,128)(2,1)S(1)} all-to-all(bf16[8,512,256]{2,1,0:T(8,128)(2,1)S(1)} %project.1), channel_id=1, replica_groups={{0,2,4,6,8,10,12,14},{1,3,5,7,9,11,13,15},{16,18,20,22,24,26,28,30},{17..., dimensions={0} | all-to-all | bytes 4194304 | tf_op jit(solution)/shard_map/all_to_all | solution.py:397
  179.3 2.3 %collective-permute-start.13 = (bf16[512,128]{1,0:T(8,128)(2,1)S(1)}, bf16[512,128]{1,0:T(8,128)(2,1)S(1)}, u32[]{:S(2)}, u32[]{:S(2)}) collective-permute-start(bf16[512,128]{1,0:T(8,128)(2,1)S(1)} %broadcast_select_fusion.2), channel_id=1, source_target_pairs={{0,1},{1,0},{2,3},{3,2},{4,5},{5,4},{6,7},{7,6},{8,9},{9,8},{10,11... | collective-permute-start | bytes 393224 | tf_op jit(solution)/shard_map/ppermute | solution.py:388
  181.6 1.0 collective-permute-done.13
  (92 shorter events, 10.2 us)
Async XLA Ops:
  0.0 18.4 %copy-start = (f32[4,2048]{1,0:T(4,128)S(1)}, f32[4,2048]{1,0:T(4,128)}, u32[]{:S(2)}) copy-start(f32[4,2048]{1,0:T(4,128)} %param.23) | copy-start | bytes 98308
  1.5 6.8 %collective-permute-start = (bf16[16,256]{1,0:T(8,128)(2,1)S(1)}, bf16[16,256]{1,0:T(8,128)(2,1)S(1)}, u32[]{:S(2)}, u32[]{:S(2)}) collective-permute-start(bf16[16,256]{1,0:T(8,128)(2,1)S(1)} %pad_maximum_fusion.5), channel_id=1, source_target_pairs={{0,16},{16,32},{32,48},{48,64},{64,80},{80,96},{96,112},{112,128},... | collective-permute-start | bytes 24584 | tf_op jit(solution)/shard_map/ppermute | solution.py:392
  9.3 2.0 %copy-start.24 = (bf16[512,256]{1,0:T(8,128)(2,1)S(1)}, bf16[512,256]{1,0:T(8,128)(2,1)}, u32[]{:S(2)}) copy-start(bf16[512,256]{1,0:T(8,128)(2,1)} %param.29) | copy-start | bytes 786436
  9.3 3.1 %copy-start.25 = (s32[512]{0:T(512)S(1)}, s32[512]{0:T(512)}, u32[]{:S(2)}) copy-start(s32[512]{0:T(512)} %param.16) | copy-start | bytes 6148
  9.5 9.7 %copy-start.26 = (f32[8]{0:T(128)S(1)}, f32[8]{0:T(128)}, u32[]{:S(2)}) copy-start(f32[8]{0:T(128)} %param.27) | copy-start | bytes 100
  11.4 2.0 %collective-permute-start.1 = (bf16[512,128]{1,0:T(8,128)(2,1)S(1)}, bf16[512,128]{1,0:T(8,128)(2,1)S(1)}, u32[]{:S(2)}, u32[]{:S(2)}) collective-permute-start(bf16[512,128]{1,0:T(8,128)(2,1)S(1)} %get-tuple-element.60), channel_id=1, source_target_pairs={{0,1},{1,0},{2,3},{3,2},{4,5},{5,4},{6,7},{7,6},{8,9},{9,8},{10,11... | collective-permute-start | bytes 393224 | tf_op jit(solution)/shard_map/ppermute | solution.py:388
  13.4 5.0 %copy-start.22 = (bf16[512,128]{1,0:T(8,128)(2,1)}, bf16[512,128]{1,0:T(8,128)(2,1)S(1)}, u32[]{:S(2)}) copy-start(bf16[512,128]{1,0:T(8,128)(2,1)S(1)} %collective-permute-done.1) | copy-start | bytes 393220
  14.1 12.5 %collective-permute-start.2 = (bf16[1024,128]{1,0:T(8,128)(2,1)}, bf16[1024,128]{1,0:T(8,128)(2,1)}, u32[]{:S(2)}, u32[]{:S(2)}) collective-permute-start(bf16[1024,128]{1,0:T(8,128)(2,1)} %pad_maximum_fusion.3), channel_id=1, source_target_pairs={{0,128},{16,144},{32,160},{48,176},{64,192},{80,208},{96,224},{112... | collective-permute-start | bytes 786440 | tf_op jit(solution)/shard_map/ppermute | solution.py:485
  19.3 56.7 %all-to-all-start = ((bf16[8,800,256]{2,1,0:T(8,128)(2,1)}), bf16[8,800,256]{2,1,0:T(8,128)(2,1)S(1)}, u32[]{:S(2)}, u32[]{:S(2)}) async-start(bf16[8,800,256]{2,1,0:T(8,128)(2,1)} %pad_maximum_fusion), calls=%async_computation | async-start | bytes 6553600 | tf_op jit(solution)/shard_map/all_to_all | solution.py:397
  28.5 14.0 %collective-permute-start.3 = (bf16[2048,128]{1,0:T(8,128)(2,1)}, bf16[2048,128]{1,0:T(8,128)(2,1)}, u32[]{:S(2)}, u32[]{:S(2)}) collective-permute-start(bf16[2048,128]{1,0:T(8,128)(2,1)} %pad_maximum_fusion.1), channel_id=1, source_target_pairs={{0,16},{16,32},{32,48},{48,64},{64,80},{80,96},{96,112},{112,0},{1... | collective-permute-start | bytes 1572872 | tf_op jit(solution)/shard_map/ppermute | solution.py:402
  28.5 14.0 %collective-permute-start.4 = (bf16[2048,128]{1,0:T(8,128)(2,1)}, bf16[2048,128]{1,0:T(8,128)(2,1)}, u32[]{:S(2)}, u32[]{:S(2)}) collective-permute-start(bf16[2048,128]{1,0:T(8,128)(2,1)} %pad_maximum_fusion.1), channel_id=1, source_target_pairs={{0,112},{16,0},{32,16},{48,32},{64,48},{80,64},{96,80},{112,96},{1... | collective-permute-start | bytes 1572872 | tf_op jit(solution)/shard_map/ppermute | solution.py:402
  34.0 2.3 %copy-start.23 = (bf16[512,128]{1,0:T(8,128)(2,1)S(1)}, bf16[512,128]{1,0:T(8,128)(2,1)}, u32[]{:S(2)}) copy-start(bf16[512,128]{1,0:T(8,128)(2,1)} %copy-done.22) | copy-start | bytes 393220
  37.3 49.0 %copy-start.15 = (f32[4,512]{1,0:T(4,128)S(1)}, f32[4,512]{1,0:T(4,128)}, u32[]{:S(2)}) copy-start(f32[4,512]{1,0:T(4,128)} %taps_x) | copy-start | bytes 24580
  37.3 48.9 %copy-start.16 = (f32[512]{0:T(512)S(1)}, f32[512]{0:T(512)}, u32[]{:S(2)}) copy-start(f32[512]{0:T(512)} %param.22) | copy-start | bytes 6148
  37.4 48.9 %copy-start.17 = (f32[8]{0:T(128)S(1)}, f32[8]{0:T(128)}, u32[]{:S(2)}) copy-start(f32[8]{0:T(128)} %param.25) | copy-start | bytes 100
  37.4 48.9 %copy-start.18 = (f32[8]{0:T(128)S(1)}, f32[8]{0:T(128)}, u32[]{:S(2)}) copy-start(f32[8]{0:T(128)} %param.26) | copy-start | bytes 100
  42.5 13.0 %collective-permute-start.5 = (bf16[2048,128]{1,0:T(8,128)(2,1)}, bf16[2048,128]{1,0:T(8,128)(2,1)S(1)}, u32[]{:S(2)}, u32[]{:S(2)}) collective-permute-start(bf16[2048,128]{1,0:T(8,128)(2,1)} %collective-permute-done.3), channel_id=1, source_target_pairs={{0,16},{16,32},{32,48},{48,64},{64,80},{80,96},{96,112},{112,0},{1... | collective-permute-start | bytes 1572872 | tf_op jit(solution)/shard_map/ppermute | solution.py:402
  42.5 13.0 %collective-permute-start.6 = (bf16[2048,128]{1,0:T(8,128)(2,1)}, bf16[2048,128]{1,0:T(8,128)(2,1)S(1)}, u32[]{:S(2)}, u32[]{:S(2)}) collective-permute-start(bf16[2048,128]{1,0:T(8,128)(2,1)} %collective-permute-done.4), channel_id=1, source_target_pairs={{0,112},{16,0},{32,16},{48,32},{64,48},{80,64},{96,80},{112,96},{1... | collective-permute-start | bytes 1572872 | tf_op jit(solution)/shard_map/ppermute | solution.py:402
  55.5 11.9 %collective-permute-start.7 = (bf16[2048,128]{1,0:T(8,128)(2,1)S(1)}, bf16[2048,128]{1,0:T(8,128)(2,1)S(1)}, u32[]{:S(2)}, u32[]{:S(2)}) collective-permute-start(bf16[2048,128]{1,0:T(8,128)(2,1)S(1)} %collective-permute-done.5), channel_id=1, source_target_pairs={{0,16},{16,32},{32,48},{48,64},{64,80},{80,96},{96,112},{112,0},{1... | collective-permute-start | bytes 1572872 | tf_op jit(solution)/shard_map/ppermute | solution.py:402
  55.5 12.0 %collective-permute-start.8 = (bf16[2048,128]{1,0:T(8,128)(2,1)S(1)}, bf16[2048,128]{1,0:T(8,128)(2,1)S(1)}, u32[]{:S(2)}, u32[]{:S(2)}) collective-permute-start(bf16[2048,128]{1,0:T(8,128)(2,1)S(1)} %collective-permute-done.6), channel_id=1, source_target_pairs={{0,112},{16,0},{32,16},{48,32},{64,48},{80,64},{96,80},{112,96},{1... | collective-permute-start | bytes 1572872 | tf_op jit(solution)/shard_map/ppermute | solution.py:402
  67.4 6.5 %collective-permute-start.9 = (bf16[1024,128]{1,0:T(8,128)(2,1)S(1)}, bf16[1024,128]{1,0:T(8,128)(2,1)S(1)}, u32[]{:S(2)}, u32[]{:S(2)}) collective-permute-start(bf16[1024,128]{1,0:T(8,128)(2,1)S(1)} %slice.62), channel_id=1, source_target_pairs={{0,16},{16,32},{32,48},{48,64},{64,80},{80,96},{96,112},{112,0},{1... | collective-permute-start | bytes 786440 | tf_op jit(solution)/shard_map/ppermute | solution.py:402
  67.5 6.4 %collective-permute-start.10 = (bf16[1024,128]{1,0:T(8,128)(2,1)S(1)}, bf16[1024,128]{1,0:T(8,128)(2,1)S(1)}, u32[]{:S(2)}, u32[]{:S(2)}) collective-permute-start(bf16[1024,128]{1,0:T(8,128)(2,1)S(1)} %slice.63), channel_id=1, source_target_pairs={{0,112},{16,0},{32,16},{48,32},{64,48},{80,64},{96,80},{112,96},{1... | collective-permute-start | bytes 786440 | tf_op jit(solution)/shard_map/ppermute | solution.py:402
  74.0 2.0 %copy-start.3 = (bf16[8,2048,128]{2,1,0:T(8,128)(2,1)}, bf16[8,2048,128]{2,1,0:T(8,128)(2,1)S(1)}, u32[]{:S(2)}) copy-start(bf16[8,2048,128]{2,1,0:T(8,128)(2,1)S(1)} %bitcast_dynamic-update-slice_fusion.7.w) | copy-start | bytes 12582916
  76.0 10.3 %collective-permute-start.11 = (bf16[8,800,256]{2,1,0:T(8,128)(2,1)S(1)}, bf16[8,800,256]{2,1,0:T(8,128)(2,1)S(1)}, u32[]{:S(2)}, u32[]{:S(2)}) collective-permute-start(bf16[8,800,256]{2,1,0:T(8,128)(2,1)S(1)} %all-to-all-done.own), channel_id=1, source_target_pairs={{0,1},{1,0},{2,3},{3,2},{4,5},{5,4},{6,7},{7,6},{8,9},{9,8},{10,11... | collective-permute-start | bytes 9830408 | tf_op jit(solution)/shard_map/ppermute | solution.py:388
  86.3 1.0 copy-start.11
  87.3 2.2 %copy-start.14 = (bf16[4096,512]{1,0:T(8,128)(2,1)S(1)}, bf16[4096,512]{1,0:T(8,128)(2,1)}, u32[]{:S(2)}) copy-start(bf16[4096,512]{1,0:T(8,128)(2,1)} %w_x.1) | copy-start | bytes 12582916
  89.4 11.1 %copy-start.5 = (bf16[8,800,256]{2,1,0:T(8,128)(2,1)}, bf16[8,800,256]{2,1,0:T(8,128)(2,1)S(1)}, u32[]{:S(2)}) copy-start(bf16[8,800,256]{2,1,0:T(8,128)(2,1)S(1)} %collective-permute-done.11.sib) | copy-start | bytes 9830404
  100.5 15.1 %all-to-all-start.1 = ((bf16[16,16,512]{2,1,0:T(8,128)(2,1)}), bf16[16,16,512]{2,1,0:T(8,128)(2,1)}, u32[]{:S(2)}, u32[]{:S(2)}) async-start(bf16[16,16,512]{2,1,0:T(8,128)(2,1)} %get-tuple-element.42), calls=%async_computation.1 | async-start | bytes 524288 | tf_op jit(solution)/shard_map/all_to_all | solution.py:425
  106.6 2.2 %copy-start.1 = (bf16[4096,512]{1,0:T(8,128)(2,1)S(1)}, bf16[4096,512]{1,0:T(8,128)(2,1)}, u32[]{:S(2)}) copy-start(bf16[4096,512]{1,0:T(8,128)(2,1)} %w_z.1) | copy-start | bytes 12582916
  108.8 1.9 %copy-start.6 = (bf16[8,800,256]{2,1,0:T(8,128)(2,1)S(1)}, bf16[8,800,256]{2,1,0:T(8,128)(2,1)}, u32[]{:S(2)}) copy-start(bf16[8,800,256]{2,1,0:T(8,128)(2,1)} %copy-done.5) | copy-start | bytes 9830404
  110.8 14.1 %copy-start.20 = (bf16[128,512]{1,0:T(8,128)(2,1)S(1)}, bf16[128,512]{1,0:T(8,128)(2,1)}, u32[]{:S(2)}) copy-start(bf16[128,512]{1,0:T(8,128)(2,1)} %get-tuple-element.51.s0) | copy-start | bytes 393220
  110.8 14.1 %copy-start.21 = (f32[16,512]{1,0:T(8,128)S(1)}, f32[16,512]{1,0:T(8,128)}, u32[]{:S(2)}) copy-start(f32[16,512]{1,0:T(8,128)} %get-tuple-element.50.hrow) | copy-start | bytes 98308
  110.8 21.6 %copy-start.13 = (f32[512]{0:T(512)S(1)}, f32[512]{0:T(512)}, u32[]{:S(2)}) copy-start(f32[512]{0:T(512)} %param.28) | copy-start | bytes 6148
  115.6 16.8 %copy-start.2 = (f32[512,512]{1,0:T(8,128)S(1)}, f32[512,512]{1,0:T(8,128)}, u32[]{:S(2)}) copy-start(f32[512,512]{1,0:T(8,128)} %gate.1.gates) | copy-start | bytes 3145732
  117.4 15.0 %all-to-all-start.2 = ((bf16[16,8,512]{2,1,0:T(8,128)(2,1)}), bf16[16,8,512]{2,1,0:T(8,128)(2,1)S(1)}, u32[]{:S(2)}, u32[]{:S(2)}) async-start(bf16[16,8,512]{2,1,0:T(8,128)(2,1)} %bitcast.29), calls=%async_computation.2 | async-start | bytes 262144 | tf_op jit(solution)/shard_map/all_to_all | solution.py:425
  124.9 1.0 copy-start.7
  125.9 0.9 copy-start.9
  126.8 0.9 copy-start.12
  127.8 1.0 copy-start.19
  132.4 1.0 copy-start.8
  133.4 0.9 copy-start.10
  135.6 4.1 %collective-permute-start.12 = (bf16[512,640]{1,0:T(8,128)(2,1)S(1)}, bf16[512,640]{1,0:T(8,128)(2,1)S(1)}, u32[]{:S(2)}, u32[]{:S(2)}) collective-permute-start(bf16[512,640]{1,0:T(8,128)(2,1)S(1)} %join.1.own), channel_id=1, source_target_pairs={{0,1},{1,0},{2,3},{3,2},{4,5},{5,4},{6,7},{7,6},{8,9},{9,8},{10,11... | collective-permute-start | bytes 1966088 | tf_op jit(solution)/shard_map/ppermute | solution.py:388
  139.7 2.2 %copy-start.4 = (bf16[8,2048,128]{2,1,0:T(8,128)(2,1)S(1)}, bf16[8,2048,128]{2,1,0:T(8,128)(2,1)}, u32[]{:S(2)}) copy-start(bf16[8,2048,128]{2,1,0:T(8,128)(2,1)} %copy-done.3) | copy-start | bytes 12582916
  179.3 3.3 %collective-permute-start.13 = (bf16[512,128]{1,0:T(8,128)(2,1)S(1)}, bf16[512,128]{1,0:T(8,128)(2,1)S(1)}, u32[]{:S(2)}, u32[]{:S(2)}) collective-permute-start(bf16[512,128]{1,0:T(8,128)(2,1)S(1)} %broadcast_select_fusion.2), channel_id=1, source_target_pairs={{0,1},{1,0},{2,3},{3,2},{4,5},{5,4},{6,7},{7,6},{8,9},{9,8},{10,11... | collective-permute-start | bytes 393224 | tf_op jit(solution)/shard_map/ppermute | solution.py:388
  182.7 0.7 copy-start.27

commit v8 on v7

--- a/solution.py
+++ b/solution.py
@@ -258,7 +258,9 @@
     return over_chips(gate_kernel, blocked, [], shapes, scratch, 16, flops, "gate")[0]
 
 
-def intra_kernel(xc, bcc, hcol, hrow, s0, cols, seg_row, skip, y):
+def intra_kernel(xc, bcc, hcol, hrow, s0, cols, seg_row, skip, y, c_out, decays):
+    c_out[...] = bcc[:, N:]
+    decays[...] = hcol[...]
     for block in range(2):
         intra_block(block * L, xc, bcc, hcol, hrow, s0, cols, seg_row, skip, y)
 
@@ -291,11 +293,12 @@
 
 
 def intra(*args):
+    shapes = [((ROWS, CH), F32), ((ROWS, N), BF16), ((ROWS, 128), F32)]
     return pl.pallas_call(
         intra_kernel,
         in_specs=[VMEM] * len(args),
-        out_specs=VMEM,
-        out_shape=jax.ShapeDtypeStruct((ROWS, CH), F32),
+        out_specs=[VMEM] * len(shapes),
+        out_shape=[jax.ShapeDtypeStruct(*shape) for shape in shapes],
         compiler_params=params(12),
         cost_estimate=pl.CostEstimate(
             flops=2 * ROWS * L * CH * 4, bytes_accessed=4 * 2**20, transcendentals=2 * 10**6
@@ -326,9 +329,9 @@
     )(pieces)
 
 
-def join_kernel(y, gates, bcc, hcol, state, gain, out):
+def join_kernel(y, gates, cc, hcol, state, gain, out):
     for at in range(0, ROWS, 128):
-        c_vals = bcc[at : at + 128, N:]
+        c_vals = cc[at : at + 128, :]
         carried = spread(hcol[at : at + 128, 2 * HEADS : 3 * HEADS])
         total = y[at : at + 128, :] + carried * dot(c_vals, state[...])
         gated = total * gates[at : at + 128, :]
@@ -353,27 +356,40 @@
     )(*args)
 
 
-def project_kernel(place, own, sib, w, out):
+def project_kernel(place, own, sib, near, far, out):
     del place
     square = own[:, CH:].astype(F32) + sib[:, CH:].astype(F32)
     scale = lax.rsqrt((square[:, 0:1] + square[:, 64:65]) / (2.0 * CH) + NORM_EPS)
     values = jnp.concatenate([own[:, :CH], sib[:, :CH]], axis=1)
-    rows = jnp.concatenate([w[0], w[1]], axis=1)
-    out[0] = (dot(values, rows) * scale).astype(BF16)
-
-
-def project(own, sib, w_all, y_low):
-    def columns(chip, place):
-        return lax.rem(chip, 4), lax.rem(lax.div(chip, 4) + place[0], 2), 0
-
+    is_near = pl.program_id(0) < CHIPS // 2
+    for wanted, ref in ((is_near, near), (jnp.logical_not(is_near), far)):
+
+        @pl.when(wanted)
+        def _():
+            rows = jnp.concatenate([ref[0], ref[1]], axis=1)
+            out[0] = (dot(values, rows) * scale).astype(BF16)
+
+
+def project(own, sib, near, far, y_low):
+    half = CHIPS // 2
     whole = pl.BlockSpec(own.shape, lambda i, place: (0, 0))
+    columns = lambda at: pl.BlockSpec((2, 2 * CH, 128), at)
+
+    def sent(i, place):
+        return lax.rem(i, half) + half * lax.rem(lax.div(i, half) + place[0], 2), 0, 0
+
     return pl.pallas_call(
         project_kernel,
         grid_spec=pltpu.PrefetchScalarGridSpec(
             num_scalar_prefetch=1,
             grid=(CHIPS,),
-            in_specs=[whole, whole, pl.BlockSpec((2, 2 * CH, 128), columns)],
-            out_specs=pl.BlockSpec((1, ROWS, 256), lambda i, place: (i, 0, 0)),
+            in_specs=[
+                whole,
+                whole,
+                columns(lambda i, place: (jnp.minimum(i, half - 1), 0, 0)),
+                columns(lambda i, place: (jnp.maximum(i - half, 0), 0, 0)),
+            ],
+            out_specs=pl.BlockSpec((1, ROWS, 256), sent),
         ),
         out_shape=jax.ShapeDtypeStruct((CHIPS, ROWS, 256), BF16),
         compiler_params=params(14, True),
@@ -381,7 +397,7 @@
             flops=8 * ROWS * CH * 2048, bytes_accessed=8 * 2**20, transcendentals=0
         ),
         name="project",
-    )(y_low[None], own, sib, w_all)
+    )(y_low[None], own, sib, near, far)
 
 
 def swapped(value, bit):
@@ -482,15 +498,15 @@
     w_pair = jnp.concatenate(
         [pick(core, *halves), swapped(pick(core, halves[1], halves[0]), 1)], axis=0
     )
-    w_far = lax.ppermute(w_pair, "ctx", [(i, i ^ Z_RING) for i in range(2 * Z_RING)])
-    w_all = gathered_along_z(jnp.concatenate([w_pair, w_far], axis=0))
+    w_near = gathered_along_z(w_pair)
 
     cols, seg_row = document_columns(seg_ids, ids_prior)
     taps_bc = lax.dynamic_slice_in_dim(conv_bc, chip * 2 * N, 2 * N, 1)
     bias_bc = lax.dynamic_slice_in_dim(conv_bc_bias, chip * 2 * N, 2 * N, 0)[None]
     skip = jnp.repeat(skip_gain, P_SIZE)[None]
     fixed = [cols, conv_x, conv_x_bias[None], taps_bc, bias_bc, dt_bias[None], decay_rate[None]]
-    own, w_all, fixed, seg_row, skip = together(own, w_all, fixed, seg_row, skip)
+    own, w_near, fixed, seg_row, skip = together(own, w_near, fixed, seg_row, skip)
+    w_far = lax.ppermute(w_near, "ctx", [(i, i ^ Z_RING) for i in range(2 * Z_RING)])
     sib = swapped(own, 1)
     xc, bcc, hcol, hrow, s0, pay = scan_input(own, sib, w_x, fixed)
     own, sib, pay = together(own, sib, pay)
@@ -498,9 +514,9 @@
     gates = gate(own, sib, w_z)
     pieces, gates, xc, bcc = together(pieces, gates, xc, bcc)
     state = between_slabs(prefix(pieces).reshape(CTX, 8, CH)).reshape(N, CH)
-    y = intra(xc, bcc, hcol, hrow, s0, fixed[0], seg_row, skip)
-    mine = join(y, gates, bcc, hcol, state, norm_weight[None])
-    parts = between_chips(project(mine, swapped(mine, 1), w_all, y_low))
+    y, cc, decays = intra(xc, bcc, hcol, hrow, s0, fixed[0], seg_row, skip)
+    mine = join(y, gates, cc, decays, state, norm_weight[None])
+    parts = between_chips(project(mine, swapped(mine, 1), w_near, w_far, y_low))
     total = jnp.sum(parts.astype(F32), axis=0).astype(BF16)
     parts = (total[:, :128], total[:, 128:])
     kept = pick(core, *parts)

time: 185 us -> 185 us (level)
  starting transfers between devices: 50.3 us -> 46.3 us
  Pallas kernels: 24.8 us -> 28.4 us
  waiting for transfers between devices: 36.1 us -> 39.3 us
  blocking collectives: 32.9 us -> 30.5 us
    ppermute x8, waiting for transfers between devices: 25.8 us -> 7.15 us  [along_z(): return lax.ppermute(value, 'ctx', pairs)]
    all_to_all x2, waiting for transfers between devices: 1.83 us -> 16 us  [between_slabs(): return lax.all_to_all(value, 'ctx', 0, 0)]
    all_to_all x1, waiting for transfers between devices: 0.01 us -> 8.13 us  [between_chips(): return lax.all_to_all(value, 'tp', 0, 0, axis_index_groups=same_core)]
    unnamed x56 -> x48, local copies, waits for them, and re-layouts: 17.9 us -> 12.5 us
    dynamic_update_slice x8, local copies, waits for them, and re-layouts: 2.59 us -> 7.53 us  [put(): return lax.dynamic_update_slice(held, piece[None], at)]
    ppermute x1, starting transfers between devices: 4.28 us -> 0.4 us  [local(): lax.ppermute(w_near, 'ctx', [(i, i ^ Z_RING) for i in range(2 * Z_RING)])]
    pallas_call x1, Pallas kernels: 4.07 us -> 7.76 us  [project(): pl.pallas_call(project_kernel, grid_spec=pltpu.PrefetchScalarGridSpec(num...]
    ppermute x4, starting transfers between devices: 10.5 us -> 7.62 us  [swapped(): return lax.ppermute(value, 'tp', [(i, i ^ bit) for i in range(16)])]
  transfers between devices with their start and end apart: 17 -> 17, of which waited for: 9 -> 10; matrix products, arithmetic and copies ran while one was open for 8% -> 12% of each run, Pallas kernels for 4% -> 11%
where the time goes in v8:
time: 185 us; the launch traced here: 184 us
  starting transfers between devices  46.3 us (25%)
  waiting for transfers between devices  39.3 us (21%)
  local copies, waits for them, and re-layouts  30.6 us (17%)
  blocking collectives  30.5 us (16%)
  Pallas kernels  28.4 us (15%)
  other arithmetic  8.31 us (4%)
    all_to_all x1, blocking collectives, between_chips(): return lax.all_to_all(value, 'tp', 0, 0, axis_index_groups=same_core)  30.5 us
    all_to_all x2, waiting for transfers between devices, between_slabs(): return lax.all_to_all(value, 'ctx', 0, 0)  16 us
    pallas_call x2, Pallas kernels, over_chips(): pl.pallas_call(kernel, grid=(CHIPS // 2,), in_specs=[spec for _, spec in...  15.9 us
    all_to_all x2, starting transfers between devices, between_slabs(): return lax.all_to_all(value, 'ctx', 0, 0)  15.2 us
    unnamed x48, local copies, waits for them, and re-layouts  12.5 us
    ppermute x8, starting transfers between devices, along_z(): return lax.ppermute(value, 'ctx', pairs)  11.9 us
    all_to_all x1, waiting for transfers between devices, between_chips(): return lax.all_to_all(value, 'tp', 0, 0, axis_index_groups=same_core)  8.13 us
    ppermute x4, waiting for transfers between devices, swapped(): return lax.ppermute(value, 'tp', [(i, i ^ bit) for i in range(16)])  8.06 us
  transfers between devices with their start and end apart: 17, of which 10 were waited for; matrix products, arithmetic and copies ran while one was open for 12% of the time, Pallas kernels for 11%

profile of v8, /device:TPU:1, one launch (start us, length us, event | category | flops | bytes accessed | tf_op | source)
XLA Modules:
  0.0 183.7 jit_solution(7113299321791392860)
XLA Ops:
  1.6 4.4 %collective-permute-start = (bf16[16,256]{1,0:T(8,128)(2,1)S(1)}, bf16[16,256]{1,0:T(8,128)(2,1)S(1)}, u32[]{:S(2)}, u32[]{:S(2)}) collective-permute-start(bf16[16,256]{1,0:T(8,128)(2,1)S(1)} %pad_maximum_fusion.4), channel_id=1, source_target_pairs={{0,16},{16,32},{32,48},{48,64},{64,80},{80,96},{96,112},{112,128},... | collective-permute-start | bytes 24584 | tf_op jit(solution)/shard_map/ppermute | solution.py:408
  5.9 1.4 fusion.5
  8.1 0.9 copy.29
  9.0 1.5 copy.28
  11.6 1.8 pad_maximum_fusion
  13.4 6.8 %all-to-all-start = ((bf16[8,800,256]{2,1,0:T(8,128)(2,1)}), bf16[8,800,256]{2,1,0:T(8,128)(2,1)S(1)}, u32[]{:S(2)}, u32[]{:S(2)}) async-start(bf16[8,800,256]{2,1,0:T(8,128)(2,1)} %pad_maximum_fusion), calls=%async_computation | async-start | bytes 6553600 | tf_op jit(solution)/shard_map/all_to_all | solution.py:413
  20.2 1.0 broadcast_select_fusion.5
  21.2 1.3 collective-permute-start.1
  24.8 1.6 collective-permute-start.2
  26.5 2.0 %collective-permute-start.3 = (bf16[1024,128]{1,0:T(8,128)(2,1)}, bf16[1024,128]{1,0:T(8,128)(2,1)}, u32[]{:S(2)}, u32[]{:S(2)}) collective-permute-start(bf16[1024,128]{1,0:T(8,128)(2,1)} %pad_maximum_fusion.2), channel_id=1, source_target_pairs={{0,112},{16,0},{32,16},{48,32},{64,48},{80,64},{96,80},{112,96},{1... | collective-permute-start | bytes 786440 | tf_op jit(solution)/shard_map/ppermute | solution.py:418
  28.5 2.0 %compare_convert_fusion = (f32[512]{0:T(512)S(1)}, f32[512]{0:T(512)S(1)}, f32[512]{0:T(512)S(1)}, f32[512]{0:T(512)S(1)}, f32[512]{0:T(512)S(1)}, /*index=5*/f32[512]{0:T(512)S(1)}) fusion(s32[512]{0:T(512)S(1)} %copy-done.21, s32[]{:T(128)} %bitcast.22, s32[]{:T(128)} %bitcast.20, s32[]{:T(128)} %bitcast.18, s32[515]{0:T(1024)S(1)} %pad_add_fusion), kind=kLoop, calls=%fused_computation.28 | loop fusion | flops 6144 | bytes 20492 | tf_op jit(solution)/shard_map/stack | solution.py:459
  30.6 0.8 copy.30
  31.4 1.7 pad.9.cols
  33.1 1.6 broadcast_in_dim.69
  35.6 2.7 %collective-permute-start.5 = (bf16[1024,128]{1,0:T(8,128)(2,1)}, bf16[1024,128]{1,0:T(8,128)(2,1)S(1)}, u32[]{:S(2)}, u32[]{:S(2)}) collective-permute-start(bf16[1024,128]{1,0:T(8,128)(2,1)} %collective-permute-done.3), channel_id=1, source_target_pairs={{0,112},{16,0},{32,16},{48,32},{64,48},{80,64},{96,80},{112,96},{1... | collective-permute-start | bytes 786440 | tf_op jit(solution)/shard_map/ppermute | solution.py:418
  38.2 1.7 bitcast_dynamic-update-slice_fusion.5
  39.9 1.7 bitcast_dynamic-update-slice_fusion.4
  41.6 2.6 %collective-permute-done.4 = bf16[1024,128]{1,0:T(8,128)(2,1)S(1)} collective-permute-done((bf16[1024,128]{1,0:T(8,128)(2,1)}, bf16[1024,128]{1,0:T(8,128)(2,1)S(1)}, u32[]{:S(2)}, u32[]{:S(2)}) %collective-permute-start.4) | collective-permute-done | bytes 262176 | tf_op jit(solution)/shard_map/ppermute | solution.py:418
  44.2 2.7 %collective-permute-start.7 = (bf16[1024,128]{1,0:T(8,128)(2,1)S(1)}, bf16[1024,128]{1,0:T(8,128)(2,1)S(1)}, u32[]{:S(2)}, u32[]{:S(2)}) collective-permute-start(bf16[1024,128]{1,0:T(8,128)(2,1)S(1)} %collective-permute-done.5), channel_id=1, source_target_pairs={{0,112},{16,0},{32,16},{48,32},{64,48},{80,64},{96,80},{112,96},{1... | collective-permute-start | bytes 786440 | tf_op jit(solution)/shard_map/ppermute | solution.py:418
  48.3 3.4 %collective-permute-done.6 = bf16[1024,128]{1,0:T(8,128)(2,1)S(1)} collective-permute-done((bf16[1024,128]{1,0:T(8,128)(2,1)S(1)}, bf16[1024,128]{1,0:T(8,128)(2,1)S(1)}, u32[]{:S(2)}, u32[]{:S(2)}) %collective-permute-start.6) | collective-permute-done | bytes 262176 | tf_op jit(solution)/shard_map/ppermute | solution.py:418
  51.8 2.7 %collective-permute-start.9 = (bf16[512,128]{1,0:T(8,128)(2,1)S(1)}, bf16[512,128]{1,0:T(8,128)(2,1)S(1)}, u32[]{:S(2)}, u32[]{:S(2)}) collective-permute-start(bf16[512,128]{1,0:T(8,128)(2,1)S(1)} %slice.63), channel_id=1, source_target_pairs={{0,112},{16,0},{32,16},{48,32},{64,48},{80,64},{96,80},{112,96},{1... | collective-permute-start | bytes 393224 | tf_op jit(solution)/shard_map/ppermute | solution.py:418
  56.0 1.1 collective-permute-done.8
  58.4 8.1 %all-to-all-done.own = bf16[8,800,256]{2,1,0:T(8,128)(2,1)S(1)} async-done(((bf16[8,800,256]{2,1,0:T(8,128)(2,1)}), bf16[8,800,256]{2,1,0:T(8,128)(2,1)S(1)}, u32[]{:S(2)}, u32[]{:S(2)}) %all-to-all-start) | async-done | bytes 3276832 | tf_op jit(solution)/shard_map/all_to_all | solution.py:413
  66.6 1.8 collective-permute-start.10
  68.7 5.1 %collective-permute-done.10.sib = bf16[8,800,256]{2,1,0:T(8,128)(2,1)S(1)} collective-permute-done((bf16[8,800,256]{2,1,0:T(8,128)(2,1)S(1)}, bf16[8,800,256]{2,1,0:T(8,128)(2,1)S(1)}, u32[]{:S(2)}, u32[]{:S(2)}) %collective-permute-start.10) | collective-permute-done | bytes 3276832 | tf_op jit(solution)/shard_map/ppermute | solution.py:404
  73.8 0.9 copy-done.5
  74.8 2.2 %copy-done.8 = bf16[4096,512]{1,0:T(8,128)(2,1)S(1)} copy-done((bf16[4096,512]{1,0:T(8,128)(2,1)S(1)}, bf16[4096,512]{1,0:T(8,128)(2,1)}, u32[]{:S(2)}) %copy-start.8) | copy-done | bytes 4194328
  77.0 11.1 %scan_input.1 = (bf16[512,512]{1,0:T(8,128)(2,1)}, bf16[512,256]{1,0:T(8,128)(2,1)}, f32[512,128]{1,0:T(8,128)}, f32[16,512]{1,0:T(8,128)}, bf16[128,512]{1,0:T(8,128)(2,1)}, /*index=5*/bf16[16,16,512]{2,1,0:T(8,128)(2,1)}) custom-call(bf16[8,800,256]{2,1,0:T(8,128)(2,1)S(1)} %all-to-all-done.own, bf16[8,800,256]{2,1,0:T(8,128)(2,1)S(1)} %collective-permute-done.10.sib, ...), custom_call_target="tpu_custom_call" | custom-call | flops 3391094784 | bytes 8388608 | tf_op jit(solution)/shard_map/scan_input/pallas_call | solution.py:198
  88.0 7.6 %all-to-all-start.1 = ((bf16[16,16,512]{2,1,0:T(8,128)(2,1)}), bf16[16,16,512]{2,1,0:T(8,128)(2,1)}, u32[]{:S(2)}, u32[]{:S(2)}) async-start(bf16[16,16,512]{2,1,0:T(8,128)(2,1)} %get-tuple-element.45), calls=%async_computation.1 | async-start | bytes 524288 | tf_op jit(solution)/shard_map/all_to_all | solution.py:441
  95.6 2.2 %copy-done.1 = bf16[4096,512]{1,0:T(8,128)(2,1)S(1)} copy-done((bf16[4096,512]{1,0:T(8,128)(2,1)S(1)}, bf16[4096,512]{1,0:T(8,128)(2,1)}, u32[]{:S(2)}) %copy-start.1) | copy-done | bytes 4194328
  97.8 1.9 %copy-done.4 = bf16[8,800,256]{2,1,0:T(8,128)(2,1)S(1)} copy-done((bf16[8,800,256]{2,1,0:T(8,128)(2,1)S(1)}, bf16[8,800,256]{2,1,0:T(8,128)(2,1)}, u32[]{:S(2)}) %copy-start.4) | copy-done | bytes 3276824
  99.7 4.8 %gate.1.gates = f32[512,512]{1,0:T(8,128)} custom-call(bf16[8,800,256]{2,1,0:T(8,128)(2,1)S(1)} %all-to-all-done.own, bf16[8,800,256]{2,1,0:T(8,128)(2,1)S(1)} %copy-done.4, bf16[4096,512]{1,0:T(8,128)(2,1)S(1)} %copy-done.1), custom_call_target="tpu_custom_call" | custom-call | flops 2147483648 | bytes 8388608 | tf_op jit(solution)/shard_map/gate/pallas_call | solution.py:198
  104.6 14.2 %all-to-all-done.1.pieces = bf16[16,16,512]{2,1,0:T(8,128)(2,1)} async-done(((bf16[16,16,512]{2,1,0:T(8,128)(2,1)}), bf16[16,16,512]{2,1,0:T(8,128)(2,1)}, u32[]{:S(2)}, u32[]{:S(2)}) %all-to-all-start.1) | async-done | bytes 262176 | tf_op jit(solution)/shard_map/all_to_all | solution.py:441
  118.7 1.7 prefix.1
  120.4 7.6 %all-to-all-start.2 = ((bf16[16,8,512]{2,1,0:T(8,128)(2,1)}), bf16[16,8,512]{2,1,0:T(8,128)(2,1)S(1)}, u32[]{:S(2)}, u32[]{:S(2)}) async-start(bf16[16,8,512]{2,1,0:T(8,128)(2,1)} %bitcast.29), calls=%async_computation.2 | async-start | bytes 262144 | tf_op jit(solution)/shard_map/all_to_all | solution.py:441
  128.1 0.9 copy-done.6
  129.0 1.0 copy-done.13
  130.1 0.9 copy-done.14
  131.0 0.9 copy-done.15
  132.0 1.8 intra.1
  133.8 1.8 all-to-all-done.2
  135.6 1.3 join.1.own
  136.9 2.2 %collective-permute-start.11 = (bf16[512,640]{1,0:T(8,128)(2,1)S(1)}, bf16[512,640]{1,0:T(8,128)(2,1)S(1)}, u32[]{:S(2)}, u32[]{:S(2)}) collective-permute-start(bf16[512,640]{1,0:T(8,128)(2,1)S(1)} %join.1.own), channel_id=1, source_target_pairs={{0,1},{1,0},{2,3},{3,2},{4,5},{5,4},{6,7},{7,6},{8,9},{9,8},{10,11... | collective-permute-start | bytes 1966088 | tf_op jit(solution)/shard_map/ppermute | solution.py:404
  139.1 1.7 collective-permute-done.11.sib
  140.9 7.8 %project.1 = bf16[8,512,256]{2,1,0:T(8,128)(2,1)S(1)} custom-call(s32[1]{0:T(128)} %bitcast.place, bf16[512,640]{1,0:T(8,128)(2,1)S(1)} %join.1.own, bf16[512,640]{1,0:T(8,128)(2,1)S(1)} %collective-permute-done.11.sib, bf16[8,1024,128]{2,1,0:T(8,128)(2,1)} %bitcast_dynamic-update-slice_fusion.7.near, bf16[8,1024,128]{2,1,0:T(8,128)(2,1)} %collective-permute-done.12.far), custom_call_target="tpu_custom_call" | custom-call | flops 4294967296 | bytes 8388608 | tf_op jit(solution)/shard_map/project/pallas_call | solution.py:381
  148.6 30.5 %all_to_all.20 = bf16[8,512,256]{2,1,0:T(8,128)(2,1)S(1)} all-to-all(bf16[8,512,256]{2,1,0:T(8,128)(2,1)S(1)} %project.1), channel_id=1, replica_groups={{0,2,4,6,8,10,12,14},{1,3,5,7,9,11,13,15},{16,18,20,22,24,26,28,30},{17..., dimensions={0} | all-to-all | bytes 4194304 | tf_op jit(solution)/shard_map/all_to_all | solution.py:413
  179.5 2.3 %collective-permute-start.13 = (bf16[512,128]{1,0:T(8,128)(2,1)S(1)}, bf16[512,128]{1,0:T(8,128)(2,1)S(1)}, u32[]{:S(2)}, u32[]{:S(2)}) collective-permute-start(bf16[512,128]{1,0:T(8,128)(2,1)S(1)} %broadcast_select_fusion.2), channel_id=1, source_target_pairs={{0,1},{1,0},{2,3},{3,2},{4,5},{5,4},{6,7},{7,6},{8,9},{9,8},{10,11... | collective-permute-start | bytes 393224 | tf_op jit(solution)/shard_map/ppermute | solution.py:404
  181.9 1.0 collective-permute-done.13
  (83 shorter events, 12.5 us)
Async XLA Ops:
  0.0 7.4 %copy-start = (f32[4,2048]{1,0:T(4,128)S(1)}, f32[4,2048]{1,0:T(4,128)}, u32[]{:S(2)}) copy-start(f32[4,2048]{1,0:T(4,128)} %param.23) | copy-start | bytes 98308
  0.0 11.4 %copy-start.20 = (bf16[512,256]{1,0:T(8,128)(2,1)S(1)}, bf16[512,256]{1,0:T(8,128)(2,1)}, u32[]{:S(2)}) copy-start(bf16[512,256]{1,0:T(8,128)(2,1)} %param.15) | copy-start | bytes 786436
  0.0 11.3 %copy-start.22 = (f32[8]{0:T(128)S(1)}, f32[8]{0:T(128)}, u32[]{:S(2)}) copy-start(f32[8]{0:T(128)} %param.27) | copy-start | bytes 100
  1.6 9.8 %collective-permute-start = (bf16[16,256]{1,0:T(8,128)(2,1)S(1)}, bf16[16,256]{1,0:T(8,128)(2,1)S(1)}, u32[]{:S(2)}, u32[]{:S(2)}) collective-permute-start(bf16[16,256]{1,0:T(8,128)(2,1)S(1)} %pad_maximum_fusion.4), channel_id=1, source_target_pairs={{0,16},{16,32},{32,48},{48,64},{64,80},{80,96},{96,112},{112,128},... | collective-permute-start | bytes 24584 | tf_op jit(solution)/shard_map/ppermute | solution.py:408
  13.4 9.7 %copy-start.21 = (s32[512]{0:T(512)S(1)}, s32[512]{0:T(512)}, u32[]{:S(2)}) copy-start(s32[512]{0:T(512)} %param.16) | copy-start | bytes 6148
  13.4 53.2 %all-to-all-start = ((bf16[8,800,256]{2,1,0:T(8,128)(2,1)}), bf16[8,800,256]{2,1,0:T(8,128)(2,1)S(1)}, u32[]{:S(2)}, u32[]{:S(2)}) async-start(bf16[8,800,256]{2,1,0:T(8,128)(2,1)} %pad_maximum_fusion), calls=%async_computation | async-start | bytes 6553600 | tf_op jit(solution)/shard_map/all_to_all | solution.py:413
  21.2 2.3 %collective-permute-start.1 = (bf16[512,128]{1,0:T(8,128)(2,1)S(1)}, bf16[512,128]{1,0:T(8,128)(2,1)S(1)}, u32[]{:S(2)}, u32[]{:S(2)}) collective-permute-start(bf16[512,128]{1,0:T(8,128)(2,1)S(1)} %get-tuple-element.66), channel_id=1, source_target_pairs={{0,1},{1,0},{2,3},{3,2},{4,5},{5,4},{6,7},{7,6},{8,9},{9,8},{10,11... | collective-permute-start | bytes 393224 | tf_op jit(solution)/shard_map/ppermute | solution.py:404
  23.5 0.6 copy-start.18
  24.8 10.6 %collective-permute-start.2 = (bf16[1024,128]{1,0:T(8,128)(2,1)}, bf16[1024,128]{1,0:T(8,128)(2,1)}, u32[]{:S(2)}, u32[]{:S(2)}) collective-permute-start(bf16[1024,128]{1,0:T(8,128)(2,1)} %pad_maximum_fusion.2), channel_id=1, source_target_pairs={{0,16},{16,32},{32,48},{48,64},{64,80},{80,96},{96,112},{112,0},{1... | collective-permute-start | bytes 786440 | tf_op jit(solution)/shard_map/ppermute | solution.py:418
  26.5 9.1 %collective-permute-start.3 = (bf16[1024,128]{1,0:T(8,128)(2,1)}, bf16[1024,128]{1,0:T(8,128)(2,1)}, u32[]{:S(2)}, u32[]{:S(2)}) collective-permute-start(bf16[1024,128]{1,0:T(8,128)(2,1)} %pad_maximum_fusion.2), channel_id=1, source_target_pairs={{0,112},{16,0},{32,16},{48,32},{64,48},{80,64},{96,80},{112,96},{1... | collective-permute-start | bytes 786440 | tf_op jit(solution)/shard_map/ppermute | solution.py:418
  31.4 3.3 %copy-start.19 = (bf16[512,128]{1,0:T(8,128)(2,1)S(1)}, bf16[512,128]{1,0:T(8,128)(2,1)}, u32[]{:S(2)}) copy-start(bf16[512,128]{1,0:T(8,128)(2,1)} %copy-done.18) | copy-start | bytes 393220
  35.5 38.4 %copy-start.9 = (f32[4,512]{1,0:T(4,128)S(1)}, f32[4,512]{1,0:T(4,128)}, u32[]{:S(2)}) copy-start(f32[4,512]{1,0:T(4,128)} %taps_x) | copy-start | bytes 24580
  35.5 38.4 %copy-start.10 = (f32[512]{0:T(512)S(1)}, f32[512]{0:T(512)}, u32[]{:S(2)}) copy-start(f32[512]{0:T(512)} %param.22) | copy-start | bytes 6148
  35.5 38.4 %copy-start.11 = (f32[8]{0:T(128)S(1)}, f32[8]{0:T(128)}, u32[]{:S(2)}) copy-start(f32[8]{0:T(128)} %param.25) | copy-start | bytes 100
  35.5 38.4 %copy-start.12 = (f32[8]{0:T(128)S(1)}, f32[8]{0:T(128)}, u32[]{:S(2)}) copy-start(f32[8]{0:T(128)} %param.26) | copy-start | bytes 100
  35.5 8.7 %collective-permute-start.4 = (bf16[1024,128]{1,0:T(8,128)(2,1)}, bf16[1024,128]{1,0:T(8,128)(2,1)S(1)}, u32[]{:S(2)}, u32[]{:S(2)}) collective-permute-start(bf16[1024,128]{1,0:T(8,128)(2,1)} %collective-permute-done.2), channel_id=1, source_target_pairs={{0,16},{16,32},{32,48},{48,64},{64,80},{80,96},{96,112},{112,0},{1... | collective-permute-start | bytes 786440 | tf_op jit(solution)/shard_map/ppermute | solution.py:418
  35.6 8.6 %collective-permute-start.5 = (bf16[1024,128]{1,0:T(8,128)(2,1)}, bf16[1024,128]{1,0:T(8,128)(2,1)S(1)}, u32[]{:S(2)}, u32[]{:S(2)}) collective-permute-start(bf16[1024,128]{1,0:T(8,128)(2,1)} %collective-permute-done.3), channel_id=1, source_target_pairs={{0,112},{16,0},{32,16},{48,32},{64,48},{80,64},{96,80},{112,96},{1... | collective-permute-start | bytes 786440 | tf_op jit(solution)/shard_map/ppermute | solution.py:418
  44.2 7.5 %collective-permute-start.6 = (bf16[1024,128]{1,0:T(8,128)(2,1)S(1)}, bf16[1024,128]{1,0:T(8,128)(2,1)S(1)}, u32[]{:S(2)}, u32[]{:S(2)}) collective-permute-start(bf16[1024,128]{1,0:T(8,128)(2,1)S(1)} %collective-permute-done.4), channel_id=1, source_target_pairs={{0,16},{16,32},{32,48},{48,64},{64,80},{80,96},{96,112},{112,0},{1... | collective-permute-start | bytes 786440 | tf_op jit(solution)/shard_map/ppermute | solution.py:418
  44.2 7.6 %collective-permute-start.7 = (bf16[1024,128]{1,0:T(8,128)(2,1)S(1)}, bf16[1024,128]{1,0:T(8,128)(2,1)S(1)}, u32[]{:S(2)}, u32[]{:S(2)}) collective-permute-start(bf16[1024,128]{1,0:T(8,128)(2,1)S(1)} %collective-permute-done.5), channel_id=1, source_target_pairs={{0,112},{16,0},{32,16},{48,32},{64,48},{80,64},{96,80},{112,96},{1... | collective-permute-start | bytes 786440 | tf_op jit(solution)/shard_map/ppermute | solution.py:418
  51.7 5.4 %collective-permute-start.8 = (bf16[512,128]{1,0:T(8,128)(2,1)S(1)}, bf16[512,128]{1,0:T(8,128)(2,1)S(1)}, u32[]{:S(2)}, u32[]{:S(2)}) collective-permute-start(bf16[512,128]{1,0:T(8,128)(2,1)S(1)} %slice.62), channel_id=1, source_target_pairs={{0,16},{16,32},{32,48},{48,64},{64,80},{80,96},{96,112},{112,0},{1... | collective-permute-start | bytes 393224 | tf_op jit(solution)/shard_map/ppermute | solution.py:418
  51.8 6.0 %collective-permute-start.9 = (bf16[512,128]{1,0:T(8,128)(2,1)S(1)}, bf16[512,128]{1,0:T(8,128)(2,1)S(1)}, u32[]{:S(2)}, u32[]{:S(2)}) collective-permute-start(bf16[512,128]{1,0:T(8,128)(2,1)S(1)} %slice.63), channel_id=1, source_target_pairs={{0,112},{16,0},{32,16},{48,32},{64,48},{80,64},{96,80},{112,96},{1... | collective-permute-start | bytes 393224 | tf_op jit(solution)/shard_map/ppermute | solution.py:418
  66.6 7.2 %collective-permute-start.10 = (bf16[8,800,256]{2,1,0:T(8,128)(2,1)S(1)}, bf16[8,800,256]{2,1,0:T(8,128)(2,1)S(1)}, u32[]{:S(2)}, u32[]{:S(2)}) collective-permute-start(bf16[8,800,256]{2,1,0:T(8,128)(2,1)S(1)} %all-to-all-done.own), channel_id=1, source_target_pairs={{0,1},{1,0},{2,3},{3,2},{4,5},{5,4},{6,7},{7,6},{8,9},{9,8},{10,11... | collective-permute-start | bytes 9830408 | tf_op jit(solution)/shard_map/ppermute | solution.py:404
  68.3 70.8 %collective-permute-start.12 = (bf16[8,1024,128]{2,1,0:T(8,128)(2,1)}, bf16[8,1024,128]{2,1,0:T(8,128)(2,1)}, u32[]{:S(2)}, u32[]{:S(2)}) collective-permute-start(bf16[8,1024,128]{2,1,0:T(8,128)(2,1)} %bitcast_dynamic-update-slice_fusion.7.near), channel_id=1, source_target_pairs={{0,128},{16,144},{32,160},{48,176},{64,192},{80,208},{96,224},{112... | collective-permute-start | bytes 6291464 | tf_op jit(solution)/shard_map/ppermute | solution.py:509
  73.8 1.0 copy-start.5
  74.8 2.2 %copy-start.8 = (bf16[4096,512]{1,0:T(8,128)(2,1)S(1)}, bf16[4096,512]{1,0:T(8,128)(2,1)}, u32[]{:S(2)}) copy-start(bf16[4096,512]{1,0:T(8,128)(2,1)} %w_x.1) | copy-start | bytes 12582916
  77.0 11.1 %copy-start.3 = (bf16[8,800,256]{2,1,0:T(8,128)(2,1)}, bf16[8,800,256]{2,1,0:T(8,128)(2,1)S(1)}, u32[]{:S(2)}) copy-start(bf16[8,800,256]{2,1,0:T(8,128)(2,1)S(1)} %collective-permute-done.10.sib) | copy-start | bytes 9830404
  88.0 30.7 %all-to-all-start.1 = ((bf16[16,16,512]{2,1,0:T(8,128)(2,1)}), bf16[16,16,512]{2,1,0:T(8,128)(2,1)}, u32[]{:S(2)}, u32[]{:S(2)}) async-start(bf16[16,16,512]{2,1,0:T(8,128)(2,1)} %get-tuple-element.45), calls=%async_computation.1 | async-start | bytes 524288 | tf_op jit(solution)/shard_map/all_to_all | solution.py:441
  95.6 2.2 %copy-start.1 = (bf16[4096,512]{1,0:T(8,128)(2,1)S(1)}, bf16[4096,512]{1,0:T(8,128)(2,1)}, u32[]{:S(2)}) copy-start(bf16[4096,512]{1,0:T(8,128)(2,1)} %w_z.1) | copy-start | bytes 12582916
  97.8 1.9 %copy-start.4 = (bf16[8,800,256]{2,1,0:T(8,128)(2,1)S(1)}, bf16[8,800,256]{2,1,0:T(8,128)(2,1)}, u32[]{:S(2)}) copy-start(bf16[8,800,256]{2,1,0:T(8,128)(2,1)} %copy-done.3) | copy-start | bytes 9830404
  99.7 28.4 %copy-start.16 = (bf16[128,512]{1,0:T(8,128)(2,1)S(1)}, bf16[128,512]{1,0:T(8,128)(2,1)}, u32[]{:S(2)}) copy-start(bf16[128,512]{1,0:T(8,128)(2,1)} %get-tuple-element.54.s0) | copy-start | bytes 393220
  99.7 28.4 %copy-start.17 = (f32[16,512]{1,0:T(8,128)S(1)}, f32[16,512]{1,0:T(8,128)}, u32[]{:S(2)}) copy-start(f32[16,512]{1,0:T(8,128)} %get-tuple-element.53.hrow) | copy-start | bytes 98308
  118.7 16.9 %copy-start.7 = (f32[512]{0:T(512)S(1)}, f32[512]{0:T(512)}, u32[]{:S(2)}) copy-start(f32[512]{0:T(512)} %param.28) | copy-start | bytes 6148
  120.4 15.2 %copy-start.2 = (f32[512,512]{1,0:T(8,128)S(1)}, f32[512,512]{1,0:T(8,128)}, u32[]{:S(2)}) copy-start(f32[512,512]{1,0:T(8,128)} %gate.1.gates) | copy-start | bytes 3145732
  120.4 15.2 %all-to-all-start.2 = ((bf16[16,8,512]{2,1,0:T(8,128)(2,1)}), bf16[16,8,512]{2,1,0:T(8,128)(2,1)S(1)}, u32[]{:S(2)}, u32[]{:S(2)}) async-start(bf16[16,8,512]{2,1,0:T(8,128)(2,1)} %bitcast.29), calls=%async_computation.2 | async-start | bytes 262144 | tf_op jit(solution)/shard_map/all_to_all | solution.py:441
  128.1 1.0 copy-start.6
  129.0 1.0 copy-start.13
  130.1 0.9 copy-start.14
  131.0 0.9 copy-start.15
  136.9 3.9 %collective-permute-start.11 = (bf16[512,640]{1,0:T(8,128)(2,1)S(1)}, bf16[512,640]{1,0:T(8,128)(2,1)S(1)}, u32[]{:S(2)}, u32[]{:S(2)}) collective-permute-start(bf16[512,640]{1,0:T(8,128)(2,1)S(1)} %join.1.own), channel_id=1, source_target_pairs={{0,1},{1,0},{2,3},{3,2},{4,5},{5,4},{6,7},{7,6},{8,9},{9,8},{10,11... | collective-permute-start | bytes 1966088 | tf_op jit(solution)/shard_map/ppermute | solution.py:404
  179.5 3.3 %collective-permute-start.13 = (bf16[512,128]{1,0:T(8,128)(2,1)S(1)}, bf16[512,128]{1,0:T(8,128)(2,1)S(1)}, u32[]{:S(2)}, u32[]{:S(2)}) collective-permute-start(bf16[512,128]{1,0:T(8,128)(2,1)S(1)} %broadcast_select_fusion.2), channel_id=1, source_target_pairs={{0,1},{1,0},{2,3},{3,2},{4,5},{5,4},{6,7},{7,6},{8,9},{9,8},{10,11... | collective-permute-start | bytes 393224 | tf_op jit(solution)/shard_map/ppermute | solution.py:404
  182.9 0.7 copy-start.23

commit v9 on v8

--- a/solution.py
+++ b/solution.py
@@ -356,24 +356,30 @@
     )(*args)
 
 
-def project_kernel(place, own, sib, near, far, out):
+def project_kernel(place, own, sib, near, far_own, far_sib, out):
     del place
     square = own[:, CH:].astype(F32) + sib[:, CH:].astype(F32)
     scale = lax.rsqrt((square[:, 0:1] + square[:, 64:65]) / (2.0 * CH) + NORM_EPS)
     values = jnp.concatenate([own[:, :CH], sib[:, :CH]], axis=1)
-    is_near = pl.program_id(0) < CHIPS // 2
-    for wanted, ref in ((is_near, near), (jnp.logical_not(is_near), far)):
-
-        @pl.when(wanted)
-        def _():
-            rows = jnp.concatenate([ref[0], ref[1]], axis=1)
-            out[0] = (dot(values, rows) * scale).astype(BF16)
-
-
-def project(own, sib, near, far, y_low):
+
+    def send(rows):
+        out[0] = (dot(values, rows) * scale).astype(BF16)
+
+    @pl.when(pl.program_id(0) < CHIPS // 2)
+    def _():
+        send(jnp.concatenate([near[0], near[1]], axis=1))
+
+    @pl.when(pl.program_id(0) >= CHIPS // 2)
+    def _():
+        sides = [jnp.concatenate([ref[0], ref[1]], axis=1) for ref in (far_own, far_sib)]
+        send(jnp.concatenate(sides, axis=0))
+
+
+def project(own, sib, w_held, w_late, y_low):
     half = CHIPS // 2
     whole = pl.BlockSpec(own.shape, lambda i, place: (0, 0))
-    columns = lambda at: pl.BlockSpec((2, 2 * CH, 128), at)
+    first = lambda i, place: (jnp.minimum(i, half - 1), 0, 0)
+    then = lambda row: lambda i, place: (jnp.maximum(i - half, 0), row, 0)
 
     def sent(i, place):
         return lax.rem(i, half) + half * lax.rem(lax.div(i, half) + place[0], 2), 0, 0
@@ -386,8 +392,9 @@
             in_specs=[
                 whole,
                 whole,
-                columns(lambda i, place: (jnp.minimum(i, half - 1), 0, 0)),
-                columns(lambda i, place: (jnp.maximum(i - half, 0), 0, 0)),
+                pl.BlockSpec((2, 2 * CH, 128), first),
+                pl.BlockSpec((2, CH, 128), then(2)),
+                pl.BlockSpec((2, CH, 128), then(0)),
             ],
             out_specs=pl.BlockSpec((1, ROWS, 256), sent),
         ),
@@ -397,7 +404,7 @@
             flops=8 * ROWS * CH * 2048, bytes_accessed=8 * 2**20, transcendentals=0
         ),
         name="project",
-    )(y_low[None], own, sib, near, far)
+    )(y_low[None], own, sib, w_held, w_held, w_late)
 
 
 def swapped(value, bit):
@@ -411,6 +418,10 @@
 def between_chips(value):
     same_core = [[2 * chip + core for chip in range(CHIPS)] for core in range(CORES)]
     return lax.all_to_all(value, "tp", 0, 0, axis_index_groups=same_core)
+
+
+def across_y(value):
+    return lax.ppermute(value, "ctx", [(i, i ^ Z_RING) for i in range(CTX)])
 
 
 def along_z(value, steps):
@@ -491,22 +502,27 @@
     shared = jnp.concatenate([halo, tokens], axis=0)
     shared = jnp.broadcast_to(shared[None], (CHIPS, ALL_ROWS, FEAT))
     sent = jnp.concatenate([shared, w_cols], axis=1)
-    sent, w_out = together(sent, w_out)
+    sent, w_out, seg_ids, conv_bc, conv_bc_bias, skip_gain = together(
+        sent, w_out, seg_ids, conv_bc, conv_bc_bias, skip_gain
+    )
     own = between_chips(sent)
 
     halves = (w_out[:, :128], w_out[:, 128:])
-    w_pair = jnp.concatenate(
-        [pick(core, *halves), swapped(pick(core, halves[1], halves[0]), 1)], axis=0
-    )
-    w_near = gathered_along_z(w_pair)
+    w_kept = pick(core, *halves)
+    w_own_far = across_y(w_kept)
+    w_sib = swapped(pick(core, halves[1], halves[0]), 1)
+    w_held = gathered_along_z(jnp.concatenate([w_kept, w_sib, w_own_far], axis=0))
 
     cols, seg_row = document_columns(seg_ids, ids_prior)
     taps_bc = lax.dynamic_slice_in_dim(conv_bc, chip * 2 * N, 2 * N, 1)
     bias_bc = lax.dynamic_slice_in_dim(conv_bc_bias, chip * 2 * N, 2 * N, 0)[None]
     skip = jnp.repeat(skip_gain, P_SIZE)[None]
     fixed = [cols, conv_x, conv_x_bias[None], taps_bc, bias_bc, dt_bias[None], decay_rate[None]]
-    own, w_near, fixed, seg_row, skip = together(own, w_near, fixed, seg_row, skip)
-    w_far = lax.ppermute(w_near, "ctx", [(i, i ^ Z_RING) for i in range(2 * Z_RING)])
+    w_rest = w_held[:, CH : 2 * CH]
+    own, w_held, w_rest, fixed, seg_row, skip = together(
+        own, w_held, w_rest, fixed, seg_row, skip
+    )
+    w_late = across_y(w_rest)
     sib = swapped(own, 1)
     xc, bcc, hcol, hrow, s0, pay = scan_input(own, sib, w_x, fixed)
     own, sib, pay = together(own, sib, pay)
@@ -515,8 +531,9 @@
     pieces, gates, xc, bcc = together(pieces, gates, xc, bcc)
     state = between_slabs(prefix(pieces).reshape(CTX, 8, CH)).reshape(N, CH)
     y, cc, decays = intra(xc, bcc, hcol, hrow, s0, fixed[0], seg_row, skip)
+    state, w_late, w_held = together(state, w_late, w_held)
     mine = join(y, gates, cc, decays, state, norm_weight[None])
-    parts = between_chips(project(mine, swapped(mine, 1), w_near, w_far, y_low))
+    parts = between_chips(project(mine, swapped(mine, 1), w_held, w_late, y_low))
     total = jnp.sum(parts.astype(F32), axis=0).astype(BF16)
     parts = (total[:, :128], total[:, 128:])
     kept = pick(core, *parts)

time: 185 us -> 215 us (1.16)
  waiting for transfers between devices: 39.3 us -> 52.9 us
  starting transfers between devices: 46.3 us -> 57.5 us
  blocking collectives: 30.5 us -> 33.4 us
    ppermute x1 -> x2, waiting for transfers between devices: 0.01 us -> 25.7 us  [across_y(): return lax.ppermute(value, 'ctx', [(i, i ^ Z_RING) for i in range(CTX)])]
    all_to_all x2, waiting for transfers between devices: 16 us -> 0.01 us  [between_slabs(): return lax.all_to_all(value, 'ctx', 0, 0)]
    ppermute x8, waiting for transfers between devices: 7.15 us -> 18.7 us  [along_z(): return lax.ppermute(value, 'ctx', pairs)]
    ppermute x4, starting transfers between devices: 7.62 us -> 17.9 us  [swapped(): return lax.ppermute(value, 'tp', [(i, i ^ bit) for i in range(16)])]
    all_to_all x1, waiting for transfers between devices: 8.13 us -> 0.01 us  [between_chips(): return lax.all_to_all(value, 'tp', 0, 0, axis_index_groups=same_core)]
    unnamed x48 -> x62, local copies, waits for them, and re-layouts: 12.5 us -> 20.2 us
    dynamic_update_slice x8, local copies, waits for them, and re-layouts: 7.53 us -> 2.38 us  [put(): return lax.dynamic_update_slice(held, piece[None], at)]
    all_to_all x1, blocking collectives: 30.5 us -> 33.4 us  [between_chips(): return lax.all_to_all(value, 'tp', 0, 0, axis_index_groups=same_core)]
  transfers between devices with their start and end apart: 17 -> 18, of which waited for: 10 -> 7; matrix products, arithmetic and copies ran while one was open for 12% -> 7% of each run, Pallas kernels for 11% -> 9%
where the time goes in v9:
time: 215 us; the launch traced here: 213 us
  starting transfers between devices  57.5 us (27%)
  waiting for transfers between devices  52.9 us (25%)
  blocking collectives  33.4 us (16%)
  local copies, waits for them, and re-layouts  32.2 us (15%)
  Pallas kernels  29 us (13%)
  other arithmetic  7.96 us (4%)
    all_to_all x1, blocking collectives, between_chips(): return lax.all_to_all(value, 'tp', 0, 0, axis_index_groups=same_core)  33.4 us
    ppermute x2, waiting for transfers between devices, across_y(): return lax.ppermute(value, 'ctx', [(i, i ^ Z_RING) for i in range(CTX)])  25.7 us
    unnamed x62, local copies, waits for them, and re-layouts  20.2 us
    ppermute x8, waiting for transfers between devices, along_z(): return lax.ppermute(value, 'ctx', pairs)  18.7 us
    ppermute x4, starting transfers between devices, swapped(): return lax.ppermute(value, 'tp', [(i, i ^ bit) for i in range(16)])  17.9 us
    pallas_call x2, Pallas kernels, over_chips(): pl.pallas_call(kernel, grid=(CHIPS // 2,), in_specs=[spec for _, spec in...  15.9 us
    all_to_all x2, starting transfers between devices, between_slabs(): return lax.all_to_all(value, 'ctx', 0, 0)  14.6 us
    ppermute x8, starting transfers between devices, along_z(): return lax.ppermute(value, 'ctx', pairs)  10.9 us
  transfers between devices with their start and end apart: 18, of which 7 were waited for; matrix products, arithmetic and copies ran while one was open for 7% of the time, Pallas kernels for 9%

profile of v9, /device:TPU:1, one launch (start us, length us, event | category | flops | bytes accessed | tf_op | source)
XLA Modules:
  0.0 213.5 jit_solution(4220525186424366579)
XLA Ops:
  1.5 4.4 %collective-permute-start = (bf16[16,256]{1,0:T(8,128)(2,1)S(1)}, bf16[16,256]{1,0:T(8,128)(2,1)S(1)}, u32[]{:S(2)}, u32[]{:S(2)}) collective-permute-start(bf16[16,256]{1,0:T(8,128)(2,1)S(1)} %pad_maximum_fusion.4), channel_id=1, source_target_pairs={{0,16},{16,32},{32,48},{48,64},{64,80},{80,96},{96,112},{112,128},... | collective-permute-start | bytes 24584 | tf_op jit(solution)/shard_map/ppermute | solution.py:415
  7.0 1.5 copy.28
  8.6 1.0 pad_maximum_fusion.2
  9.7 1.8 pad_maximum_fusion
  11.5 6.8 %all-to-all-start = ((bf16[8,800,256]{2,1,0:T(8,128)(2,1)}), bf16[8,800,256]{2,1,0:T(8,128)(2,1)S(1)}, u32[]{:S(2)}, u32[]{:S(2)}) async-start(bf16[8,800,256]{2,1,0:T(8,128)(2,1)} %pad_maximum_fusion), calls=%async_computation | async-start | bytes 6553600 | tf_op jit(solution)/shard_map/all_to_all | solution.py:420
  18.3 1.0 broadcast_select_fusion.4
  19.3 2.9 %collective-permute-start.2 = (bf16[512,128]{1,0:T(8,128)(2,1)S(1)}, bf16[512,128]{1,0:T(8,128)(2,1)S(1)}, u32[]{:S(2)}, u32[]{:S(2)}) collective-permute-start(bf16[512,128]{1,0:T(8,128)(2,1)S(1)} %get-tuple-element.82), channel_id=1, source_target_pairs={{0,128},{16,144},{32,160},{48,176},{64,192},{80,208},{96,224},{112... | collective-permute-start | bytes 393224 | tf_op jit(solution)/shard_map/ppermute | solution.py:424
  22.2 2.1 collective-permute-start.1
  25.6 25.7 %collective-permute-done.2 = bf16[512,128]{1,0:T(8,128)(2,1)S(1)} collective-permute-done((bf16[512,128]{1,0:T(8,128)(2,1)S(1)}, bf16[512,128]{1,0:T(8,128)(2,1)S(1)}, u32[]{:S(2)}, u32[]{:S(2)}) %collective-permute-start.2) | collective-permute-done | bytes 131104 | tf_op jit(solution)/shard_map/ppermute | solution.py:424
  52.8 2.7 %collective-permute-start.4 = (bf16[1536,128]{1,0:T(8,128)(2,1)}, bf16[1536,128]{1,0:T(8,128)(2,1)}, u32[]{:S(2)}, u32[]{:S(2)}) collective-permute-start(bf16[1536,128]{1,0:T(8,128)(2,1)} %pad_maximum_fusion.1), channel_id=1, source_target_pairs={{0,112},{16,0},{32,16},{48,32},{64,48},{80,64},{96,80},{112,96},{1... | collective-permute-start | bytes 1179656 | tf_op jit(solution)/shard_map/ppermute | solution.py:429
  55.5 2.0 compare_convert_fusion
  58.5 1.7 pad.9.cols
  61.6 2.7 %collective-permute-start.6 = (bf16[1536,128]{1,0:T(8,128)(2,1)}, bf16[1536,128]{1,0:T(8,128)(2,1)S(1)}, u32[]{:S(2)}, u32[]{:S(2)}) collective-permute-start(bf16[1536,128]{1,0:T(8,128)(2,1)} %collective-permute-done.4), channel_id=1, source_target_pairs={{0,112},{16,0},{32,16},{48,32},{64,48},{80,64},{96,80},{112,96},{1... | collective-permute-start | bytes 1179656 | tf_op jit(solution)/shard_map/ppermute | solution.py:429
  64.3 1.0 bitcast_dynamic-update-slice_fusion.5
  65.3 1.1 bitcast_dynamic-update-slice_fusion.4
  66.4 7.7 %collective-permute-done.5 = bf16[1536,128]{1,0:T(8,128)(2,1)S(1)} collective-permute-done((bf16[1536,128]{1,0:T(8,128)(2,1)}, bf16[1536,128]{1,0:T(8,128)(2,1)S(1)}, u32[]{:S(2)}, u32[]{:S(2)}) %collective-permute-start.5) | collective-permute-done | bytes 393248 | tf_op jit(solution)/shard_map/ppermute | solution.py:429
  74.1 2.7 %collective-permute-start.8 = (bf16[1536,128]{1,0:T(8,128)(2,1)S(1)}, bf16[1536,128]{1,0:T(8,128)(2,1)S(1)}, u32[]{:S(2)}, u32[]{:S(2)}) collective-permute-start(bf16[1536,128]{1,0:T(8,128)(2,1)S(1)} %collective-permute-done.6), channel_id=1, source_target_pairs={{0,112},{16,0},{32,16},{48,32},{64,48},{80,64},{96,80},{112,96},{1... | collective-permute-start | bytes 1179656 | tf_op jit(solution)/shard_map/ppermute | solution.py:429
  76.9 8.2 %collective-permute-done.7 = bf16[1536,128]{1,0:T(8,128)(2,1)S(1)} collective-permute-done((bf16[1536,128]{1,0:T(8,128)(2,1)S(1)}, bf16[1536,128]{1,0:T(8,128)(2,1)S(1)}, u32[]{:S(2)}, u32[]{:S(2)}) %collective-permute-start.7) | collective-permute-done | bytes 393248 | tf_op jit(solution)/shard_map/ppermute | solution.py:429
  85.2 2.7 %collective-permute-start.10 = (bf16[768,128]{1,0:T(8,128)(2,1)S(1)}, bf16[768,128]{1,0:T(8,128)(2,1)S(1)}, u32[]{:S(2)}, u32[]{:S(2)}) collective-permute-start(bf16[768,128]{1,0:T(8,128)(2,1)S(1)} %slice.67), channel_id=1, source_target_pairs={{0,112},{16,0},{32,16},{48,32},{64,48},{80,64},{96,80},{112,96},{1... | collective-permute-start | bytes 589832 | tf_op jit(solution)/shard_map/ppermute | solution.py:429
  88.1 2.8 %collective-permute-done.9 = bf16[768,128]{1,0:T(8,128)(2,1)S(1)} collective-permute-done((bf16[768,128]{1,0:T(8,128)(2,1)S(1)}, bf16[768,128]{1,0:T(8,128)(2,1)S(1)}, u32[]{:S(2)}, u32[]{:S(2)}) %collective-permute-start.9) | collective-permute-done | bytes 196640 | tf_op jit(solution)/shard_map/ppermute | solution.py:429
  91.0 1.1 slice.68
  92.2 1.7 copy-done.1
  93.8 11.9 %collective-permute-start.11 = (bf16[8,800,256]{2,1,0:T(8,128)(2,1)S(1)}, bf16[8,800,256]{2,1,0:T(8,128)(2,1)S(1)}, u32[]{:S(2)}, u32[]{:S(2)}) collective-permute-start(bf16[8,800,256]{2,1,0:T(8,128)(2,1)S(1)} %all-to-all-done.own), channel_id=1, source_target_pairs={{0,1},{1,0},{2,3},{3,2},{4,5},{5,4},{6,7},{7,6},{8,9},{9,8},{10,11... | collective-permute-start | bytes 9830408 | tf_op jit(solution)/shard_map/ppermute | solution.py:411
  105.8 5.4 %collective-permute-done.11.sib = bf16[8,800,256]{2,1,0:T(8,128)(2,1)S(1)} collective-permute-done((bf16[8,800,256]{2,1,0:T(8,128)(2,1)S(1)}, bf16[8,800,256]{2,1,0:T(8,128)(2,1)S(1)}, u32[]{:S(2)}, u32[]{:S(2)}) %collective-permute-start.11) | collective-permute-done | bytes 3276832 | tf_op jit(solution)/shard_map/ppermute | solution.py:411
  111.2 0.9 copy-done.9
  112.1 2.2 %copy-done.14 = bf16[4096,512]{1,0:T(8,128)(2,1)S(1)} copy-done((bf16[4096,512]{1,0:T(8,128)(2,1)S(1)}, bf16[4096,512]{1,0:T(8,128)(2,1)}, u32[]{:S(2)}) %copy-start.14) | copy-done | bytes 4194328
  114.3 11.0 %scan_input.1 = (bf16[512,512]{1,0:T(8,128)(2,1)}, bf16[512,256]{1,0:T(8,128)(2,1)}, f32[512,128]{1,0:T(8,128)}, f32[16,512]{1,0:T(8,128)}, bf16[128,512]{1,0:T(8,128)(2,1)}, /*index=5*/bf16[16,16,512]{2,1,0:T(8,128)(2,1)}) custom-call(bf16[8,800,256]{2,1,0:T(8,128)(2,1)S(1)} %all-to-all-done.own, bf16[8,800,256]{2,1,0:T(8,128)(2,1)S(1)} %collective-permute-done.11.sib, ...), custom_call_target="tpu_custom_call" | custom-call | flops 3391094784 | bytes 8388608 | tf_op jit(solution)/shard_map/scan_input/pallas_call | solution.py:198
  125.4 7.1 %all-to-all-start.1 = ((bf16[16,16,512]{2,1,0:T(8,128)(2,1)}), bf16[16,16,512]{2,1,0:T(8,128)(2,1)}, u32[]{:S(2)}, u32[]{:S(2)}) async-start(bf16[16,16,512]{2,1,0:T(8,128)(2,1)} %get-tuple-element.57), calls=%async_computation.1 | async-start | bytes 524288 | tf_op jit(solution)/shard_map/all_to_all | solution.py:452
  132.5 2.2 %copy-done.3 = bf16[4096,512]{1,0:T(8,128)(2,1)S(1)} copy-done((bf16[4096,512]{1,0:T(8,128)(2,1)S(1)}, bf16[4096,512]{1,0:T(8,128)(2,1)}, u32[]{:S(2)}) %copy-start.3) | copy-done | bytes 4194328
  134.6 1.9 copy-done.6
  136.6 4.8 %gate.1.gates = f32[512,512]{1,0:T(8,128)} custom-call(bf16[8,800,256]{2,1,0:T(8,128)(2,1)S(1)} %all-to-all-done.own, bf16[8,800,256]{2,1,0:T(8,128)(2,1)S(1)} %copy-done.6, bf16[4096,512]{1,0:T(8,128)(2,1)S(1)} %copy-done.3), custom_call_target="tpu_custom_call" | custom-call | flops 2147483648 | bytes 8388608 | tf_op jit(solution)/shard_map/gate/pallas_call | solution.py:198
  141.4 1.7 prefix.1
  143.1 7.5 %all-to-all-start.2 = ((bf16[16,8,512]{2,1,0:T(8,128)(2,1)}), bf16[16,8,512]{2,1,0:T(8,128)(2,1)S(1)}, u32[]{:S(2)}, u32[]{:S(2)}) async-start(bf16[16,8,512]{2,1,0:T(8,128)(2,1)} %bitcast.29), calls=%async_computation.2 | async-start | bytes 262144 | tf_op jit(solution)/shard_map/all_to_all | solution.py:452
  151.6 1.0 copy-done.19
  152.6 0.9 copy-done.20
  153.6 0.9 copy-done.21
  155.4 1.7 intra.1
  157.2 1.0 copy-done.7
  158.9 1.2 copy-done.4
  160.1 1.2 copy-done.8
  161.3 0.9 copy-done.12
  162.2 2.2 %join.1.own = bf16[512,640]{1,0:T(8,128)(2,1)} custom-call(f32[512,512]{1,0:T(8,128)S(1)} %copy-done.8, f32[512,512]{1,0:T(8,128)S(1)} %copy-done.4, bf16[512,128]{1,0:T(8,128)(2,1)S(1)} %get-tuple-element.71.cc, f32[512,128]{1,0:T(8,128)S(1)} %copy-done.12, bf16[128,512]{1,0:T(8,128)(2,1)S(1)} %bitcast.42, f32[1,512]{1,0:T(1,128)S(1)} %bitcast.43), custom_call_target="tpu_custom_call" | custom-call | flops 67108864 | bytes 4194304 | tf_op jit(solution)/shard_map/join/pallas_call | solution.py:346
  164.4 1.6 collective-permute-start.13
  166.0 2.1 collective-permute-done.13.sib
  168.1 7.5 %project.1 = bf16[8,512,256]{2,1,0:T(8,128)(2,1)S(1)} custom-call(s32[1]{0:T(128)} %bitcast.place, bf16[512,640]{1,0:T(8,128)(2,1)} %join.1.own, bf16[512,640]{1,0:T(8,128)(2,1)} %collective-permute-done.13.sib, bf16[8,1536,128]{2,1,0:T(8,128)(2,1)S(1)} %copy-done.2, bf16[8,1536,128]{2,1,0:T(8,128)(2,1)S(1)} %copy-done.2, ...), custom_call_target="tpu_custom_call" | custom-call | flops 4294967296 | bytes 8388608 | tf_op jit(solution)/shard_map/project/pallas_call | solution.py:387
  175.6 33.4 %all_to_all.20 = bf16[8,512,256]{2,1,0:T(8,128)(2,1)S(1)} all-to-all(bf16[8,512,256]{2,1,0:T(8,128)(2,1)S(1)} %project.1), channel_id=1, replica_groups={{0,2,4,6,8,10,12,14},{1,3,5,7,9,11,13,15},{16,18,20,22,24,26,28,30},{17..., dimensions={0} | all-to-all | bytes 4194304 | tf_op jit(solution)/shard_map/all_to_all | solution.py:420
  209.4 2.3 %collective-permute-start.14 = (bf16[512,128]{1,0:T(8,128)(2,1)S(1)}, bf16[512,128]{1,0:T(8,128)(2,1)S(1)}, u32[]{:S(2)}, u32[]{:S(2)}) collective-permute-start(bf16[512,128]{1,0:T(8,128)(2,1)S(1)} %broadcast_select_fusion.2), channel_id=1, source_target_pairs={{0,1},{1,0},{2,3},{3,2},{4,5},{5,4},{6,7},{7,6},{8,9},{9,8},{10,11... | collective-permute-start | bytes 393224 | tf_op jit(solution)/shard_map/ppermute | solution.py:411
  211.7 1.0 collective-permute-done.14
  (100 shorter events, 12.1 us)
Async XLA Ops:
  0.0 61.0 %copy-start = (f32[4,2048]{1,0:T(4,128)S(1)}, f32[4,2048]{1,0:T(4,128)}, u32[]{:S(2)}) copy-start(f32[4,2048]{1,0:T(4,128)} %param.23) | copy-start | bytes 98308
  1.5 7.1 %collective-permute-start = (bf16[16,256]{1,0:T(8,128)(2,1)S(1)}, bf16[16,256]{1,0:T(8,128)(2,1)S(1)}, u32[]{:S(2)}, u32[]{:S(2)}) collective-permute-start(bf16[16,256]{1,0:T(8,128)(2,1)S(1)} %pad_maximum_fusion.4), channel_id=1, source_target_pairs={{0,16},{16,32},{32,48},{48,64},{64,80},{80,96},{96,112},{112,128},... | collective-permute-start | bytes 24584 | tf_op jit(solution)/shard_map/ppermute | solution.py:415
  11.5 12.8 %copy-start.28 = (s32[512]{0:T(512)S(1)}, s32[512]{0:T(512)}, u32[]{:S(2)}) copy-start(s32[512]{0:T(512)} %param.16) | copy-start | bytes 6148
  11.5 46.9 %copy-start.29 = (f32[8]{0:T(128)S(1)}, f32[8]{0:T(128)}, u32[]{:S(2)}) copy-start(f32[8]{0:T(128)} %param.27) | copy-start | bytes 100
  11.5 82.3 %all-to-all-start = ((bf16[8,800,256]{2,1,0:T(8,128)(2,1)}), bf16[8,800,256]{2,1,0:T(8,128)(2,1)S(1)}, u32[]{:S(2)}, u32[]{:S(2)}) async-start(bf16[8,800,256]{2,1,0:T(8,128)(2,1)} %pad_maximum_fusion), calls=%async_computation | async-start | bytes 6553600 | tf_op jit(solution)/shard_map/all_to_all | solution.py:420
  19.3 32.1 %collective-permute-start.2 = (bf16[512,128]{1,0:T(8,128)(2,1)S(1)}, bf16[512,128]{1,0:T(8,128)(2,1)S(1)}, u32[]{:S(2)}, u32[]{:S(2)}) collective-permute-start(bf16[512,128]{1,0:T(8,128)(2,1)S(1)} %get-tuple-element.82), channel_id=1, source_target_pairs={{0,128},{16,144},{32,160},{48,176},{64,192},{80,208},{96,224},{112... | collective-permute-start | bytes 393224 | tf_op jit(solution)/shard_map/ppermute | solution.py:424
  22.2 29.2 %collective-permute-start.1 = (bf16[512,128]{1,0:T(8,128)(2,1)S(1)}, bf16[512,128]{1,0:T(8,128)(2,1)S(1)}, u32[]{:S(2)}, u32[]{:S(2)}) collective-permute-start(bf16[512,128]{1,0:T(8,128)(2,1)S(1)} %get-tuple-element.81), channel_id=1, source_target_pairs={{0,1},{1,0},{2,3},{3,2},{4,5},{5,4},{6,7},{7,6},{8,9},{9,8},{10,11... | collective-permute-start | bytes 393224 | tf_op jit(solution)/shard_map/ppermute | solution.py:411
  52.0 0.8 copy-start.26
  52.8 8.7 %collective-permute-start.3 = (bf16[1536,128]{1,0:T(8,128)(2,1)}, bf16[1536,128]{1,0:T(8,128)(2,1)}, u32[]{:S(2)}, u32[]{:S(2)}) collective-permute-start(bf16[1536,128]{1,0:T(8,128)(2,1)} %pad_maximum_fusion.1), channel_id=1, source_target_pairs={{0,16},{16,32},{32,48},{48,64},{64,80},{80,96},{96,112},{112,0},{1... | collective-permute-start | bytes 1179656 | tf_op jit(solution)/shard_map/ppermute | solution.py:429
  52.8 8.8 %collective-permute-start.4 = (bf16[1536,128]{1,0:T(8,128)(2,1)}, bf16[1536,128]{1,0:T(8,128)(2,1)}, u32[]{:S(2)}, u32[]{:S(2)}) collective-permute-start(bf16[1536,128]{1,0:T(8,128)(2,1)} %pad_maximum_fusion.1), channel_id=1, source_target_pairs={{0,112},{16,0},{32,16},{48,32},{64,48},{80,64},{96,80},{112,96},{1... | collective-permute-start | bytes 1179656 | tf_op jit(solution)/shard_map/ppermute | solution.py:429
  58.5 2.9 %copy-start.25 = (bf16[512,128]{1,0:T(8,128)(2,1)S(1)}, bf16[512,128]{1,0:T(8,128)(2,1)}, u32[]{:S(2)}) copy-start(bf16[512,128]{1,0:T(8,128)(2,1)} %copy-done.24) | copy-start | bytes 393220
  58.5 2.9 %copy-start.27 = (bf16[512,128]{1,0:T(8,128)(2,1)S(1)}, bf16[512,128]{1,0:T(8,128)(2,1)}, u32[]{:S(2)}) copy-start(bf16[512,128]{1,0:T(8,128)(2,1)} %copy-done.26) | copy-start | bytes 393220
  61.5 12.5 %collective-permute-start.5 = (bf16[1536,128]{1,0:T(8,128)(2,1)}, bf16[1536,128]{1,0:T(8,128)(2,1)S(1)}, u32[]{:S(2)}, u32[]{:S(2)}) collective-permute-start(bf16[1536,128]{1,0:T(8,128)(2,1)} %collective-permute-done.3), channel_id=1, source_target_pairs={{0,16},{16,32},{32,48},{48,64},{64,80},{80,96},{96,112},{112,0},{1... | collective-permute-start | bytes 1179656 | tf_op jit(solution)/shard_map/ppermute | solution.py:429
  61.6 12.4 %collective-permute-start.6 = (bf16[1536,128]{1,0:T(8,128)(2,1)}, bf16[1536,128]{1,0:T(8,128)(2,1)S(1)}, u32[]{:S(2)}, u32[]{:S(2)}) collective-permute-start(bf16[1536,128]{1,0:T(8,128)(2,1)} %collective-permute-done.4), channel_id=1, source_target_pairs={{0,112},{16,0},{32,16},{48,32},{64,48},{80,64},{96,80},{112,96},{1... | collective-permute-start | bytes 1179656 | tf_op jit(solution)/shard_map/ppermute | solution.py:429
  74.1 11.0 %collective-permute-start.7 = (bf16[1536,128]{1,0:T(8,128)(2,1)S(1)}, bf16[1536,128]{1,0:T(8,128)(2,1)S(1)}, u32[]{:S(2)}, u32[]{:S(2)}) collective-permute-start(bf16[1536,128]{1,0:T(8,128)(2,1)S(1)} %collective-permute-done.5), channel_id=1, source_target_pairs={{0,16},{16,32},{32,48},{48,64},{64,80},{80,96},{96,112},{112,0},{1... | collective-permute-start | bytes 1179656 | tf_op jit(solution)/shard_map/ppermute | solution.py:429
  74.1 11.2 %collective-permute-start.8 = (bf16[1536,128]{1,0:T(8,128)(2,1)S(1)}, bf16[1536,128]{1,0:T(8,128)(2,1)S(1)}, u32[]{:S(2)}, u32[]{:S(2)}) collective-permute-start(bf16[1536,128]{1,0:T(8,128)(2,1)S(1)} %collective-permute-done.6), channel_id=1, source_target_pairs={{0,112},{16,0},{32,16},{48,32},{64,48},{80,64},{96,80},{112,96},{1... | collective-permute-start | bytes 1179656 | tf_op jit(solution)/shard_map/ppermute | solution.py:429
  76.8 34.4 %copy-start.15 = (f32[4,512]{1,0:T(4,128)S(1)}, f32[4,512]{1,0:T(4,128)}, u32[]{:S(2)}) copy-start(f32[4,512]{1,0:T(4,128)} %taps_x) | copy-start | bytes 24580
  76.8 34.4 %copy-start.16 = (f32[512]{0:T(512)S(1)}, f32[512]{0:T(512)}, u32[]{:S(2)}) copy-start(f32[512]{0:T(512)} %param.22) | copy-start | bytes 6148
  76.8 34.4 %copy-start.17 = (f32[8]{0:T(128)S(1)}, f32[8]{0:T(128)}, u32[]{:S(2)}) copy-start(f32[8]{0:T(128)} %param.25) | copy-start | bytes 100
  76.8 34.4 %copy-start.18 = (f32[8]{0:T(128)S(1)}, f32[8]{0:T(128)}, u32[]{:S(2)}) copy-start(f32[8]{0:T(128)} %param.26) | copy-start | bytes 100
  85.1 5.8 %collective-permute-start.9 = (bf16[768,128]{1,0:T(8,128)(2,1)S(1)}, bf16[768,128]{1,0:T(8,128)(2,1)S(1)}, u32[]{:S(2)}, u32[]{:S(2)}) collective-permute-start(bf16[768,128]{1,0:T(8,128)(2,1)S(1)} %slice.66), channel_id=1, source_target_pairs={{0,16},{16,32},{32,48},{48,64},{64,80},{80,96},{96,112},{112,0},{1... | collective-permute-start | bytes 589832 | tf_op jit(solution)/shard_map/ppermute | solution.py:429
  85.2 5.7 %collective-permute-start.10 = (bf16[768,128]{1,0:T(8,128)(2,1)S(1)}, bf16[768,128]{1,0:T(8,128)(2,1)S(1)}, u32[]{:S(2)}, u32[]{:S(2)}) collective-permute-start(bf16[768,128]{1,0:T(8,128)(2,1)S(1)} %slice.67), channel_id=1, source_target_pairs={{0,112},{16,0},{32,16},{48,32},{64,48},{80,64},{96,80},{112,96},{1... | collective-permute-start | bytes 589832 | tf_op jit(solution)/shard_map/ppermute | solution.py:429
  92.1 1.7 copy-start.1
  93.8 17.4 %collective-permute-start.11 = (bf16[8,800,256]{2,1,0:T(8,128)(2,1)S(1)}, bf16[8,800,256]{2,1,0:T(8,128)(2,1)S(1)}, u32[]{:S(2)}, u32[]{:S(2)}) collective-permute-start(bf16[8,800,256]{2,1,0:T(8,128)(2,1)S(1)} %all-to-all-done.own), channel_id=1, source_target_pairs={{0,1},{1,0},{2,3},{3,2},{4,5},{5,4},{6,7},{7,6},{8,9},{9,8},{10,11... | collective-permute-start | bytes 9830408 | tf_op jit(solution)/shard_map/ppermute | solution.py:411
  105.7 53.1 %collective-permute-start.12 = (bf16[8,512,128]{2,1,0:T(8,128)(2,1)}, bf16[8,512,128]{2,1,0:T(8,128)(2,1)}, u32[]{:S(2)}, u32[]{:S(2)}) collective-permute-start(bf16[8,512,128]{2,1,0:T(8,128)(2,1)} %slice.68), channel_id=1, source_target_pairs={{0,128},{16,144},{32,160},{48,176},{64,192},{80,208},{96,224},{112... | collective-permute-start | bytes 3145736 | tf_op jit(solution)/shard_map/ppermute | solution.py:424
  111.2 1.0 copy-start.9
  112.1 2.2 %copy-start.14 = (bf16[4096,512]{1,0:T(8,128)(2,1)S(1)}, bf16[4096,512]{1,0:T(8,128)(2,1)}, u32[]{:S(2)}) copy-start(bf16[4096,512]{1,0:T(8,128)(2,1)} %w_x.1) | copy-start | bytes 12582916
  114.3 11.0 %copy-start.5 = (bf16[8,800,256]{2,1,0:T(8,128)(2,1)}, bf16[8,800,256]{2,1,0:T(8,128)(2,1)S(1)}, u32[]{:S(2)}) copy-start(bf16[8,800,256]{2,1,0:T(8,128)(2,1)S(1)} %collective-permute-done.11.sib) | copy-start | bytes 9830404
  125.4 16.1 %all-to-all-start.1 = ((bf16[16,16,512]{2,1,0:T(8,128)(2,1)}), bf16[16,16,512]{2,1,0:T(8,128)(2,1)}, u32[]{:S(2)}, u32[]{:S(2)}) async-start(bf16[16,16,512]{2,1,0:T(8,128)(2,1)} %get-tuple-element.57), calls=%async_computation.1 | async-start | bytes 524288 | tf_op jit(solution)/shard_map/all_to_all | solution.py:452
  132.4 2.2 %copy-start.3 = (bf16[4096,512]{1,0:T(8,128)(2,1)S(1)}, bf16[4096,512]{1,0:T(8,128)(2,1)}, u32[]{:S(2)}) copy-start(bf16[4096,512]{1,0:T(8,128)(2,1)} %w_z.1) | copy-start | bytes 12582916
  134.6 1.9 copy-start.6
  136.6 14.1 %copy-start.23 = (f32[16,512]{1,0:T(8,128)S(1)}, f32[16,512]{1,0:T(8,128)}, u32[]{:S(2)}) copy-start(f32[16,512]{1,0:T(8,128)} %get-tuple-element.65.hrow) | copy-start | bytes 98308
  141.4 17.4 %copy-start.13 = (f32[512]{0:T(512)S(1)}, f32[512]{0:T(512)}, u32[]{:S(2)}) copy-start(f32[512]{0:T(512)} %param.28) | copy-start | bytes 6148
  143.1 15.7 %all-to-all-start.2 = ((bf16[16,8,512]{2,1,0:T(8,128)(2,1)}), bf16[16,8,512]{2,1,0:T(8,128)(2,1)S(1)}, u32[]{:S(2)}, u32[]{:S(2)}) async-start(bf16[16,8,512]{2,1,0:T(8,128)(2,1)} %bitcast.29), calls=%async_computation.2 | async-start | bytes 262144 | tf_op jit(solution)/shard_map/all_to_all | solution.py:452
  150.6 1.0 copy-start.10
  151.6 1.0 copy-start.19
  152.6 0.9 copy-start.20
  153.6 0.9 copy-start.21
  154.5 0.9 copy-start.22
  155.4 12.6 %copy-start.2 = (bf16[8,1536,128]{2,1,0:T(8,128)(2,1)S(1)}, bf16[8,1536,128]{2,1,0:T(8,128)(2,1)}, u32[]{:S(2)}) copy-start(bf16[8,1536,128]{2,1,0:T(8,128)(2,1)} %copy-done.1) | copy-start | bytes 9437188
  157.2 1.0 copy-start.7
  158.1 0.7 copy-start.11
  158.8 1.2 copy-start.4
  160.1 1.2 copy-start.8
  161.3 0.9 copy-start.12
  164.4 3.6 %collective-permute-start.13 = (bf16[512,640]{1,0:T(8,128)(2,1)}, bf16[512,640]{1,0:T(8,128)(2,1)}, u32[]{:S(2)}, u32[]{:S(2)}) collective-permute-start(bf16[512,640]{1,0:T(8,128)(2,1)} %join.1.own), channel_id=1, source_target_pairs={{0,1},{1,0},{2,3},{3,2},{4,5},{5,4},{6,7},{7,6},{8,9},{9,8},{10,11... | collective-permute-start | bytes 1966088 | tf_op jit(solution)/shard_map/ppermute | solution.py:411
  209.4 3.3 %collective-permute-start.14 = (bf16[512,128]{1,0:T(8,128)(2,1)S(1)}, bf16[512,128]{1,0:T(8,128)(2,1)S(1)}, u32[]{:S(2)}, u32[]{:S(2)}) collective-permute-start(bf16[512,128]{1,0:T(8,128)(2,1)S(1)} %broadcast_select_fusion.2), channel_id=1, source_target_pairs={{0,1},{1,0},{2,3},{3,2},{4,5},{5,4},{6,7},{7,6},{8,9},{9,8},{10,11... | collective-permute-start | bytes 393224 | tf_op jit(solution)/shard_map/ppermute | solution.py:411
  212.8 0.7 copy-start.30
  (1 other events, 0.7 us)

commit v10 on v9

--- a/solution.py
+++ b/solution.py
@@ -399,7 +399,7 @@
             out_specs=pl.BlockSpec((1, ROWS, 256), sent),
         ),
         out_shape=jax.ShapeDtypeStruct((CHIPS, ROWS, 256), BF16),
-        compiler_params=params(14, True),
+        compiler_params=params(56, True),
         cost_estimate=pl.CostEstimate(
             flops=8 * ROWS * CH * 2048, bytes_accessed=8 * 2**20, transcendentals=0
         ),
@@ -493,6 +493,10 @@
     chip = rank // CORES
     y_low = (lax.axis_index("ctx") // Z_RING).astype(jnp.int32)
 
+    halves = (w_out[:, :128], w_out[:, 128:])
+    w_kept, w_given = pick(core, *halves), pick(core, halves[1], halves[0])
+    w_own_far = across_y(w_kept)
+
     w_cols = jnp.concatenate(
         [w_bc.T.reshape(CHIPS, 2 * N, FEAT), w_dt.T.reshape(CHIPS, 2 * HEADS, FEAT)], axis=1
     )
@@ -502,15 +506,12 @@
     shared = jnp.concatenate([halo, tokens], axis=0)
     shared = jnp.broadcast_to(shared[None], (CHIPS, ALL_ROWS, FEAT))
     sent = jnp.concatenate([shared, w_cols], axis=1)
-    sent, w_out, seg_ids, conv_bc, conv_bc_bias, skip_gain = together(
-        sent, w_out, seg_ids, conv_bc, conv_bc_bias, skip_gain
+    sent, w_own_far, w_given, seg_ids, conv_bc, conv_bc_bias, skip_gain = together(
+        sent, w_own_far, w_given, seg_ids, conv_bc, conv_bc_bias, skip_gain
     )
     own = between_chips(sent)
 
-    halves = (w_out[:, :128], w_out[:, 128:])
-    w_kept = pick(core, *halves)
-    w_own_far = across_y(w_kept)
-    w_sib = swapped(pick(core, halves[1], halves[0]), 1)
+    w_sib = swapped(w_given, 1)
     w_held = gathered_along_z(jnp.concatenate([w_kept, w_sib, w_own_far], axis=0))
 
     cols, seg_row = document_columns(seg_ids, ids_prior)
@@ -525,13 +526,12 @@
     w_late = across_y(w_rest)
     sib = swapped(own, 1)
     xc, bcc, hcol, hrow, s0, pay = scan_input(own, sib, w_x, fixed)
-    own, sib, pay = together(own, sib, pay)
+    own, sib, pay, w_late = together(own, sib, pay, w_late)
     pieces = between_slabs(pay)
     gates = gate(own, sib, w_z)
     pieces, gates, xc, bcc = together(pieces, gates, xc, bcc)
     state = between_slabs(prefix(pieces).reshape(CTX, 8, CH)).reshape(N, CH)
     y, cc, decays = intra(xc, bcc, hcol, hrow, s0, fixed[0], seg_row, skip)
-    state, w_late, w_held = together(state, w_late, w_held)
     mine = join(y, gates, cc, decays, state, norm_weight[None])
     parts = between_chips(project(mine, swapped(mine, 1), w_held, w_late, y_low))
     total = jnp.sum(parts.astype(F32), axis=0).astype(BF16)

time: 215 us -> 187 us (0.87)
  waiting for transfers between devices: 52.9 us -> 35.9 us
  starting transfers between devices: 57.5 us -> 48.1 us
  local copies, waits for them, and re-layouts: 32.2 us -> 28.8 us
    ppermute x2, waiting for transfers between devices: 25.7 us -> 5.04 us  [across_y(): return lax.ppermute(value, 'ctx', [(i, i ^ Z_RING) for i in range(CTX)])]
    ppermute x4, starting transfers between devices: 17.9 us -> 10.4 us  [swapped(): return lax.ppermute(value, 'tp', [(i, i ^ bit) for i in range(16)])]
    unnamed x62 -> x60, local copies, waits for them, and re-layouts: 20.2 us -> 16.7 us
  transfers between devices with their start and end apart: 18 -> 18, of which waited for: 7 -> 11; matrix products, arithmetic and copies ran while one was open for 7% -> 10% of each run, Pallas kernels for 9% -> 9%
where the time goes in v10:
time: 187 us; the launch traced here: 185 us
  starting transfers between devices  48.1 us (26%)
  waiting for transfers between devices  35.9 us (19%)
  blocking collectives  33.9 us (18%)
  Pallas kernels  29.8 us (16%)
  local copies, waits for them, and re-layouts  28.8 us (15%)
  other arithmetic  8.56 us (5%)
    all_to_all x1, blocking collectives, between_chips(): return lax.all_to_all(value, 'tp', 0, 0, axis_index_groups=same_core)  33.9 us
    ppermute x8, waiting for transfers between devices, along_z(): return lax.ppermute(value, 'ctx', pairs)  20.3 us
    unnamed x60, local copies, waits for them, and re-layouts  16.7 us
    pallas_call x2, Pallas kernels, over_chips(): pl.pallas_call(kernel, grid=(CHIPS // 2,), in_specs=[spec for _, spec in...  15.9 us
    all_to_all x2, starting transfers between devices, between_slabs(): return lax.all_to_all(value, 'ctx', 0, 0)  14.5 us
    ppermute x8, starting transfers between devices, along_z(): return lax.ppermute(value, 'ctx', pairs)  11.1 us
    ppermute x4, starting transfers between devices, swapped(): return lax.ppermute(value, 'tp', [(i, i ^ bit) for i in range(16)])  10.4 us
    pallas_call x1, Pallas kernels, project(): pl.pallas_call(project_kernel, grid_spec=pltpu.PrefetchScalarGridSpec(num...  9.15 us
  transfers between devices with their start and end apart: 18, of which 11 were waited for; matrix products, arithmetic and copies ran while one was open for 10% of the time, Pallas kernels for 9%

profile of v10, /device:TPU:1, one launch (start us, length us, event | category | flops | bytes accessed | tf_op | source)
XLA Modules:
  0.0 185.5 jit_solution(12827119863297109459)
XLA Ops:
  1.6 4.4 %collective-permute-start = (bf16[16,256]{1,0:T(8,128)(2,1)S(1)}, bf16[16,256]{1,0:T(8,128)(2,1)S(1)}, u32[]{:S(2)}, u32[]{:S(2)}) collective-permute-start(bf16[16,256]{1,0:T(8,128)(2,1)S(1)} %pad_maximum_fusion.4), channel_id=1, source_target_pairs={{0,16},{16,32},{32,48},{48,64},{64,80},{80,96},{96,112},{112,128},... | collective-permute-start | bytes 24584 | tf_op jit(solution)/shard_map/ppermute | solution.py:415
  6.0 1.6 broadcast_select_fusion.4
  7.6 1.3 collective-permute-start.1
  9.8 1.5 copy.28
  12.3 1.8 pad_maximum_fusion
  14.7 6.4 %all-to-all-start = ((bf16[8,800,256]{2,1,0:T(8,128)(2,1)}), bf16[8,800,256]{2,1,0:T(8,128)(2,1)S(1)}, u32[]{:S(2)}, u32[]{:S(2)}) async-start(bf16[8,800,256]{2,1,0:T(8,128)(2,1)} %pad_maximum_fusion), calls=%async_computation | async-start | bytes 6553600 | tf_op jit(solution)/shard_map/all_to_all | solution.py:420
  21.1 1.5 collective-permute-start.2
  24.4 1.7 pad_maximum_fusion.1
  26.1 1.6 collective-permute-start.3
  27.8 1.4 collective-permute-start.4
  29.2 2.0 %compare_convert_fusion = (f32[512]{0:T(512)S(1)}, f32[512]{0:T(512)S(1)}, f32[512]{0:T(512)S(1)}, f32[512]{0:T(512)S(1)}, f32[512]{0:T(512)S(1)}, /*index=5*/f32[512]{0:T(512)S(1)}) fusion(s32[512]{0:T(512)S(1)} %copy-done.25, s32[]{:T(128)} %bitcast.22, s32[]{:T(128)} %bitcast.20, s32[]{:T(128)} %bitcast.18, s32[515]{0:T(1024)S(1)} %pad_add_fusion), kind=kLoop, calls=%fused_computation.28 | loop fusion | flops 6144 | bytes 20492 | tf_op jit(solution)/shard_map/stack | solution.py:470
  32.2 1.7 pad.9.cols
  35.2 3.5 %collective-permute-done.3 = bf16[1536,128]{1,0:T(8,128)(2,1)} collective-permute-done((bf16[1536,128]{1,0:T(8,128)(2,1)}, bf16[1536,128]{1,0:T(8,128)(2,1)}, u32[]{:S(2)}, u32[]{:S(2)}) %collective-permute-start.3) | collective-permute-done | bytes 393248 | tf_op jit(solution)/shard_map/ppermute | solution.py:429
  38.7 2.7 %collective-permute-start.6 = (bf16[1536,128]{1,0:T(8,128)(2,1)}, bf16[1536,128]{1,0:T(8,128)(2,1)S(1)}, u32[]{:S(2)}, u32[]{:S(2)}) collective-permute-start(bf16[1536,128]{1,0:T(8,128)(2,1)} %collective-permute-done.4), channel_id=1, source_target_pairs={{0,112},{16,0},{32,16},{48,32},{64,48},{80,64},{96,80},{112,96},{1... | collective-permute-start | bytes 1179656 | tf_op jit(solution)/shard_map/ppermute | solution.py:429
  41.4 1.0 bitcast_dynamic-update-slice_fusion.5
  42.4 1.1 bitcast_dynamic-update-slice_fusion.4
  43.5 6.4 %collective-permute-done.5 = bf16[1536,128]{1,0:T(8,128)(2,1)S(1)} collective-permute-done((bf16[1536,128]{1,0:T(8,128)(2,1)}, bf16[1536,128]{1,0:T(8,128)(2,1)S(1)}, u32[]{:S(2)}, u32[]{:S(2)}) %collective-permute-start.5) | collective-permute-done | bytes 393248 | tf_op jit(solution)/shard_map/ppermute | solution.py:429
  49.9 2.6 %collective-permute-start.8 = (bf16[1536,128]{1,0:T(8,128)(2,1)S(1)}, bf16[1536,128]{1,0:T(8,128)(2,1)S(1)}, u32[]{:S(2)}, u32[]{:S(2)}) collective-permute-start(bf16[1536,128]{1,0:T(8,128)(2,1)S(1)} %collective-permute-done.6), channel_id=1, source_target_pairs={{0,112},{16,0},{32,16},{48,32},{64,48},{80,64},{96,80},{112,96},{1... | collective-permute-start | bytes 1179656 | tf_op jit(solution)/shard_map/ppermute | solution.py:429
  52.7 7.2 %collective-permute-done.7 = bf16[1536,128]{1,0:T(8,128)(2,1)S(1)} collective-permute-done((bf16[1536,128]{1,0:T(8,128)(2,1)S(1)}, bf16[1536,128]{1,0:T(8,128)(2,1)S(1)}, u32[]{:S(2)}, u32[]{:S(2)}) %collective-permute-start.7) | collective-permute-done | bytes 393248 | tf_op jit(solution)/shard_map/ppermute | solution.py:429
  60.0 2.7 %collective-permute-start.10 = (bf16[768,128]{1,0:T(8,128)(2,1)S(1)}, bf16[768,128]{1,0:T(8,128)(2,1)S(1)}, u32[]{:S(2)}, u32[]{:S(2)}) collective-permute-start(bf16[768,128]{1,0:T(8,128)(2,1)S(1)} %slice.67), channel_id=1, source_target_pairs={{0,112},{16,0},{32,16},{48,32},{64,48},{80,64},{96,80},{112,96},{1... | collective-permute-start | bytes 589832 | tf_op jit(solution)/shard_map/ppermute | solution.py:429
  62.9 3.1 %collective-permute-done.9 = bf16[768,128]{1,0:T(8,128)(2,1)S(1)} collective-permute-done((bf16[768,128]{1,0:T(8,128)(2,1)S(1)}, bf16[768,128]{1,0:T(8,128)(2,1)S(1)}, u32[]{:S(2)}, u32[]{:S(2)}) %collective-permute-start.9) | collective-permute-done | bytes 196640 | tf_op jit(solution)/shard_map/ppermute | solution.py:429
  66.1 1.7 copy-done.19
  67.8 1.0 slice.68
  68.8 3.5 %collective-permute-start.11 = (bf16[8,800,256]{2,1,0:T(8,128)(2,1)S(1)}, bf16[8,800,256]{2,1,0:T(8,128)(2,1)S(1)}, u32[]{:S(2)}, u32[]{:S(2)}) collective-permute-start(bf16[8,800,256]{2,1,0:T(8,128)(2,1)S(1)} %all-to-all-done.own), channel_id=1, source_target_pairs={{0,1},{1,0},{2,3},{3,2},{4,5},{5,4},{6,7},{7,6},{8,9},{9,8},{10,11... | collective-permute-start | bytes 9830408 | tf_op jit(solution)/shard_map/ppermute | solution.py:411
  72.4 5.5 %collective-permute-done.11.sib = bf16[8,800,256]{2,1,0:T(8,128)(2,1)S(1)} collective-permute-done((bf16[8,800,256]{2,1,0:T(8,128)(2,1)S(1)}, bf16[8,800,256]{2,1,0:T(8,128)(2,1)S(1)}, u32[]{:S(2)}, u32[]{:S(2)}) %collective-permute-start.11) | collective-permute-done | bytes 3276832 | tf_op jit(solution)/shard_map/ppermute | solution.py:411
  77.9 0.9 copy-done.6
  78.8 2.2 %copy-done.9 = bf16[4096,512]{1,0:T(8,128)(2,1)S(1)} copy-done((bf16[4096,512]{1,0:T(8,128)(2,1)S(1)}, bf16[4096,512]{1,0:T(8,128)(2,1)}, u32[]{:S(2)}) %copy-start.9) | copy-done | bytes 4194328
  81.0 11.0 %scan_input.1 = (bf16[512,512]{1,0:T(8,128)(2,1)}, bf16[512,256]{1,0:T(8,128)(2,1)}, f32[512,128]{1,0:T(8,128)}, f32[16,512]{1,0:T(8,128)}, bf16[128,512]{1,0:T(8,128)(2,1)}, /*index=5*/bf16[16,16,512]{2,1,0:T(8,128)(2,1)}) custom-call(bf16[8,800,256]{2,1,0:T(8,128)(2,1)S(1)} %all-to-all-done.own, bf16[8,800,256]{2,1,0:T(8,128)(2,1)S(1)} %collective-permute-done.11.sib, ...), custom_call_target="tpu_custom_call" | custom-call | flops 3391094784 | bytes 8388608 | tf_op jit(solution)/shard_map/scan_input/pallas_call | solution.py:198
  92.0 5.0 %collective-permute-done.12.far_sib = bf16[8,512,128]{2,1,0:T(8,128)(2,1)S(1)} collective-permute-done((bf16[8,512,128]{2,1,0:T(8,128)(2,1)}, bf16[8,512,128]{2,1,0:T(8,128)(2,1)S(1)}, u32[]{:S(2)}, u32[]{:S(2)}) %collective-permute-start.12) | collective-permute-done | bytes 1048608 | tf_op jit(solution)/shard_map/ppermute | solution.py:424
  97.1 1.0 copy-done.27
  98.1 7.0 %all-to-all-start.1 = ((bf16[16,16,512]{2,1,0:T(8,128)(2,1)}), bf16[16,16,512]{2,1,0:T(8,128)(2,1)}, u32[]{:S(2)}, u32[]{:S(2)}) async-start(bf16[16,16,512]{2,1,0:T(8,128)(2,1)} %get-tuple-element.58), calls=%async_computation.1 | async-start | bytes 524288 | tf_op jit(solution)/shard_map/all_to_all | solution.py:452
  105.1 2.2 %copy-done.1 = bf16[4096,512]{1,0:T(8,128)(2,1)S(1)} copy-done((bf16[4096,512]{1,0:T(8,128)(2,1)S(1)}, bf16[4096,512]{1,0:T(8,128)(2,1)}, u32[]{:S(2)}) %copy-start.1) | copy-done | bytes 4194328
  107.3 1.9 %copy-done.4 = bf16[8,800,256]{2,1,0:T(8,128)(2,1)S(1)} copy-done((bf16[8,800,256]{2,1,0:T(8,128)(2,1)S(1)}, bf16[8,800,256]{2,1,0:T(8,128)(2,1)}, u32[]{:S(2)}) %copy-start.4) | copy-done | bytes 3276824
  109.2 4.9 %gate.1.gates = f32[512,512]{1,0:T(8,128)} custom-call(bf16[8,800,256]{2,1,0:T(8,128)(2,1)S(1)} %all-to-all-done.own, bf16[8,800,256]{2,1,0:T(8,128)(2,1)S(1)} %copy-done.4, bf16[4096,512]{1,0:T(8,128)(2,1)S(1)} %copy-done.1), custom_call_target="tpu_custom_call" | custom-call | flops 2147483648 | bytes 8388608 | tf_op jit(solution)/shard_map/gate/pallas_call | solution.py:198
  114.1 1.8 prefix.1
  115.8 7.5 %all-to-all-start.2 = ((bf16[16,8,512]{2,1,0:T(8,128)(2,1)}), bf16[16,8,512]{2,1,0:T(8,128)(2,1)S(1)}, u32[]{:S(2)}, u32[]{:S(2)}) async-start(bf16[16,8,512]{2,1,0:T(8,128)(2,1)} %bitcast.29), calls=%async_computation.2 | async-start | bytes 262144 | tf_op jit(solution)/shard_map/all_to_all | solution.py:452
  124.3 1.0 copy-done.14
  125.3 0.9 copy-done.15
  126.3 0.9 copy-done.16
  127.2 1.7 intra.1
  129.0 1.9 %all-to-all-done.2 = bf16[16,8,512]{2,1,0:T(8,128)(2,1)S(1)} async-done(((bf16[16,8,512]{2,1,0:T(8,128)(2,1)}), bf16[16,8,512]{2,1,0:T(8,128)(2,1)S(1)}, u32[]{:S(2)}, u32[]{:S(2)}) %all-to-all-start.2) | async-done | bytes 131104 | tf_op jit(solution)/shard_map/all_to_all | solution.py:452
  130.9 1.3 join.1.own
  132.2 3.1 %collective-permute-start.13 = (bf16[512,640]{1,0:T(8,128)(2,1)S(1)}, bf16[512,640]{1,0:T(8,128)(2,1)S(1)}, u32[]{:S(2)}, u32[]{:S(2)}) collective-permute-start(bf16[512,640]{1,0:T(8,128)(2,1)S(1)} %join.1.own), channel_id=1, source_target_pairs={{0,1},{1,0},{2,3},{3,2},{4,5},{5,4},{6,7},{7,6},{8,9},{9,8},{10,11... | collective-permute-start | bytes 1966088 | tf_op jit(solution)/shard_map/ppermute | solution.py:411
  135.2 1.7 collective-permute-done.13.sib
  137.9 9.1 %project.1 = bf16[8,512,256]{2,1,0:T(8,128)(2,1)} custom-call(s32[1]{0:T(128)} %bitcast.place, bf16[512,640]{1,0:T(8,128)(2,1)} %copy-done.5, bf16[512,640]{1,0:T(8,128)(2,1)} %copy-done.28, bf16[8,1536,128]{2,1,0:T(8,128)(2,1)} %copy-done.19, bf16[8,1536,128]{2,1,0:T(8,128)(2,1)} %copy-done.19, bf16[8,512,128]{2,1,0:T(8,128)(2,1)} %copy-done.27), custom_call_target="tpu_custom_call" | custom-call | flops 4294967296 | bytes 8388608 | tf_op jit(solution)/shard_map/project/pallas_call | solution.py:387
  147.0 33.9 %all_to_all.20 = bf16[8,512,256]{2,1,0:T(8,128)(2,1)S(1)} all-to-all(bf16[8,512,256]{2,1,0:T(8,128)(2,1)} %project.1), channel_id=1, replica_groups={{0,2,4,6,8,10,12,14},{1,3,5,7,9,11,13,15},{16,18,20,22,24,26,28,30},{17..., dimensions={0} | all-to-all | bytes 4194304 | tf_op jit(solution)/shard_map/all_to_all | solution.py:420
  181.4 2.3 %collective-permute-start.14 = (bf16[512,128]{1,0:T(8,128)(2,1)S(1)}, bf16[512,128]{1,0:T(8,128)(2,1)S(1)}, u32[]{:S(2)}, u32[]{:S(2)}) collective-permute-start(bf16[512,128]{1,0:T(8,128)(2,1)S(1)} %broadcast_select_fusion.2), channel_id=1, source_target_pairs={{0,1},{1,0},{2,3},{3,2},{4,5},{5,4},{6,7},{7,6},{8,9},{9,8},{10,11... | collective-permute-start | bytes 393224 | tf_op jit(solution)/shard_map/ppermute | solution.py:411
  183.7 1.0 collective-permute-done.14
  (98 shorter events, 11.7 us)
Async XLA Ops:
  0.0 34.7 %copy-start = (f32[4,2048]{1,0:T(4,128)S(1)}, f32[4,2048]{1,0:T(4,128)}, u32[]{:S(2)}) copy-start(f32[4,2048]{1,0:T(4,128)} %param.23) | copy-start | bytes 98308
  0.0 12.1 %copy-start.24 = (bf16[512,256]{1,0:T(8,128)(2,1)S(1)}, bf16[512,256]{1,0:T(8,128)(2,1)}, u32[]{:S(2)}) copy-start(bf16[512,256]{1,0:T(8,128)(2,1)} %param.15) | copy-start | bytes 786436
  1.6 9.8 %collective-permute-start = (bf16[16,256]{1,0:T(8,128)(2,1)S(1)}, bf16[16,256]{1,0:T(8,128)(2,1)S(1)}, u32[]{:S(2)}, u32[]{:S(2)}) collective-permute-start(bf16[16,256]{1,0:T(8,128)(2,1)S(1)} %pad_maximum_fusion.4), channel_id=1, source_target_pairs={{0,16},{16,32},{32,48},{48,64},{64,80},{80,96},{96,112},{112,128},... | collective-permute-start | bytes 24584 | tf_op jit(solution)/shard_map/ppermute | solution.py:415
  7.6 6.4 %collective-permute-start.1 = (bf16[512,128]{1,0:T(8,128)(2,1)S(1)}, bf16[512,128]{1,0:T(8,128)(2,1)S(1)}, u32[]{:S(2)}, u32[]{:S(2)}) collective-permute-start(bf16[512,128]{1,0:T(8,128)(2,1)S(1)} %get-tuple-element.80), channel_id=1, source_target_pairs={{0,128},{16,144},{32,160},{48,176},{64,192},{80,208},{96,224},{112... | collective-permute-start | bytes 393224 | tf_op jit(solution)/shard_map/ppermute | solution.py:424
  14.0 0.7 copy-start.20
  14.0 8.5 %copy-start.25 = (s32[512]{0:T(512)S(1)}, s32[512]{0:T(512)}, u32[]{:S(2)}) copy-start(s32[512]{0:T(512)} %param.16) | copy-start | bytes 6148
  14.1 18.0 %copy-start.26 = (f32[8]{0:T(128)S(1)}, f32[8]{0:T(128)}, u32[]{:S(2)}) copy-start(f32[8]{0:T(128)} %param.27) | copy-start | bytes 100
  14.7 54.1 %all-to-all-start = ((bf16[8,800,256]{2,1,0:T(8,128)(2,1)}), bf16[8,800,256]{2,1,0:T(8,128)(2,1)S(1)}, u32[]{:S(2)}, u32[]{:S(2)}) async-start(bf16[8,800,256]{2,1,0:T(8,128)(2,1)} %pad_maximum_fusion), calls=%async_computation | async-start | bytes 6553600 | tf_op jit(solution)/shard_map/all_to_all | solution.py:420
  21.1 2.7 %collective-permute-start.2 = (bf16[512,128]{1,0:T(8,128)(2,1)}, bf16[512,128]{1,0:T(8,128)(2,1)S(1)}, u32[]{:S(2)}, u32[]{:S(2)}) collective-permute-start(bf16[512,128]{1,0:T(8,128)(2,1)} %get-tuple-element.42), channel_id=1, source_target_pairs={{0,1},{1,0},{2,3},{3,2},{4,5},{5,4},{6,7},{7,6},{8,9},{9,8},{10,11... | collective-permute-start | bytes 393224 | tf_op jit(solution)/shard_map/ppermute | solution.py:411
  23.8 0.7 copy-start.22
  26.1 12.6 %collective-permute-start.3 = (bf16[1536,128]{1,0:T(8,128)(2,1)}, bf16[1536,128]{1,0:T(8,128)(2,1)}, u32[]{:S(2)}, u32[]{:S(2)}) collective-permute-start(bf16[1536,128]{1,0:T(8,128)(2,1)} %pad_maximum_fusion.1), channel_id=1, source_target_pairs={{0,16},{16,32},{32,48},{48,64},{64,80},{80,96},{96,112},{112,0},{1... | collective-permute-start | bytes 1179656 | tf_op jit(solution)/shard_map/ppermute | solution.py:429
  27.8 10.9 %collective-permute-start.4 = (bf16[1536,128]{1,0:T(8,128)(2,1)}, bf16[1536,128]{1,0:T(8,128)(2,1)}, u32[]{:S(2)}, u32[]{:S(2)}) collective-permute-start(bf16[1536,128]{1,0:T(8,128)(2,1)} %pad_maximum_fusion.1), channel_id=1, source_target_pairs={{0,112},{16,0},{32,16},{48,32},{64,48},{80,64},{96,80},{112,96},{1... | collective-permute-start | bytes 1179656 | tf_op jit(solution)/shard_map/ppermute | solution.py:429
  32.2 2.9 %copy-start.21 = (bf16[512,128]{1,0:T(8,128)(2,1)S(1)}, bf16[512,128]{1,0:T(8,128)(2,1)}, u32[]{:S(2)}) copy-start(bf16[512,128]{1,0:T(8,128)(2,1)} %copy-done.20) | copy-start | bytes 393220
  32.2 2.9 %copy-start.23 = (bf16[512,128]{1,0:T(8,128)(2,1)S(1)}, bf16[512,128]{1,0:T(8,128)(2,1)}, u32[]{:S(2)}) copy-start(bf16[512,128]{1,0:T(8,128)(2,1)} %copy-done.22) | copy-start | bytes 393220
  38.7 11.2 %collective-permute-start.5 = (bf16[1536,128]{1,0:T(8,128)(2,1)}, bf16[1536,128]{1,0:T(8,128)(2,1)S(1)}, u32[]{:S(2)}, u32[]{:S(2)}) collective-permute-start(bf16[1536,128]{1,0:T(8,128)(2,1)} %collective-permute-done.3), channel_id=1, source_target_pairs={{0,16},{16,32},{32,48},{48,64},{64,80},{80,96},{96,112},{112,0},{1... | collective-permute-start | bytes 1179656 | tf_op jit(solution)/shard_map/ppermute | solution.py:429
  38.7 11.3 %collective-permute-start.6 = (bf16[1536,128]{1,0:T(8,128)(2,1)}, bf16[1536,128]{1,0:T(8,128)(2,1)S(1)}, u32[]{:S(2)}, u32[]{:S(2)}) collective-permute-start(bf16[1536,128]{1,0:T(8,128)(2,1)} %collective-permute-done.4), channel_id=1, source_target_pairs={{0,112},{16,0},{32,16},{48,32},{64,48},{80,64},{96,80},{112,96},{1... | collective-permute-start | bytes 1179656 | tf_op jit(solution)/shard_map/ppermute | solution.py:429
  49.9 10.0 %collective-permute-start.7 = (bf16[1536,128]{1,0:T(8,128)(2,1)S(1)}, bf16[1536,128]{1,0:T(8,128)(2,1)S(1)}, u32[]{:S(2)}, u32[]{:S(2)}) collective-permute-start(bf16[1536,128]{1,0:T(8,128)(2,1)S(1)} %collective-permute-done.5), channel_id=1, source_target_pairs={{0,16},{16,32},{32,48},{48,64},{64,80},{80,96},{96,112},{112,0},{1... | collective-permute-start | bytes 1179656 | tf_op jit(solution)/shard_map/ppermute | solution.py:429
  49.9 10.1 %collective-permute-start.8 = (bf16[1536,128]{1,0:T(8,128)(2,1)S(1)}, bf16[1536,128]{1,0:T(8,128)(2,1)S(1)}, u32[]{:S(2)}, u32[]{:S(2)}) collective-permute-start(bf16[1536,128]{1,0:T(8,128)(2,1)S(1)} %collective-permute-done.6), channel_id=1, source_target_pairs={{0,112},{16,0},{32,16},{48,32},{64,48},{80,64},{96,80},{112,96},{1... | collective-permute-start | bytes 1179656 | tf_op jit(solution)/shard_map/ppermute | solution.py:429
  52.6 25.3 %copy-start.10 = (f32[4,512]{1,0:T(4,128)S(1)}, f32[4,512]{1,0:T(4,128)}, u32[]{:S(2)}) copy-start(f32[4,512]{1,0:T(4,128)} %taps_x) | copy-start | bytes 24580
  52.6 25.3 %copy-start.11 = (f32[512]{0:T(512)S(1)}, f32[512]{0:T(512)}, u32[]{:S(2)}) copy-start(f32[512]{0:T(512)} %param.22) | copy-start | bytes 6148
  52.6 25.2 %copy-start.12 = (f32[8]{0:T(128)S(1)}, f32[8]{0:T(128)}, u32[]{:S(2)}) copy-start(f32[8]{0:T(128)} %param.25) | copy-start | bytes 100
  52.6 25.2 %copy-start.13 = (f32[8]{0:T(128)S(1)}, f32[8]{0:T(128)}, u32[]{:S(2)}) copy-start(f32[8]{0:T(128)} %param.26) | copy-start | bytes 100
  59.9 6.1 %collective-permute-start.9 = (bf16[768,128]{1,0:T(8,128)(2,1)S(1)}, bf16[768,128]{1,0:T(8,128)(2,1)S(1)}, u32[]{:S(2)}, u32[]{:S(2)}) collective-permute-start(bf16[768,128]{1,0:T(8,128)(2,1)S(1)} %slice.66), channel_id=1, source_target_pairs={{0,16},{16,32},{32,48},{48,64},{64,80},{80,96},{96,112},{112,0},{1... | collective-permute-start | bytes 589832 | tf_op jit(solution)/shard_map/ppermute | solution.py:429
  60.0 6.0 %collective-permute-start.10 = (bf16[768,128]{1,0:T(8,128)(2,1)S(1)}, bf16[768,128]{1,0:T(8,128)(2,1)S(1)}, u32[]{:S(2)}, u32[]{:S(2)}) collective-permute-start(bf16[768,128]{1,0:T(8,128)(2,1)S(1)} %slice.67), channel_id=1, source_target_pairs={{0,112},{16,0},{32,16},{48,32},{64,48},{80,64},{96,80},{112,96},{1... | collective-permute-start | bytes 589832 | tf_op jit(solution)/shard_map/ppermute | solution.py:429
  66.1 1.7 copy-start.19
  68.8 9.0 %collective-permute-start.11 = (bf16[8,800,256]{2,1,0:T(8,128)(2,1)S(1)}, bf16[8,800,256]{2,1,0:T(8,128)(2,1)S(1)}, u32[]{:S(2)}, u32[]{:S(2)}) collective-permute-start(bf16[8,800,256]{2,1,0:T(8,128)(2,1)S(1)} %all-to-all-done.own), channel_id=1, source_target_pairs={{0,1},{1,0},{2,3},{3,2},{4,5},{5,4},{6,7},{7,6},{8,9},{9,8},{10,11... | collective-permute-start | bytes 9830408 | tf_op jit(solution)/shard_map/ppermute | solution.py:411
  72.4 24.7 %collective-permute-start.12 = (bf16[8,512,128]{2,1,0:T(8,128)(2,1)}, bf16[8,512,128]{2,1,0:T(8,128)(2,1)S(1)}, u32[]{:S(2)}, u32[]{:S(2)}) collective-permute-start(bf16[8,512,128]{2,1,0:T(8,128)(2,1)} %slice.68), channel_id=1, source_target_pairs={{0,128},{16,144},{32,160},{48,176},{64,192},{80,208},{96,224},{112... | collective-permute-start | bytes 3145736 | tf_op jit(solution)/shard_map/ppermute | solution.py:424
  77.9 1.0 copy-start.6
  78.8 2.2 %copy-start.9 = (bf16[4096,512]{1,0:T(8,128)(2,1)S(1)}, bf16[4096,512]{1,0:T(8,128)(2,1)}, u32[]{:S(2)}) copy-start(bf16[4096,512]{1,0:T(8,128)(2,1)} %w_x.1) | copy-start | bytes 12582916
  81.0 11.0 %copy-start.3 = (bf16[8,800,256]{2,1,0:T(8,128)(2,1)}, bf16[8,800,256]{2,1,0:T(8,128)(2,1)S(1)}, u32[]{:S(2)}) copy-start(bf16[8,800,256]{2,1,0:T(8,128)(2,1)S(1)} %collective-permute-done.11.sib) | copy-start | bytes 9830404
  97.1 1.0 copy-start.27
  98.1 16.0 %all-to-all-start.1 = ((bf16[16,16,512]{2,1,0:T(8,128)(2,1)}), bf16[16,16,512]{2,1,0:T(8,128)(2,1)}, u32[]{:S(2)}, u32[]{:S(2)}) async-start(bf16[16,16,512]{2,1,0:T(8,128)(2,1)} %get-tuple-element.58), calls=%async_computation.1 | async-start | bytes 524288 | tf_op jit(solution)/shard_map/all_to_all | solution.py:452
  105.1 2.2 %copy-start.1 = (bf16[4096,512]{1,0:T(8,128)(2,1)S(1)}, bf16[4096,512]{1,0:T(8,128)(2,1)}, u32[]{:S(2)}) copy-start(bf16[4096,512]{1,0:T(8,128)(2,1)} %w_z.1) | copy-start | bytes 12582916
  107.3 1.9 %copy-start.4 = (bf16[8,800,256]{2,1,0:T(8,128)(2,1)S(1)}, bf16[8,800,256]{2,1,0:T(8,128)(2,1)}, u32[]{:S(2)}) copy-start(bf16[8,800,256]{2,1,0:T(8,128)(2,1)} %copy-done.3) | copy-start | bytes 9830404
  109.2 14.1 %copy-start.17 = (bf16[128,512]{1,0:T(8,128)(2,1)S(1)}, bf16[128,512]{1,0:T(8,128)(2,1)}, u32[]{:S(2)}) copy-start(bf16[128,512]{1,0:T(8,128)(2,1)} %get-tuple-element.67.s0) | copy-start | bytes 393220
  109.2 14.1 %copy-start.18 = (f32[16,512]{1,0:T(8,128)S(1)}, f32[16,512]{1,0:T(8,128)}, u32[]{:S(2)}) copy-start(f32[16,512]{1,0:T(8,128)} %get-tuple-element.66.hrow) | copy-start | bytes 98308
  109.2 21.6 %copy-start.8 = (f32[512]{0:T(512)S(1)}, f32[512]{0:T(512)}, u32[]{:S(2)}) copy-start(f32[512]{0:T(512)} %param.28) | copy-start | bytes 6148
  114.1 16.8 %copy-start.2 = (f32[512,512]{1,0:T(8,128)S(1)}, f32[512,512]{1,0:T(8,128)}, u32[]{:S(2)}) copy-start(f32[512,512]{1,0:T(8,128)} %gate.1.gates) | copy-start | bytes 3145732
  115.8 15.0 %all-to-all-start.2 = ((bf16[16,8,512]{2,1,0:T(8,128)(2,1)}), bf16[16,8,512]{2,1,0:T(8,128)(2,1)S(1)}, u32[]{:S(2)}, u32[]{:S(2)}) async-start(bf16[16,8,512]{2,1,0:T(8,128)(2,1)} %bitcast.29), calls=%async_computation.2 | async-start | bytes 262144 | tf_op jit(solution)/shard_map/all_to_all | solution.py:452
  123.4 1.0 copy-start.7
  124.3 1.0 copy-start.14
  125.3 0.9 copy-start.15
  126.3 0.9 copy-start.16
  132.2 4.8 %copy-start.5 = (bf16[512,640]{1,0:T(8,128)(2,1)}, bf16[512,640]{1,0:T(8,128)(2,1)S(1)}, u32[]{:S(2)}) copy-start(bf16[512,640]{1,0:T(8,128)(2,1)S(1)} %join.1.own) | copy-start | bytes 1966084
  132.2 4.8 %collective-permute-start.13 = (bf16[512,640]{1,0:T(8,128)(2,1)S(1)}, bf16[512,640]{1,0:T(8,128)(2,1)S(1)}, u32[]{:S(2)}, u32[]{:S(2)}) collective-permute-start(bf16[512,640]{1,0:T(8,128)(2,1)S(1)} %join.1.own), channel_id=1, source_target_pairs={{0,1},{1,0},{2,3},{3,2},{4,5},{5,4},{6,7},{7,6},{8,9},{9,8},{10,11... | collective-permute-start | bytes 1966088 | tf_op jit(solution)/shard_map/ppermute | solution.py:411
  137.0 0.9 copy-start.28
  181.4 3.3 %collective-permute-start.14 = (bf16[512,128]{1,0:T(8,128)(2,1)S(1)}, bf16[512,128]{1,0:T(8,128)(2,1)S(1)}, u32[]{:S(2)}, u32[]{:S(2)}) collective-permute-start(bf16[512,128]{1,0:T(8,128)(2,1)S(1)} %broadcast_select_fusion.2), channel_id=1, source_target_pairs={{0,1},{1,0},{2,3},{3,2},{4,5},{5,4},{6,7},{7,6},{8,9},{9,8},{10,11... | collective-permute-start | bytes 393224 | tf_op jit(solution)/shard_map/ppermute | solution.py:411
  184.8 0.7 copy-start.29

commit v11 on v7

--- a/solution.py
+++ b/solution.py
@@ -258,7 +258,9 @@
     return over_chips(gate_kernel, blocked, [], shapes, scratch, 16, flops, "gate")[0]
 
 
-def intra_kernel(xc, bcc, hcol, hrow, s0, cols, seg_row, skip, y):
+def intra_kernel(xc, bcc, hcol, hrow, s0, cols, seg_row, skip, y, c_out, decays):
+    c_out[...] = bcc[:, N:]
+    decays[...] = hcol[...]
     for block in range(2):
         intra_block(block * L, xc, bcc, hcol, hrow, s0, cols, seg_row, skip, y)
 
@@ -291,11 +293,12 @@
 
 
 def intra(*args):
+    shapes = [((ROWS, CH), F32), ((ROWS, N), BF16), ((ROWS, 128), F32)]
     return pl.pallas_call(
         intra_kernel,
         in_specs=[VMEM] * len(args),
-        out_specs=VMEM,
-        out_shape=jax.ShapeDtypeStruct((ROWS, CH), F32),
+        out_specs=[VMEM] * len(shapes),
+        out_shape=[jax.ShapeDtypeStruct(*shape) for shape in shapes],
         compiler_params=params(12),
         cost_estimate=pl.CostEstimate(
             flops=2 * ROWS * L * CH * 4, bytes_accessed=4 * 2**20, transcendentals=2 * 10**6
@@ -326,9 +329,9 @@
     )(pieces)
 
 
-def join_kernel(y, gates, bcc, hcol, state, gain, out):
+def join_kernel(y, gates, cc, hcol, state, gain, out):
     for at in range(0, ROWS, 128):
-        c_vals = bcc[at : at + 128, N:]
+        c_vals = cc[at : at + 128, :]
         carried = spread(hcol[at : at + 128, 2 * HEADS : 3 * HEADS])
         total = y[at : at + 128, :] + carried * dot(c_vals, state[...])
         gated = total * gates[at : at + 128, :]
@@ -397,28 +400,28 @@
     return lax.all_to_all(value, "tp", 0, 0, axis_index_groups=same_core)
 
 
+def across_y(value):
+    return lax.ppermute(value, "ctx", [(i, i ^ Z_RING) for i in range(CTX)])
+
+
 def along_z(value, steps):
     pairs = [(i, i // Z_RING * Z_RING + (i + steps) % Z_RING) for i in range(CTX)]
     return lax.ppermute(value, "ctx", pairs)
 
 
+def put_along_z(held, piece, distance, row=0):
+    place = (lax.axis_index("ctx") + distance) % Z_RING
+    return lax.dynamic_update_slice(held, piece[None], (place, row, 0))
+
+
 def gathered_along_z(mine):
-    rows, lanes = mine.shape
-    z_place = lax.axis_index("ctx") % Z_RING
-    held = jnp.zeros((Z_RING, rows, lanes), mine.dtype)
-
-    def put(held, piece, distance, row=0):
-        at = ((z_place + distance) % Z_RING, row, 0)
-        return lax.dynamic_update_slice(held, piece[None], at)
-
-    held = put(held, mine, 0)
+    held = jnp.zeros((Z_RING,) + mine.shape, mine.dtype)
+    held = put_along_z(held, mine, 0)
     above, below = mine, mine
     for distance in range(1, Z_RING // 2):
         below, above = along_z(below, 1), along_z(above, -1)
-        held = put(put(held, below, -distance), above, distance)
-    half = rows // 2
-    below, above = along_z(below[:half], 1), along_z(above[half:], -1)
-    return put(put(held, below, Z_RING // 2), above, Z_RING // 2, half)
+        held = put_along_z(put_along_z(held, below, -distance), above, distance)
+    return held, below, above
 
 
 def between_slabs(value):
@@ -466,6 +469,8 @@
     chip = rank // CORES
     y_low = (lax.axis_index("ctx") // Z_RING).astype(jnp.int32)
 
+    w_across = across_y(w_out)
+
     w_cols = jnp.concatenate(
         [w_bc.T.reshape(CHIPS, 2 * N, FEAT), w_dt.T.reshape(CHIPS, 2 * HEADS, FEAT)], axis=1
     )
@@ -475,31 +480,36 @@
     shared = jnp.concatenate([halo, tokens], axis=0)
     shared = jnp.broadcast_to(shared[None], (CHIPS, ALL_ROWS, FEAT))
     sent = jnp.concatenate([shared, w_cols], axis=1)
-    sent, w_out = together(sent, w_out)
+    sent, w_across, w_out, seg_ids, conv_bc, conv_bc_bias, skip_gain = together(
+        sent, w_across, w_out, seg_ids, conv_bc, conv_bc_bias, skip_gain
+    )
     own = between_chips(sent)
 
-    halves = (w_out[:, :128], w_out[:, 128:])
-    w_pair = jnp.concatenate(
-        [pick(core, *halves), swapped(pick(core, halves[1], halves[0]), 1)], axis=0
-    )
-    w_far = lax.ppermute(w_pair, "ctx", [(i, i ^ Z_RING) for i in range(2 * Z_RING)])
-    w_all = gathered_along_z(jnp.concatenate([w_pair, w_far], axis=0))
+    w_blocks = jnp.stack([w_out, w_across])
+    halves = (w_blocks[:, :, :128], w_blocks[:, :, 128:])
+    w_kept, w_sib = pick(core, *halves), swapped(pick(core, halves[1], halves[0]), 1)
+    w_both = jnp.stack([w_kept, w_sib], axis=1).reshape(4 * CH, 128)
+    w_held, below, above = gathered_along_z(w_both)
 
     cols, seg_row = document_columns(seg_ids, ids_prior)
     taps_bc = lax.dynamic_slice_in_dim(conv_bc, chip * 2 * N, 2 * N, 1)
     bias_bc = lax.dynamic_slice_in_dim(conv_bc_bias, chip * 2 * N, 2 * N, 0)[None]
     skip = jnp.repeat(skip_gain, P_SIZE)[None]
     fixed = [cols, conv_x, conv_x_bias[None], taps_bc, bias_bc, dt_bias[None], decay_rate[None]]
-    own, w_all, fixed, seg_row, skip = together(own, w_all, fixed, seg_row, skip)
+    own, w_held, below, above, fixed, seg_row, skip = together(
+        own, w_held, below, above, fixed, seg_row, skip
+    )
+    last = along_z(below[: 2 * CH], 1), along_z(above[2 * CH :], -1)
     sib = swapped(own, 1)
     xc, bcc, hcol, hrow, s0, pay = scan_input(own, sib, w_x, fixed)
-    own, sib, pay = together(own, sib, pay)
+    own, sib, pay, last = together(own, sib, pay, last)
+    w_all = put_along_z(put_along_z(w_held, last[0], 4), last[1], 4, 2 * CH)
     pieces = between_slabs(pay)
     gates = gate(own, sib, w_z)
     pieces, gates, xc, bcc = together(pieces, gates, xc, bcc)
     state = between_slabs(prefix(pieces).reshape(CTX, 8, CH)).reshape(N, CH)
-    y = intra(xc, bcc, hcol, hrow, s0, fixed[0], seg_row, skip)
-    mine = join(y, gates, bcc, hcol, state, norm_weight[None])
+    y, cc, decays = intra(xc, bcc, hcol, hrow, s0, fixed[0], seg_row, skip)
+    mine = join(y, gates, cc, decays, state, norm_weight[None])
     parts = between_chips(project(mine, swapped(mine, 1), w_all, y_low))
     total = jnp.sum(parts.astype(F32), axis=0).astype(BF16)
     parts = (total[:, :128], total[:, 128:])

time: 185 us -> 180 us (0.973)
  waiting for transfers between devices: 36.1 us -> 22.6 us
  local copies, waits for them, and re-layouts: 29.2 us -> 40 us
  starting transfers between devices: 50.3 us -> 46.2 us
  Pallas kernels: 24.8 us -> 27.2 us
    dynamic_update_slice x8 -> x9, local copies, waits for them, and re-layouts: 2.59 us -> 12.5 us  [put_along_z(): return lax.dynamic_update_slice(held, piece[None], (place, row, 0))]
    ppermute x4, waiting for transfers between devices: 8.51 us -> 1.51 us  [swapped(): return lax.ppermute(value, 'tp', [(i, i ^ bit) for i in range(16)])]
    ppermute x8, waiting for transfers between devices: 25.8 us -> 18.8 us  [along_z(): return lax.ppermute(value, 'ctx', pairs)]
    unnamed x56 -> x52, local copies, waits for them, and re-layouts: 17.9 us -> 14.2 us
    ppermute x1, starting transfers between devices: 4.28 us -> 1.39 us  [across_y(): return lax.ppermute(value, 'ctx', [(i, i ^ Z_RING) for i in range(CTX)])]
    concatenate x2 -> x0, other arithmetic: 2.56 us -> none  [the longest x1 1.81 us: local(): w_all = gathered_along_z(jnp.concatenate([w_pair, w_far], axis=0))]
    pallas_call x1, Pallas kernels: 4.07 us -> 6.61 us  [project(): pl.pallas_call(project_kernel, grid_spec=pltpu.PrefetchScalarGridSpec(num...]
    ppermute x4, starting transfers between devices: 10.5 us -> 8.15 us  [swapped(): return lax.ppermute(value, 'tp', [(i, i ^ bit) for i in range(16)])]
  transfers between devices with their start and end apart: 17 -> 17, of which waited for: 9 -> 7; matrix products, arithmetic and copies ran while one was open for 8% -> 17% of each run, Pallas kernels for 4% -> 10%
where the time goes in v11:
time: 180 us; the launch traced here: 178 us
  starting transfers between devices  46.2 us (26%)
  local copies, waits for them, and re-layouts  40 us (22%)
  blocking collectives  34.2 us (19%)
  Pallas kernels  27.2 us (15%)
  waiting for transfers between devices  22.6 us (13%)
  other arithmetic  8.05 us (4%)
    all_to_all x1, blocking collectives, between_chips(): return lax.all_to_all(value, 'tp', 0, 0, axis_index_groups=same_core)  34.2 us
    ppermute x8, waiting for transfers between devices, along_z(): return lax.ppermute(value, 'ctx', pairs)  18.8 us
    pallas_call x2, Pallas kernels, over_chips(): pl.pallas_call(kernel, grid=(CHIPS // 2,), in_specs=[spec for _, spec in...  15.9 us
    unnamed x52, local copies, waits for them, and re-layouts  14.2 us
    all_to_all x2, starting transfers between devices, between_slabs(): return lax.all_to_all(value, 'ctx', 0, 0)  13.2 us
    dynamic_update_slice x9, local copies, waits for them, and re-layouts, put_along_z(): return lax.dynamic_update_slice(held, piece[None], (place, row, 0))  12.5 us
    ppermute x8, starting transfers between devices, along_z(): return lax.ppermute(value, 'ctx', pairs)  12.3 us
    ppermute x4, starting transfers between devices, swapped(): return lax.ppermute(value, 'tp', [(i, i ^ bit) for i in range(16)])  8.15 us
  transfers between devices with their start and end apart: 17, of which 7 were waited for; matrix products, arithmetic and copies ran while one was open for 17% of the time, Pallas kernels for 10%

profile of v11, /device:TPU:1, one launch (start us, length us, event | category | flops | bytes accessed | tf_op | source)
XLA Modules:
  0.0 178.5 jit_solution(17102579312773452413)
XLA Ops:
  1.5 4.4 %collective-permute-start = (bf16[16,256]{1,0:T(8,128)(2,1)S(1)}, bf16[16,256]{1,0:T(8,128)(2,1)S(1)}, u32[]{:S(2)}, u32[]{:S(2)}) collective-permute-start(bf16[16,256]{1,0:T(8,128)(2,1)S(1)} %pad_maximum_fusion.5), channel_id=1, source_target_pairs={{0,16},{16,32},{32,48},{48,64},{64,80},{80,96},{96,112},{112,128},... | collective-permute-start | bytes 24584 | tf_op jit(solution)/shard_map/ppermute | solution.py:395
  5.9 1.4 collective-permute-start.1
  8.2 1.5 copy.32
  9.8 1.0 pad_maximum_fusion.2
  10.9 1.8 %pad_maximum_fusion = bf16[8,800,256]{2,1,0:T(8,128)(2,1)} fusion(bf16[8,16,256]{2,1,0:T(8,128)(2,1)S(1)} %bitcast.55, bf16[8,256,256]{2,1,0:T(8,128)(2,1)S(1)} %bitcast.53, bf16[8,528,256]{2,1,0:T(8,128)(2,1)S(1)} %broadcast_in_dim.65), kind=kLoop, calls=%fused_computation | loop fusion | flops 9830400 | bytes 6553600 | tf_op jit(solution)/shard_map/concatenate | solution.py:482
  13.9 1.9 %collective-permute-start.2 = (bf16[2,512,128]{2,1,0:T(8,128)(2,1)}, bf16[2,512,128]{2,1,0:T(8,128)(2,1)}, u32[]{:S(2)}, u32[]{:S(2)}) collective-permute-start(bf16[2,512,128]{2,1,0:T(8,128)(2,1)} %get-tuple-element.82), channel_id=1, source_target_pairs={{0,1},{1,0},{2,3},{3,2},{4,5},{5,4},{6,7},{7,6},{8,9},{9,8},{10,11... | collective-permute-start | bytes 786440 | tf_op jit(solution)/shard_map/ppermute | solution.py:391
  16.5 6.8 %all-to-all-start = ((bf16[8,800,256]{2,1,0:T(8,128)(2,1)}), bf16[8,800,256]{2,1,0:T(8,128)(2,1)S(1)}, u32[]{:S(2)}, u32[]{:S(2)}) async-start(bf16[8,800,256]{2,1,0:T(8,128)(2,1)} %pad_maximum_fusion), calls=%async_computation | async-start | bytes 6553600 | tf_op jit(solution)/shard_map/all_to_all | solution.py:400
  24.0 1.1 pad_maximum_fusion.1
  25.9 1.6 collective-permute-start.3
  27.5 2.3 %collective-permute-start.4 = (bf16[2048,128]{1,0:T(8,128)(2,1)}, bf16[2048,128]{1,0:T(8,128)(2,1)}, u32[]{:S(2)}, u32[]{:S(2)}) collective-permute-start(bf16[2048,128]{1,0:T(8,128)(2,1)} %bitcast.10), channel_id=1, source_target_pairs={{0,112},{16,0},{32,16},{48,32},{64,48},{80,64},{96,80},{112,96},{1... | collective-permute-start | bytes 1572872 | tf_op jit(solution)/shard_map/ppermute | solution.py:409
  29.8 1.9 %compare_convert_fusion = (f32[512]{0:T(512)S(1)}, f32[512]{0:T(512)S(1)}, f32[512]{0:T(512)S(1)}, f32[512]{0:T(512)S(1)}, f32[512]{0:T(512)S(1)}, /*index=5*/f32[512]{0:T(512)S(1)}) fusion(s32[512]{0:T(512)S(1)} %copy-done.23, s32[]{:T(128)} %bitcast.25, s32[]{:T(128)} %bitcast.23, s32[]{:T(128)} %bitcast.21, s32[515]{0:T(1024)S(1)} %pad_add_fusion), kind=kLoop, calls=%fused_computation.32 | loop fusion | flops 6144 | bytes 20492 | tf_op jit(solution)/shard_map/stack | solution.py:446
  32.8 1.7 pad.9.cols
  35.2 2.5 %broadcast_in_dim.66 = bf16[8,2048,128]{2,1,0:T(8,128)(2,1)} broadcast(bf16[]{:T(256)} %constant.97.clone.1), dimensions={} | broadcast | bytes 4194306 | tf_op jit(solution)/shard_map/broadcast_in_dim | solution.py:418
  37.7 1.9 %constant_dynamic-update-slice_fusion = bf16[8,2048,128]{2,1,0:T(8,128)(2,1)} fusion(bf16[8,2048,128]{2,1,0:T(8,128)(2,1)} %broadcast_in_dim.66, bf16[1,2048,128]{2,1,0:T(8,128)(2,1)} %bitcast.9, s32[]{:T(128)S(6)} %select_n.116), kind=kLoop, calls=%fused_computation.25 | loop fusion | bytes 1048580 | tf_op jit(solution)/shard_map/dynamic_update_slice | solution.py:414
  39.6 2.6 %collective-permute-done.3 = bf16[2048,128]{1,0:T(8,128)(2,1)} collective-permute-done((bf16[2048,128]{1,0:T(8,128)(2,1)}, bf16[2048,128]{1,0:T(8,128)(2,1)}, u32[]{:S(2)}, u32[]{:S(2)}) %collective-permute-start.3) | collective-permute-done | bytes 524320 | tf_op jit(solution)/shard_map/ppermute | solution.py:409
  42.2 2.7 %collective-permute-start.6 = (bf16[2048,128]{1,0:T(8,128)(2,1)}, bf16[2048,128]{1,0:T(8,128)(2,1)S(1)}, u32[]{:S(2)}, u32[]{:S(2)}) collective-permute-start(bf16[2048,128]{1,0:T(8,128)(2,1)} %collective-permute-done.4), channel_id=1, source_target_pairs={{0,112},{16,0},{32,16},{48,32},{64,48},{80,64},{96,80},{112,96},{1... | collective-permute-start | bytes 1572872 | tf_op jit(solution)/shard_map/ppermute | solution.py:409
  44.9 1.9 %bitcast_dynamic-update-slice_fusion.5 = bf16[8,2048,128]{2,1,0:T(8,128)(2,1)} fusion(bf16[8,2048,128]{2,1,0:T(8,128)(2,1)} %constant_dynamic-update-slice_fusion, s32[]{:T(128)S(6)} %select_n.118, bf16[2048,128]{1,0:T(8,128)(2,1)} %collective-permute-done.3), kind=kLoop, calls=%fused_computation.9 | loop fusion | bytes 1048580 | tf_op jit(solution)/shard_map/dynamic_update_slice | solution.py:414
  46.8 1.9 %bitcast_dynamic-update-slice_fusion.4 = bf16[8,2048,128]{2,1,0:T(8,128)(2,1)} fusion(bf16[8,2048,128]{2,1,0:T(8,128)(2,1)} %bitcast_dynamic-update-slice_fusion.5, s32[]{:T(128)S(6)} %select_n.120, bf16[2048,128]{1,0:T(8,128)(2,1)} %collective-permute-done.4), kind=kLoop, calls=%fused_computation.8 | loop fusion | bytes 1048580 | tf_op jit(solution)/shard_map/dynamic_update_slice | solution.py:414
  48.7 7.6 %collective-permute-done.5 = bf16[2048,128]{1,0:T(8,128)(2,1)S(1)} collective-permute-done((bf16[2048,128]{1,0:T(8,128)(2,1)}, bf16[2048,128]{1,0:T(8,128)(2,1)S(1)}, u32[]{:S(2)}, u32[]{:S(2)}) %collective-permute-start.5) | collective-permute-done | bytes 524320 | tf_op jit(solution)/shard_map/ppermute | solution.py:409
  56.3 2.7 %collective-permute-start.8 = (bf16[2048,128]{1,0:T(8,128)(2,1)S(1)}, bf16[2048,128]{1,0:T(8,128)(2,1)S(1)}, u32[]{:S(2)}, u32[]{:S(2)}) collective-permute-start(bf16[2048,128]{1,0:T(8,128)(2,1)S(1)} %collective-permute-done.6), channel_id=1, source_target_pairs={{0,112},{16,0},{32,16},{48,32},{64,48},{80,64},{96,80},{112,96},{1... | collective-permute-start | bytes 1572872 | tf_op jit(solution)/shard_map/ppermute | solution.py:409
  60.7 8.6 %collective-permute-done.7 = bf16[2048,128]{1,0:T(8,128)(2,1)S(1)} collective-permute-done((bf16[2048,128]{1,0:T(8,128)(2,1)S(1)}, bf16[2048,128]{1,0:T(8,128)(2,1)S(1)}, u32[]{:S(2)}, u32[]{:S(2)}) %collective-permute-start.7) | collective-permute-done | bytes 524320 | tf_op jit(solution)/shard_map/ppermute | solution.py:409
  72.0 2.6 %collective-permute-start.9 = (bf16[8,800,256]{2,1,0:T(8,128)(2,1)S(1)}, bf16[8,800,256]{2,1,0:T(8,128)(2,1)S(1)}, u32[]{:S(2)}, u32[]{:S(2)}) collective-permute-start(bf16[8,800,256]{2,1,0:T(8,128)(2,1)S(1)} %all-to-all-done.own), channel_id=1, source_target_pairs={{0,1},{1,0},{2,3},{3,2},{4,5},{5,4},{6,7},{7,6},{8,9},{9,8},{10,11... | collective-permute-start | bytes 9830408 | tf_op jit(solution)/shard_map/ppermute | solution.py:391
  74.6 1.0 slice.58
  75.6 1.0 slice.59
  76.6 2.9 %collective-permute-start.11 = (bf16[1024,128]{1,0:T(8,128)(2,1)S(1)}, bf16[1024,128]{1,0:T(8,128)(2,1)S(1)}, u32[]{:S(2)}, u32[]{:S(2)}) collective-permute-start(bf16[1024,128]{1,0:T(8,128)(2,1)S(1)} %slice.59), channel_id=1, source_target_pairs={{0,112},{16,0},{32,16},{48,32},{64,48},{80,64},{96,80},{112,96},{1... | collective-permute-start | bytes 786440 | tf_op jit(solution)/shard_map/ppermute | solution.py:409
  80.1 0.9 copy-done.5
  81.0 2.2 %copy-done.8 = bf16[4096,512]{1,0:T(8,128)(2,1)S(1)} copy-done((bf16[4096,512]{1,0:T(8,128)(2,1)S(1)}, bf16[4096,512]{1,0:T(8,128)(2,1)}, u32[]{:S(2)}) %copy-start.8) | copy-done | bytes 4194328
  83.2 11.0 %scan_input.1 = (bf16[512,512]{1,0:T(8,128)(2,1)}, bf16[512,256]{1,0:T(8,128)(2,1)}, f32[512,128]{1,0:T(8,128)}, f32[16,512]{1,0:T(8,128)}, bf16[128,512]{1,0:T(8,128)(2,1)}, /*index=5*/bf16[16,16,512]{2,1,0:T(8,128)(2,1)}) custom-call(bf16[8,800,256]{2,1,0:T(8,128)(2,1)S(1)} %all-to-all-done.own, bf16[8,800,256]{2,1,0:T(8,128)(2,1)S(1)} %collective-permute-done.9.sib, ...), custom_call_target="tpu_custom_call" | custom-call | flops 3391094784 | bytes 8388608 | tf_op jit(solution)/shard_map/scan_input/pallas_call | solution.py:198
  95.6 5.7 %all-to-all-start.1 = ((bf16[16,16,512]{2,1,0:T(8,128)(2,1)}), bf16[16,16,512]{2,1,0:T(8,128)(2,1)}, u32[]{:S(2)}, u32[]{:S(2)}) async-start(bf16[16,16,512]{2,1,0:T(8,128)(2,1)} %get-tuple-element.61), calls=%async_computation.1 | async-start | bytes 524288 | tf_op jit(solution)/shard_map/all_to_all | solution.py:428
  101.3 2.2 %copy-done.1 = bf16[4096,512]{1,0:T(8,128)(2,1)S(1)} copy-done((bf16[4096,512]{1,0:T(8,128)(2,1)S(1)}, bf16[4096,512]{1,0:T(8,128)(2,1)}, u32[]{:S(2)}) %copy-start.1) | copy-done | bytes 4194328
  103.5 1.9 %copy-done.4 = bf16[8,800,256]{2,1,0:T(8,128)(2,1)S(1)} copy-done((bf16[8,800,256]{2,1,0:T(8,128)(2,1)S(1)}, bf16[8,800,256]{2,1,0:T(8,128)(2,1)}, u32[]{:S(2)}) %copy-start.4) | copy-done | bytes 3276824
  105.5 4.8 %gate.1.gates = f32[512,512]{1,0:T(8,128)} custom-call(bf16[8,800,256]{2,1,0:T(8,128)(2,1)S(1)} %all-to-all-done.own, bf16[8,800,256]{2,1,0:T(8,128)(2,1)S(1)} %copy-done.4, bf16[4096,512]{1,0:T(8,128)(2,1)S(1)} %copy-done.1), custom_call_target="tpu_custom_call" | custom-call | flops 2147483648 | bytes 8388608 | tf_op jit(solution)/shard_map/gate/pallas_call | solution.py:198
  110.3 1.7 prefix.1
  112.0 7.5 %all-to-all-start.2 = ((bf16[16,8,512]{2,1,0:T(8,128)(2,1)}), bf16[16,8,512]{2,1,0:T(8,128)(2,1)S(1)}, u32[]{:S(2)}, u32[]{:S(2)}) async-start(bf16[16,8,512]{2,1,0:T(8,128)(2,1)} %bitcast.32), calls=%async_computation.2 | async-start | bytes 262144 | tf_op jit(solution)/shard_map/all_to_all | solution.py:428
  119.6 0.9 copy-done.6
  120.5 1.0 copy-done.13
  121.6 0.9 copy-done.14
  122.5 0.9 copy-done.15
  123.5 1.7 intra.1
  125.2 1.9 %all-to-all-done.2 = bf16[16,8,512]{2,1,0:T(8,128)(2,1)S(1)} async-done(((bf16[16,8,512]{2,1,0:T(8,128)(2,1)}), bf16[16,8,512]{2,1,0:T(8,128)(2,1)S(1)}, u32[]{:S(2)}, u32[]{:S(2)}) %all-to-all-start.2) | async-done | bytes 131104 | tf_op jit(solution)/shard_map/all_to_all | solution.py:428
  127.1 1.3 join.1.own
  128.4 2.4 %collective-permute-start.12 = (bf16[512,640]{1,0:T(8,128)(2,1)S(1)}, bf16[512,640]{1,0:T(8,128)(2,1)S(1)}, u32[]{:S(2)}, u32[]{:S(2)}) collective-permute-start(bf16[512,640]{1,0:T(8,128)(2,1)S(1)} %join.1.own), channel_id=1, source_target_pairs={{0,1},{1,0},{2,3},{3,2},{4,5},{5,4},{6,7},{7,6},{8,9},{9,8},{10,11... | collective-permute-start | bytes 1966088 | tf_op jit(solution)/shard_map/ppermute | solution.py:391
  130.8 1.7 bitcast_dynamic-update-slice_fusion.7
  132.4 1.7 bitcast_dynamic-update-slice_fusion.6.w
  134.1 6.6 %project.1 = bf16[8,512,256]{2,1,0:T(8,128)(2,1)S(1)} custom-call(s32[1]{0:T(128)} %bitcast.place, bf16[512,640]{1,0:T(8,128)(2,1)S(1)} %join.1.own, bf16[512,640]{1,0:T(8,128)(2,1)S(1)} %collective-permute-done.12.sib, bf16[8,2048,128]{2,1,0:T(8,128)(2,1)} %bitcast_dynamic-update-slice_fusion.6.w), custom_call_target="tpu_custom_call" | custom-call | flops 4294967296 | bytes 8388608 | tf_op jit(solution)/shard_map/project/pallas_call | solution.py:373
  140.7 34.2 %all_to_all.20 = bf16[8,512,256]{2,1,0:T(8,128)(2,1)S(1)} all-to-all(bf16[8,512,256]{2,1,0:T(8,128)(2,1)S(1)} %project.1), channel_id=1, replica_groups={{0,2,4,6,8,10,12,14},{1,3,5,7,9,11,13,15},{16,18,20,22,24,26,28,30},{17..., dimensions={0} | all-to-all | bytes 4194304 | tf_op jit(solution)/shard_map/all_to_all | solution.py:400
  175.4 1.3 collective-permute-start.13
  176.7 1.0 collective-permute-done.13
  (88 shorter events, 15.4 us)
Async XLA Ops:
  0.0 35.2 %copy-start = (f32[4,2048]{1,0:T(4,128)S(1)}, f32[4,2048]{1,0:T(4,128)}, u32[]{:S(2)}) copy-start(f32[4,2048]{1,0:T(4,128)} %param.23) | copy-start | bytes 98308
  1.5 8.3 %collective-permute-start = (bf16[16,256]{1,0:T(8,128)(2,1)S(1)}, bf16[16,256]{1,0:T(8,128)(2,1)S(1)}, u32[]{:S(2)}, u32[]{:S(2)}) collective-permute-start(bf16[16,256]{1,0:T(8,128)(2,1)S(1)} %pad_maximum_fusion.5), channel_id=1, source_target_pairs={{0,16},{16,32},{32,48},{48,64},{64,80},{80,96},{96,112},{112,128},... | collective-permute-start | bytes 24584 | tf_op jit(solution)/shard_map/ppermute | solution.py:395
  5.9 7.2 %collective-permute-start.1 = (bf16[512,256]{1,0:T(8,128)(2,1)}, bf16[512,256]{1,0:T(8,128)(2,1)S(1)}, u32[]{:S(2)}, u32[]{:S(2)}) collective-permute-start(bf16[512,256]{1,0:T(8,128)(2,1)} %param.29), channel_id=1, source_target_pairs={{0,128},{16,144},{32,160},{48,176},{64,192},{80,208},{96,224},{112... | collective-permute-start | bytes 786440 | tf_op jit(solution)/shard_map/ppermute | solution.py:404
  10.7 2.3 %copy-start.22 = (bf16[512,256]{1,0:T(8,128)(2,1)S(1)}, bf16[512,256]{1,0:T(8,128)(2,1)}, u32[]{:S(2)}) copy-start(bf16[512,256]{1,0:T(8,128)(2,1)} %param.29) | copy-start | bytes 786436
  12.7 10.5 %copy-start.23 = (s32[512]{0:T(512)S(1)}, s32[512]{0:T(512)}, u32[]{:S(2)}) copy-start(s32[512]{0:T(512)} %param.16) | copy-start | bytes 6148
  13.9 10.0 %collective-permute-start.2 = (bf16[2,512,128]{2,1,0:T(8,128)(2,1)}, bf16[2,512,128]{2,1,0:T(8,128)(2,1)}, u32[]{:S(2)}, u32[]{:S(2)}) collective-permute-start(bf16[2,512,128]{2,1,0:T(8,128)(2,1)} %get-tuple-element.82), channel_id=1, source_target_pairs={{0,1},{1,0},{2,3},{3,2},{4,5},{5,4},{6,7},{7,6},{8,9},{9,8},{10,11... | collective-permute-start | bytes 786440 | tf_op jit(solution)/shard_map/ppermute | solution.py:391
  16.5 16.2 %copy-start.24 = (f32[8]{0:T(128)S(1)}, f32[8]{0:T(128)}, u32[]{:S(2)}) copy-start(f32[8]{0:T(128)} %param.27) | copy-start | bytes 100
  16.5 55.5 %all-to-all-start = ((bf16[8,800,256]{2,1,0:T(8,128)(2,1)}), bf16[8,800,256]{2,1,0:T(8,128)(2,1)S(1)}, u32[]{:S(2)}, u32[]{:S(2)}) async-start(bf16[8,800,256]{2,1,0:T(8,128)(2,1)} %pad_maximum_fusion), calls=%async_computation | async-start | bytes 6553600 | tf_op jit(solution)/shard_map/all_to_all | solution.py:400
  25.9 16.4 %collective-permute-start.3 = (bf16[2048,128]{1,0:T(8,128)(2,1)}, bf16[2048,128]{1,0:T(8,128)(2,1)}, u32[]{:S(2)}, u32[]{:S(2)}) collective-permute-start(bf16[2048,128]{1,0:T(8,128)(2,1)} %bitcast.10), channel_id=1, source_target_pairs={{0,16},{16,32},{32,48},{48,64},{64,80},{80,96},{96,112},{112,0},{1... | collective-permute-start | bytes 1572872 | tf_op jit(solution)/shard_map/ppermute | solution.py:409
  27.5 14.7 %collective-permute-start.4 = (bf16[2048,128]{1,0:T(8,128)(2,1)}, bf16[2048,128]{1,0:T(8,128)(2,1)}, u32[]{:S(2)}, u32[]{:S(2)}) collective-permute-start(bf16[2048,128]{1,0:T(8,128)(2,1)} %bitcast.10), channel_id=1, source_target_pairs={{0,112},{16,0},{32,16},{48,32},{64,48},{80,64},{96,80},{112,96},{1... | collective-permute-start | bytes 1572872 | tf_op jit(solution)/shard_map/ppermute | solution.py:409
  37.7 42.3 %copy-start.9 = (f32[4,512]{1,0:T(4,128)S(1)}, f32[4,512]{1,0:T(4,128)}, u32[]{:S(2)}) copy-start(f32[4,512]{1,0:T(4,128)} %taps_x) | copy-start | bytes 24580
  37.7 42.3 %copy-start.10 = (f32[512]{0:T(512)S(1)}, f32[512]{0:T(512)}, u32[]{:S(2)}) copy-start(f32[512]{0:T(512)} %param.22) | copy-start | bytes 6148
  37.7 42.3 %copy-start.11 = (f32[8]{0:T(128)S(1)}, f32[8]{0:T(128)}, u32[]{:S(2)}) copy-start(f32[8]{0:T(128)} %param.25) | copy-start | bytes 100
  37.7 42.3 %copy-start.12 = (f32[8]{0:T(128)S(1)}, f32[8]{0:T(128)}, u32[]{:S(2)}) copy-start(f32[8]{0:T(128)} %param.26) | copy-start | bytes 100
  42.2 14.1 %collective-permute-start.5 = (bf16[2048,128]{1,0:T(8,128)(2,1)}, bf16[2048,128]{1,0:T(8,128)(2,1)S(1)}, u32[]{:S(2)}, u32[]{:S(2)}) collective-permute-start(bf16[2048,128]{1,0:T(8,128)(2,1)} %collective-permute-done.3), channel_id=1, source_target_pairs={{0,16},{16,32},{32,48},{48,64},{64,80},{80,96},{96,112},{112,0},{1... | collective-permute-start | bytes 1572872 | tf_op jit(solution)/shard_map/ppermute | solution.py:409
  42.2 14.1 %collective-permute-start.6 = (bf16[2048,128]{1,0:T(8,128)(2,1)}, bf16[2048,128]{1,0:T(8,128)(2,1)S(1)}, u32[]{:S(2)}, u32[]{:S(2)}) collective-permute-start(bf16[2048,128]{1,0:T(8,128)(2,1)} %collective-permute-done.4), channel_id=1, source_target_pairs={{0,112},{16,0},{32,16},{48,32},{64,48},{80,64},{96,80},{112,96},{1... | collective-permute-start | bytes 1572872 | tf_op jit(solution)/shard_map/ppermute | solution.py:409
  56.3 13.0 %collective-permute-start.7 = (bf16[2048,128]{1,0:T(8,128)(2,1)S(1)}, bf16[2048,128]{1,0:T(8,128)(2,1)S(1)}, u32[]{:S(2)}, u32[]{:S(2)}) collective-permute-start(bf16[2048,128]{1,0:T(8,128)(2,1)S(1)} %collective-permute-done.5), channel_id=1, source_target_pairs={{0,16},{16,32},{32,48},{48,64},{64,80},{80,96},{96,112},{112,0},{1... | collective-permute-start | bytes 1572872 | tf_op jit(solution)/shard_map/ppermute | solution.py:409
  56.3 13.9 %collective-permute-start.8 = (bf16[2048,128]{1,0:T(8,128)(2,1)S(1)}, bf16[2048,128]{1,0:T(8,128)(2,1)S(1)}, u32[]{:S(2)}, u32[]{:S(2)}) collective-permute-start(bf16[2048,128]{1,0:T(8,128)(2,1)S(1)} %collective-permute-done.6), channel_id=1, source_target_pairs={{0,112},{16,0},{32,16},{48,32},{64,48},{80,64},{96,80},{112,96},{1... | collective-permute-start | bytes 1572872 | tf_op jit(solution)/shard_map/ppermute | solution.py:409
  69.3 1.0 copy-start.18
  70.3 0.9 copy-start.19
  72.0 8.1 %collective-permute-start.9 = (bf16[8,800,256]{2,1,0:T(8,128)(2,1)S(1)}, bf16[8,800,256]{2,1,0:T(8,128)(2,1)S(1)}, u32[]{:S(2)}, u32[]{:S(2)}) collective-permute-start(bf16[8,800,256]{2,1,0:T(8,128)(2,1)S(1)} %all-to-all-done.own), channel_id=1, source_target_pairs={{0,1},{1,0},{2,3},{3,2},{4,5},{5,4},{6,7},{7,6},{8,9},{9,8},{10,11... | collective-permute-start | bytes 9830408 | tf_op jit(solution)/shard_map/ppermute | solution.py:391
  75.5 18.7 %collective-permute-start.10 = (bf16[1024,128]{1,0:T(8,128)(2,1)S(1)}, bf16[1024,128]{1,0:T(8,128)(2,1)S(1)}, u32[]{:S(2)}, u32[]{:S(2)}) collective-permute-start(bf16[1024,128]{1,0:T(8,128)(2,1)S(1)} %slice.58), channel_id=1, source_target_pairs={{0,16},{16,32},{32,48},{48,64},{64,80},{80,96},{96,112},{112,0},{1... | collective-permute-start | bytes 786440 | tf_op jit(solution)/shard_map/ppermute | solution.py:409
  76.6 18.3 %collective-permute-start.11 = (bf16[1024,128]{1,0:T(8,128)(2,1)S(1)}, bf16[1024,128]{1,0:T(8,128)(2,1)S(1)}, u32[]{:S(2)}, u32[]{:S(2)}) collective-permute-start(bf16[1024,128]{1,0:T(8,128)(2,1)S(1)} %slice.59), channel_id=1, source_target_pairs={{0,112},{16,0},{32,16},{48,32},{64,48},{80,64},{96,80},{112,96},{1... | collective-permute-start | bytes 786440 | tf_op jit(solution)/shard_map/ppermute | solution.py:409
  80.0 1.0 copy-start.5
  81.0 2.2 %copy-start.8 = (bf16[4096,512]{1,0:T(8,128)(2,1)S(1)}, bf16[4096,512]{1,0:T(8,128)(2,1)}, u32[]{:S(2)}) copy-start(bf16[4096,512]{1,0:T(8,128)(2,1)} %w_x.1) | copy-start | bytes 12582916
  83.2 11.0 %copy-start.3 = (bf16[8,800,256]{2,1,0:T(8,128)(2,1)}, bf16[8,800,256]{2,1,0:T(8,128)(2,1)S(1)}, u32[]{:S(2)}) copy-start(bf16[8,800,256]{2,1,0:T(8,128)(2,1)S(1)} %collective-permute-done.9.sib) | copy-start | bytes 9830404
  94.2 0.7 copy-start.20
  94.9 0.7 copy-start.21
  95.6 14.7 %all-to-all-start.1 = ((bf16[16,16,512]{2,1,0:T(8,128)(2,1)}), bf16[16,16,512]{2,1,0:T(8,128)(2,1)}, u32[]{:S(2)}, u32[]{:S(2)}) async-start(bf16[16,16,512]{2,1,0:T(8,128)(2,1)} %get-tuple-element.61), calls=%async_computation.1 | async-start | bytes 524288 | tf_op jit(solution)/shard_map/all_to_all | solution.py:428
  101.3 2.2 %copy-start.1 = (bf16[4096,512]{1,0:T(8,128)(2,1)S(1)}, bf16[4096,512]{1,0:T(8,128)(2,1)}, u32[]{:S(2)}) copy-start(bf16[4096,512]{1,0:T(8,128)(2,1)} %w_z.1) | copy-start | bytes 12582916
  103.5 1.9 %copy-start.4 = (bf16[8,800,256]{2,1,0:T(8,128)(2,1)S(1)}, bf16[8,800,256]{2,1,0:T(8,128)(2,1)}, u32[]{:S(2)}) copy-start(bf16[8,800,256]{2,1,0:T(8,128)(2,1)} %copy-done.3) | copy-start | bytes 9830404
  105.4 14.1 %copy-start.16 = (bf16[128,512]{1,0:T(8,128)(2,1)S(1)}, bf16[128,512]{1,0:T(8,128)(2,1)}, u32[]{:S(2)}) copy-start(bf16[128,512]{1,0:T(8,128)(2,1)} %get-tuple-element.70.s0) | copy-start | bytes 393220
  105.4 14.1 %copy-start.17 = (f32[16,512]{1,0:T(8,128)S(1)}, f32[16,512]{1,0:T(8,128)}, u32[]{:S(2)}) copy-start(f32[16,512]{1,0:T(8,128)} %get-tuple-element.69.hrow) | copy-start | bytes 98308
  105.4 21.6 %copy-start.7 = (f32[512]{0:T(512)S(1)}, f32[512]{0:T(512)}, u32[]{:S(2)}) copy-start(f32[512]{0:T(512)} %param.28) | copy-start | bytes 6148
  110.3 16.8 %copy-start.2 = (f32[512,512]{1,0:T(8,128)S(1)}, f32[512,512]{1,0:T(8,128)}, u32[]{:S(2)}) copy-start(f32[512,512]{1,0:T(8,128)} %gate.1.gates) | copy-start | bytes 3145732
  112.0 15.0 %all-to-all-start.2 = ((bf16[16,8,512]{2,1,0:T(8,128)(2,1)}), bf16[16,8,512]{2,1,0:T(8,128)(2,1)S(1)}, u32[]{:S(2)}, u32[]{:S(2)}) async-start(bf16[16,8,512]{2,1,0:T(8,128)(2,1)} %bitcast.32), calls=%async_computation.2 | async-start | bytes 262144 | tf_op jit(solution)/shard_map/all_to_all | solution.py:428
  119.6 1.0 copy-start.6
  120.5 1.0 copy-start.13
  121.6 0.9 copy-start.14
  122.5 0.9 copy-start.15
  128.4 5.7 %collective-permute-start.12 = (bf16[512,640]{1,0:T(8,128)(2,1)S(1)}, bf16[512,640]{1,0:T(8,128)(2,1)S(1)}, u32[]{:S(2)}, u32[]{:S(2)}) collective-permute-start(bf16[512,640]{1,0:T(8,128)(2,1)S(1)} %join.1.own), channel_id=1, source_target_pairs={{0,1},{1,0},{2,3},{3,2},{4,5},{5,4},{6,7},{7,6},{8,9},{9,8},{10,11... | collective-permute-start | bytes 1966088 | tf_op jit(solution)/shard_map/ppermute | solution.py:391
  175.4 2.3 %collective-permute-start.13 = (bf16[512,128]{1,0:T(8,128)(2,1)S(1)}, bf16[512,128]{1,0:T(8,128)(2,1)S(1)}, u32[]{:S(2)}, u32[]{:S(2)}) collective-permute-start(bf16[512,128]{1,0:T(8,128)(2,1)S(1)} %broadcast_select_fusion.3), channel_id=1, source_target_pairs={{0,1},{1,0},{2,3},{3,2},{4,5},{5,4},{6,7},{7,6},{8,9},{9,8},{10,11... | collective-permute-start | bytes 393224 | tf_op jit(solution)/shard_map/ppermute | solution.py:391
  177.8 0.7 copy-start.25

commit v12 on v11

--- a/solution.py
+++ b/solution.py
@@ -409,9 +409,9 @@
     return lax.ppermute(value, "ctx", pairs)
 
 
-def put_along_z(held, piece, distance, row=0):
+def put_along_z(held, piece, distance):
     place = (lax.axis_index("ctx") + distance) % Z_RING
-    return lax.dynamic_update_slice(held, piece[None], (place, row, 0))
+    return lax.dynamic_update_slice(held, piece[None], (place, 0, 0))
 
 
 def gathered_along_z(mine):
@@ -421,7 +421,7 @@
     for distance in range(1, Z_RING // 2):
         below, above = along_z(below, 1), along_z(above, -1)
         held = put_along_z(put_along_z(held, below, -distance), above, distance)
-    return held, below, above
+    return held, below
 
 
 def between_slabs(value):
@@ -489,21 +489,21 @@
     halves = (w_blocks[:, :, :128], w_blocks[:, :, 128:])
     w_kept, w_sib = pick(core, *halves), swapped(pick(core, halves[1], halves[0]), 1)
     w_both = jnp.stack([w_kept, w_sib], axis=1).reshape(4 * CH, 128)
-    w_held, below, above = gathered_along_z(w_both)
+    w_held, below = gathered_along_z(w_both)
 
     cols, seg_row = document_columns(seg_ids, ids_prior)
     taps_bc = lax.dynamic_slice_in_dim(conv_bc, chip * 2 * N, 2 * N, 1)
     bias_bc = lax.dynamic_slice_in_dim(conv_bc_bias, chip * 2 * N, 2 * N, 0)[None]
     skip = jnp.repeat(skip_gain, P_SIZE)[None]
     fixed = [cols, conv_x, conv_x_bias[None], taps_bc, bias_bc, dt_bias[None], decay_rate[None]]
-    own, w_held, below, above, fixed, seg_row, skip = together(
-        own, w_held, below, above, fixed, seg_row, skip
+    own, w_held, below, fixed, seg_row, skip = together(
+        own, w_held, below, fixed, seg_row, skip
     )
-    last = along_z(below[: 2 * CH], 1), along_z(above[2 * CH :], -1)
+    last = along_z(below, 1)
     sib = swapped(own, 1)
     xc, bcc, hcol, hrow, s0, pay = scan_input(own, sib, w_x, fixed)
     own, sib, pay, last = together(own, sib, pay, last)
-    w_all = put_along_z(put_along_z(w_held, last[0], 4), last[1], 4, 2 * CH)
+    w_all = put_along_z(w_held, last, 4)
     pieces = between_slabs(pay)
     gates = gate(own, sib, w_z)
     pieces, gates, xc, bcc = together(pieces, gates, xc, bcc)

time: 180 us -> 177 us (0.983)
  local copies, waits for them, and re-layouts: 40 us -> 35.1 us
  waiting for transfers between devices: 22.6 us -> 27.4 us
  starting transfers between devices: 46.2 us -> 43.9 us
    ppermute x4, waiting for transfers between devices: 1.51 us -> 6.46 us  [swapped(): return lax.ppermute(value, 'tp', [(i, i ^ bit) for i in range(16)])]
    ppermute x8 -> x7, starting transfers between devices: 12.3 us -> 9.31 us  [along_z(): return lax.ppermute(value, 'ctx', pairs)]
    slice x2 -> x0, local copies, waits for them, and re-layouts: 1.94 us -> none  [local(): last = (along_z(below[:2 * CH], 1), along_z(above[2 * CH:], -1))]
    dynamic_update_slice x9 -> x8, local copies, waits for them, and re-layouts: 12.5 us -> 11 us  [put_along_z(): return lax.dynamic_update_slice(held, piece[None], (place, 0, 0))]
    unnamed x52 -> x48, local copies, waits for them, and re-layouts: 14.2 us -> 12.8 us
    ppermute x8 -> x7, waiting for transfers between devices: 18.8 us -> 18.7 us  [along_z(): return lax.ppermute(value, 'ctx', pairs)]
  transfers between devices with their start and end apart: 17 -> 16, of which waited for: 7 -> 7; matrix products, arithmetic and copies ran while one was open for 17% -> 16% of each run, Pallas kernels for 10% -> 10%
where the time goes in v12:
time: 177 us; the launch traced here: 176 us
  starting transfers between devices  43.9 us (25%)
  local copies, waits for them, and re-layouts  35.1 us (20%)
  blocking collectives  33.5 us (19%)
  waiting for transfers between devices  27.4 us (15%)
  Pallas kernels  27.2 us (15%)
  other arithmetic  8.15 us (5%)
    all_to_all x1, blocking collectives, between_chips(): return lax.all_to_all(value, 'tp', 0, 0, axis_index_groups=same_core)  33.5 us
    ppermute x7, waiting for transfers between devices, along_z(): return lax.ppermute(value, 'ctx', pairs)  18.7 us
    pallas_call x2, Pallas kernels, over_chips(): pl.pallas_call(kernel, grid=(CHIPS // 2,), in_specs=[spec for _, spec in...  15.8 us
    all_to_all x2, starting transfers between devices, between_slabs(): return lax.all_to_all(value, 'ctx', 0, 0)  13.2 us
    unnamed x48, local copies, waits for them, and re-layouts  12.8 us
    dynamic_update_slice x8, local copies, waits for them, and re-layouts, put_along_z(): return lax.dynamic_update_slice(held, piece[None], (place, 0, 0))  11 us
    ppermute x7, starting transfers between devices, along_z(): return lax.ppermute(value, 'ctx', pairs)  9.31 us
    ppermute x4, starting transfers between devices, swapped(): return lax.ppermute(value, 'tp', [(i, i ^ bit) for i in range(16)])  8.87 us
  transfers between devices with their start and end apart: 16, of which 7 were waited for; matrix products, arithmetic and copies ran while one was open for 16% of the time, Pallas kernels for 10%

profile of v12, /device:TPU:1, one launch (start us, length us, event | category | flops | bytes accessed | tf_op | source)
XLA Modules:
  0.0 175.5 jit_solution(347341399648062990)
XLA Ops:
  1.5 4.4 %collective-permute-start = (bf16[16,256]{1,0:T(8,128)(2,1)S(1)}, bf16[16,256]{1,0:T(8,128)(2,1)S(1)}, u32[]{:S(2)}, u32[]{:S(2)}) collective-permute-start(bf16[16,256]{1,0:T(8,128)(2,1)S(1)} %pad_maximum_fusion.5), channel_id=1, source_target_pairs={{0,16},{16,32},{32,48},{48,64},{64,80},{80,96},{96,112},{112,128},... | collective-permute-start | bytes 24584 | tf_op jit(solution)/shard_map/ppermute | solution.py:395
  5.9 1.4 collective-permute-start.1
  7.3 0.9 copy.33
  8.2 1.5 copy.32
  9.8 1.0 pad_maximum_fusion.2
  10.9 1.8 %pad_maximum_fusion = bf16[8,800,256]{2,1,0:T(8,128)(2,1)} fusion(bf16[8,16,256]{2,1,0:T(8,128)(2,1)S(1)} %bitcast.53, bf16[8,256,256]{2,1,0:T(8,128)(2,1)S(1)} %bitcast.51, bf16[8,528,256]{2,1,0:T(8,128)(2,1)S(1)} %broadcast_in_dim.62), kind=kLoop, calls=%fused_computation | loop fusion | flops 9830400 | bytes 6553600 | tf_op jit(solution)/shard_map/concatenate | solution.py:482
  13.0 0.9 select_bitcast_fusion
  14.0 1.9 %collective-permute-start.2 = (bf16[2,512,128]{2,1,0:T(8,128)(2,1)}, bf16[2,512,128]{2,1,0:T(8,128)(2,1)}, u32[]{:S(2)}, u32[]{:S(2)}) collective-permute-start(bf16[2,512,128]{2,1,0:T(8,128)(2,1)} %get-tuple-element.78), channel_id=1, source_target_pairs={{0,1},{1,0},{2,3},{3,2},{4,5},{5,4},{6,7},{7,6},{8,9},{9,8},{10,11... | collective-permute-start | bytes 786440 | tf_op jit(solution)/shard_map/ppermute | solution.py:391
  16.5 6.8 %all-to-all-start = ((bf16[8,800,256]{2,1,0:T(8,128)(2,1)}), bf16[8,800,256]{2,1,0:T(8,128)(2,1)S(1)}, u32[]{:S(2)}, u32[]{:S(2)}) async-start(bf16[8,800,256]{2,1,0:T(8,128)(2,1)} %pad_maximum_fusion), calls=%async_computation | async-start | bytes 6553600 | tf_op jit(solution)/shard_map/all_to_all | solution.py:400
  24.0 1.1 pad_maximum_fusion.1
  25.9 1.6 collective-permute-start.3
  27.5 2.3 %collective-permute-start.4 = (bf16[2048,128]{1,0:T(8,128)(2,1)}, bf16[2048,128]{1,0:T(8,128)(2,1)}, u32[]{:S(2)}, u32[]{:S(2)}) collective-permute-start(bf16[2048,128]{1,0:T(8,128)(2,1)} %bitcast.10), channel_id=1, source_target_pairs={{0,112},{16,0},{32,16},{48,32},{64,48},{80,64},{96,80},{112,96},{1... | collective-permute-start | bytes 1572872 | tf_op jit(solution)/shard_map/ppermute | solution.py:409
  29.8 2.0 %compare_convert_fusion = (f32[512]{0:T(512)S(1)}, f32[512]{0:T(512)S(1)}, f32[512]{0:T(512)S(1)}, f32[512]{0:T(512)S(1)}, f32[512]{0:T(512)S(1)}, /*index=5*/f32[512]{0:T(512)S(1)}) fusion(s32[512]{0:T(512)S(1)} %copy-done.21, s32[]{:T(128)} %bitcast.25, s32[]{:T(128)} %bitcast.23, s32[]{:T(128)} %bitcast.21, s32[515]{0:T(1024)S(1)} %pad_add_fusion), kind=kLoop, calls=%fused_computation.31 | loop fusion | flops 6144 | bytes 20492 | tf_op jit(solution)/shard_map/stack | solution.py:446
  32.9 1.7 pad.9.cols
  35.3 2.5 %broadcast_in_dim.63 = bf16[8,2048,128]{2,1,0:T(8,128)(2,1)} broadcast(bf16[]{:T(256)} %constant.94.clone.1), dimensions={} | broadcast | bytes 4194306 | tf_op jit(solution)/shard_map/broadcast_in_dim | solution.py:418
  37.8 1.9 %constant_dynamic-update-slice_fusion = bf16[8,2048,128]{2,1,0:T(8,128)(2,1)} fusion(bf16[8,2048,128]{2,1,0:T(8,128)(2,1)} %broadcast_in_dim.63, bf16[1,2048,128]{2,1,0:T(8,128)(2,1)} %bitcast.9, s32[]{:T(128)S(6)} %select_n.113), kind=kLoop, calls=%fused_computation.24 | loop fusion | bytes 1048580 | tf_op jit(solution)/shard_map/dynamic_update_slice | solution.py:414
  39.8 2.5 %collective-permute-done.3 = bf16[2048,128]{1,0:T(8,128)(2,1)} collective-permute-done((bf16[2048,128]{1,0:T(8,128)(2,1)}, bf16[2048,128]{1,0:T(8,128)(2,1)}, u32[]{:S(2)}, u32[]{:S(2)}) %collective-permute-start.3) | collective-permute-done | bytes 524320 | tf_op jit(solution)/shard_map/ppermute | solution.py:409
  42.3 2.7 %collective-permute-start.6 = (bf16[2048,128]{1,0:T(8,128)(2,1)}, bf16[2048,128]{1,0:T(8,128)(2,1)S(1)}, u32[]{:S(2)}, u32[]{:S(2)}) collective-permute-start(bf16[2048,128]{1,0:T(8,128)(2,1)} %collective-permute-done.4), channel_id=1, source_target_pairs={{0,112},{16,0},{32,16},{48,32},{64,48},{80,64},{96,80},{112,96},{1... | collective-permute-start | bytes 1572872 | tf_op jit(solution)/shard_map/ppermute | solution.py:409
  44.9 1.9 %bitcast_dynamic-update-slice_fusion.6 = bf16[8,2048,128]{2,1,0:T(8,128)(2,1)} fusion(bf16[8,2048,128]{2,1,0:T(8,128)(2,1)} %constant_dynamic-update-slice_fusion, s32[]{:T(128)S(6)} %select_n.115, bf16[2048,128]{1,0:T(8,128)(2,1)} %collective-permute-done.3), kind=kLoop, calls=%fused_computation.10 | loop fusion | bytes 1048580 | tf_op jit(solution)/shard_map/dynamic_update_slice | solution.py:414
  46.8 1.9 %bitcast_dynamic-update-slice_fusion.5 = bf16[8,2048,128]{2,1,0:T(8,128)(2,1)} fusion(bf16[8,2048,128]{2,1,0:T(8,128)(2,1)} %bitcast_dynamic-update-slice_fusion.6, s32[]{:T(128)S(6)} %select_n.117, bf16[2048,128]{1,0:T(8,128)(2,1)} %collective-permute-done.4), kind=kLoop, calls=%fused_computation.9 | loop fusion | bytes 1048580 | tf_op jit(solution)/shard_map/dynamic_update_slice | solution.py:414
  48.7 7.6 %collective-permute-done.5 = bf16[2048,128]{1,0:T(8,128)(2,1)S(1)} collective-permute-done((bf16[2048,128]{1,0:T(8,128)(2,1)}, bf16[2048,128]{1,0:T(8,128)(2,1)S(1)}, u32[]{:S(2)}, u32[]{:S(2)}) %collective-permute-start.5) | collective-permute-done | bytes 524320 | tf_op jit(solution)/shard_map/ppermute | solution.py:409
  56.3 2.7 %collective-permute-start.8 = (bf16[2048,128]{1,0:T(8,128)(2,1)S(1)}, bf16[2048,128]{1,0:T(8,128)(2,1)S(1)}, u32[]{:S(2)}, u32[]{:S(2)}) collective-permute-start(bf16[2048,128]{1,0:T(8,128)(2,1)S(1)} %collective-permute-done.6), channel_id=1, source_target_pairs={{0,112},{16,0},{32,16},{48,32},{64,48},{80,64},{96,80},{112,96},{1... | collective-permute-start | bytes 1572872 | tf_op jit(solution)/shard_map/ppermute | solution.py:409
  60.7 8.6 %collective-permute-done.7 = bf16[2048,128]{1,0:T(8,128)(2,1)S(1)} collective-permute-done((bf16[2048,128]{1,0:T(8,128)(2,1)S(1)}, bf16[2048,128]{1,0:T(8,128)(2,1)S(1)}, u32[]{:S(2)}, u32[]{:S(2)}) %collective-permute-start.7) | collective-permute-done | bytes 524320 | tf_op jit(solution)/shard_map/ppermute | solution.py:409
  69.3 0.9 bitcast_dynamic-update-slice_fusion.2
  71.1 2.6 %collective-permute-start.9 = (bf16[8,800,256]{2,1,0:T(8,128)(2,1)S(1)}, bf16[8,800,256]{2,1,0:T(8,128)(2,1)S(1)}, u32[]{:S(2)}, u32[]{:S(2)}) collective-permute-start(bf16[8,800,256]{2,1,0:T(8,128)(2,1)S(1)} %all-to-all-done.own), channel_id=1, source_target_pairs={{0,1},{1,0},{2,3},{3,2},{4,5},{5,4},{6,7},{7,6},{8,9},{9,8},{10,11... | collective-permute-start | bytes 9830408 | tf_op jit(solution)/shard_map/ppermute | solution.py:391
  73.7 5.5 %collective-permute-done.9.sib = bf16[8,800,256]{2,1,0:T(8,128)(2,1)S(1)} collective-permute-done((bf16[8,800,256]{2,1,0:T(8,128)(2,1)S(1)}, bf16[8,800,256]{2,1,0:T(8,128)(2,1)S(1)}, u32[]{:S(2)}, u32[]{:S(2)}) %collective-permute-start.9) | collective-permute-done | bytes 3276832 | tf_op jit(solution)/shard_map/ppermute | solution.py:391
  79.2 0.9 copy-done.5
  80.2 2.2 %copy-done.8 = bf16[4096,512]{1,0:T(8,128)(2,1)S(1)} copy-done((bf16[4096,512]{1,0:T(8,128)(2,1)S(1)}, bf16[4096,512]{1,0:T(8,128)(2,1)}, u32[]{:S(2)}) %copy-start.8) | copy-done | bytes 4194328
  82.3 11.0 %scan_input.1 = (bf16[512,512]{1,0:T(8,128)(2,1)}, bf16[512,256]{1,0:T(8,128)(2,1)}, f32[512,128]{1,0:T(8,128)}, f32[16,512]{1,0:T(8,128)}, bf16[128,512]{1,0:T(8,128)(2,1)}, /*index=5*/bf16[16,16,512]{2,1,0:T(8,128)(2,1)}) custom-call(bf16[8,800,256]{2,1,0:T(8,128)(2,1)S(1)} %all-to-all-done.own, bf16[8,800,256]{2,1,0:T(8,128)(2,1)S(1)} %collective-permute-done.9.sib, ...), custom_call_target="tpu_custom_call" | custom-call | flops 3391094784 | bytes 8388608 | tf_op jit(solution)/shard_map/scan_input/pallas_call | solution.py:198
  94.2 5.7 %all-to-all-start.1 = ((bf16[16,16,512]{2,1,0:T(8,128)(2,1)}), bf16[16,16,512]{2,1,0:T(8,128)(2,1)}, u32[]{:S(2)}, u32[]{:S(2)}) async-start(bf16[16,16,512]{2,1,0:T(8,128)(2,1)} %get-tuple-element.58), calls=%async_computation.1 | async-start | bytes 524288 | tf_op jit(solution)/shard_map/all_to_all | solution.py:428
  99.9 2.2 %copy-done.1 = bf16[4096,512]{1,0:T(8,128)(2,1)S(1)} copy-done((bf16[4096,512]{1,0:T(8,128)(2,1)S(1)}, bf16[4096,512]{1,0:T(8,128)(2,1)}, u32[]{:S(2)}) %copy-start.1) | copy-done | bytes 4194328
  102.1 1.9 %copy-done.4 = bf16[8,800,256]{2,1,0:T(8,128)(2,1)S(1)} copy-done((bf16[8,800,256]{2,1,0:T(8,128)(2,1)S(1)}, bf16[8,800,256]{2,1,0:T(8,128)(2,1)}, u32[]{:S(2)}) %copy-start.4) | copy-done | bytes 3276824
  104.0 4.8 %gate.1.gates = f32[512,512]{1,0:T(8,128)} custom-call(bf16[8,800,256]{2,1,0:T(8,128)(2,1)S(1)} %all-to-all-done.own, bf16[8,800,256]{2,1,0:T(8,128)(2,1)S(1)} %copy-done.4, bf16[4096,512]{1,0:T(8,128)(2,1)S(1)} %copy-done.1), custom_call_target="tpu_custom_call" | custom-call | flops 2147483648 | bytes 8388608 | tf_op jit(solution)/shard_map/gate/pallas_call | solution.py:198
  108.8 1.7 prefix.1
  110.6 7.5 %all-to-all-start.2 = ((bf16[16,8,512]{2,1,0:T(8,128)(2,1)}), bf16[16,8,512]{2,1,0:T(8,128)(2,1)S(1)}, u32[]{:S(2)}, u32[]{:S(2)}) async-start(bf16[16,8,512]{2,1,0:T(8,128)(2,1)} %bitcast.32), calls=%async_computation.2 | async-start | bytes 262144 | tf_op jit(solution)/shard_map/all_to_all | solution.py:428
  118.1 0.9 copy-done.6
  119.1 1.0 copy-done.13
  120.1 0.9 copy-done.14
  121.1 0.9 copy-done.15
  122.0 1.7 intra.1
  123.7 1.9 %all-to-all-done.2 = bf16[16,8,512]{2,1,0:T(8,128)(2,1)S(1)} async-done(((bf16[16,8,512]{2,1,0:T(8,128)(2,1)}), bf16[16,8,512]{2,1,0:T(8,128)(2,1)S(1)}, u32[]{:S(2)}, u32[]{:S(2)}) %all-to-all-start.2) | async-done | bytes 131104 | tf_op jit(solution)/shard_map/all_to_all | solution.py:428
  125.6 1.3 join.1.own
  126.9 2.4 %collective-permute-start.11 = (bf16[512,640]{1,0:T(8,128)(2,1)S(1)}, bf16[512,640]{1,0:T(8,128)(2,1)S(1)}, u32[]{:S(2)}, u32[]{:S(2)}) collective-permute-start(bf16[512,640]{1,0:T(8,128)(2,1)S(1)} %join.1.own), channel_id=1, source_target_pairs={{0,1},{1,0},{2,3},{3,2},{4,5},{5,4},{6,7},{7,6},{8,9},{9,8},{10,11... | collective-permute-start | bytes 1966088 | tf_op jit(solution)/shard_map/ppermute | solution.py:391
  129.3 1.9 %bitcast_dynamic-update-slice_fusion.w = bf16[8,2048,128]{2,1,0:T(8,128)(2,1)} fusion(bf16[8,2048,128]{2,1,0:T(8,128)(2,1)} %bitcast_dynamic-update-slice_fusion.1, s32[]{:T(128)S(6)} %select_n.129, bf16[2048,128]{1,0:T(8,128)(2,1)} %copy-done.18), kind=kLoop, calls=%fused_computation.4 | loop fusion | bytes 1048580 | tf_op jit(solution)/shard_map/dynamic_update_slice | solution.py:414
  131.2 6.6 %project.1 = bf16[8,512,256]{2,1,0:T(8,128)(2,1)S(1)} custom-call(s32[1]{0:T(128)} %bitcast.place, bf16[512,640]{1,0:T(8,128)(2,1)S(1)} %join.1.own, bf16[512,640]{1,0:T(8,128)(2,1)S(1)} %collective-permute-done.11.sib, bf16[8,2048,128]{2,1,0:T(8,128)(2,1)} %bitcast_dynamic-update-slice_fusion.w), custom_call_target="tpu_custom_call" | custom-call | flops 4294967296 | bytes 8388608 | tf_op jit(solution)/shard_map/project/pallas_call | solution.py:373
  137.8 33.5 %all_to_all.20 = bf16[8,512,256]{2,1,0:T(8,128)(2,1)S(1)} all-to-all(bf16[8,512,256]{2,1,0:T(8,128)(2,1)S(1)} %project.1), channel_id=1, replica_groups={{0,2,4,6,8,10,12,14},{1,3,5,7,9,11,13,15},{16,18,20,22,24,26,28,30},{17..., dimensions={0} | all-to-all | bytes 4194304 | tf_op jit(solution)/shard_map/all_to_all | solution.py:400
  171.7 2.1 %collective-permute-start.12 = (bf16[512,128]{1,0:T(8,128)(2,1)S(1)}, bf16[512,128]{1,0:T(8,128)(2,1)S(1)}, u32[]{:S(2)}, u32[]{:S(2)}) collective-permute-start(bf16[512,128]{1,0:T(8,128)(2,1)S(1)} %broadcast_select_fusion.3), channel_id=1, source_target_pairs={{0,1},{1,0},{2,3},{3,2},{4,5},{5,4},{6,7},{7,6},{8,9},{9,8},{10,11... | collective-permute-start | bytes 393224 | tf_op jit(solution)/shard_map/ppermute | solution.py:391
  173.7 1.0 collective-permute-done.12
  (79 shorter events, 10.6 us)
Async XLA Ops:
  0.0 35.3 %copy-start = (f32[4,2048]{1,0:T(4,128)S(1)}, f32[4,2048]{1,0:T(4,128)}, u32[]{:S(2)}) copy-start(f32[4,2048]{1,0:T(4,128)} %param.23) | copy-start | bytes 98308
  1.5 8.3 %collective-permute-start = (bf16[16,256]{1,0:T(8,128)(2,1)S(1)}, bf16[16,256]{1,0:T(8,128)(2,1)S(1)}, u32[]{:S(2)}, u32[]{:S(2)}) collective-permute-start(bf16[16,256]{1,0:T(8,128)(2,1)S(1)} %pad_maximum_fusion.5), channel_id=1, source_target_pairs={{0,16},{16,32},{32,48},{48,64},{64,80},{80,96},{96,112},{112,128},... | collective-permute-start | bytes 24584 | tf_op jit(solution)/shard_map/ppermute | solution.py:395
  5.9 7.2 %collective-permute-start.1 = (bf16[512,256]{1,0:T(8,128)(2,1)}, bf16[512,256]{1,0:T(8,128)(2,1)S(1)}, u32[]{:S(2)}, u32[]{:S(2)}) collective-permute-start(bf16[512,256]{1,0:T(8,128)(2,1)} %param.29), channel_id=1, source_target_pairs={{0,128},{16,144},{32,160},{48,176},{64,192},{80,208},{96,224},{112... | collective-permute-start | bytes 786440 | tf_op jit(solution)/shard_map/ppermute | solution.py:404
  10.7 2.3 %copy-start.20 = (bf16[512,256]{1,0:T(8,128)(2,1)S(1)}, bf16[512,256]{1,0:T(8,128)(2,1)}, u32[]{:S(2)}) copy-start(bf16[512,256]{1,0:T(8,128)(2,1)} %param.29) | copy-start | bytes 786436
  12.7 10.5 %copy-start.21 = (s32[512]{0:T(512)S(1)}, s32[512]{0:T(512)}, u32[]{:S(2)}) copy-start(s32[512]{0:T(512)} %param.16) | copy-start | bytes 6148
  14.0 10.0 %collective-permute-start.2 = (bf16[2,512,128]{2,1,0:T(8,128)(2,1)}, bf16[2,512,128]{2,1,0:T(8,128)(2,1)}, u32[]{:S(2)}, u32[]{:S(2)}) collective-permute-start(bf16[2,512,128]{2,1,0:T(8,128)(2,1)} %get-tuple-element.78), channel_id=1, source_target_pairs={{0,1},{1,0},{2,3},{3,2},{4,5},{5,4},{6,7},{7,6},{8,9},{9,8},{10,11... | collective-permute-start | bytes 786440 | tf_op jit(solution)/shard_map/ppermute | solution.py:391
  16.5 16.3 %copy-start.22 = (f32[8]{0:T(128)S(1)}, f32[8]{0:T(128)}, u32[]{:S(2)}) copy-start(f32[8]{0:T(128)} %param.27) | copy-start | bytes 100
  16.5 54.6 %all-to-all-start = ((bf16[8,800,256]{2,1,0:T(8,128)(2,1)}), bf16[8,800,256]{2,1,0:T(8,128)(2,1)S(1)}, u32[]{:S(2)}, u32[]{:S(2)}) async-start(bf16[8,800,256]{2,1,0:T(8,128)(2,1)} %pad_maximum_fusion), calls=%async_computation | async-start | bytes 6553600 | tf_op jit(solution)/shard_map/all_to_all | solution.py:400
  25.9 16.4 %collective-permute-start.3 = (bf16[2048,128]{1,0:T(8,128)(2,1)}, bf16[2048,128]{1,0:T(8,128)(2,1)}, u32[]{:S(2)}, u32[]{:S(2)}) collective-permute-start(bf16[2048,128]{1,0:T(8,128)(2,1)} %bitcast.10), channel_id=1, source_target_pairs={{0,16},{16,32},{32,48},{48,64},{64,80},{80,96},{96,112},{112,0},{1... | collective-permute-start | bytes 1572872 | tf_op jit(solution)/shard_map/ppermute | solution.py:409
  27.5 14.7 %collective-permute-start.4 = (bf16[2048,128]{1,0:T(8,128)(2,1)}, bf16[2048,128]{1,0:T(8,128)(2,1)}, u32[]{:S(2)}, u32[]{:S(2)}) collective-permute-start(bf16[2048,128]{1,0:T(8,128)(2,1)} %bitcast.10), channel_id=1, source_target_pairs={{0,112},{16,0},{32,16},{48,32},{64,48},{80,64},{96,80},{112,96},{1... | collective-permute-start | bytes 1572872 | tf_op jit(solution)/shard_map/ppermute | solution.py:409
  37.8 41.4 %copy-start.9 = (f32[4,512]{1,0:T(4,128)S(1)}, f32[4,512]{1,0:T(4,128)}, u32[]{:S(2)}) copy-start(f32[4,512]{1,0:T(4,128)} %taps_x) | copy-start | bytes 24580
  37.8 41.4 %copy-start.10 = (f32[512]{0:T(512)S(1)}, f32[512]{0:T(512)}, u32[]{:S(2)}) copy-start(f32[512]{0:T(512)} %param.22) | copy-start | bytes 6148
  37.8 41.4 %copy-start.11 = (f32[8]{0:T(128)S(1)}, f32[8]{0:T(128)}, u32[]{:S(2)}) copy-start(f32[8]{0:T(128)} %param.25) | copy-start | bytes 100
  37.8 41.4 %copy-start.12 = (f32[8]{0:T(128)S(1)}, f32[8]{0:T(128)}, u32[]{:S(2)}) copy-start(f32[8]{0:T(128)} %param.26) | copy-start | bytes 100
  42.2 14.1 %collective-permute-start.5 = (bf16[2048,128]{1,0:T(8,128)(2,1)}, bf16[2048,128]{1,0:T(8,128)(2,1)S(1)}, u32[]{:S(2)}, u32[]{:S(2)}) collective-permute-start(bf16[2048,128]{1,0:T(8,128)(2,1)} %collective-permute-done.3), channel_id=1, source_target_pairs={{0,16},{16,32},{32,48},{48,64},{64,80},{80,96},{96,112},{112,0},{1... | collective-permute-start | bytes 1572872 | tf_op jit(solution)/shard_map/ppermute | solution.py:409
  42.3 14.1 %collective-permute-start.6 = (bf16[2048,128]{1,0:T(8,128)(2,1)}, bf16[2048,128]{1,0:T(8,128)(2,1)S(1)}, u32[]{:S(2)}, u32[]{:S(2)}) collective-permute-start(bf16[2048,128]{1,0:T(8,128)(2,1)} %collective-permute-done.4), channel_id=1, source_target_pairs={{0,112},{16,0},{32,16},{48,32},{64,48},{80,64},{96,80},{112,96},{1... | collective-permute-start | bytes 1572872 | tf_op jit(solution)/shard_map/ppermute | solution.py:409
  56.3 13.0 %collective-permute-start.7 = (bf16[2048,128]{1,0:T(8,128)(2,1)S(1)}, bf16[2048,128]{1,0:T(8,128)(2,1)S(1)}, u32[]{:S(2)}, u32[]{:S(2)}) collective-permute-start(bf16[2048,128]{1,0:T(8,128)(2,1)S(1)} %collective-permute-done.5), channel_id=1, source_target_pairs={{0,16},{16,32},{32,48},{48,64},{64,80},{80,96},{96,112},{112,0},{1... | collective-permute-start | bytes 1572872 | tf_op jit(solution)/shard_map/ppermute | solution.py:409
  56.3 13.9 %collective-permute-start.8 = (bf16[2048,128]{1,0:T(8,128)(2,1)S(1)}, bf16[2048,128]{1,0:T(8,128)(2,1)S(1)}, u32[]{:S(2)}, u32[]{:S(2)}) collective-permute-start(bf16[2048,128]{1,0:T(8,128)(2,1)S(1)} %collective-permute-done.6), channel_id=1, source_target_pairs={{0,112},{16,0},{32,16},{48,32},{64,48},{80,64},{96,80},{112,96},{1... | collective-permute-start | bytes 1572872 | tf_op jit(solution)/shard_map/ppermute | solution.py:409
  69.3 1.0 copy-start.19
  71.1 8.1 %collective-permute-start.9 = (bf16[8,800,256]{2,1,0:T(8,128)(2,1)S(1)}, bf16[8,800,256]{2,1,0:T(8,128)(2,1)S(1)}, u32[]{:S(2)}, u32[]{:S(2)}) collective-permute-start(bf16[8,800,256]{2,1,0:T(8,128)(2,1)S(1)} %all-to-all-done.own), channel_id=1, source_target_pairs={{0,1},{1,0},{2,3},{3,2},{4,5},{5,4},{6,7},{7,6},{8,9},{9,8},{10,11... | collective-permute-start | bytes 9830408 | tf_op jit(solution)/shard_map/ppermute | solution.py:391
  73.7 19.6 %collective-permute-start.10 = (bf16[2048,128]{1,0:T(8,128)(2,1)}, bf16[2048,128]{1,0:T(8,128)(2,1)S(1)}, u32[]{:S(2)}, u32[]{:S(2)}) collective-permute-start(bf16[2048,128]{1,0:T(8,128)(2,1)} %copy-done.19), channel_id=1, source_target_pairs={{0,16},{16,32},{32,48},{48,64},{64,80},{80,96},{96,112},{112,0},{1... | collective-permute-start | bytes 1572872 | tf_op jit(solution)/shard_map/ppermute | solution.py:409
  79.2 1.0 copy-start.5
  80.2 2.2 %copy-start.8 = (bf16[4096,512]{1,0:T(8,128)(2,1)S(1)}, bf16[4096,512]{1,0:T(8,128)(2,1)}, u32[]{:S(2)}) copy-start(bf16[4096,512]{1,0:T(8,128)(2,1)} %w_x.1) | copy-start | bytes 12582916
  82.3 11.0 %copy-start.3 = (bf16[8,800,256]{2,1,0:T(8,128)(2,1)}, bf16[8,800,256]{2,1,0:T(8,128)(2,1)S(1)}, u32[]{:S(2)}) copy-start(bf16[8,800,256]{2,1,0:T(8,128)(2,1)S(1)} %collective-permute-done.9.sib) | copy-start | bytes 9830404
  93.3 0.8 copy-start.18
  94.2 14.6 %all-to-all-start.1 = ((bf16[16,16,512]{2,1,0:T(8,128)(2,1)}), bf16[16,16,512]{2,1,0:T(8,128)(2,1)}, u32[]{:S(2)}, u32[]{:S(2)}) async-start(bf16[16,16,512]{2,1,0:T(8,128)(2,1)} %get-tuple-element.58), calls=%async_computation.1 | async-start | bytes 524288 | tf_op jit(solution)/shard_map/all_to_all | solution.py:428
  99.9 2.2 %copy-start.1 = (bf16[4096,512]{1,0:T(8,128)(2,1)S(1)}, bf16[4096,512]{1,0:T(8,128)(2,1)}, u32[]{:S(2)}) copy-start(bf16[4096,512]{1,0:T(8,128)(2,1)} %w_z.1) | copy-start | bytes 12582916
  102.0 1.9 %copy-start.4 = (bf16[8,800,256]{2,1,0:T(8,128)(2,1)S(1)}, bf16[8,800,256]{2,1,0:T(8,128)(2,1)}, u32[]{:S(2)}) copy-start(bf16[8,800,256]{2,1,0:T(8,128)(2,1)} %copy-done.3) | copy-start | bytes 9830404
  104.0 14.1 %copy-start.16 = (bf16[128,512]{1,0:T(8,128)(2,1)S(1)}, bf16[128,512]{1,0:T(8,128)(2,1)}, u32[]{:S(2)}) copy-start(bf16[128,512]{1,0:T(8,128)(2,1)} %get-tuple-element.67.s0) | copy-start | bytes 393220
  104.0 14.1 %copy-start.17 = (f32[16,512]{1,0:T(8,128)S(1)}, f32[16,512]{1,0:T(8,128)}, u32[]{:S(2)}) copy-start(f32[16,512]{1,0:T(8,128)} %get-tuple-element.66.hrow) | copy-start | bytes 98308
  104.0 21.6 %copy-start.7 = (f32[512]{0:T(512)S(1)}, f32[512]{0:T(512)}, u32[]{:S(2)}) copy-start(f32[512]{0:T(512)} %param.28) | copy-start | bytes 6148
  108.8 16.8 %copy-start.2 = (f32[512,512]{1,0:T(8,128)S(1)}, f32[512,512]{1,0:T(8,128)}, u32[]{:S(2)}) copy-start(f32[512,512]{1,0:T(8,128)} %gate.1.gates) | copy-start | bytes 3145732
  110.6 15.0 %all-to-all-start.2 = ((bf16[16,8,512]{2,1,0:T(8,128)(2,1)}), bf16[16,8,512]{2,1,0:T(8,128)(2,1)S(1)}, u32[]{:S(2)}, u32[]{:S(2)}) async-start(bf16[16,8,512]{2,1,0:T(8,128)(2,1)} %bitcast.32), calls=%async_computation.2 | async-start | bytes 262144 | tf_op jit(solution)/shard_map/all_to_all | solution.py:428
  118.1 1.0 copy-start.6
  119.1 1.0 copy-start.13
  120.1 0.9 copy-start.14
  121.1 0.9 copy-start.15
  126.9 4.2 %collective-permute-start.11 = (bf16[512,640]{1,0:T(8,128)(2,1)S(1)}, bf16[512,640]{1,0:T(8,128)(2,1)S(1)}, u32[]{:S(2)}, u32[]{:S(2)}) collective-permute-start(bf16[512,640]{1,0:T(8,128)(2,1)S(1)} %join.1.own), channel_id=1, source_target_pairs={{0,1},{1,0},{2,3},{3,2},{4,5},{5,4},{6,7},{7,6},{8,9},{9,8},{10,11... | collective-permute-start | bytes 1966088 | tf_op jit(solution)/shard_map/ppermute | solution.py:391
  171.7 3.0 %collective-permute-start.12 = (bf16[512,128]{1,0:T(8,128)(2,1)S(1)}, bf16[512,128]{1,0:T(8,128)(2,1)S(1)}, u32[]{:S(2)}, u32[]{:S(2)}) collective-permute-start(bf16[512,128]{1,0:T(8,128)(2,1)S(1)} %broadcast_select_fusion.3), channel_id=1, source_target_pairs={{0,1},{1,0},{2,3},{3,2},{4,5},{5,4},{6,7},{7,6},{8,9},{9,8},{10,11... | collective-permute-start | bytes 393224 | tf_op jit(solution)/shard_map/ppermute | solution.py:391
  174.8 0.7 copy-start.23
